TPU v7x, 32 devices: a whole 2x2x4 slice. The times are simulated.
32 devices in a mesh: img: 4 (over y, x), row: 8 (over z, core).
Axes of the slice: x: 2, y: 2, z: 4, core: 2. Of those that a mesh axis runs over, the one named last changes fastest.
Arguments:
- pixels: bfloat16 [8, 32, 64, 256], P('img', 'row'), may hold values from -6 to 6
- heights: int32 [8], P('img'), may hold values from 1 to 32, as said below
- timesteps: int32 [8], P('img'), may hold values from 0 to 999
- norm1_gain: bfloat16 [256], replicated, may hold values from 0.25 to 1.75
- norm1_bias: bfloat16 [256], replicated, may hold values from -1.75 to 1.75
- conv1_weight: bfloat16 [3, 3, 256, 256], replicated, may hold values from -0.125 to 0.125
- conv1_bias: bfloat16 [256], replicated, may hold values from -3 to 3
- time_weight: bfloat16 [1024, 512], replicated, may hold values from -0.1875 to 0.1875
- time_bias: bfloat16 [512], replicated, may hold values from -3 to 3
- norm2_gain: bfloat16 [256], replicated, may hold values from 0.25 to 1.75
- norm2_bias: bfloat16 [256], replicated, may hold values from -1.75 to 1.75
- conv2_weight: bfloat16 [3, 3, 256, 256], replicated, may hold values from -0.125 to 0.125
- conv2_bias: bfloat16 [256], replicated, may hold values from -3 to 3
- norm3_gain: bfloat16 [256], replicated, may hold values from 0.25 to 1.75
- norm3_bias: bfloat16 [256], replicated, may hold values from -1.75 to 1.75
- qkv_weight: bfloat16 [256, 768], replicated, may hold values from -0.375 to 0.375
- qv_bias: bfloat16 [512], replicated, may hold values from -3 to 3
- out_weight: bfloat16 [256, 256], replicated, may hold values from -7 to 7
- out_bias: bfloat16 [256], replicated, may hold values from -3 to 3
- grad_out: bfloat16 [8, 32, 64, 256], P('img', 'row'), may hold values from -6 to 6
Outputs:
- block_out: bfloat16 [8, 32, 64, 256], P('img', 'row')
- grad_pixels: bfloat16 [8, 32, 64, 256], P('img', 'row')
- norm1_gain_grad: float32 [256], replicated
- norm1_bias_grad: float32 [256], replicated
- conv1_weight_grad: float32 [3, 3, 256, 256], replicated
- conv1_bias_grad: float32 [256], replicated
- time_weight_grad: float32 [1024, 512], replicated
- time_bias_grad: float32 [512], replicated
- norm2_gain_grad: float32 [256], replicated
- norm2_bias_grad: float32 [256], replicated
- conv2_weight_grad: float32 [3, 3, 256, 256], replicated
- conv2_bias_grad: float32 [256], replicated
- norm3_gain_grad: float32 [256], replicated
- norm3_bias_grad: float32 [256], replicated
- qkv_weight_grad: float32 [256, 768], replicated
- qv_bias_grad: float32 [512], replicated
- out_weight_grad: float32 [256, 256], replicated
- out_bias_grad: float32 [256], replicated
Inputs may be any that keep to these rules, and one draw needn't show every extreme that they name: `heights`: each image has at least one valid row; in every block of 2 consecutive images one image has all 32 rows valid.
All inputs are finite; a program needn't handle non-finite values.
Results may differ from a plain program's by a relative error of at most 0.015.
Values may be sent and summed in bfloat16 or wider, within the bound.
No kernel may reach another device: no remote copies, remote signals or barrier semaphores. Data moves between devices by JAX's collectives and lax.ppermute only.
A program may use at most 384 MiB of HBM per device.

v0:
```python
import math

import jax
import jax.numpy as jnp
from jax import lax
from jax.sharding import PartitionSpec as P

GROUPS = 32
HEADS = 4


EPSILON = 1e-05
MASKED = -1000000000.0
PRECISE = lax.Precision.HIGHEST


def with_halo(cells, sides, width):
    for axis, dim in sides:
        count = lax.axis_size(axis)
        ends = count - 1
        head = lax.slice_in_dim(cells, 0, width, axis=dim)
        tail = lax.slice_in_dim(cells, cells.shape[dim] - width, cells.shape[dim], axis=dim)
        cells = jnp.concatenate(
            [
                lax.ppermute(tail, axis, [(i, (i + 1) % count) for i in range(ends)]),
                cells,
                lax.ppermute(head, axis, [((i + 1) % count, i) for i in range(ends)]),
            ],
            axis=dim,
        )
    return cells


def embed_steps(timesteps, time_width):
    half_dim = time_width // 2
    frequency = jnp.exp(-math.log(10000.0) * jnp.arange(half_dim, dtype=jnp.float32) / half_dim)
    angles = timesteps.astype(jnp.float32)[:, None] * frequency[None, :]
    return jnp.concatenate([jnp.cos(angles), jnp.sin(angles)], axis=1)


def silu_slope(pre_act):
    sigmoid = jax.nn.sigmoid(pre_act)
    return sigmoid * (1.0 + pre_act * (1.0 - sigmoid))


def with_rims(field_in):
    return with_halo(field_in, (("row", 1),), 1)


def conv_rows(padded, kernel):
    return lax.conv_general_dilated(
        padded,
        kernel,
        (1, 1),
        ((0, 0), (1, 1)),
        dimension_numbers=("NHWC", "HWIO", "NHWC"),
        preferred_element_type=jnp.float32,
    )


def flipped(kernel):
    return jnp.transpose(kernel[::-1, ::-1], (0, 1, 3, 2))


def kernel_grad(padded, grad_field):
    row_count = grad_field.shape[1]
    col_count = grad_field.shape[2]
    widened = jnp.pad(padded, ((0, 0), (0, 0), (1, 1), (0, 0)))
    tap_rows = []
    for tap_row in range(3):
        tap_line = []
        for tap_col in range(3):
            window = widened[:, tap_row : tap_row + row_count, tap_col : tap_col + col_count, :]
            tap_line.append(
                jnp.einsum("brwc,brwd->cd", window, grad_field, preferred_element_type=jnp.float32)
            )
        tap_rows.append(jnp.stack(tap_line))
    return jnp.stack(tap_rows)


def norm_forward(field_in, cell_mask, cell_count, group_count):
    shaped = field_in.reshape(field_in.shape[:3] + (group_count, field_in.shape[3] // group_count))
    first_sum = lax.psum(jnp.sum(shaped * cell_mask, axis=(1, 2, 4)), "row")
    center = first_sum / cell_count[:, None]
    centred = shaped - center[:, None, None, :, None]
    spread_sum = lax.psum(jnp.sum(jnp.square(centred * cell_mask), axis=(1, 2, 4)), "row")
    spread = spread_sum / cell_count[:, None]
    inverse = lax.rsqrt(spread + EPSILON)
    return (centred * inverse[:, None, None, :, None], inverse)


def norm_backward(grad_normed, normalized, inverse, gain_in, cell_mask, cell_count):
    full_shape = grad_normed.shape
    flat_norm = normalized.reshape(full_shape)
    gain_grad = jnp.sum(grad_normed * flat_norm, axis=(0, 1, 2))
    shift_grad = jnp.sum(grad_normed, axis=(0, 1, 2))
    scaled = (grad_normed * gain_in).reshape(normalized.shape)
    sum_plain, sum_cross = lax.psum(
        (
            jnp.sum(scaled * cell_mask, axis=(1, 2, 4)),
            jnp.sum(scaled * normalized * cell_mask, axis=(1, 2, 4)),
        ),
        "row",
    )
    mean_plain = sum_plain / cell_count[:, None]
    mean_cross = sum_cross / cell_count[:, None]
    grad_in = (
        (
            scaled
            - mean_plain[:, None, None, :, None]
            - normalized * mean_cross[:, None, None, :, None]
        )
        * inverse[:, None, None, :, None]
        * cell_mask
    )
    return (grad_in.reshape(full_shape), gain_grad, shift_grad)


def local(
    pixels,
    heights,
    timesteps,
    norm1_gain,
    norm1_bias,
    conv1_weight,
    conv1_bias,
    time_weight,
    time_bias,
    norm2_gain,
    norm2_bias,
    conv2_weight,
    conv2_bias,
    norm3_gain,
    norm3_bias,
    qkv_weight,
    qv_bias,
    out_weight,
    out_bias,
    grad_out,
):
    image_count, row_count, col_count, channels = pixels.shape
    group_count = GROUPS
    head_count = HEADS
    head_width = channels // head_count
    query_count = row_count * col_count
    scaling = head_width ** (-0.5)
    head_shape = (image_count, query_count, head_count, head_width)
    row_ids = lax.axis_index("row") * row_count + jnp.arange(row_count, dtype=jnp.int32)
    row_valid = row_ids[None, :] < heights[:, None]
    row_mask = row_valid.astype(jnp.float32)
    cell_rows = row_mask[:, :, None, None]
    cell_mask = row_mask[:, :, None, None, None]
    own_valid = jnp.repeat(row_valid, col_count, axis=1)[:, None, None, :]
    cell_count = heights.astype(jnp.float32) * (col_count * (channels // group_count))
    gain_one = norm1_gain.astype(jnp.float32)
    gain_two = norm2_gain.astype(jnp.float32)
    gain_three = norm3_gain.astype(jnp.float32)
    field_in = pixels.astype(jnp.float32)
    normed_one, inverse_one = norm_forward(field_in, cell_mask, cell_count, group_count)
    pre_one = normed_one.reshape(field_in.shape) * gain_one + norm1_bias.astype(jnp.float32)
    act_one = (jax.nn.silu(pre_one) * cell_rows).astype(jnp.bfloat16)
    padded_one = with_rims(act_one)
    conv_one = conv_rows(padded_one, conv1_weight) + conv1_bias.astype(jnp.float32)
    time_act = jax.nn.silu(embed_steps(timesteps, time_weight.shape[0]))
    shifts = jnp.dot(
        time_act, time_weight.astype(jnp.float32), precision=PRECISE
    ) + time_bias.astype(jnp.float32)
    scale_part = 1.0 + shifts[:, None, None, :channels]
    shift_part = shifts[:, None, None, channels:]
    normed_two, inverse_two = norm_forward(conv_one, cell_mask, cell_count, group_count)
    affine_two = normed_two.reshape(field_in.shape) * gain_two + norm2_bias.astype(jnp.float32)
    pre_two = affine_two * scale_part + shift_part
    act_two = (jax.nn.silu(pre_two) * cell_rows).astype(jnp.bfloat16)
    padded_two = with_rims(act_two)
    residual = field_in + (conv_rows(padded_two, conv2_weight) + conv2_bias.astype(jnp.float32))
    normed_three, inverse_three = norm_forward(residual, cell_mask, cell_count, group_count)
    act_three = (
        normed_three.reshape(field_in.shape) * gain_three + norm3_bias.astype(jnp.float32)
    ).astype(jnp.bfloat16)
    projected = jnp.einsum(
        "brwc,cd->brwd", act_three, qkv_weight, preferred_element_type=jnp.float32
    )
    qv_float = qv_bias.astype(jnp.float32)
    queries = (projected[..., :channels] + qv_float[:channels]).astype(jnp.bfloat16)
    keys_own = projected[..., channels : 2 * channels].astype(jnp.bfloat16)
    values_own = (projected[..., 2 * channels :] + qv_float[channels:]).astype(jnp.bfloat16)
    query_heads = queries.reshape(head_shape)
    key_heads = keys_own.reshape(head_shape)
    value_heads = values_own.reshape(head_shape)

    def flatten_rows(piece_arr):
        return piece_arr.reshape(
            image_count, piece_arr.shape[1] * col_count, head_count, head_width
        )

    def key_mask(span_rows):
        key_rows = jnp.arange(span_rows, dtype=jnp.int32)
        return jnp.repeat(key_rows[None, :] < heights[:, None], col_count, axis=1)[:, None, None, :]

    top_init = jnp.full((image_count, query_count, head_count), MASKED, jnp.float32)
    piece_keys = lax.all_gather(keys_own, "row", axis=1, tiled=True)
    piece_values = lax.all_gather(values_own, "row", axis=1, tiled=True)
    key_valid = key_mask(piece_keys.shape[1])
    scores = (
        jnp.einsum(
            "bqhd,bkhd->bqhk",
            query_heads,
            flatten_rows(piece_keys),
            preferred_element_type=jnp.float32,
        )
        * scaling
    )
    scores = jnp.where(key_valid, scores, MASKED)
    new_top = jnp.maximum(top_init, jnp.max(scores, axis=3))
    weights = jnp.where(key_valid, jnp.exp(scores - new_top[..., None]), 0.0)
    running_total = jnp.sum(weights, axis=3)
    running_acc = jnp.einsum(
        "bqhk,bkhd->bqhd",
        weights.astype(jnp.bfloat16),
        flatten_rows(piece_values),
        preferred_element_type=jnp.float32,
    )
    attn_float = running_acc / running_total[..., None]
    log_total = new_top + jnp.log(running_total)
    attended = attn_float.reshape(pixels.shape).astype(jnp.bfloat16)
    output_proj = jnp.einsum(
        "brwc,cd->brwd", attended, out_weight, preferred_element_type=jnp.float32
    ) + out_bias.astype(jnp.float32)
    block_out = ((residual + output_proj) * cell_rows).astype(jnp.bfloat16)
    grad_proj = grad_out.astype(jnp.float32) * cell_rows
    grad_proj_low = grad_proj.astype(jnp.bfloat16)
    out_weight_grad = jnp.einsum(
        "brwc,brwd->cd", attended, grad_proj_low, preferred_element_type=jnp.float32
    )
    out_bias_grad = jnp.sum(grad_proj, axis=(0, 1, 2))
    grad_attended = jnp.einsum(
        "brwd,cd->brwc", grad_proj_low, out_weight, preferred_element_type=jnp.float32
    ).astype(jnp.bfloat16)
    grad_heads = grad_attended.reshape(head_shape)
    delta_own = jnp.sum(grad_heads.astype(jnp.float32) * attn_float, axis=3)
    stat_shape = (image_count, row_count, col_count, head_count)
    all_lse, all_delta = (
        lax.all_gather(log_total.reshape(stat_shape), "row", axis=1, tiled=True),
        lax.all_gather(delta_own.reshape(stat_shape), "row", axis=1, tiled=True),
    )
    piece_keys = lax.all_gather(keys_own, "row", axis=1, tiled=True)
    piece_values = lax.all_gather(values_own, "row", axis=1, tiled=True)
    flat_keys = flatten_rows(piece_keys)
    key_valid = key_mask(piece_keys.shape[1])
    scores = (
        jnp.einsum("bqhd,bkhd->bqhk", query_heads, flat_keys, preferred_element_type=jnp.float32)
        * scaling
    )
    soft_weights = jnp.where(key_valid, jnp.exp(scores - log_total[..., None]), 0.0)
    grad_probs = jnp.einsum(
        "bqhd,bkhd->bqhk",
        grad_heads,
        flatten_rows(piece_values),
        preferred_element_type=jnp.float32,
    )
    grad_scores = (soft_weights * (grad_probs - delta_own[..., None])).astype(jnp.bfloat16)
    grad_query_sum = jnp.einsum(
        "bqhk,bkhd->bqhd", grad_scores, flat_keys, preferred_element_type=jnp.float32
    )
    piece_queries = lax.all_gather(queries, "row", axis=1, tiled=True)
    piece_grads = lax.all_gather(grad_attended, "row", axis=1, tiled=True)
    flat_queries = flatten_rows(piece_queries)
    flat_grads = flatten_rows(piece_grads)
    span_rows = piece_queries.shape[1]
    piece_lse = all_lse.reshape(image_count, span_rows * col_count, head_count)
    piece_delta = all_delta.reshape(image_count, span_rows * col_count, head_count)
    scores = (
        jnp.einsum("bqhd,bkhd->bqhk", flat_queries, key_heads, preferred_element_type=jnp.float32)
        * scaling
    )
    soft_weights = jnp.where(own_valid, jnp.exp(scores - piece_lse[..., None]), 0.0)
    value_term = jnp.einsum(
        "bqhk,bqhd->bkhd",
        soft_weights.astype(jnp.bfloat16),
        flat_grads,
        preferred_element_type=jnp.float32,
    )
    grad_probs = jnp.einsum(
        "bqhd,bkhd->bqhk", flat_grads, value_heads, preferred_element_type=jnp.float32
    )
    grad_scores = (soft_weights * (grad_probs - piece_delta[..., None])).astype(jnp.bfloat16)
    key_term = jnp.einsum(
        "bqhk,bqhd->bkhd", grad_scores, flat_queries, preferred_element_type=jnp.float32
    )
    key_term, value_term = (key_term, value_term)
    grad_queries = (grad_query_sum * scaling).reshape(pixels.shape).astype(jnp.bfloat16)
    grad_keys = (key_term * scaling).reshape(pixels.shape).astype(jnp.bfloat16)
    grad_values = value_term.reshape(pixels.shape).astype(jnp.bfloat16)
    grad_projected = jnp.concatenate([grad_queries, grad_keys, grad_values], axis=3)
    qkv_weight_grad = jnp.einsum(
        "brwc,brwd->cd", act_three, grad_projected, preferred_element_type=jnp.float32
    )
    qv_bias_grad = jnp.concatenate(
        [
            jnp.sum(grad_queries.astype(jnp.float32), axis=(0, 1, 2)),
            jnp.sum(grad_values.astype(jnp.float32), axis=(0, 1, 2)),
        ]
    )
    grad_act_three = jnp.einsum(
        "brwd,cd->brwc", grad_projected, qkv_weight, preferred_element_type=jnp.float32
    )
    grad_res_attn, norm3_gain_grad, norm3_bias_grad = norm_backward(
        grad_act_three, normed_three, inverse_three, gain_three, cell_mask, cell_count
    )
    grad_residual = grad_proj + grad_res_attn
    grad_conv_two = grad_residual.astype(jnp.bfloat16)
    conv2_bias_grad = jnp.sum(grad_residual, axis=(0, 1, 2))
    conv2_weight_grad = kernel_grad(padded_two, grad_conv_two)
    grad_act_two = conv_rows(with_rims(grad_conv_two), flipped(conv2_weight)) * cell_rows
    grad_pre_two = grad_act_two * silu_slope(pre_two)
    scale_grad = jnp.sum(grad_pre_two * affine_two, axis=(1, 2))
    shift_grad = jnp.sum(grad_pre_two, axis=(1, 2))
    shift_grads = jnp.concatenate([scale_grad, shift_grad], axis=1)
    grad_conv_one, norm2_gain_grad, norm2_bias_grad = norm_backward(
        grad_pre_two * scale_part, normed_two, inverse_two, gain_two, cell_mask, cell_count
    )
    conv_one_low = grad_conv_one.astype(jnp.bfloat16)
    conv1_bias_grad = jnp.sum(grad_conv_one, axis=(0, 1, 2))
    conv1_weight_grad = kernel_grad(padded_one, conv_one_low)
    grad_act_one = conv_rows(with_rims(conv_one_low), flipped(conv1_weight)) * cell_rows
    grad_pre_one = grad_act_one * silu_slope(pre_one)
    grad_field_norm, norm1_gain_grad, norm1_bias_grad = norm_backward(
        grad_pre_one, normed_one, inverse_one, gain_one, cell_mask, cell_count
    )
    grad_pixels = (grad_residual + grad_field_norm).astype(jnp.bfloat16)
    time_weight_grad = jnp.dot(time_act.T, shift_grads, precision=PRECISE)
    time_bias_grad = jnp.sum(shift_grads, axis=0)
    summed = lax.psum(
        (
            norm1_gain_grad,
            norm1_bias_grad,
            conv1_weight_grad,
            conv1_bias_grad,
            time_weight_grad,
            time_bias_grad,
            norm2_gain_grad,
            norm2_bias_grad,
            conv2_weight_grad,
            conv2_bias_grad,
            norm3_gain_grad,
            norm3_bias_grad,
            qkv_weight_grad,
            qv_bias_grad,
            out_weight_grad,
            out_bias_grad,
        ),
        ("img", "row"),
    )
    return (
        block_out,
        grad_pixels,
        summed[0],
        summed[1],
        summed[2],
        summed[3],
        summed[4],
        summed[5],
        summed[6],
        summed[7],
        summed[8],
        summed[9],
        summed[10],
        summed[11],
        summed[12],
        summed[13],
        summed[14],
        summed[15],
    )


def solution(mesh):
    placed = (
        P("img", "row", None, None),
        P("img"),
        P("img"),
        P(),
        P(),
        P(),
        P(),
        P(),
        P(),
        P(),
        P(),
        P(),
        P(),
        P(),
        P(),
        P(),
        P(),
        P(),
        P(),
        P("img", "row", None, None),
    )
    return jax.shard_map(
        local,
        mesh=mesh,
        in_specs=placed,
        out_specs=(
            P("img", "row", None, None),
            P("img", "row", None, None),
            P(),
            P(),
            P(),
            P(),
            P(),
            P(),
            P(),
            P(),
            P(),
            P(),
            P(),
            P(),
            P(),
            P(),
            P(),
            P(),
        ),
        check_vma=False,
    )
```

profile of v0, /device:TPU:0, one launch (start us, length us, event | category | flops | bytes accessed | tf_op | source)
XLA Modules:
  0.0 593.7 jit_solution(13019425545235126055)
XLA Ops:
  10.1 18.1 %psum.196 = f32[2,32]{1,0:T(2,128)S(1)} all-reduce(f32[2,32]{1,0:T(2,128)S(1)} %reduce_sum.285), channel_id=1, replica_groups=mesh['img'=4,'row'=8] {'row'}, use_global_device_ids=true, to_apply=%region_2.0 | all-reduce | flops 64 | bytes 512 | tf_op jit(solution)/shard_map/psum | solution.py:83
  29.7 13.6 %psum.197 = f32[2,32]{1,0:T(2,128)S(1)} all-reduce(f32[2,32]{1,0:T(2,128)S(1)} %reduce_sum.288), channel_id=1, replica_groups=mesh['img'=4,'row'=8] {'row'}, use_global_device_ids=true, to_apply=%region_5.6 | all-reduce | flops 64 | bytes 512 | tf_op jit(solution)/shard_map/psum | solution.py:86
  49.2 2.0 convolution_convert_fusion
  56.0 15.3 %psum.198 = f32[2,32]{1,0:T(2,128)S(1)} all-reduce(f32[2,32]{1,0:T(2,128)S(1)} %reduce_sum.348), channel_id=1, replica_groups=mesh['img'=4,'row'=8] {'row'}, use_global_device_ids=true, to_apply=%region_8.9 | all-reduce | flops 64 | bytes 512 | tf_op jit(solution)/shard_map/psum | solution.py:83
  72.5 13.8 %psum.199 = f32[2,32]{1,0:T(2,128)S(1)} all-reduce(f32[2,32]{1,0:T(2,128)S(1)} %reduce_sum.351), channel_id=1, replica_groups=mesh['img'=4,'row'=8] {'row'}, use_global_device_ids=true, to_apply=%region_11.12 | all-reduce | flops 64 | bytes 512 | tf_op jit(solution)/shard_map/psum | solution.py:86
  86.9 2.8 multiply_convert_fusion
  99.1 16.0 %psum.200 = f32[2,32]{1,0:T(2,128)S(1)} all-reduce(f32[2,32]{1,0:T(2,128)S(1)} %reduce_sum.354), channel_id=1, replica_groups=mesh['img'=4,'row'=8] {'row'}, use_global_device_ids=true, to_apply=%region_14.15 | all-reduce | flops 64 | bytes 512 | tf_op jit(solution)/shard_map/psum | solution.py:83
  115.7 13.6 %psum.201 = f32[2,32]{1,0:T(2,128)S(1)} all-reduce(f32[2,32]{1,0:T(2,128)S(1)} %reduce_sum.357), channel_id=1, replica_groups=mesh['img'=4,'row'=8] {'row'}, use_global_device_ids=true, to_apply=%region_17.18 | all-reduce | flops 64 | bytes 512 | tf_op jit(solution)/shard_map/psum | solution.py:86
  133.0 2.1 fusion.108
  136.7 2.0 copy.267
  139.4 2.1 reshape.253
  141.4 2.1 reshape.254
  144.7 7.1 %reshape.368 = bf16[2,2048,4,64]{3,2,1,0:T(4,128)(2,1)} reshape(bf16[2,32,64,256]{3,2,1,0:T(8,128)(2,1)} %all-gather.11.cloned.1.call-done) | data formatting | bytes 4194304 | tf_op jit(solution)/shard_map/reshape | solution.py:192
  151.8 6.9 %copy.337 = bf16[2,2048,4,64]{1,3,2,0:T(8,128)(2,1)} copy(bf16[2,2048,4,64]{3,2,1,0:T(4,128)(2,1)} %reshape.368) | data formatting | bytes 4194304 | tf_op jit(solution)/shard_map/reshape | solution.py:192
  160.4 7.1 %reshape.364 = bf16[2,2048,4,64]{3,2,1,0:T(4,128)(2,1)} reshape(bf16[2,32,64,256]{3,2,1,0:T(8,128)(2,1)} %all-gather.7.cloned.1.call-done) | data formatting | bytes 4194304 | tf_op jit(solution)/shard_map/reshape | solution.py:192
  167.4 7.0 %copy.333 = bf16[2,2048,4,64]{1,3,2,0:T(8,128)(2,1)} copy(bf16[2,2048,4,64]{3,2,1,0:T(4,128)(2,1)} %reshape.364) | data formatting | bytes 4194304 | tf_op jit(solution)/shard_map/reshape | solution.py:192
  174.4 9.1 %fusion.8 = (f32[2,256,4]{1,2,0:T(4,128)S(1)}, f32[2,4,2048,256]{3,2,1,0:T(8,128)}) fusion(pred[2,2048]{1,0:T(4,128)(4,1)S(1)} %broadcast_in_dim.37, bf16[2,2048,4,64]{1,3,2,0:T(8,128)(2,1)} %copy.333, bf16[2,256,4,64]{3,2,1,0:T(4,128)(2,1)} %reshape.250), kind=kOutput, calls=%fused_computation.14 | convolution fusion | flops 549451776 | bytes 19148800 | tf_op jit(solution)/shard_map/bqhd,bkhd->bqhk/dot_general | solution.py:205
  183.6 7.6 %all-gather.5.cloned.1.call-done = bf16[2,32,64,256]{3,2,1,0:T(8,128)(2,1)} async-done(((bf16[2,4,64,256]{3,2,1,0:T(8,128)(2,1)}), bf16[2,32,64,256]{3,2,1,0:T(8,128)(2,1)}) %all-gather.5.cloned.1.call-update) | async-done | bytes 2097168 | tf_op jit(solution)/shard_map/all_gather | solution.py:202
  191.2 7.1 %reshape.363 = bf16[2,2048,4,64]{3,2,1,0:T(4,128)(2,1)} reshape(bf16[2,32,64,256]{3,2,1,0:T(8,128)(2,1)} %all-gather.5.cloned.1.call-done) | data formatting | bytes 4194304 | tf_op jit(solution)/shard_map/reshape | solution.py:192
  198.2 7.1 %copy.332 = bf16[2,2048,4,64]{1,3,2,0:T(8,128)(2,1)} copy(bf16[2,2048,4,64]{3,2,1,0:T(4,128)(2,1)} %reshape.363) | data formatting | bytes 4194304 | tf_op jit(solution)/shard_map/reshape | solution.py:192
  205.3 8.2 %fusion.10 = f32[2,256,4]{1,2,0:T(4,128)S(1)} fusion(f32[2,4,2048,256]{3,2,1,0:T(8,128)} %get-tuple-element.97, f32[2,256,4]{1,2,0:T(4,128)S(1)} %broadcast_maximum_fusion, pred[2,2048]{1,0:T(4,128)(4,1)S(1)} %broadcast_in_dim.37), kind=kLoop, calls=%fused_computation.16 | loop fusion | flops 20969472 | bytes 16797696 | tf_op jit(solution)/shard_map/reduce_sum | solution.py:216
  214.2 9.4 %multiply_reduce_fusion.4 = (f32[2,256,4]{1,2,0:T(4,128)S(1)}, bf16[2,256,4,64]{1,3,2,0:T(8,128)(2,1)}) fusion(bf16[2,256,4,64]{1,3,2,0:T(8,128)(2,1)S(1)} %copy-done.39, f32[2,256,4]{1,2,0:T(4,128)S(1)} %fusion.10, bf16[2,2048,4,64]{1,3,2,0:T(8,128)(2,1)} %copy.332, f32[2,4,2048,256]{3,2,1,0:T(8,128)} %get-tuple-element.97, ...), kind=kOutput, calls=%fused_computation.171 | convolution fusion | flops 558495744 | bytes 19427328 | tf_op jit(solution)/shard_map/bqhk,bkhd->bqhd/dot_general | solution.py:217
  224.2 12.4 %convert_reduce_fusion.1 = (f32[4,64]{1,0:T(4,128)}, bf16[2,4,64,256]{3,2,1,0:T(8,128)(2,1)}) fusion(bf16[2,2048,4,64]{1,3,2,0:T(8,128)(2,1)} %copy.333, f32[2,4,2048,256]{3,2,1,0:T(8,128)} %get-tuple-element.97, f32[2,256,4]{1,2,0:T(4,128)S(1)} %get-tuple-element.68, f32[2,256,4]{1,2,0:T(4,128)S(1)} %log_add_fusion, ...), kind=kOutput, calls=%fused_computation.165 | convolution fusion | flops 1099431680 | bytes 21517312 | tf_op jit(solution)/shard_map/bqhk,bkhd->bqhd/dot_general | solution.py:262
  236.7 2.0 reshape.366
  240.7 13.9 %all_gather.23 = f32[2,32,64,4]{2,3,0,1:T(4,128)S(1)} all-gather(f32[2,4,64,4]{2,3,0,1:T(4,128)S(1)} %copy.273), channel_id=1, replica_groups=mesh['img'=4,'row'=8] {'row'}, dimensions={1}, use_global_device_ids=true | all-gather | bytes 73728 | tf_op jit(solution)/shard_map/all_gather | solution.py:243
  255.4 7.1 %reshape.367 = bf16[2,2048,4,64]{3,2,1,0:T(4,128)(2,1)} reshape(bf16[2,32,64,256]{3,2,1,0:T(8,128)(2,1)} %all-gather.9.cloned.1.call-done) | data formatting | bytes 4194304 | tf_op jit(solution)/shard_map/reshape | solution.py:192
  262.5 6.9 %copy.336 = bf16[2,2048,4,64]{1,3,2,0:T(8,128)(2,1)} copy(bf16[2,2048,4,64]{3,2,1,0:T(4,128)(2,1)} %reshape.367) | data formatting | bytes 4194304 | tf_op jit(solution)/shard_map/reshape | solution.py:192
  269.5 14.0 %all_gather.25 = f32[2,32,64,4]{2,3,0,1:T(4,128)S(1)} all-gather(f32[2,4,64,4]{2,3,0,1:T(4,128)S(1)} %copy.277), channel_id=1, replica_groups=mesh['img'=4,'row'=8] {'row'}, dimensions={1}, use_global_device_ids=true | all-gather | bytes 73728 | tf_op jit(solution)/shard_map/all_gather | solution.py:244
  284.2 10.0 %fusion.112 = f32[2,4,256,2048]{3,2,1,0:T(8,128)} fusion(bf16[2,2048,4,64]{1,3,2,0:T(8,128)(2,1)} %copy.336, bf16[2,256,4,64]{3,2,1,0:T(4,128)(2,1)} %reshape.253), kind=kOutput, calls=%fused_computation.160 | convolution fusion | flops 536870912 | bytes 19136512 | tf_op jit(solution)/shard_map/bqhd,bkhd->bqhk/dot_general | solution.py:273
  294.2 9.0 %convert_reduce_fusion = (f32[4,64]{1,0:T(4,128)}, bf16[2,4,64,256]{3,2,1,0:T(8,128)(2,1)}) fusion(bf16[2,2048,4,64]{1,3,2,0:T(8,128)(2,1)S(1)} %copy-done.17, f32[2,4,256,2048]{3,2,1,0:T(8,128)} %fusion.112, f32[2,2048,4]{1,2,0:T(4,128)S(1)} %copy-done.57, pred[2,256]{1,0:T(4,128)(4,1)S(1)} %copy-done.101), kind=kOutput, calls=%fused_computation.164 | convolution fusion | flops 554041088 | bytes 19203584 | tf_op jit(solution)/shard_map/bqhk,bqhd->bkhd/dot_general | solution.py:277
  303.2 14.6 %fusion.54 = bf16[2,256,4,64]{1,3,2,0:T(8,128)(2,1)} fusion(bf16[2,2048,4,64]{1,3,2,0:T(8,128)(2,1)} %copy.336, f32[2,4,256,2048]{3,2,1,0:T(8,128)} %fusion.112, f32[2,2048,4]{1,2,0:T(4,128)S(1)} %copy-done.58, f32[2,2048,4]{1,2,0:T(4,128)S(1)} %copy-done.57, pred[2,256]{1,0:T(4,128)(4,1)} %broadcast_in_dim.47, bf16[2,2048,4,64]{1,3,2,0:T(8,128)(2,1)} %copy.337, ...), kind=kOutput, calls=%fused_computation.70 | convolution fusion | flops 1099169792 | bytes 21627392 | tf_op jit(solution)/shard_map/bqhk,bqhd->bkhd/dot_general | solution.py:287
  317.7 2.1 reshape.369
  319.8 2.0 copy.338
  321.8 2.0 reshape.370
  323.8 2.0 copy.339
  325.9 2.4 convolution_bitcast_fusion
  328.3 2.8 multiply_reduce_fusion
  331.5 15.4 %all-reduce.6 = (f32[2,32]{1,0:T(2,128)S(1)}, f32[2,32]{1,0:T(2,128)S(1)}) all-reduce(f32[2,32]{1,0:T(2,128)S(1)} %reduce_sum.365, f32[2,32]{1,0:T(2,128)S(1)} %reduce_sum.362), channel_id=1, replica_groups=mesh['img'=4,'row'=8] {'row'}, use_global_device_ids=true, to_apply=%region_26.27 | all-reduce | flops 128 | bytes 1024 | tf_op jit(solution)/shard_map/psum | solution.py:98
  356.9 1.9 collective-permute-start.4
  360.3 2.0 reshape.365
  362.3 2.0 copy.334
  372.2 2.1 multiply_multiply_fusion.2
  377.6 14.8 %all-reduce.5 = (f32[2,32]{1,0:T(2,128)S(1)}, f32[2,32]{1,0:T(2,128)S(1)}) all-reduce(f32[2,32]{1,0:T(2,128)S(1)} %reduce_sum.371, f32[2,32]{1,0:T(2,128)S(1)} %reduce_sum.368), channel_id=1, replica_groups=mesh['img'=4,'row'=8] {'row'}, use_global_device_ids=true, to_apply=%region_32.33 | all-reduce | flops 128 | bytes 1024 | tf_op jit(solution)/shard_map/psum | solution.py:98
  398.7 3.2 fusion.140
  415.4 17.9 %all-reduce.4 = (f32[2,32]{1,0:T(2,128)S(1)}, f32[2,32]{1,0:T(2,128)S(1)}) all-reduce(f32[2,32]{1,0:T(2,128)S(1)} %reduce_sum.377, f32[2,32]{1,0:T(2,128)S(1)} %reduce_sum.374), channel_id=1, replica_groups=mesh['img'=4,'row'=8] {'row'}, use_global_device_ids=true, to_apply=%region_38.39 | all-reduce | flops 128 | bytes 1024 | tf_op jit(solution)/shard_map/psum | solution.py:98
  433.8 38.3 %all-reduce.2 = (f32[256]{0:T(256)}, f32[256]{0:T(256)}, f32[256]{0:T(256)}, f32[512]{0:T(512)}, f32[256]{0:T(256)}, /*index=5*/f32[256]{0:T(256)}, f32[256]{0:T...) all-reduce(f32[256]{0:T(256)S(1)} %get-tuple-element.20, ...), channel_id=1, replica_groups=mesh['img'=4,'row'=8] {'img','row'}, use_global_device_ids=true, to_apply=%region_40.41 | all-reduce | flops 3328 | bytes 26624 | tf_op jit(solution)/shard_map/psum | solution.py:333
  473.0 104.7 %all-reduce.9.cloned.1.call-done = (f32[3,3,256,256]{3,2,1,0:T(8,128)}, f32[1024,512]{1,0:T(8,128)}, f32[3,3,256,256]{3,2,1,0:T(8,128)}, f32[256,768]{1,0:T(8,128)}, f32[256,256]{1,0:T(8,128)}) async-done(((f32[3,3,256,256]{3,2,1,0:T(8,128)}, f32[1024,512]{1,0:T(8,128)}, f32[3,3,256,256]{3,2,1,0:T(8,128)}, f32[256,768]{1,0:T(8,128)}, f32[256,256]{1,0:T(8,128)}), (f32[3,3,256,256]{3,2,1,0:T(8,128)}, ...) | async-done | bytes 7864336 | tf_op jit(solution)/shard_map/psum | solution.py:333
  577.7 3.4 copy.441
  (468 shorter events, 88.6 us)
Async XLA Ops:
  7.2 89.7 %copy-start = (bf16[3,3,256,256]{3,2,1,0:T(8,128)(2,1)S(1)}, bf16[3,3,256,256]{3,2,1,0:T(8,128)(2,1)}, u32[]{:S(2)}) copy-start(bf16[3,3,256,256]{3,2,1,0:T(8,128)(2,1)} %param.31) | copy-start | bytes 3538948
  7.2 44.1 %copy-start.107 = (s32[2]{0:T(128)S(1)}, s32[2]{0:T(128)}, u32[]{:S(2)}) copy-start(s32[2]{0:T(128)} %param.22) | copy-start | bytes 28
  7.2 44.1 %copy-start.100 = (bf16[512]{0:T(512)(128)(2,1)S(1)}, bf16[512]{0:T(512)(128)(2,1)}, u32[]{:S(2)}) copy-start(bf16[512]{0:T(512)(128)(2,1)} %param.28) | copy-start | bytes 3076
  7.2 44.3 %copy-start.25 = (bf16[1024,512]{1,0:T(8,128)(2,1)S(1)}, bf16[1024,512]{1,0:T(8,128)(2,1)}, u32[]{:S(2)}) copy-start(bf16[1024,512]{1,0:T(8,128)(2,1)} %param.27) | copy-start | bytes 3145732
  7.2 44.8 %copy-start.108 = (bf16[256]{0:T(256)(128)(2,1)S(1)}, bf16[256]{0:T(256)(128)(2,1)}, u32[]{:S(2)}) copy-start(bf16[256]{0:T(256)(128)(2,1)} %param.26) | copy-start | bytes 1540
  7.2 44.8 %copy-start.109 = (bf16[256]{0:T(256)(128)(2,1)S(1)}, bf16[256]{0:T(256)(128)(2,1)}, u32[]{:S(2)}) copy-start(bf16[256]{0:T(256)(128)(2,1)} %param.29) | copy-start | bytes 1540
  7.3 44.8 %copy-start.110 = (bf16[256]{0:T(256)(128)(2,1)S(1)}, bf16[256]{0:T(256)(128)(2,1)}, u32[]{:S(2)}) copy-start(bf16[256]{0:T(256)(128)(2,1)} %param.30) | copy-start | bytes 1540
  7.3 137.4 %all-gather.11.cloned.1.call-start = ((), (), s32[]{:S(2)}) async-start(), calls=%async_computation.3 | async-start | bytes 2359296 | tf_op jit(solution)/shard_map/all_gather | solution.py:266
  46.1 6.0 %collective-permute-start = (bf16[2,1,64,256]{3,2,1,0:T(8,128)(2,1)S(1)}, bf16[2,1,64,256]{3,2,1,0:T(8,128)(2,1)S(1)}, u32[]{:S(2)}, u32[]{:S(2)}) collective-permute-start(bf16[2,1,64,256]{3,2,1,0:T(8,128)(2,1)S(1)} %get-tuple-element.80), channel_id=1, source_target_pairs={{0,1},{1,2},{2,3},{3,4},{4,5},{5,6},{6,7},{8,9},{9,10},{10,11},{11... | collective-permute-start | bytes 196616 | tf_op jit(solution)/shard_map/ppermute | solution.py:25
  47.9 4.2 collective-permute-start.1
  51.2 109.1 %all-gather.7.cloned.1.call-start = ((), (), s32[]{:S(2)}) async-start(), calls=%async_computation.1 | async-start | bytes 2359296 | tf_op jit(solution)/shard_map/all_gather | solution.py:201
  52.1 34.8 %copy-start.78 = (f32[256]{0:T(256)}, f32[256]{0:T(256)S(1)}, u32[]{:S(2)}) copy-start(f32[256]{0:T(256)S(1)} %convert_element_type.163) | copy-start | bytes 3076
  52.1 34.8 %copy-start.83 = (f32[256]{0:T(256)}, f32[256]{0:T(256)S(1)}, u32[]{:S(2)}) copy-start(f32[256]{0:T(256)S(1)} %convert_element_type.164) | copy-start | bytes 3076
  55.3 16.5 %copy-start.12 = (f32[4,16,9,256]{3,1,2,0:T(8,128)}, f32[4,16,9,256]{3,1,2,0:T(8,128)S(1)}, u32[]{:S(2)}) copy-start(f32[4,16,9,256]{3,1,2,0:T(8,128)S(1)} %get-tuple-element.95) | copy-start | bytes 1769476
  89.9 3.4 collective-permute-start.2
  91.6 3.1 collective-permute-start.3
  93.0 36.6 %copy-start.85 = (f32[256]{0:T(256)}, f32[256]{0:T(256)S(1)}, u32[]{:S(2)}) copy-start(f32[256]{0:T(256)S(1)} %convert_element_type.169) | copy-start | bytes 3076
  93.0 36.6 %copy-start.98 = (f32[256]{0:T(256)}, f32[256]{0:T(256)S(1)}, u32[]{:S(2)}) copy-start(f32[256]{0:T(256)S(1)} %convert_element_type.170) | copy-start | bytes 3076
  98.9 34.1 %copy-start.93 = (bf16[512]{0:T(512)(128)(2,1)S(1)}, bf16[512]{0:T(512)(128)(2,1)}, u32[]{:S(2)}) copy-start(bf16[512]{0:T(512)(128)(2,1)} %param.36) | copy-start | bytes 3076
  115.3 19.7 %copy-start.64 = (f32[2,256]{1,0:T(2,128)}, f32[2,256]{1,0:T(2,128)S(1)}, u32[]{:S(2)}) copy-start(f32[2,256]{1,0:T(2,128)S(1)} %sub.158) | copy-start | bytes 6148
  132.9 58.3 %all-gather.5.cloned.1.call-start = ((), (), s32[]{:S(2)}) async-start(), calls=%async_computation | async-start | bytes 2359296 | tf_op jit(solution)/shard_map/all_gather | solution.py:202
  135.1 120.3 %all-gather.9.cloned.1.call-start = ((), (), s32[]{:S(2)}) async-start(), calls=%async_computation.2 | async-start | bytes 2359296 | tf_op jit(solution)/shard_map/all_gather | solution.py:265
  144.6 433.1 %all-reduce.9.cloned.1.call-start = ((), (), s32[]{:S(2)}) async-start(), calls=%async_computation.4 | async-start | bytes 15728640 | tf_op jit(solution)/shard_map/psum | solution.py:333
  205.3 8.9 %copy-start.39 = (bf16[2,256,4,64]{1,3,2,0:T(8,128)(2,1)S(1)}, bf16[2,256,4,64]{1,3,2,0:T(8,128)(2,1)}, u32[]{:S(2)}) copy-start(bf16[2,256,4,64]{1,3,2,0:T(8,128)(2,1)} %copy.267) | copy-start | bytes 786436
  240.0 85.8 %copy-start.40 = (bf16[2,4,64,256]{3,2,1,0:T(8,128)(2,1)}, bf16[2,4,64,256]{3,2,1,0:T(8,128)(2,1)S(1)}, u32[]{:S(2)}) copy-start(bf16[2,4,64,256]{3,2,1,0:T(8,128)(2,1)S(1)} %copy.335) | copy-start | bytes 786436
  284.2 10.0 %copy-start.17 = (bf16[2,2048,4,64]{1,3,2,0:T(8,128)(2,1)S(1)}, bf16[2,2048,4,64]{1,3,2,0:T(8,128)(2,1)}, u32[]{:S(2)}) copy-start(bf16[2,2048,4,64]{1,3,2,0:T(8,128)(2,1)} %copy.337) | copy-start | bytes 6291460
  284.2 10.0 %copy-start.57 = (f32[2,2048,4]{1,2,0:T(4,128)S(1)}, f32[2,2048,4]{1,2,0:T(4,128)}, u32[]{:S(2)}) copy-start(f32[2,2048,4]{1,2,0:T(4,128)} %sub.167) | copy-start | bytes 196612
  284.2 10.0 %copy-start.101 = (pred[2,256]{1,0:T(4,128)(4,1)S(1)}, pred[2,256]{1,0:T(4,128)(4,1)}, u32[]{:S(2)}) copy-start(pred[2,256]{1,0:T(4,128)(4,1)} %broadcast_in_dim.47) | copy-start | bytes 1540
  294.2 9.0 %copy-start.58 = (f32[2,2048,4]{1,2,0:T(4,128)S(1)}, f32[2,2048,4]{1,2,0:T(4,128)}, u32[]{:S(2)}) copy-start(f32[2,2048,4]{1,2,0:T(4,128)} %sub.170) | copy-start | bytes 196612
  328.3 19.1 %copy-start.14 = (bf16[2,4,64,256]{3,2,1,0:T(8,128)(2,1)S(1)}, bf16[2,4,64,256]{3,2,1,0:T(8,128)(2,1)}, u32[]{:S(2)}) copy-start(bf16[2,4,64,256]{3,2,1,0:T(8,128)(2,1)} %param.39) | copy-start | bytes 786436
  328.3 19.1 %copy-start.67 = (f32[2,256]{1,0:T(2,128)S(1)}, f32[2,256]{1,0:T(2,128)}, u32[]{:S(2)}) copy-start(f32[2,256]{1,0:T(2,128)} %copy-done.64) | copy-start | bytes 6148
  328.3 19.1 %copy-start.75 = (f32[2,256]{1,0:T(2,128)S(1)}, f32[2,256]{1,0:T(2,128)}, u32[]{:S(2)}) copy-start(f32[2,256]{1,0:T(2,128)} %copy-done.72) | copy-start | bytes 6148
  328.3 19.1 %copy-start.88 = (f32[256]{0:T(256)S(1)}, f32[256]{0:T(256)}, u32[]{:S(2)}) copy-start(f32[256]{0:T(256)} %copy-done.85) | copy-start | bytes 3076
  353.3 11.0 %copy-start.56 = (bf16[2,1,64,256]{3,2,1,0:T(8,128)(2,1)S(1)}, bf16[2,1,64,256]{3,2,1,0:T(8,128)(2,1)}, u32[]{:S(2)}) copy-start(bf16[2,1,64,256]{3,2,1,0:T(8,128)(2,1)} %copy-done.55) | copy-start | bytes 196612
  356.2 10.6 %copy-start.54 = (bf16[2,1,64,256]{3,2,1,0:T(8,128)(2,1)S(1)}, bf16[2,1,64,256]{3,2,1,0:T(8,128)(2,1)}, u32[]{:S(2)}) copy-start(bf16[2,1,64,256]{3,2,1,0:T(8,128)(2,1)} %copy-done.53) | copy-start | bytes 196612
  356.9 13.0 %collective-permute-start.4 = (bf16[2,1,64,256]{3,2,1,0:T(8,128)(2,1)}, bf16[2,1,64,256]{3,2,1,0:T(8,128)(2,1)}, u32[]{:S(2)}, u32[]{:S(2)}) collective-permute-start(bf16[2,1,64,256]{3,2,1,0:T(8,128)(2,1)} %get-tuple-element.78), channel_id=1, source_target_pairs={{0,1},{1,2},{2,3},{3,4},{4,5},{5,6},{6,7},{8,9},{9,10},{10,11},{11... | collective-permute-start | bytes 196616 | tf_op jit(solution)/shard_map/ppermute | solution.py:25
  358.8 11.1 %collective-permute-start.5 = (bf16[2,1,64,256]{3,2,1,0:T(8,128)(2,1)}, bf16[2,1,64,256]{3,2,1,0:T(8,128)(2,1)}, u32[]{:S(2)}, u32[]{:S(2)}) collective-permute-start(bf16[2,1,64,256]{3,2,1,0:T(8,128)(2,1)} %get-tuple-element.79), channel_id=1, source_target_pairs={{1,0},{2,1},{3,2},{4,3},{5,4},{6,5},{7,6},{9,8},{10,9},{11,10},{12... | collective-permute-start | bytes 196616 | tf_op jit(solution)/shard_map/ppermute | solution.py:27
  375.6 19.0 %copy-start.84 = (f32[256]{0:T(256)S(1)}, f32[256]{0:T(256)}, u32[]{:S(2)}) copy-start(f32[256]{0:T(256)} %copy-done.83) | copy-start | bytes 3076
  406.2 4.7 collective-permute-start.6
  407.7 3.3 collective-permute-start.7
  413.9 19.8 %copy-start.80 = (f32[512]{0:T(512)S(1)}, f32[512]{0:T(512)}, u32[]{:S(2)}) copy-start(f32[512]{0:T(512)} %pad_maximum_fusion.9) | copy-start | bytes 6148
  414.0 19.8 %copy-start.89 = (f32[256]{0:T(256)S(1)}, f32[256]{0:T(256)}, u32[]{:S(2)}) copy-start(f32[256]{0:T(256)} %get-tuple-element.52) | copy-start | bytes 3076
  414.0 19.8 %copy-start.90 = (f32[256]{0:T(256)S(1)}, f32[256]{0:T(256)}, u32[]{:S(2)}) copy-start(f32[256]{0:T(256)} %get-tuple-element.22) | copy-start | bytes 3076
  414.0 19.8 %copy-start.91 = (f32[256]{0:T(256)S(1)}, f32[256]{0:T(256)}, u32[]{:S(2)}) copy-start(f32[256]{0:T(256)} %get-tuple-element.23) | copy-start | bytes 3076
  414.0 19.8 %copy-start.92 = (f32[256]{0:T(256)S(1)}, f32[256]{0:T(256)}, u32[]{:S(2)}) copy-start(f32[256]{0:T(256)} %get-tuple-element.28) | copy-start | bytes 3076
  414.0 19.8 %copy-start.102 = (f32[256]{0:T(256)S(1)}, f32[256]{0:T(256)}, u32[]{:S(2)}) copy-start(f32[256]{0:T(256)} %get-tuple-element.18) | copy-start | bytes 3076
  414.0 19.8 %copy-start.103 = (f32[256]{0:T(256)S(1)}, f32[256]{0:T(256)}, u32[]{:S(2)}) copy-start(f32[256]{0:T(256)} %get-tuple-element.26) | copy-start | bytes 3076
  414.0 58.1 %copy-start.6 = (f32[2,4,64,256]{3,2,1,0:T(8,128)S(1)}, f32[2,4,64,256]{3,2,1,0:T(8,128)}, u32[]{:S(2)}) copy-start(f32[2,4,64,256]{3,2,1,0:T(8,128)} %copy-done.5) | copy-start | bytes 1572868
  (80 other events, 262.6 us)
Sparse Core Ops, SparseCore 0:
  51.3 29.3 all-gather.10
  133.0 27.2 all-gather.6
  162.5 28.5 all-gather.4
  192.6 28.5 all-gather.8
  404.4 173.2 all-reduce.8
where the time goes:
time: 604 us; the launch traced here: 594 us
  blocking collectives  205 us (34%)
  waiting for transfers between devices  115 us (19%)
  local copies, waits for them, and re-layouts  113 us (19%)
  matrix products  95.1 us (16%)
  other arithmetic  36.7 us (6%)
  between operations  16.5 us (3%)
  starting transfers between devices  12.7 us (2%)
    psum x1, waiting for transfers between devices, local(): lax.psum((norm1_gain_grad, norm1_bias_grad, conv1_weight_grad, conv1_bias...  105 us
    reshape x8, local copies, waits for them, and re-layouts, flatten_rows(): piece_arr.reshape(image_count, piece_arr.shape[1] * col_count, head_count...  56.3 us
    psum x3, blocking collectives, norm_forward(): first_sum = lax.psum(jnp.sum(shaped * cell_mask, axis=(1, 2, 4)), 'row')  49.4 us
    psum x3, blocking collectives, norm_backward(): lax.psum((jnp.sum(scaled * cell_mask, axis=(1, 2, 4)), jnp.sum(scaled * n...  48.1 us
    psum x3, blocking collectives, norm_forward(): lax.psum(jnp.sum(jnp.square(centred * cell_mask), axis=(1, 2, 4)), 'row')  41 us
    psum x1, blocking collectives, local(): lax.psum((norm1_gain_grad, norm1_bias_grad, conv1_weight_grad, conv1_bias...  38.3 us
    unnamed x241, local copies, waits for them, and re-layouts  15.2 us
    dot_general x1, matrix products, local(): jnp.einsum('bqhk,bqhd->bkhd', grad_scores, flat_queries, preferred_elemen...  14.6 us
  transfers between devices with their start and end apart: 13, of which 4 were waited for; matrix products, arithmetic and copies ran while one was open for 23% of the time, Pallas kernels for 0%

commit v1 on v0

--- a/solution.py
+++ b/solution.py
@@ -3,6 +3,8 @@
 import jax
 import jax.numpy as jnp
 from jax import lax
+from jax.experimental import pallas as pl
+from jax.experimental.pallas import tpu as pltpu
 from jax.sharding import PartitionSpec as P
 
 GROUPS = 32
@@ -116,7 +118,7 @@
     return (grad_in.reshape(full_shape), gain_grad, shift_grad)
 
 
-def local(
+def local_rows(
     pixels,
     heights,
     timesteps,
@@ -373,6 +375,843 @@
     )
 
 
+def mib(count):
+    return pltpu.CompilerParams(vmem_limit_bytes=count * 2**20)
+
+
+def dot(left, right):
+    return jnp.dot(left, right, preferred_element_type=jnp.float32)
+
+
+def dot_rows(left, right):
+    return lax.dot_general(
+        left, right, (((1,), (1,)), ((), ())), preferred_element_type=jnp.float32
+    )
+
+
+def fold(tile):
+    return jnp.sum(tile.reshape(-1, 8, tile.shape[1]), axis=0)
+
+
+def group_sums(row, width):
+    channels = row.shape[1]
+    rows = lax.broadcasted_iota(jnp.int32, (channels, channels), 0) // width
+    cols = lax.broadcasted_iota(jnp.int32, (channels, channels), 1) // width
+    same = jnp.where(rows == cols, 1.0, 0.0).astype(jnp.float32)
+    wide = jnp.broadcast_to(row, (8, channels))
+    return jnp.dot(wide, same, precision=PRECISE, preferred_element_type=jnp.float32)[0:1]
+
+
+def row_at(index, cols):
+    return pl.ds(pl.multiple_of(index * cols, cols), cols)
+
+
+def total_of(tile):
+    return jnp.sum(tile, axis=0, keepdims=True)
+
+
+def field_stats(read, height, rows, cols, channels):
+    width = channels // GROUPS
+    cells = (height * (cols * width)).astype(jnp.float32)
+    zero = jnp.zeros((8, channels), jnp.float32)
+
+    def valid(index):
+        return jnp.where(index < height, 1.0, 0.0).astype(jnp.float32)
+
+    def add(index, total):
+        return total + fold(read(index) * valid(index))
+
+    total = lax.fori_loop(0, rows, add, zero, unroll=2)
+    mean = group_sums(total_of(total), width) / cells
+
+    def add_square(index, total):
+        return total + fold(jnp.square((read(index) - mean) * valid(index)))
+
+    total = lax.fori_loop(0, rows, add_square, zero, unroll=2)
+    spread = group_sums(total_of(total), width) / cells
+    return mean, lax.rsqrt(spread + EPSILON)
+
+
+def put_shifted(ref, index, tile, cols):
+    channels = tile.shape[1]
+    column = lax.broadcasted_iota(jnp.int32, tile.shape, 0)
+    before = jnp.where(column == 0, 0.0, pltpu.roll(tile, 1, 0))
+    after = jnp.where(column == cols - 1, 0.0, pltpu.roll(tile, cols - 1, 0))
+    at = row_at(index + 1, cols)
+    ref[at, 0:channels] = before.astype(jnp.bfloat16)
+    ref[at, channels : 2 * channels] = tile.astype(jnp.bfloat16)
+    ref[at, 2 * channels : 3 * channels] = after.astype(jnp.bfloat16)
+
+
+def clear_rims(ref, cols):
+    edge = jnp.zeros((cols, ref.shape[1]), ref.dtype)
+    ref[0:cols, :] = edge
+    ref[ref.shape[0] - cols : ref.shape[0], :] = edge
+
+
+def conv_shifted(shifted, weight, out, bias, cols):
+    step = 8 * cols
+
+    def block(index, carry):
+        base = index * step
+        total = bias
+        for tap in range(3):
+            at = pl.ds(pl.multiple_of(base + tap * cols, cols), step)
+            total = total + dot(shifted[at, :], weight[tap])
+        out[pl.ds(pl.multiple_of(base, step), step), :] = total
+        return carry
+
+    lax.fori_loop(0, out.shape[0] // step, block, 0)
+
+
+def pick_own(shifted, chosen, out):
+    step = out.shape[0] // 4
+
+    def block(index, carry):
+        at = pl.ds(pl.multiple_of(index * step, 16), step)
+        out[at, :] = dot(shifted[at, :], chosen[...]).astype(jnp.bfloat16)
+        return carry
+
+    lax.fori_loop(0, 4, block, 0)
+
+
+def kernel_quarter(grad, shifted_own, grad_t, out, cols):
+    cells = grad.shape[0]
+    for start in range(0, cells, 256):
+        grad_t[:, start : start + 256] = jnp.transpose(grad[start : start + 256, :]).astype(
+            jnp.bfloat16
+        )
+    width = shifted_own.shape[1]
+    for tap in range(3):
+        part = dot(grad_t[...], shifted_own[tap * cols : tap * cols + cells, :])
+        out[tap * width : (tap + 1) * width, :] = jnp.transpose(part).astype(jnp.bfloat16)
+
+
+def forward_kernel(place, *refs):
+    blocks = refs[:8]
+    w_one, w_two, vec, chosen = refs[8:12]
+    pix, conv_one, residual, act_three, own_one, own_two, stats, shifted = refs[12:]
+    cells, channels = pix.shape
+    block_cells = blocks[0].shape[0]
+    cols = (own_one.shape[0] - cells) // 2
+    rows = cells // cols
+    spot, height = place[0], place[1]
+    for step, block in enumerate(blocks):
+        at = pl.ds(pl.multiple_of((spot ^ step) * block_cells, block_cells), block_cells)
+        pix[at, :] = block[...]
+    gain_one, bias_one, conv_bias_one, gain_two, bias_two = (vec[k : k + 1, :] for k in range(5))
+    scale, shift, conv_bias_two, gain_three, bias_three = (vec[k : k + 1, :] for k in range(5, 10))
+
+    def valid(index):
+        return jnp.where(index < height, 1.0, 0.0).astype(jnp.float32)
+
+    def read_pix(index):
+        return pix[row_at(index, cols), :].astype(jnp.float32)
+
+    def read_conv(index):
+        return conv_one[row_at(index, cols), :]
+
+    def read_res(index):
+        return residual[row_at(index, cols), :]
+
+    clear_rims(shifted, cols)
+    mean_one, inv_one = field_stats(read_pix, height, rows, cols, channels)
+
+    def first(index, carry):
+        pre = (read_pix(index) - mean_one) * inv_one * gain_one + bias_one
+        put_shifted(shifted, index, pre / (1.0 + jnp.exp(-pre)) * valid(index), cols)
+        return carry
+
+    lax.fori_loop(0, rows, first, 0, unroll=2)
+    conv_shifted(shifted, w_one, conv_one, conv_bias_one, cols)
+    pick_own(shifted, chosen, own_one)
+    mean_two, inv_two = field_stats(read_conv, height, rows, cols, channels)
+
+    def second(index, carry):
+        affine = (read_conv(index) - mean_two) * inv_two * gain_two + bias_two
+        pre = affine * scale + shift
+        put_shifted(shifted, index, pre / (1.0 + jnp.exp(-pre)) * valid(index), cols)
+        return carry
+
+    lax.fori_loop(0, rows, second, 0, unroll=2)
+    conv_shifted(shifted, w_two, residual, conv_bias_two, cols)
+    pick_own(shifted, chosen, own_two)
+
+    def join(index, carry):
+        at = row_at(index, cols)
+        residual[at, :] = residual[at, :] + read_pix(index)
+        return carry
+
+    lax.fori_loop(0, rows, join, 0, unroll=2)
+    mean_three, inv_three = field_stats(read_res, height, rows, cols, channels)
+
+    def third(index, carry):
+        normed = (read_res(index) - mean_three) * inv_three
+        act_three[row_at(index, cols), :] = (normed * gain_three + bias_three).astype(jnp.bfloat16)
+        return carry
+
+    lax.fori_loop(0, rows, third, 0, unroll=2)
+    stats[...] = jnp.concatenate(
+        [mean_one, inv_one, mean_two, inv_two, mean_three, inv_three, mean_one, mean_one], axis=0
+    )
+
+
+def attention_kernel(place, *refs):
+    blocks = refs[:8]
+    act_three, w_heads, w_out, biases = refs[8:12]
+    grad_proj, attended, packed, weight_rows, sums = refs[12:17]
+    query_grad, query_grad_t, key_pad, value_pad, heads_t, mixed, mask_row = refs[17:]
+    cells, channels = act_three.shape
+    block_cells = blocks[0].shape[0]
+    spot, height, cols = place[0], place[1], place[4]
+    half = mixed.shape[1] // 2
+    scaling = half**-0.5
+    valid_cells = height * cols
+    step = 256
+    total = jnp.zeros((8, channels), jnp.float32)
+    for index, block in enumerate(blocks):
+        base = pl.multiple_of((spot ^ index) * block_cells, block_cells)
+        cell = base + lax.broadcasted_iota(jnp.int32, (block_cells, channels), 0)
+        kept = jnp.where(cell < valid_cells, block[...].astype(jnp.float32), 0.0)
+        total = total + fold(kept)
+        grad_proj[pl.ds(base, block_cells), :] = kept.astype(jnp.bfloat16)
+    sums[...] = jnp.concatenate([total_of(total), jnp.zeros((7, channels), jnp.float32)], axis=0)
+
+    def project(index, carry):
+        at = pl.ds(pl.multiple_of(index * 512, 512), 512)
+        act = act_three[at, :]
+        parts = dot(act, w_heads[...]) + biases[0:1, :]
+        query = (parts[:, 0 : 2 * half].astype(jnp.bfloat16)) * jnp.bfloat16(scaling)
+        query_grad[at, :] = query + dot(grad_proj[at, :], w_out[...]).astype(jnp.bfloat16)
+        key_pad[at, :] = parts[:, 2 * half : 4 * half].astype(jnp.bfloat16)
+        value_pad[at, :] = parts[:, 4 * half : 6 * half].astype(jnp.bfloat16)
+        return carry
+
+    lax.fori_loop(0, cells // 512, project, 0)
+    lane = lax.broadcasted_iota(jnp.int32, (1, cells), 1)
+    mask_row[...] = jnp.where(lane < valid_cells, 0.0, MASKED)
+    for start in range(0, cells, step):
+        query_grad_t[:, start : start + step] = jnp.transpose(
+            query_grad[start : start + step, :].astype(jnp.float32)
+        ).astype(jnp.bfloat16)
+    heads_t[...] = jnp.zeros(heads_t.shape, jnp.float32)
+    mixed[...] = jnp.zeros(mixed.shape, jnp.bfloat16)
+
+    def query_block(index, carry):
+        at = pl.ds(pl.multiple_of(index * step, step), step)
+        both = query_grad[at, :]
+        scores = dot_rows(both, key_pad[...]) + mask_row[...]
+        top = jnp.max(scores, axis=1, keepdims=True)
+        weights = jnp.exp(scores - top)
+        probs = weights * (1.0 / jnp.sum(weights, axis=1, keepdims=True))
+        low = probs.astype(jnp.bfloat16)
+        out = dot(low, value_pad[...])
+        delta = jnp.sum(both.astype(jnp.float32) * out, axis=1, keepdims=True)
+        grad_probs = dot_rows(both, value_pad[...])
+        grad_scores = (probs * (grad_probs - delta)).astype(jnp.bfloat16)
+        mixed[at, :] = (out + dot(grad_scores, key_pad[...]) * scaling).astype(jnp.bfloat16)
+        heads_t[0:half, :] += dot(query_grad_t[0:half, at], grad_scores)
+        heads_t[half : 2 * half, :] += dot(query_grad_t[half : 2 * half, at], low)
+        return carry
+
+    lax.fori_loop(0, (valid_cells + step - 1) // step, query_block, 0)
+    for start in range(0, cells, step):
+        packed[start : start + step, :] = jnp.transpose(heads_t[:, start : start + step]).astype(
+            jnp.bfloat16
+        )
+    packed[cells : cells + cells // 2, 0:half] = mixed[0 : cells // 2, 0:half]
+    packed[cells : cells + cells // 2, half : 2 * half] = mixed[cells // 2 : cells, 0:half]
+    attended[...] = mixed[:, half : 2 * half]
+    for start in range(0, cells, step):
+        query_grad_t[:, start : start + step] = jnp.transpose(
+            mixed[start : start + step, :].astype(jnp.float32)
+        ).astype(jnp.bfloat16)
+    low_heads = heads_t[...].astype(jnp.bfloat16)
+    from_query = dot(query_grad_t[...], act_three[...])
+    from_heads = dot(low_heads, act_three[...])
+    from_out = dot(query_grad_t[...], grad_proj[...])
+    weight_rows[0:half, :] = from_query[0:half].astype(jnp.bfloat16)
+    weight_rows[half : 3 * half, :] = from_heads.astype(jnp.bfloat16)
+    weight_rows[3 * half : 4 * half, :] = from_out[half : 2 * half].astype(jnp.bfloat16)
+    ones = jnp.ones((8, cells), jnp.bfloat16)
+    query_sum = dot(ones, mixed[...])
+    value_sum = lax.dot_general(
+        ones, low_heads, (((1,), (1,)), ((), ())), preferred_element_type=jnp.float32
+    )
+    row = jnp.concatenate([query_sum, value_sum], axis=1)[0:1]
+    weight_rows[4 * half :, :] = jnp.concatenate(
+        [row, jnp.zeros((weight_rows.shape[0] - 4 * half - 1, channels), jnp.float32)], axis=0
+    ).astype(jnp.bfloat16)
+
+
+def residual_kernel(place, *refs):
+    heads = refs[:4]
+    w_key_value, w_query, grad_proj, residual, stats, vec, own_two = refs[4:11]
+    grad_res, shifted, quarter, sums, grad_act, grad_t = refs[11:]
+    cells, channels = grad_proj.shape
+    cols = (own_two.shape[0] - cells) // 2
+    rows = cells // cols
+    height, head = place[1], place[2]
+    width = channels // GROUPS
+    count = (height * (cols * width)).astype(jnp.float32)
+    half = w_query.shape[1]
+    zeros = jnp.zeros((half, channels), jnp.bfloat16)
+    halfway = cells // 2
+    step = 512
+    pairs = ((0, 1), (2, 3))
+    w_main = [
+        jnp.concatenate([w_key_value[head ^ a], w_key_value[head ^ b]], axis=0) for a, b in pairs
+    ]
+    for part in range(2):
+        w_side = []
+        for a, b in pairs:
+            left, right = w_query[head ^ a], w_query[head ^ b]
+            order = [left, zeros, right, zeros] if part == 0 else [zeros, left, zeros, right]
+            w_side.append(jnp.concatenate(order, axis=0))
+        for base in range(0, halfway, step):
+            start = part * halfway + base
+            total = None
+            for k, (a, b) in enumerate(pairs):
+                main = jnp.concatenate(
+                    [heads[a][start : start + step, :], heads[b][start : start + step, :]], axis=1
+                )
+                spot = cells + base
+                side = jnp.concatenate(
+                    [heads[a][spot : spot + step, :], heads[b][spot : spot + step, :]], axis=1
+                )
+                term = dot(main, w_main[k]) + dot(side, w_side[k])
+                total = term if total is None else total + term
+            grad_act[start : start + step, :] = total
+    mean, inverse = stats[4:5, :], stats[5:6, :]
+    gain = vec[8:9, :]
+    zero = jnp.zeros((8, channels), jnp.float32)
+
+    def normed(index):
+        return (residual[row_at(index, cols), :] - mean) * inverse
+
+    def add(index, totals):
+        grad = grad_act[row_at(index, cols), :]
+        return totals[0] + fold(grad), totals[1] + fold(grad * normed(index))
+
+    plain, cross = lax.fori_loop(0, rows, add, (zero, zero), unroll=2)
+    plain, cross = total_of(plain), total_of(cross)
+    mean_plain = group_sums(plain * gain, width) / count
+    mean_cross = group_sums(cross * gain, width) / count
+    clear_rims(shifted, cols)
+
+    def finish(index, total):
+        at = row_at(index, cols)
+        inner = (grad_act[at, :] * gain - mean_plain - normed(index) * mean_cross) * inverse
+        inner = inner * jnp.where(index < height, 1.0, 0.0).astype(jnp.float32)
+        grad = grad_proj[at, :].astype(jnp.float32) + inner
+        grad_res[at, :] = grad
+        put_shifted(shifted, index, grad, cols)
+        return total + fold(grad)
+
+    total = total_of(lax.fori_loop(0, rows, finish, zero, unroll=2))
+    kernel_quarter(grad_res, own_two, grad_t, quarter, cols)
+    sums[...] = jnp.concatenate([cross, plain, total, jnp.zeros((5, channels), jnp.float32)], axis=0)
+
+
+def second_kernel(place, shifted, weight, conv_one, stats, vec, own_one, *refs):
+    shifted_one, quarter, sums, grad_act, grad_t = refs
+    cells, channels = conv_one.shape
+    cols = (own_one.shape[0] - cells) // 2
+    rows = cells // cols
+    height = place[1]
+    width = channels // GROUPS
+    count = (height * (cols * width)).astype(jnp.float32)
+    mean, inverse = stats[2:3, :], stats[3:4, :]
+    gain, bias, scale, shift = (vec[k : k + 1, :] for k in range(3, 7))
+    zero = jnp.zeros((8, channels), jnp.float32)
+
+    def valid(index):
+        return jnp.where(index < height, 1.0, 0.0).astype(jnp.float32)
+
+    def normed(index):
+        return (conv_one[row_at(index, cols), :] - mean) * inverse
+
+    conv_shifted(shifted, weight, grad_act, 0.0, cols)
+
+    def add(index, totals):
+        at = row_at(index, cols)
+        unit = normed(index)
+        pre = (unit * gain + bias) * scale + shift
+        sigmoid = 1.0 / (1.0 + jnp.exp(-pre))
+        grad = grad_act[at, :] * valid(index) * (sigmoid * (1.0 + pre * (1.0 - sigmoid)))
+        grad_act[at, :] = grad
+        return totals[0] + fold(grad), totals[1] + fold(grad * unit)
+
+    plain, cross = lax.fori_loop(0, rows, add, (zero, zero), unroll=2)
+    plain, cross = total_of(plain), total_of(cross)
+    factor = gain * scale
+    mean_plain = group_sums(plain * factor, width) / count
+    mean_cross = group_sums(cross * factor, width) / count
+    clear_rims(shifted_one, cols)
+
+    def finish(index, total):
+        at = row_at(index, cols)
+        grad = (grad_act[at, :] * factor - mean_plain - normed(index) * mean_cross) * inverse
+        grad = grad * valid(index)
+        grad_act[at, :] = grad
+        put_shifted(shifted_one, index, grad, cols)
+        return total + fold(grad)
+
+    total = total_of(lax.fori_loop(0, rows, finish, zero, unroll=2))
+    kernel_quarter(grad_act, own_one, grad_t, quarter, cols)
+    sums[...] = jnp.concatenate([cross, plain, total, jnp.zeros((5, channels), jnp.float32)], axis=0)
+
+
+def first_kernel(place, shifted, weight, pix, grad_res, stats, vec, out, sums, grad_act):
+    cells, channels = pix.shape
+    block_cells = out.shape[1]
+    cols = (shifted.shape[0] - cells) // 2
+    rows = cells // cols
+    spot, height = place[0], place[1]
+    width = channels // GROUPS
+    count = (height * (cols * width)).astype(jnp.float32)
+    mean, inverse = stats[0:1, :], stats[1:2, :]
+    gain, bias = vec[0:1, :], vec[1:2, :]
+    zero = jnp.zeros((8, channels), jnp.float32)
+
+    def valid(index):
+        return jnp.where(index < height, 1.0, 0.0).astype(jnp.float32)
+
+    def normed(at):
+        return (pix[at, :].astype(jnp.float32) - mean) * inverse
+
+    conv_shifted(shifted, weight, grad_act, 0.0, cols)
+
+    def add(index, totals):
+        at = row_at(index, cols)
+        unit = normed(at)
+        pre = unit * gain + bias
+        sigmoid = 1.0 / (1.0 + jnp.exp(-pre))
+        grad = grad_act[at, :] * valid(index) * (sigmoid * (1.0 + pre * (1.0 - sigmoid)))
+        grad_act[at, :] = grad
+        return totals[0] + fold(grad), totals[1] + fold(grad * unit)
+
+    plain, cross = lax.fori_loop(0, rows, add, (zero, zero), unroll=2)
+    plain, cross = total_of(plain), total_of(cross)
+    mean_plain = group_sums(plain * gain, width) / count
+    mean_cross = group_sums(cross * gain, width) / count
+    block_rows = block_cells // cols
+    for part in range(2):
+        first_row = (spot ^ (4 * part)) * block_rows
+        for line in range(block_rows):
+            at = row_at(first_row + line, cols)
+            grad = (grad_act[at, :] * gain - mean_plain - normed(at) * mean_cross) * inverse
+            grad = grad_res[at, :] + grad * valid(first_row + line)
+            out[part, line * cols : (line + 1) * cols, :] = grad.astype(jnp.bfloat16)
+    sums[...] = jnp.concatenate([cross, plain, jnp.zeros((6, channels), jnp.float32)], axis=0)
+
+
+def block_kernel(place, *refs):
+    heads = refs[:4]
+    w_out, residual, vec, out = refs[4:]
+    channels = residual.shape[1]
+    block_cells = out.shape[1]
+    spot, height, head, cols = place[0], place[1], place[2], place[4]
+    for part in range(2):
+        base = pl.multiple_of((spot ^ (4 * part)) * block_cells, block_cells)
+        total = residual[pl.ds(base, block_cells), :] + vec[10:11, :]
+        for step in range(4):
+            total = total + dot(heads[step][part], w_out[head ^ step])
+        cell = base + lax.broadcasted_iota(jnp.int32, (block_cells, channels), 0)
+        out[part] = jnp.where(cell < height * cols, total, 0.0).astype(jnp.bfloat16)
+
+
+def place_kernel(place, *refs):
+    parts, out, gathered = refs[:8], refs[8], refs[9]
+    head, column = place[2], place[3]
+    lines = parts[0].shape[1]
+    for far in range(4):
+        for near in range(2):
+            part = parts[far * 2 + near]
+            for other in range(2):
+                quarter = head ^ (near + 2 * other)
+                at = pl.ds(pl.multiple_of((column ^ far) * lines, 16), lines)
+                gathered[quarter, at, :] = part[other]
+    return out
+
+
+def swap(value, axis, step):
+    count = lax.axis_size(axis)
+    return lax.ppermute(value, axis, [(k, k ^ step) for k in range(count)])
+
+
+def pick(stacked, index):
+    return lax.dynamic_index_in_dim(stacked, index, 0, keepdims=False)
+
+
+def reduce_quarters(value, column, image):
+    lines = value.shape[0] // 4
+    parts = value.reshape(4, lines, value.shape[1])
+    total = pick(parts, column).astype(jnp.float32)
+    got = [swap(pick(parts, column ^ step), "img", step) for step in (1, 2, 3)]
+    for part in got:
+        total = total + part.astype(jnp.float32)
+    halves = total.reshape(2, lines // 2, value.shape[1])
+    away = swap(pick(halves, 1 - image).astype(jnp.bfloat16), "row", 4)
+    return (pick(halves, image) + away.astype(jnp.float32)).astype(jnp.bfloat16)
+
+
+def gather_quarters(chunk, image, column, head):
+    other = swap(chunk, "row", 4)
+    first = jnp.where(image == 0, chunk, other)
+    second = jnp.where(image == 0, other, chunk)
+    own = jnp.concatenate([first, second], axis=0)
+    pair = jnp.stack([own, swap(own, "row", 2)])
+    columns = [pair] + [swap(pair, "img", step) for step in (1, 2, 3)]
+    return columns, [swap(part, "row", 1) for part in columns]
+
+
+def ordered(columns, mates, column, head):
+    near = jnp.stack(columns)
+    far = jnp.stack(mates)
+    both = jnp.stack([near, far])
+    chunks = [pick(jnp.swapaxes(both, 0, 1), column ^ k) for k in range(4)]
+    line = jnp.stack(chunks)
+    line = jnp.transpose(line, (2, 1, 0, 3, 4)).reshape(4, -1, line.shape[-1])
+    return jnp.stack([pick(line, head ^ k) for k in range(4)])
+
+
+def tiled_out(*shapes):
+    return [jax.ShapeDtypeStruct(shape, kind) for shape, kind in shapes]
+
+
+def call(kernel, outs, scratch, limit, place, *operands):
+    spec = pl.BlockSpec(memory_space=pltpu.VMEM)
+    return pl.pallas_call(
+        kernel,
+        out_shape=tiled_out(*outs),
+        in_specs=[pl.BlockSpec(memory_space=pltpu.SMEM)] + [spec] * len(operands),
+        out_specs=[spec] * len(outs),
+        scratch_shapes=scratch,
+        compiler_params=mib(limit),
+    )(place, *operands)
+
+
+def gather_field(mine, theirs):
+    near = swap(mine, "row", 2)
+    far = swap(theirs, "row", 4)
+    far_near = swap(far, "row", 2)
+    return [
+        mine,
+        swap(mine, "row", 1),
+        near,
+        swap(near, "row", 1),
+        far,
+        swap(far, "row", 1),
+        far_near,
+        swap(far_near, "row", 1),
+    ]
+
+
+def local_image(
+    pixels,
+    heights,
+    timesteps,
+    norm1_gain,
+    norm1_bias,
+    conv1_weight,
+    conv1_bias,
+    time_weight,
+    time_bias,
+    norm2_gain,
+    norm2_bias,
+    conv2_weight,
+    conv2_bias,
+    norm3_gain,
+    norm3_bias,
+    qkv_weight,
+    qv_bias,
+    out_weight,
+    out_bias,
+    grad_out,
+):
+    images, row_count, cols, channels = pixels.shape
+    block_cells = row_count * cols
+    cells = block_cells * lax.axis_size("row")
+    half = channels // HEADS
+    spot = lax.axis_index("row")
+    column = lax.axis_index("img")
+    image = spot // HEADS
+    head = spot % HEADS
+    low, full = jnp.bfloat16, jnp.float32
+    height = pick(heights, image)
+    place = jnp.stack([spot, height, head, column, jnp.int32(cols)]).astype(jnp.int32)
+    pixel_blocks = pixels.reshape(images, block_cells, channels)
+    grad_blocks = grad_out.reshape(images, block_cells, channels)
+    field = gather_field(pick(pixel_blocks, image), pick(pixel_blocks, 1 - image))
+    field = list(lax.optimization_barrier(tuple(field)))
+    grad_mine, grad_theirs = pick(grad_blocks, image), pick(grad_blocks, 1 - image)
+    grads = gather_field(grad_mine, grad_theirs)
+
+    time_act = jax.nn.silu(embed_steps(timesteps, time_weight.shape[0]))
+    own_time = lax.dynamic_slice_in_dim(time_act, image, 1, axis=0)
+    shifts = jnp.dot(own_time, time_weight.astype(full), precision=PRECISE) + time_bias.astype(full)
+    vec = jnp.concatenate(
+        [
+            jnp.stack(
+                [
+                    norm1_gain.astype(full),
+                    norm1_bias.astype(full),
+                    conv1_bias.astype(full),
+                    norm2_gain.astype(full),
+                    norm2_bias.astype(full),
+                    1.0 + shifts[0, :channels],
+                    shifts[0, channels:],
+                    conv2_bias.astype(full),
+                    norm3_gain.astype(full),
+                    norm3_bias.astype(full),
+                    out_bias.astype(full),
+                ]
+            ),
+            jnp.zeros((5, channels), full),
+        ],
+        axis=0,
+    )
+    w_one = conv1_weight.reshape(3, 3 * channels, channels)
+    w_two = conv2_weight.reshape(3, 3 * channels, channels)
+    w_one_back = flipped(conv1_weight).reshape(3, 3 * channels, channels)
+    w_two_back = flipped(conv2_weight).reshape(3, 3 * channels, channels)
+    source = jnp.arange(3 * channels)[:, None]
+    target = jnp.arange(3 * half)[None, :]
+    wanted = target // half * channels + head * half + target % half
+    chosen = (source == wanted).astype(low)
+    rim_cells = cells + 2 * cols
+
+    pix, conv_one, residual, act_three, own_one, own_two, stats = call(
+        forward_kernel,
+        (
+            ((cells, channels), low),
+            ((cells, channels), full),
+            ((cells, channels), full),
+            ((cells, channels), low),
+            ((rim_cells, 3 * half), low),
+            ((rim_cells, 3 * half), low),
+            ((8, channels), full),
+        ),
+        [pltpu.VMEM((rim_cells, 3 * channels), low)],
+        40,
+        place,
+        *field,
+        w_one,
+        w_two,
+        vec,
+        chosen,
+    )
+
+    head_weight = pick(jnp.moveaxis(qkv_weight.reshape(channels, 3, HEADS, half), 2, 0), head)
+    empty = jnp.zeros((channels, half), low)
+    w_heads = jnp.concatenate(
+        [head_weight[:, 0], empty, head_weight[:, 1], empty, empty, head_weight[:, 2]], axis=1
+    )
+    head_bias = pick(jnp.moveaxis(qv_bias.reshape(2, HEADS, half), 1, 0), head).astype(full)
+    none = jnp.zeros((half,), full)
+    biases = jnp.concatenate([head_bias[0], none, none, none, none, head_bias[1]])[None, :]
+    out_heads = out_weight.reshape(HEADS, half, channels)
+    w_out = jnp.concatenate([empty, pick(out_heads, head).T], axis=1)
+    grad_proj, attended, packed, weight_rows, out_sums = call(
+        attention_kernel,
+        (
+            ((cells, channels), low),
+            ((cells, half), low),
+            ((cells + cells // 2, 2 * half), low),
+            ((5 * half, channels), low),
+            ((8, channels), full),
+        ),
+        [
+            pltpu.VMEM((cells, 2 * half), low),
+            pltpu.VMEM((2 * half, cells), low),
+            pltpu.VMEM((cells, 2 * half), low),
+            pltpu.VMEM((cells, 2 * half), low),
+            pltpu.VMEM((2 * half, cells), full),
+            pltpu.VMEM((cells, 2 * half), low),
+            pltpu.VMEM((1, cells), full),
+        ],
+        48,
+        place,
+        *grads,
+        act_three,
+        w_heads,
+        w_out,
+        biases,
+    )
+
+    packed_near = swap(packed, "row", 2)
+    packed_all = [packed, swap(packed, "row", 1), packed_near, swap(packed_near, "row", 1)]
+    qkv_t = jnp.transpose(qkv_weight).reshape(3, HEADS, half, channels)
+    w_key_value = jnp.concatenate([qkv_t[1], qkv_t[2]], axis=1)
+    grad_res, shifted_two, quarter_two, sums_three = call(
+        residual_kernel,
+        (
+            ((cells, channels), full),
+            ((rim_cells, 3 * channels), low),
+            ((9 * half, channels), low),
+            ((8, channels), full),
+        ),
+        [pltpu.VMEM((cells, channels), full), pltpu.VMEM((channels, cells), low)],
+        40,
+        place,
+        *packed_all,
+        w_key_value,
+        qkv_t[0],
+        grad_proj,
+        residual,
+        stats,
+        vec,
+        own_two,
+    )
+    early = jnp.concatenate([quarter_two, weight_rows], axis=0)
+    early_chunk = reduce_quarters(early, column, image)
+
+    shifted_one, quarter_one, sums_two = call(
+        second_kernel,
+        (
+            ((rim_cells, 3 * channels), low),
+            ((9 * half, channels), low),
+            ((8, channels), full),
+        ),
+        [pltpu.VMEM((cells, channels), full), pltpu.VMEM((channels, cells), low)],
+        40,
+        place,
+        shifted_two,
+        w_two_back,
+        conv_one,
+        stats,
+        vec,
+        own_one,
+    )
+    late_chunk = reduce_quarters(quarter_one, column, image)
+
+    grad_pair, sums_one = call(
+        first_kernel,
+        (((2, block_cells, channels), low), ((8, channels), full)),
+        [pltpu.VMEM((cells, channels), full)],
+        40,
+        place,
+        shifted_one,
+        w_one_back,
+        pix,
+        grad_res,
+        stats,
+        vec,
+    )
+
+    by_block = attended.reshape(2, HEADS, block_cells, half)
+
+    def blocks_for(step):
+        target = head ^ step
+        return jnp.stack(
+            [pick(pick(by_block, image), target), pick(pick(by_block, 1 - image), target)]
+        )
+
+    heads_got = [blocks_for(0)] + [swap(blocks_for(step), "row", step) for step in (1, 2, 3)]
+    (block_pair,) = call(
+        block_kernel,
+        (((2, block_cells, channels), low),),
+        [],
+        24,
+        place,
+        *heads_got,
+        out_heads,
+        residual,
+        vec,
+    )
+    out_pair = jnp.stack([block_pair[0], grad_pair[0]])
+    away_pair = swap(jnp.stack([block_pair[1], grad_pair[1]]), "row", 4)
+    first_pair = jnp.where(image == 0, out_pair, away_pair)
+    second_pair = jnp.where(image == 0, away_pair, out_pair)
+    finished = jnp.stack([first_pair, second_pair], axis=1).reshape((2,) + pixels.shape)
+
+    plain, cross = sums_two[1], sums_two[0]
+    scale_grad = vec[3] * cross + vec[4] * plain
+    which = column * images + image
+    all_images = images * lax.axis_size("img")
+    own_line = (jnp.arange(all_images) == which).astype(full)
+    shift_lines = own_line[:, None] * jnp.concatenate([scale_grad, plain])[None, :]
+    own_step = pick(timesteps, image).astype(full)
+    step_line = jnp.pad(own_line * own_step, (0, channels - all_images))
+    small = jnp.concatenate(
+        [
+            jnp.stack(
+                [
+                    sums_one[0],
+                    sums_one[1],
+                    sums_two[2],
+                    vec[5] * cross,
+                    vec[5] * plain,
+                    sums_three[2],
+                    sums_three[0],
+                    sums_three[1],
+                    out_sums[0],
+                    step_line,
+                ]
+            ),
+            shift_lines.reshape(2 * all_images, channels),
+        ],
+        axis=0,
+    )
+    small = jnp.where(head == 0, small, 0.0)
+    for axis, step in (("row", 1), ("row", 2), ("row", 4), ("img", 1), ("img", 2)):
+        small = small + swap(small, axis, step)
+    steps_all = small[9, :all_images]
+    shift_grads = small[10:].reshape(all_images, 2 * channels)
+    time_all = jax.nn.silu(embed_steps(steps_all, time_weight.shape[0]))
+    time_weight_grad = jnp.dot(time_all.T, shift_grads, precision=PRECISE)
+    time_bias_grad = jnp.sum(shift_grads, axis=0)
+
+    early_all = ordered(*gather_quarters(early_chunk, image, column, head), column, head)
+    late_all = ordered(*gather_quarters(late_chunk, image, column, head), column, head)
+
+    def kernel_full(rows_of):
+        taps = rows_of.reshape(HEADS, 3, 3, half, channels)
+        taps = jnp.transpose(taps, (1, 2, 0, 3, 4)).reshape(3, 3, channels, channels)
+        return taps.astype(full)
+
+    nine = 9 * half
+    conv1_weight_grad = kernel_full(late_all)
+    conv2_weight_grad = kernel_full(early_all[:, :nine])
+    proj_rows = early_all[:, nine : nine + 3 * half].reshape(HEADS, 3, half, channels)
+    qkv_weight_grad = jnp.transpose(proj_rows, (3, 1, 0, 2)).reshape(channels, -1).astype(full)
+    out_weight_grad = (
+        early_all[:, nine + 3 * half : nine + 4 * half].reshape(channels, channels).astype(full)
+    )
+    bias_row = early_all[:, nine + 4 * half].astype(full)
+    qv_bias_grad = jnp.concatenate(
+        [bias_row[:, :half].reshape(-1), bias_row[:, 3 * half :].reshape(-1)]
+    )
+    return (
+        finished[0],
+        finished[1],
+        small[0],
+        small[1],
+        conv1_weight_grad,
+        small[2],
+        time_weight_grad,
+        time_bias_grad,
+        small[3],
+        small[4],
+        conv2_weight_grad,
+        small[5],
+        small[6],
+        small[7],
+        qkv_weight_grad,
+        qv_bias_grad,
+        out_weight_grad,
+        small[8],
+    )
+
+
+def local(*arrays):
+    pixels = arrays[0]
+    if lax.axis_size("row") == pixels.shape[0] * HEADS and lax.axis_size("img") == 4:
+        return local_image(*arrays)
+    return local_rows(*arrays)
+
+
 def solution(mesh):
     placed = (
         P("img", "row", None, None),

time: 604 us -> 212 us (0.35); the launches traced: 594 us -> 211 us
  blocking collectives: 205 us -> 0 us
  matrix products: 95.1 us -> 3.69 us
  local copies, waits for them, and re-layouts: 113 us -> 44.8 us
  waiting for transfers between devices: 115 us -> 48.1 us
  Pallas kernels: 0 us -> 61 us
  starting transfers between devices: 12.7 us -> 43.5 us
  other arithmetic: 36.7 us -> 7.65 us
  between operations: 16.5 us -> 2.68 us
    psum x10 -> x0, blocking collectives: 177 us -> none  [the longest x3 49.4 us: norm_forward(): first_sum = lax.psum(jnp.sum(shaped * cell_mask, axis=(1, 2, 4)), 'row')]
    psum x1 -> x0, waiting for transfers between devices: 105 us -> none  [local(): lax.psum((norm1_gain_grad, norm1_bias_grad, conv1_weight_grad, conv1_bias...]
    dot_general x32 -> x2, matrix products: 89.7 us -> 3.69 us  [the longest x1 3.18 us: local_image(): time_weight_grad = jnp.dot(time_all.T, shift_grads, precision=PRECISE)]
    reshape x15 -> x4, local copies, waits for them, and re-layouts: 65.1 us -> 0.26 us  [the longest x1 0.08 us: local_image(): bias_row[:, 3 * half:].reshape(-1)]
    pallas_call x0 -> x6, Pallas kernels: none -> 61 us  [call(): pl.pallas_call(kernel, out_shape=tiled_out(*outs), in_specs=[pl.BlockSpec...]
    ppermute x8 -> x52, waiting for transfers between devices: 1.44 us -> 48.1 us  [swap(): return lax.ppermute(value, axis, [(k, k ^ step) for k in range(count)])]
    ppermute x8 -> x52, starting transfers between devices: 12.3 us -> 43.5 us  [swap(): return lax.ppermute(value, axis, [(k, k ^ step) for k in range(count)])]
    all_gather x2 -> x0, blocking collectives: 27.9 us -> none  [the longest x1 14 us: local(): lax.all_gather(delta_own.reshape(stat_shape), 'row', axis=1, tiled=True)]
  transfers between devices with their start and end apart: 13 -> 52, of which waited for: 4 -> 18; matrix products, arithmetic and copies ran while one was open for 23% -> 15% of each run, Pallas kernels for 0% -> 9%
where the time goes in v1:
time: 212 us; the launch traced here: 211 us
  Pallas kernels  61 us (29%)
  waiting for transfers between devices  48.1 us (23%)
  local copies, waits for them, and re-layouts  44.8 us (21%)
  starting transfers between devices  43.5 us (21%)
  other arithmetic  7.65 us (4%)
  matrix products  3.69 us (2%)
  between operations  2.68 us (1%)
    pallas_call x6, Pallas kernels, call(): pl.pallas_call(kernel, out_shape=tiled_out(*outs), in_specs=[pl.BlockSpec...  61 us
    ppermute x52, waiting for transfers between devices, swap(): return lax.ppermute(value, axis, [(k, k ^ step) for k in range(count)])  48.1 us
    ppermute x52, starting transfers between devices, swap(): return lax.ppermute(value, axis, [(k, k ^ step) for k in range(count)])  43.5 us
    unnamed x131, local copies, waits for them, and re-layouts  18.4 us
    transpose x4, local copies, waits for them, and re-layouts, flipped(): return jnp.transpose(kernel[::-1, ::-1], (0, 1, 3, 2))  7.4 us
  transfers between devices with their start and end apart: 52, of which 18 were waited for; matrix products, arithmetic and copies ran while one was open for 15% of the time, Pallas kernels for 9%

profile of v1, /device:TPU:0, one launch (start us, length us, event | category | flops | bytes accessed | tf_op | source)
XLA Modules:
  0.0 211.5 jit_solution(13779926508633725761)
XLA Ops:
  0.7 1.1 dynamic-slice_bitcast_fusion
  2.4 2.6 %collective-permute-start.8 = (bf16[256,256]{1,0:T(8,128)(2,1)S(1)}, bf16[256,256]{1,0:T(8,128)(2,1)S(1)}, u32[]{:S(2)}, u32[]{:S(2)}) collective-permute-start(bf16[256,256]{1,0:T(8,128)(2,1)S(1)} %get-tuple-element.47.refs_0_), channel_id=1, source_target_pairs={{0,2},{1,3},{2,0},{3,1},{4,6},{5,7},{6,4},{7,5},{8,10},{9,11},{10,... | collective-permute-start | bytes 393224 | tf_op jit(solution)/shard_map/ppermute | solution.py:840
  5.0 1.6 dynamic-slice_bitcast_fusion.2
  6.7 3.0 %collective-permute-start.3 = (bf16[256,256]{1,0:T(8,128)(2,1)S(1)}, bf16[256,256]{1,0:T(8,128)(2,1)}, u32[]{:S(2)}, u32[]{:S(2)}) collective-permute-start(bf16[256,256]{1,0:T(8,128)(2,1)S(1)} %get-tuple-element.155), channel_id=1, source_target_pairs={{0,4},{1,5},{2,6},{3,7},{4,0},{5,1},{6,2},{7,3},{8,12},{9,13},{10,... | collective-permute-start | bytes 393224 | tf_op jit(solution)/shard_map/ppermute | solution.py:840
  12.6 9.1 %collective-permute-done.10.refs_4_ = bf16[256,256]{1,0:T(8,128)(2,1)S(1)} collective-permute-done((bf16[256,256]{1,0:T(8,128)(2,1)S(1)}, bf16[256,256]{1,0:T(8,128)(2,1)S(1)}, u32[]{:S(2)}, u32[]{:S(2)}) %collective-permute-start.10) | collective-permute-done | bytes 131104 | tf_op jit(solution)/shard_map/ppermute | solution.py:840
  22.6 1.2 collective-permute-start.5
  26.1 1.2 stack.229.place
  28.2 2.4 %collective-permute-done.5.refs_6_ = bf16[256,256]{1,0:T(8,128)(2,1)} collective-permute-done((bf16[256,256]{1,0:T(8,128)(2,1)}, bf16[256,256]{1,0:T(8,128)(2,1)}, u32[]{:S(2)}, u32[]{:S(2)}) %collective-permute-start.5) | collective-permute-done | bytes 131104 | tf_op jit(solution)/shard_map/ppermute | solution.py:840
  33.3 1.3 copy-done.3
  41.5 17.7 %shard_map.331 = (bf16[2048,256]{1,0:T(8,128)(2,1)S(1)}, f32[2048,256]{1,0:T(8,128)S(1)}, f32[2048,256]{1,0:T(8,128)S(1)}, bf16[2048,256]{1,0:T(8,128)(2,1)S(1)}...) custom-call(s32[5]{0:T(128)S(1)} %copy-done.37, ...), custom_call_target="tpu_custom_call" | custom-call | tf_op jit(solution)/shard_map/pallas_call | solution.py:885
  59.3 1.3 copy-done.5
  62.6 1.0 copy-done.11
  64.2 22.1 %shard_map.332 = (bf16[2048,256]{1,0:T(8,128)(2,1)S(1)}, bf16[2048,64]{1,0:T(8,128)(2,1)S(1)}, bf16[3072,128]{1,0:T(8,128)(2,1)}, bf16[320,256]{1,0:T(8,128)(2,1)S(1)}, f32[8,256]{1,0:T(8,128)S(1)}) custom-call(s32[5]{0:T(128)S(1)} %copy-done.38, bf16[256,256]{1,0:T(8,128)(2,1)} %get-tuple-element.156.refs_0_, ...), custom_call_target="tpu_custom_call" | custom-call | tf_op jit(solution)/shard_map/pallas_call | solution.py:885
  90.9 1.7 copy.62
  94.4 1.1 reverse_bitcast_fusion.1
  95.5 1.6 copy.64
  97.0 2.4 %reverse_bitcast_fusion = bf16[3,3,256,256]{2,3,1,0:T(8,128)(2,1)} fusion(bf16[3,3,256,256]{3,2,1,0:T(8,128)(2,1)} %param.25), kind=kLoop, calls=%fused_computation.22 | loop fusion | bytes 2359296 | tf_op jit(solution)/shard_map/transpose | solution.py:64
  99.4 2.4 %copy.65 = bf16[3,3,256,256]{3,2,1,0:T(8,128)(2,1)} copy(bf16[3,3,256,256]{2,3,1,0:T(8,128)(2,1)} %reverse_bitcast_fusion) | data formatting | bytes 2359296 | tf_op jit(solution)/shard_map/transpose | solution.py:64
  103.7 5.7 %collective-permute-done.18.refs_2_ = bf16[3072,128]{1,0:T(8,128)(2,1)} collective-permute-done((bf16[3072,128]{1,0:T(8,128)(2,1)}, bf16[3072,128]{1,0:T(8,128)(2,1)}, u32[]{:S(2)}, u32[]{:S(2)}) %collective-permute-start.18) | collective-permute-done | bytes 786464 | tf_op jit(solution)/shard_map/ppermute | solution.py:840
  109.5 1.1 dynamic-slice_bitcast_fusion.11
  113.5 4.2 %collective-permute-done.15.refs_2_ = bf16[2,256,64]{2,1,0:T(8,128)(2,1)S(1)} collective-permute-done((bf16[2,256,64]{2,1,0:T(8,128)(2,1)S(1)}, bf16[2,256,64]{2,1,0:T(8,128)(2,1)S(1)}, u32[]{:S(2)}, u32[]{:S(2)}) %collective-permute-start.15) | collective-permute-done | bytes 65568 | tf_op jit(solution)/shard_map/ppermute | solution.py:840
  120.3 6.5 %shard_map.334 = (f32[2048,256]{1,0:T(8,128)S(1)}, bf16[2176,768]{1,0:T(8,128)(2,1)S(1)}, bf16[576,256]{1,0:T(8,128)(2,1)S(1)}, f32[8,256]{1,0:T(8,128)S(1)}) custom-call(s32[5]{0:T(128)S(1)} %copy-done.39, bf16[3072,128]{1,0:T(8,128)(2,1)} %get-tuple-element.58.refs_0_, bf16[3072,128]{1,0:T(8,128)(2,1)S(1)} %collective-permute-done.17.refs_1_, ...), custom_call_target="tpu_custom_call" | custom-call | tf_op jit(solution)/shard_map/pallas_call | solution.py:885
  126.9 8.1 %shard_map.335 = (bf16[2176,768]{1,0:T(8,128)(2,1)S(1)}, bf16[576,256]{1,0:T(8,128)(2,1)S(1)}, f32[8,256]{1,0:T(8,128)S(1)}) custom-call(s32[5]{0:T(128)S(1)} %copy-done.39, bf16[2176,768]{1,0:T(8,128)(2,1)S(1)} %get-tuple-element.62.shifted, bf16[3,768,256]{2,1,0:T(8,128)(2,1)S(1)} %bitcast.209, f32[2048,256]{1,0:T(8,128)S(1)} %copy-done.6, ...), custom_call_target="tpu_custom_call" | custom-call | tf_op jit(solution)/shard_map/pallas_call | solution.py:885
  135.0 5.7 %shard_map.336 = (bf16[2,256,256]{2,1,0:T(8,128)(2,1)S(1)}, f32[8,256]{1,0:T(8,128)S(1)}) custom-call(s32[5]{0:T(128)S(1)} %copy-done.39, bf16[2176,768]{1,0:T(8,128)(2,1)S(1)} %get-tuple-element.65.shifted, bf16[3,768,256]{2,1,0:T(8,128)(2,1)S(1)} %bitcast.212, bf16[2048,256]{1,0:T(8,128)(2,1)S(1)} %copy-done.12, ...), custom_call_target="tpu_custom_call" | custom-call | tf_op jit(solution)/shard_map/pallas_call | solution.py:885
  142.3 4.6 %collective-permute-start.28 = (bf16[144,256]{1,0:T(8,128)(2,1)S(1)}, bf16[144,256]{1,0:T(8,128)(2,1)S(1)}, u32[]{:S(2)}, u32[]{:S(2)}) collective-permute-start(bf16[144,256]{1,0:T(8,128)(2,1)S(1)} %get-tuple-element.147), channel_id=1, source_target_pairs={{0,24},{8,16},{16,8},{24,0},{1,25},{9,17},{17,9},{25,1},{2,26},{10... | collective-permute-start | bytes 221192 | tf_op jit(solution)/shard_map/ppermute | solution.py:840
  147.6 1.8 collective-permute-start.22
  149.5 5.8 %collective-permute-done.22 = f32[26,256]{1,0:T(8,128)S(1)} collective-permute-done((f32[26,256]{1,0:T(8,128)S(1)}, f32[26,256]{1,0:T(8,128)S(1)}, u32[]{:S(2)}, u32[]{:S(2)}) %collective-permute-start.22) | collective-permute-done | bytes 26656 | tf_op jit(solution)/shard_map/ppermute | solution.py:840
  155.5 3.0 %collective-permute-start.29 = (bf16[72,256]{1,0:T(8,128)(2,1)S(1)}, bf16[72,256]{1,0:T(8,128)(2,1)S(1)}, u32[]{:S(2)}, u32[]{:S(2)}) collective-permute-start(bf16[72,256]{1,0:T(8,128)(2,1)S(1)} %fusion.25), channel_id=1, source_target_pairs={{0,4},{1,5},{2,6},{3,7},{4,0},{5,1},{6,2},{7,3},{8,12},{9,13},{10,... | collective-permute-start | bytes 110600 | tf_op jit(solution)/shard_map/ppermute | solution.py:840
  158.5 1.7 collective-permute-done.23
  160.2 2.1 collective-permute-start.24
  164.6 1.6 collective-permute-start.39
  166.2 1.5 collective-permute-start.25
  169.5 1.8 collective-permute-start.42
  171.5 3.2 %fusion.26 = f32[1024,512]{1,0:T(8,128)} fusion(f32[8,512]{1,0:T(8,128)S(1)} %reshape.254, f32[8,512]{1,0:T(8,128)S(1)} %get-tuple-element.189, f32[8,512]{1,0:T(8,128)S(1)} %get-tuple-element.188), kind=kOutput, calls=%fused_computation.108 | convolution fusion | flops 50372608 | bytes 2146304 | tf_op jit(solution)/shard_map/dot_general | solution.py:1163
  176.7 1.4 collective-permute-start.43
  178.1 2.5 %collective-permute-done.31 = bf16[144,256]{1,0:T(8,128)(2,1)S(1)} collective-permute-done((bf16[144,256]{1,0:T(8,128)(2,1)S(1)}, bf16[144,256]{1,0:T(8,128)(2,1)S(1)}, u32[]{:S(2)}, u32[]{:S(2)}) %collective-permute-start.31) | collective-permute-done | bytes 73760 | tf_op jit(solution)/shard_map/ppermute | solution.py:840
  180.6 1.1 collective-permute-start.34
  182.0 2.2 %collective-permute-start.32 = (bf16[2,144,256]{2,1,0:T(8,128)(2,1)S(1)}, bf16[2,144,256]{2,1,0:T(8,128)(2,1)S(1)}, u32[]{:S(2)}, u32[]{:S(2)}) collective-permute-start(bf16[2,144,256]{2,1,0:T(8,128)(2,1)S(1)} %get-tuple-element.163), channel_id=1, source_target_pairs={{0,8},{8,0},{16,24},{24,16},{1,9},{9,1},{17,25},{25,17},{2,10},{10... | collective-permute-start | bytes 442376 | tf_op jit(solution)/shard_map/ppermute | solution.py:840
  185.7 1.2 collective-permute-done.34
  186.8 1.5 collective-permute-done.33
  188.8 1.0 collective-permute-done.44
  189.9 1.1 collective-permute-start.47
  191.6 2.0 collective-permute-start.45
  194.3 5.2 %collective-permute-done.47 = bf16[2,224,256]{2,1,0:T(8,128)(2,1)S(1)} collective-permute-done((bf16[2,224,256]{2,1,0:T(8,128)(2,1)S(1)}, bf16[2,224,256]{2,1,0:T(8,128)(2,1)S(1)}, u32[]{:S(2)}, u32[]{:S(2)}) %collective-permute-start.47) | collective-permute-done | bytes 229408 | tf_op jit(solution)/shard_map/ppermute | solution.py:840
  199.4 3.6 %collective-permute-done.46 = bf16[2,224,256]{2,1,0:T(8,128)(2,1)S(1)} collective-permute-done((bf16[2,224,256]{2,1,0:T(8,128)(2,1)S(1)}, bf16[2,224,256]{2,1,0:T(8,128)(2,1)S(1)}, u32[]{:S(2)}, u32[]{:S(2)}) %collective-permute-start.46) | collective-permute-done | bytes 229408 | tf_op jit(solution)/shard_map/ppermute | solution.py:840
  203.8 1.6 copy.67
  207.0 1.6 copy.70
  208.7 1.1 copy.72
  (324 shorter events, 48.5 us)
Async XLA Ops:
  1.8 25.8 %collective-permute-start.7 = (bf16[256,256]{1,0:T(8,128)(2,1)S(1)}, bf16[256,256]{1,0:T(8,128)(2,1)S(1)}, u32[]{:S(2)}, u32[]{:S(2)}) collective-permute-start(bf16[256,256]{1,0:T(8,128)(2,1)S(1)} %get-tuple-element.47.refs_0_), channel_id=1, source_target_pairs={{0,1},{1,0},{2,3},{3,2},{4,5},{5,4},{6,7},{7,6},{8,9},{9,8},{10,11... | collective-permute-start | bytes 393224 | tf_op jit(solution)/shard_map/ppermute | solution.py:840
  2.4 21.5 %collective-permute-start.8 = (bf16[256,256]{1,0:T(8,128)(2,1)S(1)}, bf16[256,256]{1,0:T(8,128)(2,1)S(1)}, u32[]{:S(2)}, u32[]{:S(2)}) collective-permute-start(bf16[256,256]{1,0:T(8,128)(2,1)S(1)} %get-tuple-element.47.refs_0_), channel_id=1, source_target_pairs={{0,2},{1,3},{2,0},{3,1},{4,6},{5,7},{6,4},{7,5},{8,10},{9,11},{10,... | collective-permute-start | bytes 393224 | tf_op jit(solution)/shard_map/ppermute | solution.py:840
  6.6 15.1 %collective-permute-start.1 = (bf16[256,256]{1,0:T(8,128)(2,1)}, bf16[256,256]{1,0:T(8,128)(2,1)}, u32[]{:S(2)}, u32[]{:S(2)}) collective-permute-start(bf16[256,256]{1,0:T(8,128)(2,1)} %get-tuple-element.156.refs_0_), channel_id=1, source_target_pairs={{0,2},{1,3},{2,0},{3,1},{4,6},{5,7},{6,4},{7,5},{8,10},{9,11},{10,... | collective-permute-start | bytes 393224 | tf_op jit(solution)/shard_map/ppermute | solution.py:840
  6.7 15.9 %collective-permute-start.3 = (bf16[256,256]{1,0:T(8,128)(2,1)S(1)}, bf16[256,256]{1,0:T(8,128)(2,1)}, u32[]{:S(2)}, u32[]{:S(2)}) collective-permute-start(bf16[256,256]{1,0:T(8,128)(2,1)S(1)} %get-tuple-element.155), channel_id=1, source_target_pairs={{0,4},{1,5},{2,6},{3,7},{4,0},{5,1},{6,2},{7,3},{8,12},{9,13},{10,... | collective-permute-start | bytes 393224 | tf_op jit(solution)/shard_map/ppermute | solution.py:840
  9.7 12.0 %collective-permute-start.10 = (bf16[256,256]{1,0:T(8,128)(2,1)S(1)}, bf16[256,256]{1,0:T(8,128)(2,1)S(1)}, u32[]{:S(2)}, u32[]{:S(2)}) collective-permute-start(bf16[256,256]{1,0:T(8,128)(2,1)S(1)} %get-tuple-element.153), channel_id=1, source_target_pairs={{0,4},{1,5},{2,6},{3,7},{4,0},{5,1},{6,2},{7,3},{8,12},{9,13},{10,... | collective-permute-start | bytes 393224 | tf_op jit(solution)/shard_map/ppermute | solution.py:840
  21.7 10.0 %collective-permute-start.11 = (bf16[256,256]{1,0:T(8,128)(2,1)S(1)}, bf16[256,256]{1,0:T(8,128)(2,1)S(1)}, u32[]{:S(2)}, u32[]{:S(2)}) collective-permute-start(bf16[256,256]{1,0:T(8,128)(2,1)S(1)} %collective-permute-done.10.refs_4_), channel_id=1, source_target_pairs={{0,1},{1,0},{2,3},{3,2},{4,5},{5,4},{6,7},{7,6},{8,9},{9,8},{10,11... | collective-permute-start | bytes 393224 | tf_op jit(solution)/shard_map/ppermute | solution.py:840
  21.7 10.1 %collective-permute-start.12 = (bf16[256,256]{1,0:T(8,128)(2,1)S(1)}, bf16[256,256]{1,0:T(8,128)(2,1)S(1)}, u32[]{:S(2)}, u32[]{:S(2)}) collective-permute-start(bf16[256,256]{1,0:T(8,128)(2,1)S(1)} %collective-permute-done.10.refs_4_), channel_id=1, source_target_pairs={{0,2},{1,3},{2,0},{3,1},{4,6},{5,7},{6,4},{7,5},{8,10},{9,11},{10,... | collective-permute-start | bytes 393224 | tf_op jit(solution)/shard_map/ppermute | solution.py:840
  22.6 8.0 %collective-permute-start.5 = (bf16[256,256]{1,0:T(8,128)(2,1)}, bf16[256,256]{1,0:T(8,128)(2,1)}, u32[]{:S(2)}, u32[]{:S(2)}) collective-permute-start(bf16[256,256]{1,0:T(8,128)(2,1)} %collective-permute-done.3.refs_4_), channel_id=1, source_target_pairs={{0,2},{1,3},{2,0},{3,1},{4,6},{5,7},{6,4},{7,5},{8,10},{9,11},{10,... | collective-permute-start | bytes 393224 | tf_op jit(solution)/shard_map/ppermute | solution.py:840
  23.8 6.7 %collective-permute-start.9 = (bf16[256,256]{1,0:T(8,128)(2,1)S(1)}, bf16[256,256]{1,0:T(8,128)(2,1)S(1)}, u32[]{:S(2)}, u32[]{:S(2)}) collective-permute-start(bf16[256,256]{1,0:T(8,128)(2,1)S(1)} %collective-permute-done.8.refs_2_), channel_id=1, source_target_pairs={{0,1},{1,0},{2,3},{3,2},{4,5},{5,4},{6,7},{7,6},{8,9},{9,8},{10,11... | collective-permute-start | bytes 393224 | tf_op jit(solution)/shard_map/ppermute | solution.py:840
  27.6 36.6 %collective-permute-start = (bf16[256,256]{1,0:T(8,128)(2,1)}, bf16[256,256]{1,0:T(8,128)(2,1)S(1)}, u32[]{:S(2)}, u32[]{:S(2)}) collective-permute-start(bf16[256,256]{1,0:T(8,128)(2,1)} %get-tuple-element.156.refs_0_), channel_id=1, source_target_pairs={{0,1},{1,0},{2,3},{3,2},{4,5},{5,4},{6,7},{7,6},{8,9},{9,8},{10,11... | collective-permute-start | bytes 393224 | tf_op jit(solution)/shard_map/ppermute | solution.py:840
  30.5 33.7 %collective-permute-start.4 = (bf16[256,256]{1,0:T(8,128)(2,1)}, bf16[256,256]{1,0:T(8,128)(2,1)S(1)}, u32[]{:S(2)}, u32[]{:S(2)}) collective-permute-start(bf16[256,256]{1,0:T(8,128)(2,1)} %collective-permute-done.3.refs_4_), channel_id=1, source_target_pairs={{0,1},{1,0},{2,3},{3,2},{4,5},{5,4},{6,7},{7,6},{8,9},{9,8},{10,11... | collective-permute-start | bytes 393224 | tf_op jit(solution)/shard_map/ppermute | solution.py:840
  31.2 33.0 %collective-permute-start.2 = (bf16[256,256]{1,0:T(8,128)(2,1)}, bf16[256,256]{1,0:T(8,128)(2,1)S(1)}, u32[]{:S(2)}, u32[]{:S(2)}) collective-permute-start(bf16[256,256]{1,0:T(8,128)(2,1)} %collective-permute-done.1.refs_2_), channel_id=1, source_target_pairs={{0,1},{1,0},{2,3},{3,2},{4,5},{5,4},{6,7},{7,6},{8,9},{9,8},{10,11... | collective-permute-start | bytes 393224 | tf_op jit(solution)/shard_map/ppermute | solution.py:840
  31.7 32.5 %collective-permute-start.6 = (bf16[256,256]{1,0:T(8,128)(2,1)}, bf16[256,256]{1,0:T(8,128)(2,1)S(1)}, u32[]{:S(2)}, u32[]{:S(2)}) collective-permute-start(bf16[256,256]{1,0:T(8,128)(2,1)} %collective-permute-done.5.refs_6_), channel_id=1, source_target_pairs={{0,1},{1,0},{2,3},{3,2},{4,5},{5,4},{6,7},{7,6},{8,9},{9,8},{10,11... | collective-permute-start | bytes 393224 | tf_op jit(solution)/shard_map/ppermute | solution.py:840
  89.4 20.1 %collective-permute-start.18 = (bf16[3072,128]{1,0:T(8,128)(2,1)}, bf16[3072,128]{1,0:T(8,128)(2,1)}, u32[]{:S(2)}, u32[]{:S(2)}) collective-permute-start(bf16[3072,128]{1,0:T(8,128)(2,1)} %get-tuple-element.58.refs_0_), channel_id=1, source_target_pairs={{0,2},{1,3},{2,0},{3,1},{4,6},{5,7},{6,4},{7,5},{8,10},{9,11},{10,... | collective-permute-start | bytes 2359304 | tf_op jit(solution)/shard_map/ppermute | solution.py:840
  103.6 16.6 %collective-permute-start.17 = (bf16[3072,128]{1,0:T(8,128)(2,1)}, bf16[3072,128]{1,0:T(8,128)(2,1)S(1)}, u32[]{:S(2)}, u32[]{:S(2)}) collective-permute-start(bf16[3072,128]{1,0:T(8,128)(2,1)} %get-tuple-element.58.refs_0_), channel_id=1, source_target_pairs={{0,1},{1,0},{2,3},{3,2},{4,5},{5,4},{6,7},{7,6},{8,9},{9,8},{10,11... | collective-permute-start | bytes 2359304 | tf_op jit(solution)/shard_map/ppermute | solution.py:840
  109.5 10.8 %collective-permute-start.19 = (bf16[3072,128]{1,0:T(8,128)(2,1)}, bf16[3072,128]{1,0:T(8,128)(2,1)S(1)}, u32[]{:S(2)}, u32[]{:S(2)}) collective-permute-start(bf16[3072,128]{1,0:T(8,128)(2,1)} %collective-permute-done.18.refs_2_), channel_id=1, source_target_pairs={{0,1},{1,0},{2,3},{3,2},{4,5},{5,4},{6,7},{7,6},{8,9},{9,8},{10,11... | collective-permute-start | bytes 2359304 | tf_op jit(solution)/shard_map/ppermute | solution.py:840
  111.2 6.4 %collective-permute-start.15 = (bf16[2,256,64]{2,1,0:T(8,128)(2,1)S(1)}, bf16[2,256,64]{2,1,0:T(8,128)(2,1)S(1)}, u32[]{:S(2)}, u32[]{:S(2)}) collective-permute-start(bf16[2,256,64]{2,1,0:T(8,128)(2,1)S(1)} %pad_maximum_fusion.14), channel_id=1, source_target_pairs={{0,2},{1,3},{2,0},{3,1},{4,6},{5,7},{6,4},{7,5},{8,10},{9,11},{10,... | collective-permute-start | bytes 196616 | tf_op jit(solution)/shard_map/ppermute | solution.py:840
  112.1 6.5 %collective-permute-start.16 = (bf16[2,256,64]{2,1,0:T(8,128)(2,1)S(1)}, bf16[2,256,64]{2,1,0:T(8,128)(2,1)S(1)}, u32[]{:S(2)}, u32[]{:S(2)}) collective-permute-start(bf16[2,256,64]{2,1,0:T(8,128)(2,1)S(1)} %pad_maximum_fusion.15), channel_id=1, source_target_pairs={{0,3},{1,2},{2,1},{3,0},{4,7},{5,6},{6,5},{7,4},{8,11},{9,10},{10,... | collective-permute-start | bytes 196616 | tf_op jit(solution)/shard_map/ppermute | solution.py:840
  140.8 43.4 %collective-permute-start.20 = (bf16[2,256,256]{2,1,0:T(8,128)(2,1)S(1)}, bf16[2,256,256]{2,1,0:T(8,128)(2,1)S(1)}, u32[]{:S(2)}, u32[]{:S(2)}) collective-permute-start(bf16[2,256,256]{2,1,0:T(8,128)(2,1)S(1)} %pad_maximum_fusion.8), channel_id=1, source_target_pairs={{0,4},{1,5},{2,6},{3,7},{4,0},{5,1},{6,2},{7,3},{8,12},{9,13},{10,... | collective-permute-start | bytes 786440 | tf_op jit(solution)/shard_map/ppermute | solution.py:840
  141.5 6.1 %collective-permute-start.21 = (f32[26,256]{1,0:T(8,128)S(1)}, f32[26,256]{1,0:T(8,128)S(1)}, u32[]{:S(2)}, u32[]{:S(2)}) collective-permute-start(f32[26,256]{1,0:T(8,128)S(1)} %broadcast_select_fusion.4), channel_id=1, source_target_pairs={{0,1},{1,0},{2,3},{3,2},{4,5},{5,4},{6,7},{7,6},{8,9},{9,8},{10,11... | collective-permute-start | bytes 79880 | tf_op jit(solution)/shard_map/ppermute | solution.py:840
  142.3 13.1 %collective-permute-start.28 = (bf16[144,256]{1,0:T(8,128)(2,1)S(1)}, bf16[144,256]{1,0:T(8,128)(2,1)S(1)}, u32[]{:S(2)}, u32[]{:S(2)}) collective-permute-start(bf16[144,256]{1,0:T(8,128)(2,1)S(1)} %get-tuple-element.147), channel_id=1, source_target_pairs={{0,24},{8,16},{16,8},{24,0},{1,25},{9,17},{17,9},{25,1},{2,26},{10... | collective-permute-start | bytes 221192 | tf_op jit(solution)/shard_map/ppermute | solution.py:840
  147.0 8.4 %collective-permute-start.27 = (bf16[144,256]{1,0:T(8,128)(2,1)S(1)}, bf16[144,256]{1,0:T(8,128)(2,1)S(1)}, u32[]{:S(2)}, u32[]{:S(2)}) collective-permute-start(bf16[144,256]{1,0:T(8,128)(2,1)S(1)} %get-tuple-element.148), channel_id=1, source_target_pairs={{0,16},{8,24},{16,0},{24,8},{1,17},{9,25},{17,1},{25,9},{2,18},{10... | collective-permute-start | bytes 221192 | tf_op jit(solution)/shard_map/ppermute | solution.py:840
  147.5 8.0 %collective-permute-start.26 = (bf16[144,256]{1,0:T(8,128)(2,1)S(1)}, bf16[144,256]{1,0:T(8,128)(2,1)S(1)}, u32[]{:S(2)}, u32[]{:S(2)}) collective-permute-start(bf16[144,256]{1,0:T(8,128)(2,1)S(1)} %get-tuple-element.146), channel_id=1, source_target_pairs={{0,8},{8,0},{16,24},{24,16},{1,9},{9,1},{17,25},{25,17},{2,10},{10... | collective-permute-start | bytes 221192 | tf_op jit(solution)/shard_map/ppermute | solution.py:840
  147.6 7.7 %collective-permute-start.22 = (f32[26,256]{1,0:T(8,128)S(1)}, f32[26,256]{1,0:T(8,128)S(1)}, u32[]{:S(2)}, u32[]{:S(2)}) collective-permute-start(f32[26,256]{1,0:T(8,128)S(1)} %fusion.62), channel_id=1, source_target_pairs={{0,2},{1,3},{2,0},{3,1},{4,6},{5,7},{6,4},{7,5},{8,10},{9,11},{10,... | collective-permute-start | bytes 79880 | tf_op jit(solution)/shard_map/ppermute | solution.py:840
  155.3 4.9 %collective-permute-start.23 = (f32[26,256]{1,0:T(8,128)S(1)}, f32[26,256]{1,0:T(8,128)S(1)}, u32[]{:S(2)}, u32[]{:S(2)}) collective-permute-start(f32[26,256]{1,0:T(8,128)S(1)} %add.254), channel_id=1, source_target_pairs={{0,4},{1,5},{2,6},{3,7},{4,0},{5,1},{6,2},{7,3},{8,12},{9,13},{10,... | collective-permute-start | bytes 79880 | tf_op jit(solution)/shard_map/ppermute | solution.py:840
  155.5 10.7 %collective-permute-start.29 = (bf16[72,256]{1,0:T(8,128)(2,1)S(1)}, bf16[72,256]{1,0:T(8,128)(2,1)S(1)}, u32[]{:S(2)}, u32[]{:S(2)}) collective-permute-start(bf16[72,256]{1,0:T(8,128)(2,1)S(1)} %fusion.25), channel_id=1, source_target_pairs={{0,4},{1,5},{2,6},{3,7},{4,0},{5,1},{6,2},{7,3},{8,12},{9,13},{10,... | collective-permute-start | bytes 110600 | tf_op jit(solution)/shard_map/ppermute | solution.py:840
  160.2 4.4 %collective-permute-start.24 = (f32[26,256]{1,0:T(8,128)S(1)}, f32[26,256]{1,0:T(8,128)S(1)}, u32[]{:S(2)}, u32[]{:S(2)}) collective-permute-start(f32[26,256]{1,0:T(8,128)S(1)} %add.255), channel_id=1, source_target_pairs={{0,8},{8,0},{16,24},{24,16},{1,9},{9,1},{17,25},{25,17},{2,10},{10... | collective-permute-start | bytes 79880 | tf_op jit(solution)/shard_map/ppermute | solution.py:840
  162.3 5.9 %collective-permute-start.41 = (bf16[224,256]{1,0:T(8,128)(2,1)S(1)}, bf16[224,256]{1,0:T(8,128)(2,1)S(1)}, u32[]{:S(2)}, u32[]{:S(2)}) collective-permute-start(bf16[224,256]{1,0:T(8,128)(2,1)S(1)} %get-tuple-element.141), channel_id=1, source_target_pairs={{0,24},{8,16},{16,8},{24,0},{1,25},{9,17},{17,9},{25,1},{2,26},{10... | collective-permute-start | bytes 344072 | tf_op jit(solution)/shard_map/ppermute | solution.py:840
  163.2 6.0 %collective-permute-start.40 = (bf16[224,256]{1,0:T(8,128)(2,1)S(1)}, bf16[224,256]{1,0:T(8,128)(2,1)S(1)}, u32[]{:S(2)}, u32[]{:S(2)}) collective-permute-start(bf16[224,256]{1,0:T(8,128)(2,1)S(1)} %get-tuple-element.142), channel_id=1, source_target_pairs={{0,16},{8,24},{16,0},{24,8},{1,17},{9,25},{17,1},{25,9},{2,18},{10... | collective-permute-start | bytes 344072 | tf_op jit(solution)/shard_map/ppermute | solution.py:840
  164.6 4.8 %collective-permute-start.39 = (bf16[224,256]{1,0:T(8,128)(2,1)S(1)}, bf16[224,256]{1,0:T(8,128)(2,1)S(1)}, u32[]{:S(2)}, u32[]{:S(2)}) collective-permute-start(bf16[224,256]{1,0:T(8,128)(2,1)S(1)} %get-tuple-element.140), channel_id=1, source_target_pairs={{0,8},{8,0},{16,24},{24,16},{1,9},{9,1},{17,25},{25,17},{2,10},{10... | collective-permute-start | bytes 344072 | tf_op jit(solution)/shard_map/ppermute | solution.py:840
  166.2 5.1 %collective-permute-start.25 = (f32[26,256]{1,0:T(8,128)S(1)}, f32[26,256]{1,0:T(8,128)S(1)}, u32[]{:S(2)}, u32[]{:S(2)}) collective-permute-start(f32[26,256]{1,0:T(8,128)S(1)} %add.256), channel_id=1, source_target_pairs={{0,16},{8,24},{16,0},{24,8},{1,17},{9,25},{17,1},{25,9},{2,18},{10... | collective-permute-start | bytes 79880 | tf_op jit(solution)/shard_map/ppermute | solution.py:840
  168.2 7.7 %collective-permute-start.30 = (bf16[72,256]{1,0:T(8,128)(2,1)S(1)}, bf16[72,256]{1,0:T(8,128)(2,1)S(1)}, u32[]{:S(2)}, u32[]{:S(2)}) collective-permute-start(bf16[72,256]{1,0:T(8,128)(2,1)S(1)} %fusion.23), channel_id=1, source_target_pairs={{0,4},{1,5},{2,6},{3,7},{4,0},{5,1},{6,2},{7,3},{8,12},{9,13},{10,... | collective-permute-start | bytes 110600 | tf_op jit(solution)/shard_map/ppermute | solution.py:840
  169.5 7.2 %collective-permute-start.42 = (bf16[112,256]{1,0:T(8,128)(2,1)S(1)}, bf16[112,256]{1,0:T(8,128)(2,1)S(1)}, u32[]{:S(2)}, u32[]{:S(2)}) collective-permute-start(bf16[112,256]{1,0:T(8,128)(2,1)S(1)} %fusion.24), channel_id=1, source_target_pairs={{0,4},{1,5},{2,6},{3,7},{4,0},{5,1},{6,2},{7,3},{8,12},{9,13},{10,... | collective-permute-start | bytes 172040 | tf_op jit(solution)/shard_map/ppermute | solution.py:840
  175.9 4.7 %collective-permute-start.31 = (bf16[144,256]{1,0:T(8,128)(2,1)S(1)}, bf16[144,256]{1,0:T(8,128)(2,1)S(1)}, u32[]{:S(2)}, u32[]{:S(2)}) collective-permute-start(bf16[144,256]{1,0:T(8,128)(2,1)S(1)} %get-tuple-element.169), channel_id=1, source_target_pairs={{0,2},{1,3},{2,0},{3,1},{4,6},{5,7},{6,4},{7,5},{8,10},{9,11},{10,... | collective-permute-start | bytes 221192 | tf_op jit(solution)/shard_map/ppermute | solution.py:840
  176.7 7.5 %collective-permute-start.43 = (bf16[112,256]{1,0:T(8,128)(2,1)S(1)}, bf16[112,256]{1,0:T(8,128)(2,1)S(1)}, u32[]{:S(2)}, u32[]{:S(2)}) collective-permute-start(bf16[112,256]{1,0:T(8,128)(2,1)S(1)} %fusion.22), channel_id=1, source_target_pairs={{0,4},{1,5},{2,6},{3,7},{4,0},{5,1},{6,2},{7,3},{8,12},{9,13},{10,... | collective-permute-start | bytes 172040 | tf_op jit(solution)/shard_map/ppermute | solution.py:840
  180.6 6.2 %collective-permute-start.34 = (bf16[2,144,256]{2,1,0:T(8,128)(2,1)S(1)}, bf16[2,144,256]{2,1,0:T(8,128)(2,1)S(1)}, u32[]{:S(2)}, u32[]{:S(2)}) collective-permute-start(bf16[2,144,256]{2,1,0:T(8,128)(2,1)S(1)} %get-tuple-element.163), channel_id=1, source_target_pairs={{0,24},{8,16},{16,8},{24,0},{1,25},{9,17},{17,9},{25,1},{2,26},{10... | collective-permute-start | bytes 442376 | tf_op jit(solution)/shard_map/ppermute | solution.py:840
  181.8 6.5 %collective-permute-start.33 = (bf16[2,144,256]{2,1,0:T(8,128)(2,1)S(1)}, bf16[2,144,256]{2,1,0:T(8,128)(2,1)S(1)}, u32[]{:S(2)}, u32[]{:S(2)}) collective-permute-start(bf16[2,144,256]{2,1,0:T(8,128)(2,1)S(1)} %get-tuple-element.163), channel_id=1, source_target_pairs={{0,16},{8,24},{16,0},{24,8},{1,17},{9,25},{17,1},{25,9},{2,18},{10... | collective-permute-start | bytes 442376 | tf_op jit(solution)/shard_map/ppermute | solution.py:840
  182.0 6.3 %collective-permute-start.32 = (bf16[2,144,256]{2,1,0:T(8,128)(2,1)S(1)}, bf16[2,144,256]{2,1,0:T(8,128)(2,1)S(1)}, u32[]{:S(2)}, u32[]{:S(2)}) collective-permute-start(bf16[2,144,256]{2,1,0:T(8,128)(2,1)S(1)} %get-tuple-element.163), channel_id=1, source_target_pairs={{0,8},{8,0},{16,24},{24,16},{1,9},{9,1},{17,25},{25,17},{2,10},{10... | collective-permute-start | bytes 442376 | tf_op jit(solution)/shard_map/ppermute | solution.py:840
  184.2 6.9 %collective-permute-start.35 = (bf16[2,144,256]{2,1,0:T(8,128)(2,1)S(1)}, bf16[2,144,256]{2,1,0:T(8,128)(2,1)S(1)}, u32[]{:S(2)}, u32[]{:S(2)}) collective-permute-start(bf16[2,144,256]{2,1,0:T(8,128)(2,1)S(1)} %get-tuple-element.163), channel_id=1, source_target_pairs={{0,1},{1,0},{2,3},{3,2},{4,5},{5,4},{6,7},{7,6},{8,9},{9,8},{10,11... | collective-permute-start | bytes 442376 | tf_op jit(solution)/shard_map/ppermute | solution.py:840
  184.2 5.6 %collective-permute-start.44 = (bf16[224,256]{1,0:T(8,128)(2,1)S(1)}, bf16[224,256]{1,0:T(8,128)(2,1)S(1)}, u32[]{:S(2)}, u32[]{:S(2)}) collective-permute-start(bf16[224,256]{1,0:T(8,128)(2,1)S(1)} %get-tuple-element.165), channel_id=1, source_target_pairs={{0,2},{1,3},{2,0},{3,1},{4,6},{5,7},{6,4},{7,5},{8,10},{9,11},{10,... | collective-permute-start | bytes 344072 | tf_op jit(solution)/shard_map/ppermute | solution.py:840
  186.8 4.7 %collective-permute-start.38 = (bf16[2,144,256]{2,1,0:T(8,128)(2,1)S(1)}, bf16[2,144,256]{2,1,0:T(8,128)(2,1)S(1)}, u32[]{:S(2)}, u32[]{:S(2)}) collective-permute-start(bf16[2,144,256]{2,1,0:T(8,128)(2,1)S(1)} %collective-permute-done.34), channel_id=1, source_target_pairs={{0,1},{1,0},{2,3},{3,2},{4,5},{5,4},{6,7},{7,6},{8,9},{9,8},{10,11... | collective-permute-start | bytes 442376 | tf_op jit(solution)/shard_map/ppermute | solution.py:840
  188.3 5.3 %collective-permute-start.37 = (bf16[2,144,256]{2,1,0:T(8,128)(2,1)S(1)}, bf16[2,144,256]{2,1,0:T(8,128)(2,1)S(1)}, u32[]{:S(2)}, u32[]{:S(2)}) collective-permute-start(bf16[2,144,256]{2,1,0:T(8,128)(2,1)S(1)} %collective-permute-done.33), channel_id=1, source_target_pairs={{0,1},{1,0},{2,3},{3,2},{4,5},{5,4},{6,7},{7,6},{8,9},{9,8},{10,11... | collective-permute-start | bytes 442376 | tf_op jit(solution)/shard_map/ppermute | solution.py:840
  188.3 5.3 %collective-permute-start.36 = (bf16[2,144,256]{2,1,0:T(8,128)(2,1)S(1)}, bf16[2,144,256]{2,1,0:T(8,128)(2,1)S(1)}, u32[]{:S(2)}, u32[]{:S(2)}) collective-permute-start(bf16[2,144,256]{2,1,0:T(8,128)(2,1)S(1)} %collective-permute-done.32), channel_id=1, source_target_pairs={{0,1},{1,0},{2,3},{3,2},{4,5},{5,4},{6,7},{7,6},{8,9},{9,8},{10,11... | collective-permute-start | bytes 442376 | tf_op jit(solution)/shard_map/ppermute | solution.py:840
  189.9 9.5 %collective-permute-start.47 = (bf16[2,224,256]{2,1,0:T(8,128)(2,1)S(1)}, bf16[2,224,256]{2,1,0:T(8,128)(2,1)S(1)}, u32[]{:S(2)}, u32[]{:S(2)}) collective-permute-start(bf16[2,224,256]{2,1,0:T(8,128)(2,1)S(1)} %get-tuple-element.158), channel_id=1, source_target_pairs={{0,24},{8,16},{16,8},{24,0},{1,25},{9,17},{17,9},{25,1},{2,26},{10... | collective-permute-start | bytes 688136 | tf_op jit(solution)/shard_map/ppermute | solution.py:840
  191.1 11.9 %collective-permute-start.46 = (bf16[2,224,256]{2,1,0:T(8,128)(2,1)S(1)}, bf16[2,224,256]{2,1,0:T(8,128)(2,1)S(1)}, u32[]{:S(2)}, u32[]{:S(2)}) collective-permute-start(bf16[2,224,256]{2,1,0:T(8,128)(2,1)S(1)} %get-tuple-element.158), channel_id=1, source_target_pairs={{0,16},{8,24},{16,0},{24,8},{1,17},{9,25},{17,1},{25,9},{2,18},{10... | collective-permute-start | bytes 688136 | tf_op jit(solution)/shard_map/ppermute | solution.py:840
  191.6 11.4 %collective-permute-start.45 = (bf16[2,224,256]{2,1,0:T(8,128)(2,1)S(1)}, bf16[2,224,256]{2,1,0:T(8,128)(2,1)S(1)}, u32[]{:S(2)}, u32[]{:S(2)}) collective-permute-start(bf16[2,224,256]{2,1,0:T(8,128)(2,1)S(1)} %get-tuple-element.158), channel_id=1, source_target_pairs={{0,8},{8,0},{16,24},{24,16},{1,9},{9,1},{17,25},{25,17},{2,10},{10... | collective-permute-start | bytes 688136 | tf_op jit(solution)/shard_map/ppermute | solution.py:840
  193.6 11.9 %collective-permute-start.48 = (bf16[2,224,256]{2,1,0:T(8,128)(2,1)S(1)}, bf16[2,224,256]{2,1,0:T(8,128)(2,1)S(1)}, u32[]{:S(2)}, u32[]{:S(2)}) collective-permute-start(bf16[2,224,256]{2,1,0:T(8,128)(2,1)S(1)} %get-tuple-element.158), channel_id=1, source_target_pairs={{0,1},{1,0},{2,3},{3,2},{4,5},{5,4},{6,7},{7,6},{8,9},{9,8},{10,11... | collective-permute-start | bytes 688136 | tf_op jit(solution)/shard_map/ppermute | solution.py:840
  199.4 6.1 %collective-permute-start.51 = (bf16[2,224,256]{2,1,0:T(8,128)(2,1)S(1)}, bf16[2,224,256]{2,1,0:T(8,128)(2,1)S(1)}, u32[]{:S(2)}, u32[]{:S(2)}) collective-permute-start(bf16[2,224,256]{2,1,0:T(8,128)(2,1)S(1)} %collective-permute-done.47), channel_id=1, source_target_pairs={{0,1},{1,0},{2,3},{3,2},{4,5},{5,4},{6,7},{7,6},{8,9},{9,8},{10,11... | collective-permute-start | bytes 688136 | tf_op jit(solution)/shard_map/ppermute | solution.py:840
  (68 other events, 496.0 us)

commit v2 on v0

--- a/solution.py
+++ b/solution.py
@@ -1,8 +1,11 @@
+import functools
 import math
 
 import jax
 import jax.numpy as jnp
 from jax import lax
+from jax.experimental import pallas as pl
+from jax.experimental.pallas import tpu as pltpu
 from jax.sharding import PartitionSpec as P
 
 GROUPS = 32
@@ -116,7 +119,7 @@
     return (grad_in.reshape(full_shape), gain_grad, shift_grad)
 
 
-def local(
+def local_rows(
     pixels,
     heights,
     timesteps,
@@ -373,6 +376,1129 @@
     )
 
 
+def mib(count):
+    return pltpu.CompilerParams(vmem_limit_bytes=count * 2**20)
+
+
+def dot(left, right):
+    return jnp.dot(left, right, preferred_element_type=jnp.float32)
+
+
+def dot_rows(left, right):
+    return lax.dot_general(
+        left, right, (((1,), (1,)), ((), ())), preferred_element_type=jnp.float32
+    )
+
+
+def fold(tile):
+    return jnp.sum(tile.reshape(-1, 8, tile.shape[1]), axis=0)
+
+
+def group_sums(row, width):
+    channels = row.shape[1]
+    rows = lax.broadcasted_iota(jnp.int32, (channels, channels), 0) // width
+    cols = lax.broadcasted_iota(jnp.int32, (channels, channels), 1) // width
+    same = jnp.where(rows == cols, 1.0, 0.0).astype(jnp.bfloat16)
+    wide = jnp.broadcast_to(row, (16, channels))
+    total = None
+    for _ in range(3):
+        term = wide.astype(jnp.bfloat16)
+        wide = wide - term.astype(jnp.float32)
+        part = dot(term, same)
+        total = part if total is None else total + part
+    return total[0:1]
+
+
+def row_at(index, cols):
+    return pl.ds(pl.multiple_of(index * cols, cols), cols)
+
+
+def total_of(tile):
+    return jnp.sum(tile, axis=0, keepdims=True)
+
+
+def field_stats(read, height, rows, cols, channels):
+    width = channels // GROUPS
+    each = (height * cols).astype(jnp.float32)
+    about = jnp.sum(read(0), axis=0, keepdims=True) * (1.0 / cols)
+    zero = jnp.zeros((8, channels), jnp.float32)
+
+    def add(index, totals):
+        off = (read(index) - about) * valid_row(index, height)
+        return totals[0] + fold(off), totals[1] + fold(off * off)
+
+    first, square = lax.fori_loop(0, rows, add, (zero, zero), unroll=4)
+    first, square = total_of(first), total_of(square)
+    mean = group_sums(first + about * each, width) / (each * width)
+    shift = about - mean
+    spread = group_sums(square + 2.0 * first * shift + each * shift * shift, width)
+    return mean, lax.rsqrt(spread / (each * width) + EPSILON)
+
+
+def half_line(mean, inverse, gain, bias, scale=1.0, shift=0.0):
+    slope = inverse * gain
+    start = bias - mean * slope
+    return 0.5 * slope * scale, 0.5 * (start * scale + shift)
+
+
+def put_shifted(ref, index, tile, cols):
+    channels = tile.shape[1]
+    column = lax.broadcasted_iota(jnp.int32, tile.shape, 0)
+    before = jnp.where(column == 0, 0.0, pltpu.roll(tile, 1, 0))
+    after = jnp.where(column == cols - 1, 0.0, pltpu.roll(tile, cols - 1, 0))
+    at = row_at(index + 1, cols)
+    ref[at, 0:channels] = before.astype(jnp.bfloat16)
+    ref[at, channels : 2 * channels] = tile.astype(jnp.bfloat16)
+    ref[at, 2 * channels : 3 * channels] = after.astype(jnp.bfloat16)
+
+
+def clear_rims(ref, cols):
+    edge = jnp.zeros((cols, ref.shape[1]), ref.dtype)
+    ref[0:cols, :] = edge
+    ref[ref.shape[0] - cols : ref.shape[0], :] = edge
+
+
+def conv_shifted(shifted, weight, out, bias, cols, added=None):
+    step = 8 * cols
+
+    def block(index, carry):
+        base = index * step
+        total = bias
+        for tap in range(3):
+            at = pl.ds(pl.multiple_of(base + tap * cols, cols), step)
+            total = total + dot(shifted[at, :], weight[tap])
+        if added is not None:
+            total = total + added[pl.ds(pl.multiple_of(base, step), step), :].astype(jnp.float32)
+        out[pl.ds(pl.multiple_of(base, step), step), :] = total
+        return carry
+
+    lax.fori_loop(0, out.shape[0] // step, block, 0)
+
+
+def kernel_quarter(shifted, own_t, out, cols):
+    cells = own_t.shape[2]
+    channels = shifted.shape[1] // 3
+    width = own_t.shape[1]
+    grad = shifted[cols : cols + cells, channels : 2 * channels]
+    for tap in range(3):
+        out[tap * width : (tap + 1) * width, :] = dot(own_t[tap], grad).astype(jnp.bfloat16)
+
+
+def own_place(vec):
+    spot = lax.axis_index("row")
+    image, head = spot // HEADS, spot % HEADS
+    return spot, head, image, jnp.max(vec[11:12, :]).astype(jnp.int32)
+
+
+def started(sems, *pairs):
+    copies = [pltpu.make_async_copy(src, dst, sems.at[k]) for k, (src, dst) in enumerate(pairs)]
+    for copy in copies:
+        copy.start()
+    return copies
+
+
+def finish_all(copies):
+    for copy in copies:
+        copy.wait()
+
+
+def valid_row(index, height):
+    return jnp.where(index < height, 1.0, 0.0).astype(jnp.float32)
+
+
+def forward_kernel(vec, *refs):
+    blocks, (w_one_far, w_two_far) = refs[:8], refs[8:10]
+    act_three, pix_far, conv_far, residual_far, act_one_far, act_two_far, stats_far = refs[10:17]
+    pix, conv_one, residual, stats, w_one, w_two, shift_one, shift_two, in_sems, out_sems = refs[17:]
+    cells, channels = pix.shape
+    block_cells = blocks[0].shape[0]
+    cols = (shift_one.shape[0] - cells) // 2
+    rows = cells // cols
+    spot, _, _, height = own_place(vec)
+    pairs = []
+    for step, block in enumerate(blocks):
+        base = pl.multiple_of((spot ^ step) * block_cells, block_cells)
+        pairs.append((block, pix.at[pl.ds(base, block_cells), :]))
+    arriving = started(in_sems, *pairs, (w_one_far, w_one), (w_two_far, w_two))
+    gain_one, bias_one, conv_bias_one, gain_two, bias_two = (vec[k : k + 1, :] for k in range(5))
+    scale, shift, conv_bias_two, gain_three, bias_three = (vec[k : k + 1, :] for k in range(5, 10))
+    inner = (pl.ds(cols, cells), pl.ds(channels, channels))
+
+    def read_pix(index):
+        return pix[row_at(index, cols), :].astype(jnp.float32)
+
+    def read_conv(index):
+        return conv_one[row_at(index, cols), :]
+
+    def read_res(index):
+        return residual[row_at(index, cols), :]
+
+    def activate(read, line, shifted):
+        def body(index, carry):
+            part = read(index) * line[0] + line[1]
+            part = (part + part * jnp.tanh(part)) * valid_row(index, height)
+            put_shifted(shifted, index, part, cols)
+            return carry
+
+        lax.fori_loop(0, rows, body, 0, unroll=2)
+
+    clear_rims(shift_one, cols)
+    clear_rims(shift_two, cols)
+    finish_all(arriving[:8])
+    leaving = started(out_sems, (pix, pix_far))
+    mean_one, inv_one = field_stats(read_pix, height, rows, cols, channels)
+    activate(read_pix, half_line(mean_one, inv_one, gain_one, bias_one), shift_one)
+    leaving += started(out_sems.at[1:2], (shift_one.at[inner], act_one_far))
+    arriving[8].wait()
+    conv_shifted(shift_one, w_one, conv_one, conv_bias_one, cols)
+    leaving += started(out_sems.at[2:3], (conv_one, conv_far))
+    mean_two, inv_two = field_stats(read_conv, height, rows, cols, channels)
+    line = half_line(mean_two, inv_two, gain_two, bias_two, scale, shift)
+    activate(read_conv, line, shift_two)
+    leaving += started(out_sems.at[3:4], (shift_two.at[inner], act_two_far))
+    arriving[9].wait()
+    conv_shifted(shift_two, w_two, residual, conv_bias_two, cols, pix)
+    leaving += started(out_sems.at[4:5], (residual, residual_far))
+    mean_three, inv_three = field_stats(read_res, height, rows, cols, channels)
+    stats[...] = jnp.concatenate(
+        [mean_one, inv_one, mean_two, inv_two, mean_three, inv_three, mean_one, mean_one], axis=0
+    )
+    leaving += started(out_sems.at[5:6], (stats, stats_far))
+    slope = inv_three * gain_three
+    start = bias_three - mean_three * slope
+
+    def third(index, carry):
+        act_three[row_at(index, cols), :] = (read_res(index) * slope + start).astype(jnp.bfloat16)
+        return carry
+
+    lax.fori_loop(0, rows, third, 0, unroll=4)
+    finish_all(leaving)
+
+
+def attention_kernel(columns, vec, act_three, w_heads, w_out, biases, *refs):
+    blocks = refs[:8]
+    value_key_far, query_far, grad_far, mixed_far, sums_far = refs[8:13]
+    (
+        grad_blocks, grad_proj, value_key, query_part, sums,
+        query_grad, key_pad, value_pad, heads_t, mixed, mask_row, in_sems, out_sems,
+    ) = refs[13:]
+    cells, channels = act_three.shape
+    block_cells = blocks[0].shape[0]
+    spot, _, _, height = own_place(vec)
+    half = mixed.shape[1] // 2
+    cols = columns
+    scaling = half**-0.5
+    valid_cells = height * cols
+    step = 256
+    pairs = []
+    for index, block in enumerate(blocks):
+        base = pl.multiple_of((spot ^ index) * block_cells, block_cells)
+        pairs.append((block, grad_blocks.at[pl.ds(base, block_cells), :]))
+    arriving = started(in_sems, *pairs)
+
+    def project(index, carry):
+        at = pl.ds(pl.multiple_of(index * 512, 512), 512)
+        parts = dot(act_three[at, :], w_heads[...]) + biases[0:1, :]
+        query_grad[at, :] = parts[:, 0 : 2 * half].astype(jnp.bfloat16) * jnp.bfloat16(scaling)
+        key_pad[at, :] = parts[:, 2 * half : 4 * half].astype(jnp.bfloat16)
+        value_pad[at, :] = parts[:, 4 * half : 6 * half].astype(jnp.bfloat16)
+        query, key = parts[:, 0 : 2 * half], parts[:, 2 * half : 4 * half]
+        query_size = jnp.sum(query * query, axis=1, keepdims=True) * (scaling * scaling)
+        key_size = jnp.sum(key * key, axis=1, keepdims=True)
+        return jnp.maximum(carry[0], jnp.max(query_size)), jnp.maximum(carry[1], jnp.max(key_size))
+
+    norms = lax.fori_loop(0, cells // 512, project, (jnp.float32(0.0), jnp.float32(0.0)))
+    lane = lax.broadcasted_iota(jnp.int32, (1, cells), 1)
+    mask_row[...] = jnp.where(lane < valid_cells, 0.0, MASKED)
+    heads_t[...] = jnp.zeros(heads_t.shape, jnp.float32)
+    mixed[...] = jnp.zeros(mixed.shape, jnp.bfloat16)
+    finish_all(arriving)
+
+    def clean(index, total):
+        at = pl.ds(pl.multiple_of(index * block_cells, block_cells), block_cells)
+        cell = index * block_cells + lax.broadcasted_iota(jnp.int32, (block_cells, channels), 0)
+        kept = jnp.where(cell < valid_cells, grad_blocks[at, :].astype(jnp.float32), 0.0)
+        low = kept.astype(jnp.bfloat16)
+        grad_proj[at, :] = low
+        query_grad[at, :] = query_grad[at, :] + dot(low, w_out[...]).astype(jnp.bfloat16)
+        return total + fold(kept)
+
+    total = lax.fori_loop(
+        0, cells // block_cells, clean, jnp.zeros((8, channels), jnp.float32)
+    )
+    sums[...] = jnp.concatenate([total_of(total), jnp.zeros((7, channels), jnp.float32)], axis=0)
+    leaving = started(out_sems, (grad_proj, grad_far), (sums, sums_far))
+
+    def query_block(shifted, index, carry):
+        at = pl.ds(pl.multiple_of(index * step, step), step)
+        both = query_grad[at, :]
+        scores = dot_rows(both, key_pad[...]) + mask_row[...]
+        if shifted:
+            scores = scores - jnp.max(scores, axis=1, keepdims=True)
+        weights = jnp.exp(scores)
+        total = jnp.zeros((step, 2 * half), jnp.float32)
+        for start in range(0, cells, 2 * half):
+            total = total + weights[:, start : start + 2 * half]
+        inverse = 1.0 / jnp.sum(total, axis=1, keepdims=True)
+        low = weights.astype(jnp.bfloat16)
+        out = dot(low, value_pad[...]) * inverse
+        wide = both.astype(jnp.float32)
+        delta = jnp.sum(wide * out, axis=1, keepdims=True)
+        turned = jnp.transpose(wide * inverse).astype(jnp.bfloat16)
+        grad_probs = dot_rows(both, value_pad[...])
+        grad_scores = (low.astype(jnp.float32) * (grad_probs - delta)).astype(jnp.bfloat16)
+        grad_query = dot(grad_scores, key_pad[...]) * (inverse * scaling)
+        mixed[at, :] = (out + grad_query).astype(jnp.bfloat16)
+        heads_t[0:half, :] += dot(turned[0:half], grad_scores)
+        heads_t[half : 2 * half, :] += dot(turned[half : 2 * half], low)
+        return carry
+
+    query_most, key_most = norms
+    narrow = query_most * key_most <= 3600.0
+
+    @pl.when(narrow)
+    def _():
+        lax.fori_loop(0, cells // step, functools.partial(query_block, False), 0, unroll=2)
+
+    @pl.when(jnp.logical_not(narrow))
+    def _():
+        count = (valid_cells + step - 1) // step
+        lax.fori_loop(0, count, functools.partial(query_block, True), 0)
+
+    for start in range(0, cells, step):
+        value_key[start : start + step, :] = jnp.transpose(heads_t[:, start : start + step]).astype(
+            jnp.bfloat16
+        )
+    query_part[:, 0:half] = mixed[0 : cells // 2, 0:half]
+    query_part[:, half : 2 * half] = mixed[cells // 2 : cells, 0:half]
+    leaving += started(
+        out_sems.at[2:5], (value_key, value_key_far), (query_part, query_far), (mixed, mixed_far)
+    )
+    finish_all(leaving)
+
+
+def aside_kernel(vec, *refs):
+    act_far, (mixed_far, value_key_far, act_three_far, grad_far) = refs[0:2], refs[2:6]
+    own_far, weight_far, sends = refs[6:8], refs[8], refs[9:13]
+    acts, mixed, value_key, act_three, grad_proj, padded, own, weight_rows, in_sems, out_sems = (
+        refs[13:]
+    )
+    cells, channels = act_three.shape
+    cols = (padded.shape[0] - cells) // 2
+    lanes = mixed.shape[1]
+    half = lanes // 2
+    spot, head, image, _ = own_place(vec)
+    arriving = started(
+        in_sems,
+        (mixed_far, mixed),
+        (value_key_far, value_key),
+        (act_three_far, act_three),
+        (grad_far, grad_proj),
+        (act_far[0], acts.at[0]),
+        (act_far[1], acts.at[1]),
+    )
+    block_cells = sends[0].shape[1]
+    step = 256
+    arriving[0].wait()
+    for k, send in enumerate(sends):
+        for part in range(2):
+            block = (head ^ k) + HEADS * (image ^ part)
+            at = pl.ds(pl.multiple_of(block * block_cells, block_cells), block_cells)
+            send[part] = mixed[at, :]
+    finish_all(arriving[1:4])
+
+    def gather(index, totals):
+        at = pl.ds(pl.multiple_of(index * step, step), step)
+        low_mixed, low_heads, act = mixed[at, :], value_key[at, :], act_three[at, :]
+        mixed_t = jnp.transpose(low_mixed.astype(jnp.float32)).astype(jnp.bfloat16)
+        heads_t = jnp.transpose(low_heads.astype(jnp.float32)).astype(jnp.bfloat16)
+        return (
+            totals[0] + dot(mixed_t, act),
+            totals[1] + dot(heads_t, act),
+            totals[2] + dot(mixed_t, grad_proj[at, :]),
+            totals[3] + fold(low_mixed.astype(jnp.float32)),
+            totals[4] + fold(low_heads.astype(jnp.float32)),
+        )
+
+    square = jnp.zeros((lanes, channels), jnp.float32)
+    line = jnp.zeros((8, lanes), jnp.float32)
+    from_query, from_heads, from_out, query_sum, value_sum = lax.fori_loop(
+        0, cells // step, gather, (square, square, square, line, line)
+    )
+    weight_rows[0:half, :] = from_query[0:half].astype(jnp.bfloat16)
+    weight_rows[half : 3 * half, :] = from_heads.astype(jnp.bfloat16)
+    weight_rows[3 * half : 4 * half, :] = from_out[half:lanes].astype(jnp.bfloat16)
+    which = lax.axis_index("img") * 2 + image
+    lane = lax.broadcasted_iota(jnp.int32, (1, channels), 1)
+    now = jnp.max(vec[12:13, :]).astype(jnp.int32)
+    high = jnp.where(lane == which, (now // 32).astype(jnp.float32), 0.0)
+    rest = jnp.where(lane == which, (now % 32).astype(jnp.float32), 0.0)
+    row = jnp.concatenate([total_of(query_sum), total_of(value_sum)], axis=1)
+    below = jnp.zeros((weight_rows.shape[0] - 4 * half - 3, channels), jnp.float32)
+    weight_rows[4 * half :, :] = jnp.concatenate([row, high, rest, below], axis=0).astype(
+        jnp.bfloat16
+    )
+    source = lax.broadcasted_iota(jnp.int32, (channels, 3 * half), 0)
+    target = lax.broadcasted_iota(jnp.int32, (channels, 3 * half), 1)
+    chosen = jnp.where(source == head * half + target % half, 1.0, 0.0).astype(jnp.bfloat16)
+    lane = lax.broadcasted_iota(jnp.int32, (step, 3 * half), 1)
+    column = lax.broadcasted_iota(jnp.int32, (step, 3 * half), 0) % cols
+    leaving = started(out_sems.at[2:3], (weight_rows, weight_far))
+    for k in range(2):
+        arriving[4 + k].wait()
+        clear_rims(padded, cols)
+
+        def widen(index, carry):
+            at = pl.ds(pl.multiple_of(index * step, step), step)
+            tile = dot(acts[k, at, :], chosen)
+            before = jnp.where(column == 0, 0.0, pltpu.roll(tile, 1, 0))
+            after = jnp.where(column == cols - 1, 0.0, pltpu.roll(tile, step - 1, 0))
+            tile = jnp.where(lane < half, before, jnp.where(lane < 2 * half, tile, after))
+            padded[pl.ds(pl.multiple_of(index * step + cols, cols), step), :] = tile
+            return carry
+
+        lax.fori_loop(0, cells // step, widen, 0)
+        for tap in range(3):
+
+            def turn(index, carry):
+                at = pl.ds(pl.multiple_of(index * step + tap * cols, cols), step)
+                to = pl.ds(pl.multiple_of(index * step, step), step)
+                own[k, tap, :, to] = jnp.transpose(padded[at, :]).astype(jnp.bfloat16)
+                return carry
+
+            lax.fori_loop(0, cells // step, turn, 0)
+        leaving += started(out_sems.at[k : k + 1], (own.at[k], own_far[k]))
+    finish_all(leaving)
+
+
+def residual_kernel(vec, qkv_t, *refs):
+    heads_far, sides_far = refs[0:8:2], refs[1:8:2]
+    grad_far, residual_far, stats_far, own_far, weight_far = refs[8:13]
+    shifted, grad_res_far, quarter_far, sums_far = refs[13:17]
+    (
+        heads, sides, grad_proj, residual, stats, own_two, grad_res, quarter, sums, grad_act,
+        in_sems, out_sems,
+    ) = refs[17:]
+    cells, channels = grad_proj.shape
+    cols = (shifted.shape[0] - cells) // 2
+    rows = cells // cols
+    _, head, _, height = own_place(vec)
+    width = channels // GROUPS
+    count = (height * (cols * width)).astype(jnp.float32)
+    half = qkv_t.shape[1]
+    pairs = [(far, heads.at[head ^ k]) for k, far in enumerate(heads_far)]
+    pairs += [(far, sides.at[head ^ k]) for k, far in enumerate(sides_far)]
+    arriving = started(
+        in_sems,
+        *pairs,
+        (stats_far, stats),
+        (residual_far, residual),
+        (grad_far, grad_proj),
+        (own_far, own_two),
+        (weight_far, quarter.at[pl.ds(9 * half, 5 * half), :]),
+    )
+    zeros = jnp.zeros((half, channels), jnp.bfloat16)
+    halfway = cells // 2
+    step = 512
+    pairs = ((0, 1), (2, 3))
+    w_main = []
+    for a, b in pairs:
+        order = [HEADS + a, 2 * HEADS + a, HEADS + b, 2 * HEADS + b]
+        w_main.append(jnp.concatenate([qkv_t[k] for k in order], axis=0))
+    finish_all(arriving[:8])
+    for part in range(2):
+        w_side = []
+        for a, b in pairs:
+            left, right = qkv_t[a], qkv_t[b]
+            order = [left, zeros, right, zeros] if part == 0 else [zeros, left, zeros, right]
+            w_side.append(jnp.concatenate(order, axis=0))
+        for base in range(0, halfway, step):
+            start = part * halfway + base
+            total = None
+            for k, (a, b) in enumerate(pairs):
+                main = jnp.concatenate(
+                    [heads[a][start : start + step, :], heads[b][start : start + step, :]], axis=1
+                )
+                side = jnp.concatenate(
+                    [sides[a][base : base + step, :], sides[b][base : base + step, :]], axis=1
+                )
+                term = dot(main, w_main[k]) + dot(side, w_side[k])
+                total = term if total is None else total + term
+            grad_act[start : start + step, :] = total
+    finish_all(arriving[8:10])
+    mean, inverse = stats[4:5, :], stats[5:6, :]
+    gain = vec[8:9, :]
+    zero = jnp.zeros((8, channels), jnp.float32)
+
+    def normed(index):
+        return (residual[row_at(index, cols), :] - mean) * inverse
+
+    def add(index, totals):
+        grad = grad_act[row_at(index, cols), :]
+        return totals[0] + fold(grad), totals[1] + fold(grad * normed(index))
+
+    plain, cross = lax.fori_loop(0, rows, add, (zero, zero), unroll=2)
+    plain, cross = total_of(plain), total_of(cross)
+    mean_plain = group_sums(plain * gain, width) / count
+    mean_cross = group_sums(cross * gain, width) / count
+    clear_rims(shifted, cols)
+    arriving[10].wait()
+
+    def finish(index, total):
+        at = row_at(index, cols)
+        inner = (grad_act[at, :] * gain - mean_plain - normed(index) * mean_cross) * inverse
+        grad = grad_proj[at, :].astype(jnp.float32) + inner * valid_row(index, height)
+        grad_res[at, :] = grad
+        put_shifted(shifted, index, grad, cols)
+        return total + fold(grad)
+
+    total = total_of(lax.fori_loop(0, rows, finish, zero, unroll=2))
+    sums[...] = jnp.concatenate([cross, plain, total, jnp.zeros((5, channels), jnp.float32)], axis=0)
+    leaving = started(out_sems, (grad_res, grad_res_far), (sums, sums_far))
+    finish_all(arriving[11:])
+    kernel_quarter(shifted, own_two, quarter, cols)
+    leaving += started(out_sems.at[2:3], (quarter, quarter_far))
+    finish_all(leaving)
+
+
+def second_kernel(vec, shifted, weight_far, conv_far, stats_far, own_far, *refs):
+    sums_three_far, out_sums_far = refs[0:2]
+    shifted_one, quarter_far = refs[2:4]
+    (
+        weight, conv_one, stats, own_one, sums_three, out_sums, quarter, grad_act, in_sems, out_sems,
+    ) = refs[4:]
+    cells, channels = conv_one.shape
+    cols = (shifted.shape[0] - cells) // 2
+    rows = cells // cols
+    _, _, image, height = own_place(vec)
+    width = channels // GROUPS
+    count = (height * (cols * width)).astype(jnp.float32)
+    arriving = started(
+        in_sems,
+        (weight_far, weight),
+        (stats_far, stats),
+        (conv_far, conv_one),
+        (own_far, own_one),
+        (sums_three_far, sums_three),
+        (out_sums_far, out_sums),
+    )
+    gain, bias, scale, shift = (vec[k : k + 1, :] for k in range(3, 7))
+    zero = jnp.zeros((8, channels), jnp.float32)
+    clear_rims(shifted_one, cols)
+    arriving[0].wait()
+    conv_shifted(shifted, weight, grad_act, 0.0, cols)
+    finish_all(arriving[1:3])
+    mean, inverse = stats[2:3, :], stats[3:4, :]
+    line = half_line(mean, inverse, gain, bias, scale, shift)
+    begin = mean * inverse
+
+    def add(index, totals):
+        at = row_at(index, cols)
+        value = conv_one[at, :]
+        unit = value * inverse - begin
+        part = value * line[0] + line[1]
+        sigmoid = 0.5 + 0.5 * jnp.tanh(part)
+        slope = sigmoid + 2.0 * part * sigmoid * (1.0 - sigmoid)
+        grad = grad_act[at, :] * valid_row(index, height) * slope
+        grad_act[at, :] = grad
+        return totals[0] + fold(grad), totals[1] + fold(grad * unit)
+
+    plain, cross = lax.fori_loop(0, rows, add, (zero, zero), unroll=2)
+    plain, cross = total_of(plain), total_of(cross)
+    factor = gain * scale
+    mean_plain = group_sums(plain * factor, width) / count
+    mean_cross = group_sums(cross * factor, width) / count
+    one, two = factor * inverse, mean_cross * inverse * inverse
+    three = (mean_plain - begin * mean_cross) * inverse
+
+    def finish(index, total):
+        at = row_at(index, cols)
+        grad = grad_act[at, :] * one - conv_one[at, :] * two - three
+        grad = grad * valid_row(index, height)
+        put_shifted(shifted_one, index, grad, cols)
+        return total + fold(grad)
+
+    total = total_of(lax.fori_loop(0, rows, finish, zero, unroll=2))
+    finish_all(arriving[3:])
+    kernel_quarter(shifted_one, own_one, quarter, cols)
+    lines = [
+        sums_three[0:3, :], out_sums[0:1, :], cross * scale, plain * scale, total,
+        jnp.zeros((9, channels), jnp.float32),
+    ]
+    mine = 2 * (lax.axis_index("img") * 2 + image)
+    place = lax.broadcasted_iota(jnp.int32, (16, channels), 0)
+    both = jnp.where(place == mine, gain * cross + bias * plain, 0.0)
+    lines.append(jnp.where(place == mine + 1, plain, both))
+    base = 3 * own_one.shape[1]
+    lines.append(jnp.zeros((quarter.shape[0] - base - 32, channels), jnp.float32))
+    quarter[base:, :] = jnp.concatenate(lines, axis=0).astype(jnp.bfloat16)
+    finish_all(started(out_sems, (quarter, quarter_far)))
+
+
+def first_kernel(vec, shifted, weight_far, pix_far, grad_far, stats_far, *refs):
+    out_own_far, out_away_far, sums_far = refs[:3]
+    weight, pix, grad_res, stats, out, sums, grad_act, in_sems, out_sems = refs[3:]
+    cells, channels = pix.shape
+    block_cells = out.shape[1]
+    cols = (shifted.shape[0] - cells) // 2
+    rows = cells // cols
+    spot, _, _, height = own_place(vec)
+    width = channels // GROUPS
+    count = (height * (cols * width)).astype(jnp.float32)
+    arriving = started(
+        in_sems,
+        (weight_far, weight),
+        (stats_far, stats),
+        (pix_far, pix),
+        (grad_far, grad_res),
+    )
+    gain, bias = vec[0:1, :], vec[1:2, :]
+    zero = jnp.zeros((8, channels), jnp.float32)
+    arriving[0].wait()
+    conv_shifted(shifted, weight, grad_act, 0.0, cols)
+    finish_all(arriving[1:])
+    mean, inverse = stats[0:1, :], stats[1:2, :]
+    line = half_line(mean, inverse, gain, bias)
+    begin = mean * inverse
+
+    def normed(at):
+        return pix[at, :].astype(jnp.float32) * inverse - begin
+
+    def add(index, totals):
+        at = row_at(index, cols)
+        value = pix[at, :].astype(jnp.float32)
+        unit = value * inverse - begin
+        part = value * line[0] + line[1]
+        sigmoid = 0.5 + 0.5 * jnp.tanh(part)
+        slope = sigmoid + 2.0 * part * sigmoid * (1.0 - sigmoid)
+        grad = grad_act[at, :] * valid_row(index, height) * slope
+        grad_act[at, :] = grad
+        return totals[0] + fold(grad), totals[1] + fold(grad * unit)
+
+    plain, cross = lax.fori_loop(0, rows, add, (zero, zero), unroll=2)
+    plain, cross = total_of(plain), total_of(cross)
+    mean_plain = group_sums(plain * gain, width) / count
+    mean_cross = group_sums(cross * gain, width) / count
+    block_rows = block_cells // cols
+    for part in range(2):
+        first_row = (spot ^ (4 * part)) * block_rows
+        for line in range(block_rows):
+            at = row_at(first_row + line, cols)
+            grad = (grad_act[at, :] * gain - mean_plain - normed(at) * mean_cross) * inverse
+            grad = grad_res[at, :] + grad * valid_row(first_row + line, height)
+            out[part, line * cols : (line + 1) * cols, :] = grad.astype(jnp.bfloat16)
+    sums[...] = jnp.concatenate([cross, plain, jnp.zeros((6, channels), jnp.float32)], axis=0)
+    finish_all(
+        started(
+            out_sems, (out.at[0], out_own_far), (out.at[1], out_away_far), (sums, sums_far)
+        )
+    )
+
+
+def block_kernel(columns, vec, w_out, *refs):
+    heads, residual_far = refs[:4], refs[4]
+    out_own, out_away, residual, in_sems = refs[5:]
+    block_cells, channels = out_own.shape
+    spot, head, _, height = own_place(vec)
+    cols = columns
+    bases = [
+        pl.multiple_of((spot ^ (4 * part)) * block_cells, block_cells) for part in range(2)
+    ]
+    pairs = [
+        (residual_far.at[pl.ds(base, block_cells), :], residual.at[part])
+        for part, base in enumerate(bases)
+    ]
+    finish_all(started(in_sems, *pairs))
+    for part, out in enumerate((out_own, out_away)):
+        total = residual[part] + vec[10:11, :]
+        for step in range(4):
+            tile = heads[step][part]
+            total = total + dot(tile[:, tile.shape[1] // 2 :], w_out[head ^ step])
+        cell = bases[part] + lax.broadcasted_iota(jnp.int32, (block_cells, channels), 0)
+        out[...] = jnp.where(cell < height * cols, total, 0.0).astype(jnp.bfloat16)
+
+
+def prepare_kernel(*refs):
+    shifts, lines_far, kernels_far = refs[0], refs[1:15], refs[15:17]
+    vec, w_heads, w_out, biases, qkv_t = refs[17:22]
+    backs_far = refs[22:24]
+    kernels, backs, qkv_weight, out_weight, heights, timesteps, qv_bias, *lines = refs[24:40]
+    line_sems, in_sems, out_sems = refs[40:]
+    channels = out_weight.shape[0]
+    half = channels // HEADS
+    small = started(
+        line_sems,
+        *zip(lines_far, (*lines, qv_bias, qkv_weight, out_weight, heights, timesteps)),
+    )
+    arriving = started(
+        in_sems, *[(far, kernels.at[k]) for k, far in enumerate(kernels_far)]
+    )
+    finish_all(small)
+    spot = lax.axis_index("row")
+    image, head = spot // HEADS, spot % HEADS
+    shift_row = shifts[pl.ds(image, 1), :]
+    order = list(range(5)) + [None, None] + list(range(5, 9))
+    for line, k in enumerate(order):
+        if k is not None:
+            vec[line : line + 1, :] = lines[k][...].astype(jnp.float32).reshape(1, channels)
+    vec[5:6, :] = 1.0 + shift_row[:, :channels]
+    vec[6:7, :] = shift_row[:, channels:]
+    vec[11:12, :] = jnp.full((1, channels), heights[image].astype(jnp.float32))
+    vec[12:13, :] = jnp.full((1, channels), timesteps[image].astype(jnp.float32))
+    vec[13:16, :] = jnp.zeros((3, channels), jnp.float32)
+    source = lax.broadcasted_iota(jnp.int32, (channels, 2 * half), 0)
+    lane = lax.broadcasted_iota(jnp.int32, (channels, 2 * half), 1)
+    first = jnp.where((lane < half) & (source == head * half + lane), 1.0, 0.0)
+    second = jnp.where((lane >= half) & (source == head * half + lane - half), 1.0, 0.0)
+    first, second = first.astype(jnp.bfloat16), second.astype(jnp.bfloat16)
+    lanes = 2 * half
+    for part, taken in enumerate((first, first, second)):
+        whole = qkv_weight[:, part * channels : (part + 1) * channels]
+        w_heads[:, part * lanes : (part + 1) * lanes] = dot(whole, taken).astype(jnp.bfloat16)
+    turned = jnp.transpose(out_weight[...].astype(jnp.float32)).astype(jnp.bfloat16)
+    w_out[...] = dot(turned, second).astype(jnp.bfloat16)
+    both = qv_bias[...].astype(jnp.float32).reshape(1, 2 * channels)
+    wide = jnp.broadcast_to(both, (16, 2 * channels)).astype(jnp.bfloat16)
+    biases[:, 0:lanes] = dot(wide[:, :channels], first)[0:8]
+    biases[:, lanes : 2 * lanes] = jnp.zeros((8, lanes), jnp.float32)
+    biases[:, 2 * lanes : 3 * lanes] = dot(wide[:, channels:], second)[0:8]
+    for block in range(0, 3 * HEADS, 2):
+        whole = qkv_weight[:, block // 2 * lanes : (block // 2 + 1) * lanes].astype(jnp.float32)
+        whole = jnp.transpose(whole).astype(jnp.bfloat16)
+        qkv_t[block] = whole[0:half]
+        qkv_t[block + 1] = whole[half:lanes]
+    leaving = []
+    for k in range(2):
+        arriving[k].wait()
+
+        def turn(tap, carry):
+            tile = kernels[k, 2 - tap // 3, 2 - tap % 3].astype(jnp.float32)
+            at = pl.ds(pl.multiple_of(tap % 3 * channels, channels), channels)
+            backs[k, tap // 3, at, :] = jnp.transpose(tile).astype(jnp.bfloat16)
+            return carry
+
+        lax.fori_loop(0, 9, turn, 0)
+        leaving += started(out_sems.at[k : k + 1], (backs.at[k], backs_far[k]))
+    finish_all(leaving)
+
+
+def gathered_rows(parts, gathered):
+    spot = lax.axis_index("row")
+    head, column = spot % HEADS, lax.axis_index("img")
+    lines = parts[0].shape[1]
+    for index, part in enumerate(parts):
+        at = pl.ds(pl.multiple_of((column ^ (index // 2)) * lines, 16), lines)
+        for pair in range(2):
+            gathered[head ^ (index % 2 + 2 * pair), at, :] = part[pair]
+
+
+def place_taps(gathered, out):
+    half = out.shape[2] // HEADS
+    for quarter in range(HEADS):
+        for tap in range(9):
+            base = tap * half
+            out[tap // 3, tap % 3, quarter * half : (quarter + 1) * half, :] = gathered[
+                quarter, base : base + half, :
+            ].astype(jnp.float32)
+
+
+def late_kernel(*refs):
+    parts, ones, time_all, (out, time_out, time_bias), rows = (
+        refs[:8], refs[8:12], refs[12], refs[13:16], refs[16:25],
+    )
+    gathered, norm_one = refs[-2:]
+    gathered_rows(parts, gathered)
+    place_taps(gathered, out)
+    rest = gathered[0, 9 * (out.shape[3] // HEADS) :, :]
+    column = lax.axis_index("img")
+    for step, part in enumerate(ones):
+        norm_one[column ^ step] = part[...]
+    total = norm_one[0] + norm_one[1] + norm_one[2] + norm_one[3]
+    lines = rest[0:16, :].astype(jnp.float32)
+    whole = jnp.concatenate([total[0:2], lines[0:7]], axis=0)
+    for k, row in enumerate(rows):
+        row[...] = whole[k : k + 1].reshape(row.shape)
+    shifts = rest[16:32, :].astype(jnp.float32)
+    images = time_all.shape[0]
+    channels = shifts.shape[1]
+    pair = jnp.concatenate([shifts[2 * k : 2 * k + 1, :] for k in range(images)], axis=0)
+    other = jnp.concatenate([shifts[2 * k + 1 : 2 * k + 2, :] for k in range(images)], axis=0)
+    time_bias[...] = jnp.concatenate([total_of(pair), total_of(other)], axis=1).reshape(
+        time_bias.shape
+    )
+    for k, lines in enumerate((pair, other)):
+        time_out[:, k * channels : (k + 1) * channels] = lax.dot_general(
+            time_all[...], lines, (((0,), (0,)), ((), ())), precision=PRECISE,
+            preferred_element_type=jnp.float32,
+        )
+
+
+def early_kernel(*refs):
+    parts, (out, qkv_out, out_out, bias_out, step_out) = refs[:8], refs[8:13]
+    (gathered,) = refs[13:]
+    gathered_rows(parts, gathered)
+    place_taps(gathered, out)
+    half = out_out.shape[0] // HEADS
+    nine = 9 * half
+    sums = []
+    for quarter in range(HEADS):
+        out_out[quarter * half : (quarter + 1) * half, :] = gathered[
+            quarter, nine + 3 * half : nine + 4 * half, :
+        ].astype(jnp.float32)
+        sums.append(gathered[quarter, nine + 4 * half : nine + 4 * half + 16].astype(jnp.float32))
+    parts = [part[0:1, :half] for part in sums] + [part[0:1, 3 * half :] for part in sums]
+    bias_out[...] = jnp.concatenate(parts, axis=1).reshape(bias_out.shape)
+    step_out[...] = sums[0][0:8]
+    for part in range(3):
+        block = jnp.concatenate(
+            [
+                gathered[quarter, nine + part * half : nine + (part + 1) * half, :]
+                for quarter in range(HEADS)
+            ],
+            axis=0,
+        )
+        width = HEADS * half
+        qkv_out[:, part * width : (part + 1) * width] = jnp.transpose(block.astype(jnp.float32))
+
+
+def swap(value, axis, step):
+    count = lax.axis_size(axis)
+    return lax.ppermute(value, axis, [(k, k ^ step) for k in range(count)])
+
+
+def pick(stacked, index):
+    return lax.dynamic_index_in_dim(stacked, index, 0, keepdims=False)
+
+
+def reduce_columns(value, column):
+    lines = value.shape[0] // 4
+    parts = value.reshape(4, lines, value.shape[1])
+    got = [swap(pick(parts, column ^ step), "img", step) for step in (1, 2, 3)]
+    total = pick(parts, column).astype(jnp.float32)
+    for part in got:
+        total = total + part.astype(jnp.float32)
+    return total.astype(jnp.bfloat16)
+
+
+def both_images(total):
+    away = swap(total, "row", 4)
+    return (total.astype(jnp.float32) + away.astype(jnp.float32)).astype(jnp.bfloat16)
+
+
+def gather_quarters(own):
+    pair = jnp.stack([own, swap(own, "row", 2)])
+    near = [pair] + [swap(pair, "img", step) for step in (1, 2, 3)]
+    return [part for mine in near for part in (mine, swap(mine, "row", 1))]
+
+
+def call(kernel, near_outs, far_outs, scratch, limit, work, scalars, near, far, last_outs=()):
+    close = pl.BlockSpec(memory_space=pltpu.VMEM)
+    distant = pl.BlockSpec(memory_space=pltpu.HBM)
+    operands = list(near) + [pltpu.with_memory_space_constraint(array, pltpu.HBM) for array in far]
+    moved = sum(array.size * array.dtype.itemsize for array in operands)
+    return pl.pallas_call(
+        kernel,
+        out_shape=[jax.ShapeDtypeStruct(*kind) for kind in near_outs]
+        + [pltpu.HBM(*kind) for kind in far_outs]
+        + [jax.ShapeDtypeStruct(*kind) for kind in last_outs],
+        in_specs=[pl.BlockSpec(memory_space=pltpu.SMEM)] * len(scalars)
+        + [close] * len(near)
+        + [distant] * len(far),
+        out_specs=[close] * len(near_outs)
+        + [distant] * len(far_outs)
+        + [close] * len(last_outs),
+        scratch_shapes=[pltpu.VMEM(*kind) if isinstance(kind, tuple) else kind for kind in scratch],
+        compiler_params=mib(limit),
+        cost_estimate=pl.CostEstimate(flops=work, bytes_accessed=moved, transcendentals=0),
+    )(*scalars, *operands)
+
+
+def sems(count):
+    return pltpu.SemaphoreType.DMA((count,))
+
+
+def gather_field(mine, theirs):
+    far, far_near = swap(theirs, "row", 4), swap(theirs, "row", 6)
+    return [mine, swap(mine, "row", 1), swap(mine, "row", 2), None, far, None, far_near, None]
+
+
+def relayed(blocks, after=None):
+    sent = [blocks[2], blocks[4], blocks[6]]
+    if after is not None:
+        sent = lax.optimization_barrier((*sent, after))[:3]
+    odd = [swap(block, "row", 1) for block in sent]
+    return [
+        blocks[0], blocks[1], blocks[2], odd[0], blocks[4], odd[1], blocks[6], odd[2],
+    ]
+
+
+def local_image(
+    pixels,
+    heights,
+    timesteps,
+    norm1_gain,
+    norm1_bias,
+    conv1_weight,
+    conv1_bias,
+    time_weight,
+    time_bias,
+    norm2_gain,
+    norm2_bias,
+    conv2_weight,
+    conv2_bias,
+    norm3_gain,
+    norm3_bias,
+    qkv_weight,
+    qv_bias,
+    out_weight,
+    out_bias,
+    grad_out,
+):
+    images, row_count, cols, channels = pixels.shape
+    block_cells = row_count * cols
+    cells = block_cells * lax.axis_size("row")
+    half = channels // HEADS
+    column = lax.axis_index("img")
+    image = lax.axis_index("row") // HEADS
+    low, full = jnp.bfloat16, jnp.float32
+    pixel_blocks = pixels.reshape(images, block_cells, channels)
+    grad_blocks = grad_out.reshape(images, block_cells, channels)
+    field = gather_field(pick(pixel_blocks, image), pick(pixel_blocks, 1 - image))
+    later = (pick(grad_blocks, image), pick(grad_blocks, 1 - image), field[4], field[6])
+    later = lax.optimization_barrier(later)
+    grads = gather_field(later[0], later[1])
+    field[4], field[6] = later[2], later[3]
+    time_act = jax.nn.silu(embed_steps(timesteps, time_weight.shape[0]))
+    shifts = jnp.dot(time_act, time_weight.astype(full), precision=PRECISE) + time_bias.astype(full)
+    kernel_shape = (3, 3 * channels, channels)
+    lanes = 2 * half
+    vec, w_heads, w_out, biases, qkv_t, w_one_back, w_two_back = call(
+        prepare_kernel,
+        [
+            ((16, channels), full), ((channels, 3 * lanes), low), ((channels, lanes), low),
+            ((8, 3 * lanes), full), ((3 * HEADS, half, channels), low),
+        ],
+        [(kernel_shape, low), (kernel_shape, low)],
+        [
+            ((2, 3, 3, channels, channels), low), ((2,) + kernel_shape, low),
+            ((channels, 3 * channels), low), ((channels, channels), low),
+            pltpu.SMEM((images,), jnp.int32), pltpu.SMEM((images,), jnp.int32),
+            ((2 * channels,), low), *[((channels,), low)] * 9,
+            sems(14), sems(2), sems(2),
+        ],
+        16,
+        channels,
+        [],
+        [shifts],
+        [
+            norm1_gain, norm1_bias, conv1_bias, norm2_gain, norm2_bias, conv2_bias, norm3_gain,
+            norm3_bias, out_bias, qv_bias, qkv_weight, out_weight, heights, timesteps,
+            conv1_weight,
+            conv2_weight,
+        ],
+    )
+    field = relayed(field, vec)
+    w_one, w_two = conv1_weight.reshape(kernel_shape), conv2_weight.reshape(kernel_shape)
+    rim_cells = cells + 2 * cols
+    cost = 9 * cells * channels * channels // 2
+
+    wide, tall = (cells, channels), (rim_cells, 3 * channels)
+    rows_eight = ((8, channels), full)
+    act_three, pix, conv_one, residual, act_one, act_two, stats = call(
+        forward_kernel,
+        [(wide, low)],
+        [(wide, low), (wide, full), (wide, full), (wide, low), (wide, low), rows_eight],
+        [
+            (wide, low), (wide, full), (wide, full), rows_eight, (kernel_shape, low),
+            (kernel_shape, low), (tall, low), (tall, low), sems(10), sems(6),
+        ],
+        28,
+        cost * 16,
+        [],
+        [vec],
+        [*field, w_one, w_two],
+    )
+    grads = relayed(grads, act_three)
+    query_shape, head_shape = (cells // 2, lanes), (cells, lanes)
+    value_key, query_part, grad_proj, mixed, out_sums = call(
+        functools.partial(attention_kernel, cols),
+        [],
+        [(head_shape, low), (query_shape, low), (wide, low), (head_shape, low), rows_eight],
+        [
+            (wide, low), (wide, low), (head_shape, low), (query_shape, low), rows_eight,
+            (head_shape, low), (head_shape, low), (head_shape, low), ((lanes, cells), full),
+            (head_shape, low), ((1, cells), full), sems(8), sems(5),
+        ],
+        36,
+        cost * 20,
+        [],
+        [vec, act_three, w_heads, w_out, biases],
+        grads,
+    )
+
+    key_near, query_near = swap(value_key, "row", 2), swap(query_part, "row", 2)
+    key_mate, query_mate = swap(value_key, "row", 1), swap(query_part, "row", 1)
+    own_shape = (3, 3 * half, cells)
+    send_shape = ((2, block_cells, lanes), low)
+    own_one, own_two, weight_rows, *sends = call(
+        aside_kernel,
+        [],
+        [(own_shape, low), (own_shape, low), ((5 * half, channels), low)],
+        [
+            ((2,) + wide, low), (head_shape, low), (head_shape, low), (wide, low), (wide, low),
+            ((rim_cells, 3 * half), full), ((2,) + own_shape, low), ((5 * half, channels), low),
+            sems(6), sems(3),
+        ],
+        28,
+        cost * 6,
+        [],
+        [vec],
+        [act_one, act_two, mixed, value_key, act_three, grad_proj],
+        [send_shape] * 4,
+    )
+    key_near, query_near, own_two = lax.optimization_barrier((key_near, query_near, own_two))
+    packed_all = [
+        value_key, query_part, key_mate, query_mate,
+        key_near, query_near, swap(key_near, "row", 1), swap(query_near, "row", 1),
+    ]
+    shifted_two, grad_res, quarter_two, sums_three = call(
+        residual_kernel,
+        [(tall, low)],
+        [(wide, full), ((14 * half, channels), low), rows_eight],
+        [
+            ((HEADS,) + head_shape, low), ((HEADS,) + query_shape, low),
+            (wide, low), (wide, full), rows_eight, (own_shape, low), (wide, full),
+            ((14 * half, channels), low), rows_eight, (wide, full), sems(13), sems(3),
+        ],
+        24,
+        cost * 6,
+        [],
+        [vec, qkv_t],
+        [*packed_all, grad_proj, residual, stats, own_two, weight_rows],
+    )
+    early_total = reduce_columns(quarter_two, column)
+    *sends, shifted_two = lax.optimization_barrier((*sends, shifted_two))
+    heads_got = [sends[0]] + [swap(sends[step], "row", step) for step in (1, 2, 3)]
+    shifted_one, quarter_one = call(
+        second_kernel,
+        [(tall, low)],
+        [((10 * half, channels), low)],
+        [
+            (kernel_shape, low), (wide, full), rows_eight, (own_shape, low), rows_eight, rows_eight,
+            ((10 * half, channels), low), (wide, full), sems(6), sems(1),
+        ],
+        20,
+        cost * 7,
+        [],
+        [vec, shifted_two],
+        [w_two_back, conv_one, stats, own_one, sums_three, out_sums],
+    )
+    late_total = reduce_columns(quarter_one, column)
+    shifted_one, early_total, late_total = lax.optimization_barrier(
+        (shifted_one, early_total, late_total)
+    )
+    early_lines = early_total.shape[0]
+    both = both_images(jnp.concatenate([early_total, late_total], axis=0))
+    early_chunk, late_chunk = both[:early_lines], both[early_lines:]
+    grad_own, grad_away, sums_one = call(
+        first_kernel,
+        [],
+        [((block_cells, channels), low), ((block_cells, channels), low), rows_eight],
+        [
+            (kernel_shape, low), (wide, low), (wide, full), rows_eight,
+            ((2, block_cells, channels), low), rows_eight, (wide, full), sems(4), sems(3),
+        ],
+        20,
+        cost * 5,
+        [],
+        [vec, shifted_one],
+        [w_one_back, pix, grad_res, stats],
+    )
+    block_own, block_away = call(
+        functools.partial(block_kernel, cols),
+        [((block_cells, channels), low), ((block_cells, channels), low)],
+        [],
+        [((2, block_cells, channels), full), sems(2)],
+        8,
+        cost,
+        [],
+        [vec, out_weight.reshape(HEADS, half, channels), *heads_got],
+        [residual],
+    )
+    early_parts = gather_quarters(early_chunk)
+    late_parts = gather_quarters(late_chunk)
+    out_pair = jnp.stack([block_own, grad_own])
+    away_pair = swap(jnp.stack([block_away, grad_away]), "row", 4)
+    first_pair = jnp.where(image == 0, out_pair, away_pair)
+    second_pair = jnp.where(image == 0, away_pair, out_pair)
+    finished = jnp.stack([first_pair, second_pair], axis=1).reshape((2,) + pixels.shape)
+    norm_one = sums_one + swap(sums_one, "row", 4)
+    norm_parts = [norm_one] + [swap(norm_one, "img", step) for step in (1, 2, 3)]
+
+    nine = 9 * half
+    conv2_weight_grad, qkv_weight_grad, out_weight_grad, qv_bias_grad, steps = call(
+        early_kernel,
+        [
+            ((3, 3, channels, channels), full), ((channels, 3 * channels), full),
+            ((channels, channels), full), ((2 * channels,), full), rows_eight,
+        ],
+        [],
+        [((HEADS, nine + 5 * half, channels), low)],
+        12,
+        cost,
+        [],
+        early_parts,
+        [],
+    )
+    all_images = images * lax.axis_size("img")
+    steps_all = steps[1, :all_images] * 32.0 + steps[2, :all_images]
+    time_all = jax.nn.silu(embed_steps(steps_all, time_weight.shape[0]))
+    line = ((channels,), full)
+    conv1_weight_grad, time_weight_grad, time_bias_grad, *lines = call(
+        late_kernel,
+        [
+            ((3, 3, channels, channels), full), ((time_weight.shape[0], 2 * channels), full),
+            ((2 * channels,), full), line, line, line, line, line, line, line, line, line,
+        ],
+        [],
+        [((HEADS, 10 * half, channels), low), ((4, 8, channels), full)],
+        12,
+        cost,
+        [],
+        [*late_parts, *norm_parts, time_all],
+        [],
+    )
+    norm1_gain_grad, norm1_bias_grad, norm3_gain_grad, norm3_bias_grad, conv2_bias_grad = lines[:5]
+    out_bias_grad, norm2_gain_grad, norm2_bias_grad, conv1_bias_grad = lines[5:]
+    return (
+        finished[0],
+        finished[1],
+        norm1_gain_grad,
+        norm1_bias_grad,
+        conv1_weight_grad,
+        conv1_bias_grad,
+        time_weight_grad,
+        time_bias_grad,
+        norm2_gain_grad,
+        norm2_bias_grad,
+        conv2_weight_grad,
+        conv2_bias_grad,
+        norm3_gain_grad,
+        norm3_bias_grad,
+        qkv_weight_grad,
+        qv_bias_grad,
+        out_weight_grad,
+        out_bias_grad,
+    )
+
+
+def local(*arrays):
+    pixels = arrays[0]
+    if lax.axis_size("row") == pixels.shape[0] * HEADS and lax.axis_size("img") == 4:
+        return local_image(*arrays)
+    return local_rows(*arrays)
+
+
 def solution(mesh):
     placed = (
         P("img", "row", None, None),

time: 604 us -> 168 us (0.28); the launches traced: 594 us -> 168 us
  blocking collectives: 205 us -> 0 us
  local copies, waits for them, and re-layouts: 113 us -> 4.13 us
  matrix products: 95.1 us -> 0.51 us
  Pallas kernels: 0 us -> 80.1 us
  waiting for transfers between devices: 115 us -> 35.3 us
  other arithmetic: 36.7 us -> 4.34 us
  starting transfers between devices: 12.7 us -> 41.8 us
  between operations: 16.5 us -> 1.36 us
    psum x10 -> x0, blocking collectives: 177 us -> none  [the longest x3 49.4 us: norm_forward(): first_sum = lax.psum(jnp.sum(shaped * cell_mask, axis=(1, 2, 4)), 'row')]
    psum x1 -> x0, waiting for transfers between devices: 105 us -> none  [local(): lax.psum((norm1_gain_grad, norm1_bias_grad, conv1_weight_grad, conv1_bias...]
    dot_general x32 -> x1, matrix products: 89.7 us -> 0.51 us  [local_image(): jnp.dot(time_act, time_weight.astype(full), precision=PRECISE)]
    pallas_call x0 -> x10, Pallas kernels: none -> 80.1 us  [call(): pl.pallas_call(kernel, out_shape=[jax.ShapeDtypeStruct(*kind) for kind in...]
    reshape x15 -> x0, local copies, waits for them, and re-layouts: 65.1 us -> none  [the longest x8 56.3 us: flatten_rows(): piece_arr.reshape(image_count, piece_arr.shape[1] * col_count, head_count...]
    ppermute x8 -> x51, waiting for transfers between devices: 1.44 us -> 35.3 us  [swap(): return lax.ppermute(value, axis, [(k, k ^ step) for k in range(count)])]
    ppermute x8 -> x51, starting transfers between devices: 12.3 us -> 41.8 us  [swap(): return lax.ppermute(value, axis, [(k, k ^ step) for k in range(count)])]
    all_gather x2 -> x0, blocking collectives: 27.9 us -> none  [the longest x1 14 us: local(): lax.all_gather(delta_own.reshape(stat_shape), 'row', axis=1, tiled=True)]
  transfers between devices with their start and end apart: 13 -> 51, of which waited for: 4 -> 19; matrix products, arithmetic and copies ran while one was open for 23% -> 3% of each run, Pallas kernels for 0% -> 25%
where the time goes in v2:
time: 168 us
  Pallas kernels  80.1 us (48%)
  starting transfers between devices  41.8 us (25%)
  waiting for transfers between devices  35.3 us (21%)
  other arithmetic  4.34 us (3%)
  local copies, waits for them, and re-layouts  4.13 us (2%)
    pallas_call x10, Pallas kernels, call(): pl.pallas_call(kernel, out_shape=[jax.ShapeDtypeStruct(*kind) for kind in...  80.1 us
    ppermute x51, starting transfers between devices, swap(): return lax.ppermute(value, axis, [(k, k ^ step) for k in range(count)])  41.8 us
    ppermute x51, waiting for transfers between devices, swap(): return lax.ppermute(value, axis, [(k, k ^ step) for k in range(count)])  35.3 us
  transfers between devices with their start and end apart: 51, of which 19 were waited for; matrix products, arithmetic and copies ran while one was open for 3% of the time, Pallas kernels for 25%

profile of v2, /device:TPU:0, one launch (start us, length us, event | category | flops | bytes accessed | tf_op | source)
XLA Modules:
  0.0 167.6 jit_solution(17511800190001572533)
XLA Ops:
  0.7 1.1 dynamic-slice_bitcast_fusion
  1.8 4.1 %collective-permute-start.2 = (bf16[256,256]{1,0:T(8,128)(2,1)S(1)}, bf16[256,256]{1,0:T(8,128)(2,1)S(1)}, u32[]{:S(2)}, u32[]{:S(2)}) collective-permute-start(bf16[256,256]{1,0:T(8,128)(2,1)S(1)} %get-tuple-element.178), channel_id=1, source_target_pairs={{0,4},{1,5},{2,6},{3,7},{4,0},{5,1},{6,2},{7,3},{8,12},{9,13},{10,... | collective-permute-start | bytes 393224 | tf_op jit(solution)/shard_map/ppermute | solution.py:1166
  5.9 1.3 collective-permute-start.3
  9.5 4.8 %shard_map.331 = (f32[16,256]{1,0:T(8,128)S(1)}, bf16[256,384]{1,0:T(8,128)(2,1)S(1)}, bf16[256,128]{1,0:T(8,128)(2,1)S(1)}, f32[8,384]{1,0:T(8,128)S(1)}, bf16[...) custom-call(f32[2,512]{1,0:T(2,128)S(1)} %convolution_add_fusion.refs_0_, ...), custom_call_target="tpu_custom_call" | custom-call | flops 256 | bytes 2893328 | tf_op jit(solution)/shard_map/pallas_call | solution.py:1199
  14.4 1.5 collective-permute-done.2.refs_4_
  16.9 3.5 %collective-permute-start.10 = (bf16[256,256]{1,0:T(8,128)(2,1)S(1)}, bf16[256,256]{1,0:T(8,128)(2,1)S(1)}, u32[]{:S(2)}, u32[]{:S(2)}) collective-permute-start(bf16[256,256]{1,0:T(8,128)(2,1)S(1)} %get-tuple-element.106), channel_id=1, source_target_pairs={{0,6},{1,7},{2,4},{3,5},{4,2},{5,3},{6,0},{7,1},{8,14},{9,15},{10,... | collective-permute-start | bytes 393224 | tf_op jit(solution)/shard_map/ppermute | solution.py:1166
  20.4 0.8 collective-permute-start.9
  22.5 13.0 %shard_map.332 = (bf16[2048,256]{1,0:T(8,128)(2,1)S(1)}, bf16[2048,256]{1,0:T(8,128)(2,1)}, f32[2048,256]{1,0:T(8,128)}, f32[2048,256]{1,0:T(8,128)}, bf16[2048,...) custom-call(f32[16,256]{1,0:T(8,128)S(1)} %get-tuple-element.93.vec, bf16[256,256]{1,0:T(8,128)(2,1)} %copy-done.6, ...), custom_call_target="tpu_custom_call" | custom-call | flops 9663676416 | bytes 3424256 | tf_op jit(solution)/shard_map/pallas_call | solution.py:1199
  38.4 17.9 %shard_map.333 = (bf16[2048,128]{1,0:T(8,128)(2,1)}, bf16[1024,128]{1,0:T(8,128)(2,1)}, bf16[2048,256]{1,0:T(8,128)(2,1)}, bf16[2048,128]{1,0:T(8,128)(2,1)}, f32[8,256]{1,0:T(8,128)}) custom-call(f32[16,256]{1,0:T(8,128)S(1)} %get-tuple-element.93.vec, bf16[2048,256]{1,0:T(8,128)(2,1)S(1)} %get-tuple-element.101.act_three.refs_4_, ...), custom_call_target="tpu_custom_call" | custom-call | flops 12079595520 | bytes 2387968 | tf_op jit(solution)/shard_map/pallas_call | solution.py:1199
  56.3 1.5 collective-permute-start.16
  58.4 13.9 %shard_map.334 = (bf16[3,192,2048]{2,1,0:T(8,128)(2,1)}, bf16[3,192,2048]{2,1,0:T(8,128)(2,1)}, bf16[320,256]{1,0:T(8,128)(2,1)}, bf16[2,256,128]{2,1,0:T(8,128)...) custom-call(f32[16,256]{1,0:T(8,128)S(1)} %get-tuple-element.93.vec,, ...), custom_call_target="tpu_custom_call" | custom-call | flops 3623878656 | bytes 5259264 | tf_op jit(solution)/shard_map/pallas_call | solution.py:1199
  72.3 4.1 %collective-permute-done.17.refs_5_ = bf16[1024,128]{1,0:T(8,128)(2,1)} collective-permute-done((bf16[1024,128]{1,0:T(8,128)(2,1)}, bf16[1024,128]{1,0:T(8,128)(2,1)}, u32[]{:S(2)}, u32[]{:S(2)}) %collective-permute-start.17) | collective-permute-done | bytes 262176 | tf_op jit(solution)/shard_map/ppermute | solution.py:1166
  77.0 2.2 %collective-permute-done.15.refs_3_ = bf16[1024,128]{1,0:T(8,128)(2,1)} collective-permute-done((bf16[1024,128]{1,0:T(8,128)(2,1)S(1)}, bf16[1024,128]{1,0:T(8,128)(2,1)}, u32[]{:S(2)}, u32[]{:S(2)}) %collective-permute-start.15) | collective-permute-done | bytes 262176 | tf_op jit(solution)/shard_map/ppermute | solution.py:1166
  80.1 7.1 %shard_map.335 = (bf16[2176,768]{1,0:T(8,128)(2,1)S(1)}, f32[2048,256]{1,0:T(8,128)}, bf16[896,256]{1,0:T(8,128)(2,1)}, f32[8,256]{1,0:T(8,128)}) custom-call(f32[16,256]{1,0:T(8,128)S(1)} %get-tuple-element.93.vec, bf16[12,64,256]{2,1,0:T(8,128)(2,1)S(1)} %get-tuple-element.117.qkv_t, bf16[2048,128]{1,0:T(8,128)(2,1)} %get-tuple-element.111.refs_3_.refs_0_, ...), custom_call_target="tpu_custom_call" | custom-call | flops 3623878656 | bytes 9232384 | tf_op jit(solution)/shard_map/pallas_call | solution.py:1199
  87.2 8.6 %shard_map.337 = (bf16[2176,768]{1,0:T(8,128)(2,1)S(1)}, bf16[640,256]{1,0:T(8,128)(2,1)}) custom-call(f32[16,256]{1,0:T(8,128)S(1)} %get-tuple-element.93.vec, bf16[2176,768]{1,0:T(8,128)(2,1)S(1)} %get-tuple-element.132.shifted, bf16[3,768,256]{2,1,0:T(8,128)(2,1)} %get-tuple-element.133.weight_far, f32[2048,256]{1,0:T(8,128)} %get-tuple-element.134.conv_far, ...), custom_call_target="tpu_custom_call" | custom-call | flops 4227858432 | bytes 9019392 | tf_op jit(solution)/shard_map/pallas_call | solution.py:1199
  95.8 1.0 dynamic-slice_bitcast_fusion.9
  96.8 1.6 collective-permute-start.26
  98.4 1.5 collective-permute-start.27
  100.4 1.6 collective-permute-start.23
  102.0 1.5 collective-permute-start.24
  103.5 0.7 collective-permute-start.25
  104.2 2.0 %collective-permute-done.28 = bf16[160,256]{1,0:T(8,128)(2,1)S(1)} collective-permute-done((bf16[160,256]{1,0:T(8,128)(2,1)S(1)}, bf16[160,256]{1,0:T(8,128)(2,1)S(1)}, u32[]{:S(2)}, u32[]{:S(2)}) %collective-permute-start.28) | collective-permute-done | bytes 81952 | tf_op jit(solution)/shard_map/ppermute | solution.py:1166
  106.3 1.4 collective-permute-start.21
  107.7 0.9 fusion.6
  108.8 0.9 collective-permute-done.25
  109.8 2.9 %collective-permute-start.30 = (bf16[384,256]{1,0:T(8,128)(2,1)S(1)}, bf16[384,256]{1,0:T(8,128)(2,1)S(1)}, u32[]{:S(2)}, u32[]{:S(2)}) collective-permute-start(bf16[384,256]{1,0:T(8,128)(2,1)S(1)} %constant_dynamic-update-slice_fusion), channel_id=1, source_target_pairs={{0,4},{1,5},{2,6},{3,7},{4,0},{5,1},{6,2},{7,3},{8,12},{9,13},{10,... | collective-permute-start | bytes 589832 | tf_op jit(solution)/shard_map/ppermute | solution.py:1166
  112.7 7.0 %shard_map.338 = (bf16[256,256]{1,0:T(8,128)(2,1)}, bf16[256,256]{1,0:T(8,128)(2,1)}, f32[8,256]{1,0:T(8,128)}) custom-call(f32[16,256]{1,0:T(8,128)S(1)} %get-tuple-element.93.vec, bf16[2176,768]{1,0:T(8,128)(2,1)S(1)} %get-tuple-element.141.shifted, bf16[3,768,256]{2,1,0:T(8,128)(2,1)} %get-tuple-element.142.weight_far, ...), custom_call_target="tpu_custom_call" | custom-call | flops 3019898880 | bytes 7692288 | tf_op jit(solution)/shard_map/pallas_call | solution.py:1199
  119.9 4.7 %collective-permute-done.39 = f32[8,256]{1,0:T(8,128)S(1)} collective-permute-done((f32[8,256]{1,0:T(8,128)}, f32[8,256]{1,0:T(8,128)S(1)}, u32[]{:S(2)}, u32[]{:S(2)}) %collective-permute-start.39) | collective-permute-done | bytes 8224 | tf_op jit(solution)/shard_map/ppermute | solution.py:1166
  125.2 1.6 shard_map.336
  127.2 1.4 collective-permute-start.43
  128.6 0.7 collective-permute-start.31
  129.4 5.5 %collective-permute-done.43 = bf16[224,256]{1,0:T(8,128)(2,1)S(1)} collective-permute-done((bf16[224,256]{1,0:T(8,128)(2,1)S(1)}, bf16[224,256]{1,0:T(8,128)(2,1)S(1)}, u32[]{:S(2)}, u32[]{:S(2)}) %collective-permute-start.43) | collective-permute-done | bytes 114720 | tf_op jit(solution)/shard_map/ppermute | solution.py:1166
  135.3 1.2 collective-permute-start.47
  136.5 1.9 %collective-permute-start.49 = (bf16[2,224,256]{2,1,0:T(8,128)(2,1)S(1)}, bf16[2,224,256]{2,1,0:T(8,128)(2,1)S(1)}, u32[]{:S(2)}, u32[]{:S(2)}) collective-permute-start(bf16[2,224,256]{2,1,0:T(8,128)(2,1)S(1)} %pad_maximum_fusion.3.refs_0_), channel_id=1, source_target_pairs={{0,24},{8,16},{16,8},{24,0},{1,25},{9,17},{17,9},{25,1},{2,26},{10... | collective-permute-start | bytes 688136 | tf_op jit(solution)/shard_map/ppermute | solution.py:1166
  138.4 1.6 collective-permute-done.29
  140.1 1.6 collective-permute-done.45.refs_2_
  142.2 2.2 %collective-permute-done.49.refs_6_ = bf16[2,224,256]{2,1,0:T(8,128)(2,1)S(1)} collective-permute-done((bf16[2,224,256]{2,1,0:T(8,128)(2,1)S(1)}, bf16[2,224,256]{2,1,0:T(8,128)(2,1)S(1)}, u32[]{:S(2)}, u32[]{:S(2)}) %collective-permute-start.49) | collective-permute-done | bytes 229408 | tf_op jit(solution)/shard_map/ppermute | solution.py:1166
  144.4 0.8 pad_maximum_fusion
  145.3 2.0 %collective-permute-start.40 = (f32[8,256]{1,0:T(8,128)S(1)}, f32[8,256]{1,0:T(8,128)S(1)}, u32[]{:S(2)}, u32[]{:S(2)}) collective-permute-start(f32[8,256]{1,0:T(8,128)S(1)} %add.95.refs_8_), channel_id=1, source_target_pairs={{0,8},{8,0},{16,24},{24,16},{1,9},{9,1},{17,25},{25,17},{2,10},{10... | collective-permute-start | bytes 24584 | tf_op jit(solution)/shard_map/ppermute | solution.py:1166
  147.3 0.9 collective-permute-start.41
  148.7 0.8 collective-permute-start.35
  149.5 2.2 %collective-permute-start.37 = (bf16[2,160,256]{2,1,0:T(8,128)(2,1)S(1)}, bf16[2,160,256]{2,1,0:T(8,128)(2,1)S(1)}, u32[]{:S(2)}, u32[]{:S(2)}) collective-permute-start(bf16[2,160,256]{2,1,0:T(8,128)(2,1)S(1)} %pad_maximum_fusion.4.refs_0_), channel_id=1, source_target_pairs={{0,24},{8,16},{16,8},{24,0},{1,25},{9,17},{17,9},{25,1},{2,26},{10... | collective-permute-start | bytes 491528 | tf_op jit(solution)/shard_map/ppermute | solution.py:1166
  151.7 2.1 %shard_map.339 = (f32[3,3,256,256]{3,2,1,0:T(8,128)}, f32[256,768]{1,0:T(8,128)}, f32[256,256]{1,0:T(8,128)}, f32[512]{0:T(512)}, f32[8,256]{1,0:T(8,128)S(1)}) custom-call(bf16[2,224,256]{2,1,0:T(8,128)(2,1)S(1)} %pad_maximum_fusion.3.refs_0_, bf16[2,224,256]{2,1,0:T(8,128)(2,1)S(1)} %collective-permute-done.44.refs_1_, ...), custom_call_target="tpu_custom_call" | custom-call | flops 603979776 | bytes 1835008 | tf_op jit(solution)/shard_map/pallas_call | solution.py:1199
  153.9 1.5 collective-permute-done.33.refs_2_
  155.3 2.7 %collective-permute-done.35.refs_4_ = bf16[2,160,256]{2,1,0:T(8,128)(2,1)S(1)} collective-permute-done((bf16[2,160,256]{2,1,0:T(8,128)(2,1)S(1)}, bf16[2,160,256]{2,1,0:T(8,128)(2,1)S(1)}, u32[]{:S(2)}, u32[]{:S(2)}) %collective-permute-start.35) | collective-permute-done | bytes 163872 | tf_op jit(solution)/shard_map/ppermute | solution.py:1166
  158.7 1.7 %collective-permute-start.42 = (f32[8,256]{1,0:T(8,128)S(1)}, f32[8,256]{1,0:T(8,128)S(1)}, u32[]{:S(2)}, u32[]{:S(2)}) collective-permute-start(f32[8,256]{1,0:T(8,128)S(1)} %add.95.refs_8_), channel_id=1, source_target_pairs={{0,24},{8,16},{16,8},{24,0},{1,25},{9,17},{17,9},{25,1},{2,26},{10... | collective-permute-start | bytes 24584 | tf_op jit(solution)/shard_map/ppermute | solution.py:1166
  160.5 2.8 %collective-permute-done.42.refs_11_ = f32[8,256]{1,0:T(8,128)S(1)} collective-permute-done((f32[8,256]{1,0:T(8,128)S(1)}, f32[8,256]{1,0:T(8,128)S(1)}, u32[]{:S(2)}, u32[]{:S(2)}) %collective-permute-start.42) | collective-permute-done | bytes 8224 | tf_op jit(solution)/shard_map/ppermute | solution.py:1166
  163.3 4.1 %shard_map.340 = (f32[3,3,256,256]{3,2,1,0:T(8,128)}, f32[1024,512]{1,0:T(8,128)}, f32[512]{0:T(512)}, f32[256]{0:T(256)}, f32[256]{0:T(256)}, /*index=5*/f32[25...) custom-call(bf16[2,160,256]{2,1,0:T(8,128)(2,1)S(1)} %pad_maximum_fusio, ...), custom_call_target="tpu_custom_call" | custom-call | flops 603979776 | bytes 1376256 | tf_op jit(solution)/shard_map/pallas_call | solution.py:1199
  (141 shorter events, 13.5 us)
Async XLA Ops:
  1.8 14.1 %collective-permute-start.2 = (bf16[256,256]{1,0:T(8,128)(2,1)S(1)}, bf16[256,256]{1,0:T(8,128)(2,1)S(1)}, u32[]{:S(2)}, u32[]{:S(2)}) collective-permute-start(bf16[256,256]{1,0:T(8,128)(2,1)S(1)} %get-tuple-element.178), channel_id=1, source_target_pairs={{0,4},{1,5},{2,6},{3,7},{4,0},{5,1},{6,2},{7,3},{8,12},{9,13},{10,... | collective-permute-start | bytes 393224 | tf_op jit(solution)/shard_map/ppermute | solution.py:1166
  5.9 10.0 %collective-permute-start.3 = (bf16[256,256]{1,0:T(8,128)(2,1)S(1)}, bf16[256,256]{1,0:T(8,128)(2,1)S(1)}, u32[]{:S(2)}, u32[]{:S(2)}) collective-permute-start(bf16[256,256]{1,0:T(8,128)(2,1)S(1)} %get-tuple-element.178), channel_id=1, source_target_pairs={{0,6},{1,7},{2,4},{3,5},{4,2},{5,3},{6,0},{7,1},{8,14},{9,15},{10,... | collective-permute-start | bytes 393224 | tf_op jit(solution)/shard_map/ppermute | solution.py:1166
  7.2 9.2 %collective-permute-start.1 = (bf16[256,256]{1,0:T(8,128)(2,1)S(1)}, bf16[256,256]{1,0:T(8,128)(2,1)S(1)}, u32[]{:S(2)}, u32[]{:S(2)}) collective-permute-start(bf16[256,256]{1,0:T(8,128)(2,1)S(1)} %get-tuple-element.179.refs_0_), channel_id=1, source_target_pairs={{0,2},{1,3},{2,0},{3,1},{4,6},{5,7},{6,4},{7,5},{8,10},{9,11},{10,... | collective-permute-start | bytes 393224 | tf_op jit(solution)/shard_map/ppermute | solution.py:1166
  7.5 13.0 %collective-permute-start = (bf16[256,256]{1,0:T(8,128)(2,1)S(1)}, bf16[256,256]{1,0:T(8,128)(2,1)S(1)}, u32[]{:S(2)}, u32[]{:S(2)}) collective-permute-start(bf16[256,256]{1,0:T(8,128)(2,1)S(1)} %get-tuple-element.179.refs_0_), channel_id=1, source_target_pairs={{0,1},{1,0},{2,3},{3,2},{4,5},{5,4},{6,7},{7,6},{8,9},{9,8},{10,11... | collective-permute-start | bytes 393224 | tf_op jit(solution)/shard_map/ppermute | solution.py:1166
  16.4 4.8 %collective-permute-start.4 = (bf16[256,256]{1,0:T(8,128)(2,1)S(1)}, bf16[256,256]{1,0:T(8,128)(2,1)S(1)}, u32[]{:S(2)}, u32[]{:S(2)}) collective-permute-start(bf16[256,256]{1,0:T(8,128)(2,1)S(1)} %collective-permute-done.1.refs_2_), channel_id=1, source_target_pairs={{0,1},{1,0},{2,3},{3,2},{4,5},{5,4},{6,7},{7,6},{8,9},{9,8},{10,11... | collective-permute-start | bytes 393224 | tf_op jit(solution)/shard_map/ppermute | solution.py:1166
  16.4 5.4 %collective-permute-start.5 = (bf16[256,256]{1,0:T(8,128)(2,1)S(1)}, bf16[256,256]{1,0:T(8,128)(2,1)S(1)}, u32[]{:S(2)}, u32[]{:S(2)}) collective-permute-start(bf16[256,256]{1,0:T(8,128)(2,1)S(1)} %collective-permute-done.2.refs_4_), channel_id=1, source_target_pairs={{0,1},{1,0},{2,3},{3,2},{4,5},{5,4},{6,7},{7,6},{8,9},{9,8},{10,11... | collective-permute-start | bytes 393224 | tf_op jit(solution)/shard_map/ppermute | solution.py:1166
  16.9 4.9 %collective-permute-start.6 = (bf16[256,256]{1,0:T(8,128)(2,1)S(1)}, bf16[256,256]{1,0:T(8,128)(2,1)S(1)}, u32[]{:S(2)}, u32[]{:S(2)}) collective-permute-start(bf16[256,256]{1,0:T(8,128)(2,1)S(1)} %collective-permute-done.3.refs_6_), channel_id=1, source_target_pairs={{0,1},{1,0},{2,3},{3,2},{4,5},{5,4},{6,7},{7,6},{8,9},{9,8},{10,11... | collective-permute-start | bytes 393224 | tf_op jit(solution)/shard_map/ppermute | solution.py:1166
  16.9 18.6 %collective-permute-start.10 = (bf16[256,256]{1,0:T(8,128)(2,1)S(1)}, bf16[256,256]{1,0:T(8,128)(2,1)S(1)}, u32[]{:S(2)}, u32[]{:S(2)}) collective-permute-start(bf16[256,256]{1,0:T(8,128)(2,1)S(1)} %get-tuple-element.106), channel_id=1, source_target_pairs={{0,6},{1,7},{2,4},{3,5},{4,2},{5,3},{6,0},{7,1},{8,14},{9,15},{10,... | collective-permute-start | bytes 393224 | tf_op jit(solution)/shard_map/ppermute | solution.py:1166
  20.4 15.2 %collective-permute-start.9 = (bf16[256,256]{1,0:T(8,128)(2,1)S(1)}, bf16[256,256]{1,0:T(8,128)(2,1)S(1)}, u32[]{:S(2)}, u32[]{:S(2)}) collective-permute-start(bf16[256,256]{1,0:T(8,128)(2,1)S(1)} %get-tuple-element.106), channel_id=1, source_target_pairs={{0,4},{1,5},{2,6},{3,7},{4,0},{5,1},{6,2},{7,3},{8,12},{9,13},{10,... | collective-permute-start | bytes 393224 | tf_op jit(solution)/shard_map/ppermute | solution.py:1166
  21.2 14.3 %collective-permute-start.8 = (bf16[256,256]{1,0:T(8,128)(2,1)S(1)}, bf16[256,256]{1,0:T(8,128)(2,1)S(1)}, u32[]{:S(2)}, u32[]{:S(2)}) collective-permute-start(bf16[256,256]{1,0:T(8,128)(2,1)S(1)} %get-tuple-element.105.refs_0_), channel_id=1, source_target_pairs={{0,2},{1,3},{2,0},{3,1},{4,6},{5,7},{6,4},{7,5},{8,10},{9,11},{10,... | collective-permute-start | bytes 393224 | tf_op jit(solution)/shard_map/ppermute | solution.py:1166
  21.8 14.9 %collective-permute-start.7 = (bf16[256,256]{1,0:T(8,128)(2,1)S(1)}, bf16[256,256]{1,0:T(8,128)(2,1)S(1)}, u32[]{:S(2)}, u32[]{:S(2)}) collective-permute-start(bf16[256,256]{1,0:T(8,128)(2,1)S(1)} %get-tuple-element.105.refs_0_), channel_id=1, source_target_pairs={{0,1},{1,0},{2,3},{3,2},{4,5},{5,4},{6,7},{7,6},{8,9},{9,8},{10,11... | collective-permute-start | bytes 393224 | tf_op jit(solution)/shard_map/ppermute | solution.py:1166
  56.3 20.1 %collective-permute-start.16 = (bf16[2048,128]{1,0:T(8,128)(2,1)}, bf16[2048,128]{1,0:T(8,128)(2,1)S(1)}, u32[]{:S(2)}, u32[]{:S(2)}) collective-permute-start(bf16[2048,128]{1,0:T(8,128)(2,1)} %get-tuple-element.111.refs_3_.refs_0_), channel_id=1, source_target_pairs={{0,2},{1,3},{2,0},{3,1},{4,6},{5,7},{6,4},{7,5},{8,10},{9,11},{10,... | collective-permute-start | bytes 1572872 | tf_op jit(solution)/shard_map/ppermute | solution.py:1166
  57.8 21.4 %collective-permute-start.14 = (bf16[2048,128]{1,0:T(8,128)(2,1)}, bf16[2048,128]{1,0:T(8,128)(2,1)S(1)}, u32[]{:S(2)}, u32[]{:S(2)}) collective-permute-start(bf16[2048,128]{1,0:T(8,128)(2,1)} %get-tuple-element.111.refs_3_.refs_0_), channel_id=1, source_target_pairs={{0,1},{1,0},{2,3},{3,2},{4,5},{5,4},{6,7},{7,6},{8,9},{9,8},{10,11... | collective-permute-start | bytes 1572872 | tf_op jit(solution)/shard_map/ppermute | solution.py:1166
  57.9 18.6 %collective-permute-start.17 = (bf16[1024,128]{1,0:T(8,128)(2,1)}, bf16[1024,128]{1,0:T(8,128)(2,1)}, u32[]{:S(2)}, u32[]{:S(2)}) collective-permute-start(bf16[1024,128]{1,0:T(8,128)(2,1)} %get-tuple-element.118.refs_1_), channel_id=1, source_target_pairs={{0,2},{1,3},{2,0},{3,1},{4,6},{5,7},{6,4},{7,5},{8,10},{9,11},{10,... | collective-permute-start | bytes 786440 | tf_op jit(solution)/shard_map/ppermute | solution.py:1166
  76.4 3.0 %collective-permute-start.18 = (bf16[2048,128]{1,0:T(8,128)(2,1)S(1)}, bf16[2048,128]{1,0:T(8,128)(2,1)}, u32[]{:S(2)}, u32[]{:S(2)}) collective-permute-start(bf16[2048,128]{1,0:T(8,128)(2,1)S(1)} %collective-permute-done.16.refs_4_), channel_id=1, source_target_pairs={{0,1},{1,0},{2,3},{3,2},{4,5},{5,4},{6,7},{7,6},{8,9},{9,8},{10,11... | collective-permute-start | bytes 1572872 | tf_op jit(solution)/shard_map/ppermute | solution.py:1166
  76.5 2.8 %collective-permute-start.15 = (bf16[1024,128]{1,0:T(8,128)(2,1)S(1)}, bf16[1024,128]{1,0:T(8,128)(2,1)}, u32[]{:S(2)}, u32[]{:S(2)}) collective-permute-start(bf16[1024,128]{1,0:T(8,128)(2,1)S(1)} %copy-done.11), channel_id=1, source_target_pairs={{0,1},{1,0},{2,3},{3,2},{4,5},{5,4},{6,7},{7,6},{8,9},{9,8},{10,11... | collective-permute-start | bytes 786440 | tf_op jit(solution)/shard_map/ppermute | solution.py:1166
  77.0 2.5 %collective-permute-start.19 = (bf16[1024,128]{1,0:T(8,128)(2,1)}, bf16[1024,128]{1,0:T(8,128)(2,1)}, u32[]{:S(2)}, u32[]{:S(2)}) collective-permute-start(bf16[1024,128]{1,0:T(8,128)(2,1)} %collective-permute-done.17.refs_5_), channel_id=1, source_target_pairs={{0,1},{1,0},{2,3},{3,2},{4,5},{5,4},{6,7},{7,6},{8,9},{9,8},{10,11... | collective-permute-start | bytes 786440 | tf_op jit(solution)/shard_map/ppermute | solution.py:1166
  96.8 6.7 %collective-permute-start.26 = (bf16[160,256]{1,0:T(8,128)(2,1)S(1)}, bf16[160,256]{1,0:T(8,128)(2,1)S(1)}, u32[]{:S(2)}, u32[]{:S(2)}) collective-permute-start(bf16[160,256]{1,0:T(8,128)(2,1)S(1)} %get-tuple-element.175), channel_id=1, source_target_pairs={{0,8},{8,0},{16,24},{24,16},{1,9},{9,1},{17,25},{25,17},{2,10},{10... | collective-permute-start | bytes 245768 | tf_op jit(solution)/shard_map/ppermute | solution.py:1166
  98.4 5.8 %collective-permute-start.27 = (bf16[160,256]{1,0:T(8,128)(2,1)S(1)}, bf16[160,256]{1,0:T(8,128)(2,1)S(1)}, u32[]{:S(2)}, u32[]{:S(2)}) collective-permute-start(bf16[160,256]{1,0:T(8,128)(2,1)S(1)} %get-tuple-element.177), channel_id=1, source_target_pairs={{0,16},{8,24},{16,0},{24,8},{1,17},{9,25},{17,1},{25,9},{2,18},{10... | collective-permute-start | bytes 245768 | tf_op jit(solution)/shard_map/ppermute | solution.py:1166
  99.9 6.4 %collective-permute-start.28 = (bf16[160,256]{1,0:T(8,128)(2,1)S(1)}, bf16[160,256]{1,0:T(8,128)(2,1)S(1)}, u32[]{:S(2)}, u32[]{:S(2)}) collective-permute-start(bf16[160,256]{1,0:T(8,128)(2,1)S(1)} %get-tuple-element.176), channel_id=1, source_target_pairs={{0,24},{8,16},{16,8},{24,0},{1,25},{9,17},{17,9},{25,1},{2,26},{10... | collective-permute-start | bytes 245768 | tf_op jit(solution)/shard_map/ppermute | solution.py:1166
  100.4 8.2 %collective-permute-start.23 = (bf16[224,256]{1,0:T(8,128)(2,1)S(1)}, bf16[224,256]{1,0:T(8,128)(2,1)S(1)}, u32[]{:S(2)}, u32[]{:S(2)}) collective-permute-start(bf16[224,256]{1,0:T(8,128)(2,1)S(1)} %get-tuple-element.172), channel_id=1, source_target_pairs={{0,8},{8,0},{16,24},{24,16},{1,9},{9,1},{17,25},{25,17},{2,10},{10... | collective-permute-start | bytes 344072 | tf_op jit(solution)/shard_map/ppermute | solution.py:1166
  102.0 6.8 %collective-permute-start.24 = (bf16[224,256]{1,0:T(8,128)(2,1)S(1)}, bf16[224,256]{1,0:T(8,128)(2,1)S(1)}, u32[]{:S(2)}, u32[]{:S(2)}) collective-permute-start(bf16[224,256]{1,0:T(8,128)(2,1)S(1)} %get-tuple-element.174), channel_id=1, source_target_pairs={{0,16},{8,24},{16,0},{24,8},{1,17},{9,25},{17,1},{25,9},{2,18},{10... | collective-permute-start | bytes 344072 | tf_op jit(solution)/shard_map/ppermute | solution.py:1166
  103.5 6.2 %collective-permute-start.25 = (bf16[224,256]{1,0:T(8,128)(2,1)S(1)}, bf16[224,256]{1,0:T(8,128)(2,1)S(1)}, u32[]{:S(2)}, u32[]{:S(2)}) collective-permute-start(bf16[224,256]{1,0:T(8,128)(2,1)S(1)} %get-tuple-element.173), channel_id=1, source_target_pairs={{0,24},{8,16},{16,8},{24,0},{1,25},{9,17},{17,9},{25,1},{2,26},{10... | collective-permute-start | bytes 344072 | tf_op jit(solution)/shard_map/ppermute | solution.py:1166
  104.2 21.0 %collective-permute-start.20 = (bf16[2,256,128]{2,1,0:T(8,128)(2,1)S(1)}, bf16[2,256,128]{2,1,0:T(8,128)(2,1)S(1)}, u32[]{:S(2)}, u32[]{:S(2)}) collective-permute-start(bf16[2,256,128]{2,1,0:T(8,128)(2,1)S(1)} %get-tuple-element.128), channel_id=1, source_target_pairs={{0,1},{1,0},{2,3},{3,2},{4,5},{5,4},{6,7},{7,6},{8,9},{9,8},{10,11... | collective-permute-start | bytes 393224 | tf_op jit(solution)/shard_map/ppermute | solution.py:1166
  106.3 18.9 %collective-permute-start.21 = (bf16[2,256,128]{2,1,0:T(8,128)(2,1)S(1)}, bf16[2,256,128]{2,1,0:T(8,128)(2,1)S(1)}, u32[]{:S(2)}, u32[]{:S(2)}) collective-permute-start(bf16[2,256,128]{2,1,0:T(8,128)(2,1)S(1)} %get-tuple-element.129), channel_id=1, source_target_pairs={{0,2},{1,3},{2,0},{3,1},{4,6},{5,7},{6,4},{7,5},{8,10},{9,11},{10,... | collective-permute-start | bytes 393224 | tf_op jit(solution)/shard_map/ppermute | solution.py:1166
  108.7 16.6 %collective-permute-start.22 = (bf16[2,256,128]{2,1,0:T(8,128)(2,1)S(1)}, bf16[2,256,128]{2,1,0:T(8,128)(2,1)S(1)}, u32[]{:S(2)}, u32[]{:S(2)}) collective-permute-start(bf16[2,256,128]{2,1,0:T(8,128)(2,1)S(1)} %get-tuple-element.130), channel_id=1, source_target_pairs={{0,3},{1,2},{2,1},{3,0},{4,7},{5,6},{6,5},{7,4},{8,11},{9,10},{10,... | collective-permute-start | bytes 393224 | tf_op jit(solution)/shard_map/ppermute | solution.py:1166
  109.8 17.3 %collective-permute-start.30 = (bf16[384,256]{1,0:T(8,128)(2,1)S(1)}, bf16[384,256]{1,0:T(8,128)(2,1)S(1)}, u32[]{:S(2)}, u32[]{:S(2)}) collective-permute-start(bf16[384,256]{1,0:T(8,128)(2,1)S(1)} %constant_dynamic-update-slice_fusion), channel_id=1, source_target_pairs={{0,4},{1,5},{2,6},{3,7},{4,0},{5,1},{6,2},{7,3},{8,12},{9,13},{10,... | collective-permute-start | bytes 589832 | tf_op jit(solution)/shard_map/ppermute | solution.py:1166
  119.7 4.8 %collective-permute-start.39 = (f32[8,256]{1,0:T(8,128)}, f32[8,256]{1,0:T(8,128)S(1)}, u32[]{:S(2)}, u32[]{:S(2)}) collective-permute-start(f32[8,256]{1,0:T(8,128)} %get-tuple-element.150), channel_id=1, source_target_pairs={{0,4},{1,5},{2,6},{3,7},{4,0},{5,1},{6,2},{7,3},{8,12},{9,13},{10,... | collective-permute-start | bytes 24584 | tf_op jit(solution)/shard_map/ppermute | solution.py:1166
  126.9 13.1 %collective-permute-start.29 = (bf16[2,256,256]{2,1,0:T(8,128)(2,1)S(1)}, bf16[2,256,256]{2,1,0:T(8,128)(2,1)S(1)}, u32[]{:S(2)}, u32[]{:S(2)}) collective-permute-start(bf16[2,256,256]{2,1,0:T(8,128)(2,1)S(1)} %pad_maximum_fusion.2), channel_id=1, source_target_pairs={{0,4},{1,5},{2,6},{3,7},{4,0},{5,1},{6,2},{7,3},{8,12},{9,13},{10,... | collective-permute-start | bytes 786440 | tf_op jit(solution)/shard_map/ppermute | solution.py:1166
  127.2 7.6 %collective-permute-start.43 = (bf16[224,256]{1,0:T(8,128)(2,1)S(1)}, bf16[224,256]{1,0:T(8,128)(2,1)S(1)}, u32[]{:S(2)}, u32[]{:S(2)}) collective-permute-start(bf16[224,256]{1,0:T(8,128)(2,1)S(1)} %get-tuple-element.183), channel_id=1, source_target_pairs={{0,2},{1,3},{2,0},{3,1},{4,6},{5,7},{6,4},{7,5},{8,10},{9,11},{10,... | collective-permute-start | bytes 344072 | tf_op jit(solution)/shard_map/ppermute | solution.py:1166
  128.6 16.6 %collective-permute-start.31 = (bf16[160,256]{1,0:T(8,128)(2,1)S(1)}, bf16[160,256]{1,0:T(8,128)(2,1)S(1)}, u32[]{:S(2)}, u32[]{:S(2)}) collective-permute-start(bf16[160,256]{1,0:T(8,128)(2,1)S(1)} %get-tuple-element.185), channel_id=1, source_target_pairs={{0,2},{1,3},{2,0},{3,1},{4,6},{5,7},{6,4},{7,5},{8,10},{9,11},{10,... | collective-permute-start | bytes 245768 | tf_op jit(solution)/shard_map/ppermute | solution.py:1166
  134.8 6.9 %collective-permute-start.45 = (bf16[2,224,256]{2,1,0:T(8,128)(2,1)S(1)}, bf16[2,224,256]{2,1,0:T(8,128)(2,1)S(1)}, u32[]{:S(2)}, u32[]{:S(2)}) collective-permute-start(bf16[2,224,256]{2,1,0:T(8,128)(2,1)S(1)} %pad_maximum_fusion.3.refs_0_), channel_id=1, source_target_pairs={{0,8},{8,0},{16,24},{24,16},{1,9},{9,1},{17,25},{25,17},{2,10},{10... | collective-permute-start | bytes 688136 | tf_op jit(solution)/shard_map/ppermute | solution.py:1166
  135.3 6.6 %collective-permute-start.47 = (bf16[2,224,256]{2,1,0:T(8,128)(2,1)S(1)}, bf16[2,224,256]{2,1,0:T(8,128)(2,1)S(1)}, u32[]{:S(2)}, u32[]{:S(2)}) collective-permute-start(bf16[2,224,256]{2,1,0:T(8,128)(2,1)S(1)} %pad_maximum_fusion.3.refs_0_), channel_id=1, source_target_pairs={{0,16},{8,24},{16,0},{24,8},{1,17},{9,25},{17,1},{25,9},{2,18},{10... | collective-permute-start | bytes 688136 | tf_op jit(solution)/shard_map/ppermute | solution.py:1166
  136.5 7.9 %collective-permute-start.49 = (bf16[2,224,256]{2,1,0:T(8,128)(2,1)S(1)}, bf16[2,224,256]{2,1,0:T(8,128)(2,1)S(1)}, u32[]{:S(2)}, u32[]{:S(2)}) collective-permute-start(bf16[2,224,256]{2,1,0:T(8,128)(2,1)S(1)} %pad_maximum_fusion.3.refs_0_), channel_id=1, source_target_pairs={{0,24},{8,16},{16,8},{24,0},{1,25},{9,17},{17,9},{25,1},{2,26},{10... | collective-permute-start | bytes 688136 | tf_op jit(solution)/shard_map/ppermute | solution.py:1166
  140.1 7.2 %collective-permute-start.44 = (bf16[2,224,256]{2,1,0:T(8,128)(2,1)S(1)}, bf16[2,224,256]{2,1,0:T(8,128)(2,1)S(1)}, u32[]{:S(2)}, u32[]{:S(2)}) collective-permute-start(bf16[2,224,256]{2,1,0:T(8,128)(2,1)S(1)} %pad_maximum_fusion.3.refs_0_), channel_id=1, source_target_pairs={{0,1},{1,0},{2,3},{3,2},{4,5},{5,4},{6,7},{7,6},{8,9},{9,8},{10,11... | collective-permute-start | bytes 688136 | tf_op jit(solution)/shard_map/ppermute | solution.py:1166
  141.7 6.5 %collective-permute-start.46 = (bf16[2,224,256]{2,1,0:T(8,128)(2,1)S(1)}, bf16[2,224,256]{2,1,0:T(8,128)(2,1)S(1)}, u32[]{:S(2)}, u32[]{:S(2)}) collective-permute-start(bf16[2,224,256]{2,1,0:T(8,128)(2,1)S(1)} %collective-permute-done.45.refs_2_), channel_id=1, source_target_pairs={{0,1},{1,0},{2,3},{3,2},{4,5},{5,4},{6,7},{7,6},{8,9},{9,8},{10,11... | collective-permute-start | bytes 688136 | tf_op jit(solution)/shard_map/ppermute | solution.py:1166
  141.9 6.7 %collective-permute-start.48 = (bf16[2,224,256]{2,1,0:T(8,128)(2,1)S(1)}, bf16[2,224,256]{2,1,0:T(8,128)(2,1)S(1)}, u32[]{:S(2)}, u32[]{:S(2)}) collective-permute-start(bf16[2,224,256]{2,1,0:T(8,128)(2,1)S(1)} %collective-permute-done.47.refs_4_), channel_id=1, source_target_pairs={{0,1},{1,0},{2,3},{3,2},{4,5},{5,4},{6,7},{7,6},{8,9},{9,8},{10,11... | collective-permute-start | bytes 688136 | tf_op jit(solution)/shard_map/ppermute | solution.py:1166
  144.4 5.1 %collective-permute-start.50 = (bf16[2,224,256]{2,1,0:T(8,128)(2,1)S(1)}, bf16[2,224,256]{2,1,0:T(8,128)(2,1)S(1)}, u32[]{:S(2)}, u32[]{:S(2)}) collective-permute-start(bf16[2,224,256]{2,1,0:T(8,128)(2,1)S(1)} %collective-permute-done.49.refs_6_), channel_id=1, source_target_pairs={{0,1},{1,0},{2,3},{3,2},{4,5},{5,4},{6,7},{7,6},{8,9},{9,8},{10,11... | collective-permute-start | bytes 688136 | tf_op jit(solution)/shard_map/ppermute | solution.py:1166
  145.3 8.6 %collective-permute-start.40 = (f32[8,256]{1,0:T(8,128)S(1)}, f32[8,256]{1,0:T(8,128)S(1)}, u32[]{:S(2)}, u32[]{:S(2)}) collective-permute-start(f32[8,256]{1,0:T(8,128)S(1)} %add.95.refs_8_), channel_id=1, source_target_pairs={{0,8},{8,0},{16,24},{24,16},{1,9},{9,1},{17,25},{25,17},{2,10},{10... | collective-permute-start | bytes 24584 | tf_op jit(solution)/shard_map/ppermute | solution.py:1166
  147.3 11.4 %collective-permute-start.41 = (f32[8,256]{1,0:T(8,128)S(1)}, f32[8,256]{1,0:T(8,128)S(1)}, u32[]{:S(2)}, u32[]{:S(2)}) collective-permute-start(f32[8,256]{1,0:T(8,128)S(1)} %add.95.refs_8_), channel_id=1, source_target_pairs={{0,16},{8,24},{16,0},{24,8},{1,17},{9,25},{17,1},{25,9},{2,18},{10... | collective-permute-start | bytes 24584 | tf_op jit(solution)/shard_map/ppermute | solution.py:1166
  148.2 7.1 %collective-permute-start.33 = (bf16[2,160,256]{2,1,0:T(8,128)(2,1)S(1)}, bf16[2,160,256]{2,1,0:T(8,128)(2,1)S(1)}, u32[]{:S(2)}, u32[]{:S(2)}) collective-permute-start(bf16[2,160,256]{2,1,0:T(8,128)(2,1)S(1)} %pad_maximum_fusion.4.refs_0_), channel_id=1, source_target_pairs={{0,8},{8,0},{16,24},{24,16},{1,9},{9,1},{17,25},{25,17},{2,10},{10... | collective-permute-start | bytes 491528 | tf_op jit(solution)/shard_map/ppermute | solution.py:1166
  148.7 9.4 %collective-permute-start.35 = (bf16[2,160,256]{2,1,0:T(8,128)(2,1)S(1)}, bf16[2,160,256]{2,1,0:T(8,128)(2,1)S(1)}, u32[]{:S(2)}, u32[]{:S(2)}) collective-permute-start(bf16[2,160,256]{2,1,0:T(8,128)(2,1)S(1)} %pad_maximum_fusion.4.refs_0_), channel_id=1, source_target_pairs={{0,16},{8,24},{16,0},{24,8},{1,17},{9,25},{17,1},{25,9},{2,18},{10... | collective-permute-start | bytes 491528 | tf_op jit(solution)/shard_map/ppermute | solution.py:1166
  149.5 8.5 %collective-permute-start.37 = (bf16[2,160,256]{2,1,0:T(8,128)(2,1)S(1)}, bf16[2,160,256]{2,1,0:T(8,128)(2,1)S(1)}, u32[]{:S(2)}, u32[]{:S(2)}) collective-permute-start(bf16[2,160,256]{2,1,0:T(8,128)(2,1)S(1)} %pad_maximum_fusion.4.refs_0_), channel_id=1, source_target_pairs={{0,24},{8,16},{16,8},{24,0},{1,25},{9,17},{17,9},{25,1},{2,26},{10... | collective-permute-start | bytes 491528 | tf_op jit(solution)/shard_map/ppermute | solution.py:1166
  153.8 9.5 %collective-permute-start.32 = (bf16[2,160,256]{2,1,0:T(8,128)(2,1)S(1)}, bf16[2,160,256]{2,1,0:T(8,128)(2,1)S(1)}, u32[]{:S(2)}, u32[]{:S(2)}) collective-permute-start(bf16[2,160,256]{2,1,0:T(8,128)(2,1)S(1)} %pad_maximum_fusion.4.refs_0_), channel_id=1, source_target_pairs={{0,1},{1,0},{2,3},{3,2},{4,5},{5,4},{6,7},{7,6},{8,9},{9,8},{10,11... | collective-permute-start | bytes 491528 | tf_op jit(solution)/shard_map/ppermute | solution.py:1166
  155.3 8.0 %collective-permute-start.34 = (bf16[2,160,256]{2,1,0:T(8,128)(2,1)S(1)}, bf16[2,160,256]{2,1,0:T(8,128)(2,1)S(1)}, u32[]{:S(2)}, u32[]{:S(2)}) collective-permute-start(bf16[2,160,256]{2,1,0:T(8,128)(2,1)S(1)} %collective-permute-done.33.refs_2_), channel_id=1, source_target_pairs={{0,1},{1,0},{2,3},{3,2},{4,5},{5,4},{6,7},{7,6},{8,9},{9,8},{10,11... | collective-permute-start | bytes 491528 | tf_op jit(solution)/shard_map/ppermute | solution.py:1166
  158.0 5.3 %collective-permute-start.36 = (bf16[2,160,256]{2,1,0:T(8,128)(2,1)S(1)}, bf16[2,160,256]{2,1,0:T(8,128)(2,1)S(1)}, u32[]{:S(2)}, u32[]{:S(2)}) collective-permute-start(bf16[2,160,256]{2,1,0:T(8,128)(2,1)S(1)} %collective-permute-done.35.refs_4_), channel_id=1, source_target_pairs={{0,1},{1,0},{2,3},{3,2},{4,5},{5,4},{6,7},{7,6},{8,9},{9,8},{10,11... | collective-permute-start | bytes 491528 | tf_op jit(solution)/shard_map/ppermute | solution.py:1166
  158.0 5.3 %collective-permute-start.38 = (bf16[2,160,256]{2,1,0:T(8,128)(2,1)S(1)}, bf16[2,160,256]{2,1,0:T(8,128)(2,1)S(1)}, u32[]{:S(2)}, u32[]{:S(2)}) collective-permute-start(bf16[2,160,256]{2,1,0:T(8,128)(2,1)S(1)} %collective-permute-done.37.refs_6_), channel_id=1, source_target_pairs={{0,1},{1,0},{2,3},{3,2},{4,5},{5,4},{6,7},{7,6},{8,9},{9,8},{10,11... | collective-permute-start | bytes 491528 | tf_op jit(solution)/shard_map/ppermute | solution.py:1166
  158.7 4.6 %collective-permute-start.42 = (f32[8,256]{1,0:T(8,128)S(1)}, f32[8,256]{1,0:T(8,128)S(1)}, u32[]{:S(2)}, u32[]{:S(2)}) collective-permute-start(f32[8,256]{1,0:T(8,128)S(1)} %add.95.refs_8_), channel_id=1, source_target_pairs={{0,24},{8,16},{16,8},{24,0},{1,25},{9,17},{17,9},{25,1},{2,26},{10... | collective-permute-start | bytes 24584 | tf_op jit(solution)/shard_map/ppermute | solution.py:1166
  (29 other events, 179.5 us)

commit v3 on v2

--- a/solution.py
+++ b/solution.py
@@ -472,7 +472,7 @@
         out[pl.ds(pl.multiple_of(base, step), step), :] = total
         return carry
 
-    lax.fori_loop(0, out.shape[0] // step, block, 0)
+    lax.fori_loop(0, out.shape[0] // step, block, 0, unroll=True)
 
 
 def kernel_quarter(shifted, own_t, out, cols):
@@ -697,14 +697,16 @@
         (act_far[0], acts.at[0]),
         (act_far[1], acts.at[1]),
     )
-    block_cells = sends[0].shape[1]
+    block_cells = sends[0].shape[0]
     step = 256
     arriving[0].wait()
     for k, send in enumerate(sends):
+        tiles = []
         for part in range(2):
             block = (head ^ k) + HEADS * (image ^ part)
             at = pl.ds(pl.multiple_of(block * block_cells, block_cells), block_cells)
-            send[part] = mixed[at, :]
+            tiles.append(mixed[at, half:lanes])
+        send[...] = jnp.concatenate(tiles, axis=1)
     finish_all(arriving[1:4])
 
     def gather(index, totals):
@@ -771,18 +773,20 @@
     finish_all(leaving)
 
 
-def residual_kernel(vec, qkv_t, *refs):
+def middle_kernel(vec, qkv_t, *refs):
     heads_far, sides_far = refs[0:8:2], refs[1:8:2]
-    grad_far, residual_far, stats_far, own_far, weight_far = refs[8:13]
-    shifted, grad_res_far, quarter_far, sums_far = refs[13:17]
+    grad_far, residual_far, stats_far, own_two_far, rows_far = refs[8:13]
+    weight_far, conv_far, own_one_far, out_sums_far = refs[13:17]
+    shifted_one, grad_res_far, payload_far = refs[17], refs[18], refs[19:23]
     (
-        heads, sides, grad_proj, residual, stats, own_two, grad_res, quarter, sums, grad_act,
-        in_sems, out_sems,
-    ) = refs[17:]
+        heads, sides, grad_proj, residual, stats, own_two, grad_res, early, grad_act, shifted,
+        weight, conv_one, own_one, out_sums, late, in_sems, out_sems,
+    ) = refs[23:]
     cells, channels = grad_proj.shape
     cols = (shifted.shape[0] - cells) // 2
     rows = cells // cols
-    _, head, _, height = own_place(vec)
+    _, head, image, height = own_place(vec)
+    column = lax.axis_index("img")
     width = channels // GROUPS
     count = (height * (cols * width)).astype(jnp.float32)
     half = qkv_t.shape[1]
@@ -794,8 +798,12 @@
         (stats_far, stats),
         (residual_far, residual),
         (grad_far, grad_proj),
-        (own_far, own_two),
-        (weight_far, quarter.at[pl.ds(9 * half, 5 * half), :]),
+        (own_two_far, own_two),
+        (rows_far, early.at[pl.ds(9 * half, 5 * half), :]),
+        (weight_far, weight),
+        (conv_far, conv_one),
+        (own_one_far, own_one),
+        (out_sums_far, out_sums),
     )
     zeros = jnp.zeros((half, channels), jnp.bfloat16)
     halfway = cells // 2
@@ -853,41 +861,22 @@
         return total + fold(grad)
 
     total = total_of(lax.fori_loop(0, rows, finish, zero, unroll=2))
-    sums[...] = jnp.concatenate([cross, plain, total, jnp.zeros((5, channels), jnp.float32)], axis=0)
-    leaving = started(out_sems, (grad_res, grad_res_far), (sums, sums_far))
-    finish_all(arriving[11:])
-    kernel_quarter(shifted, own_two, quarter, cols)
-    leaving += started(out_sems.at[2:3], (quarter, quarter_far))
-    finish_all(leaving)
-
-
-def second_kernel(vec, shifted, weight_far, conv_far, stats_far, own_far, *refs):
-    sums_three_far, out_sums_far = refs[0:2]
-    shifted_one, quarter_far = refs[2:4]
-    (
-        weight, conv_one, stats, own_one, sums_three, out_sums, quarter, grad_act, in_sems, out_sems,
-    ) = refs[4:]
-    cells, channels = conv_one.shape
-    cols = (shifted.shape[0] - cells) // 2
-    rows = cells // cols
-    _, _, image, height = own_place(vec)
-    width = channels // GROUPS
-    count = (height * (cols * width)).astype(jnp.float32)
-    arriving = started(
-        in_sems,
-        (weight_far, weight),
-        (stats_far, stats),
-        (conv_far, conv_one),
-        (own_far, own_one),
-        (sums_three_far, sums_three),
-        (out_sums_far, out_sums),
-    )
+    three_lines = [cross, plain, total]
+    leaving = started(out_sems, (grad_res, grad_res_far))
+    finish_all(arriving[11:13])
+    kernel_quarter(shifted, own_two, early, cols)
+    before = early.shape[0] // 4
+    chunks = [pl.ds(pl.multiple_of((column ^ k) * before, 16), before) for k in range(4)]
+    leaving += started(
+        out_sems.at[1:5],
+        *[(early.at[at, :], far.at[pl.ds(0, before), :]) for at, far in zip(chunks, payload_far)],
+    )
+
     gain, bias, scale, shift = (vec[k : k + 1, :] for k in range(3, 7))
-    zero = jnp.zeros((8, channels), jnp.float32)
     clear_rims(shifted_one, cols)
-    arriving[0].wait()
+    arriving[13].wait()
     conv_shifted(shifted, weight, grad_act, 0.0, cols)
-    finish_all(arriving[1:3])
+    arriving[14].wait()
     mean, inverse = stats[2:3, :], stats[3:4, :]
     line = half_line(mean, inverse, gain, bias, scale, shift)
     begin = mean * inverse
@@ -919,20 +908,29 @@
         return total + fold(grad)
 
     total = total_of(lax.fori_loop(0, rows, finish, zero, unroll=2))
-    finish_all(arriving[3:])
-    kernel_quarter(shifted_one, own_one, quarter, cols)
+    finish_all(arriving[15:])
+    kernel_quarter(shifted_one, own_one, late, cols)
     lines = [
-        sums_three[0:3, :], out_sums[0:1, :], cross * scale, plain * scale, total,
+        *three_lines, out_sums[0:1, :], cross * scale, plain * scale, total,
         jnp.zeros((9, channels), jnp.float32),
     ]
-    mine = 2 * (lax.axis_index("img") * 2 + image)
+    mine = 2 * (column * 2 + image)
     place = lax.broadcasted_iota(jnp.int32, (16, channels), 0)
     both = jnp.where(place == mine, gain * cross + bias * plain, 0.0)
     lines.append(jnp.where(place == mine + 1, plain, both))
     base = 3 * own_one.shape[1]
-    lines.append(jnp.zeros((quarter.shape[0] - base - 32, channels), jnp.float32))
-    quarter[base:, :] = jnp.concatenate(lines, axis=0).astype(jnp.bfloat16)
-    finish_all(started(out_sems, (quarter, quarter_far)))
+    lines.append(jnp.zeros((late.shape[0] - base - 32, channels), jnp.float32))
+    late[base:, :] = jnp.concatenate(lines, axis=0).astype(jnp.bfloat16)
+    after = late.shape[0] // 4
+    chunks = [pl.ds(pl.multiple_of((column ^ k) * after, 16), after) for k in range(4)]
+    leaving += started(
+        out_sems.at[5:9],
+        *[
+            (late.at[at, :], far.at[pl.ds(before, after), :])
+            for at, far in zip(chunks, payload_far)
+        ],
+    )
+    finish_all(leaving)
 
 
 def first_kernel(vec, shifted, weight_far, pix_far, grad_far, stats_far, *refs):
@@ -1012,8 +1010,9 @@
     for part, out in enumerate((out_own, out_away)):
         total = residual[part] + vec[10:11, :]
         for step in range(4):
-            tile = heads[step][part]
-            total = total + dot(tile[:, tile.shape[1] // 2 :], w_out[head ^ step])
+            width = w_out.shape[1]
+            tile = heads[step][:, part * width : (part + 1) * width]
+            total = total + dot(tile, w_out[head ^ step])
         cell = bases[part] + lax.broadcasted_iota(jnp.int32, (block_cells, channels), 0)
         out[...] = jnp.where(cell < height * cols, total, 0.0).astype(jnp.bfloat16)
 
@@ -1082,14 +1081,19 @@
     finish_all(leaving)
 
 
-def gathered_rows(parts, gathered):
+def gathered_rows(parts, early, late):
     spot = lax.axis_index("row")
     head, column = spot % HEADS, lax.axis_index("img")
-    lines = parts[0].shape[1]
+    early_lines, late_lines = early.shape[1] // 4, late.shape[1] // 4
+    lines = early_lines + late_lines
     for index, part in enumerate(parts):
-        at = pl.ds(pl.multiple_of((column ^ (index // 2)) * lines, 16), lines)
+        away = column ^ (index // 2)
+        early_at = pl.ds(pl.multiple_of(away * early_lines, 16), early_lines)
+        late_at = pl.ds(pl.multiple_of(away * late_lines, 16), late_lines)
         for pair in range(2):
-            gathered[head ^ (index % 2 + 2 * pair), at, :] = part[pair]
+            quarter, base = head ^ (index % 2 + 2 * pair), pair * lines
+            early[quarter, early_at, :] = part[base : base + early_lines]
+            late[quarter, late_at, :] = part[base + early_lines : base + lines]
 
 
 def place_taps(gathered, out):
@@ -1102,63 +1106,70 @@
             ].astype(jnp.float32)
 
 
-def late_kernel(*refs):
-    parts, ones, time_all, (out, time_out, time_bias), rows = (
-        refs[:8], refs[8:12], refs[12], refs[13:16], refs[16:25],
-    )
-    gathered, norm_one = refs[-2:]
-    gathered_rows(parts, gathered)
-    place_taps(gathered, out)
-    rest = gathered[0, 9 * (out.shape[3] // HEADS) :, :]
-    column = lax.axis_index("img")
-    for step, part in enumerate(ones):
-        norm_one[column ^ step] = part[...]
-    total = norm_one[0] + norm_one[1] + norm_one[2] + norm_one[3]
-    lines = rest[0:16, :].astype(jnp.float32)
-    whole = jnp.concatenate([total[0:2], lines[0:7]], axis=0)
-    for k, row in enumerate(rows):
-        row[...] = whole[k : k + 1].reshape(row.shape)
-    shifts = rest[16:32, :].astype(jnp.float32)
-    images = time_all.shape[0]
-    channels = shifts.shape[1]
-    pair = jnp.concatenate([shifts[2 * k : 2 * k + 1, :] for k in range(images)], axis=0)
-    other = jnp.concatenate([shifts[2 * k + 1 : 2 * k + 2, :] for k in range(images)], axis=0)
-    time_bias[...] = jnp.concatenate([total_of(pair), total_of(other)], axis=1).reshape(
-        time_bias.shape
-    )
-    for k, lines in enumerate((pair, other)):
-        time_out[:, k * channels : (k + 1) * channels] = lax.dot_general(
-            time_all[...], lines, (((0,), (0,)), ((), ())), precision=PRECISE,
-            preferred_element_type=jnp.float32,
-        )
-
-
-def early_kernel(*refs):
-    parts, (out, qkv_out, out_out, bias_out, step_out) = refs[:8], refs[8:13]
-    (gathered,) = refs[13:]
-    gathered_rows(parts, gathered)
-    place_taps(gathered, out)
+def final_kernel(*refs):
+    parts, frequency = refs[:8], refs[8]
+    one_far, two_far, qkv_far, out_far, time_far = refs[9:14]
+    bias_out, time_bias, rows = refs[14], refs[15], refs[16:25]
+    early, late, norm_one, one, two, qkv_out, out_out, time_out, out_sems = refs[25:]
+    gathered_rows(parts, early, late)
+    place_taps(late, one)
+    leaving = started(out_sems, (one, one_far))
+    place_taps(early, two)
+    leaving += started(out_sems.at[1:2], (two, two_far))
     half = out_out.shape[0] // HEADS
     nine = 9 * half
     sums = []
     for quarter in range(HEADS):
-        out_out[quarter * half : (quarter + 1) * half, :] = gathered[
+        out_out[quarter * half : (quarter + 1) * half, :] = early[
             quarter, nine + 3 * half : nine + 4 * half, :
         ].astype(jnp.float32)
-        sums.append(gathered[quarter, nine + 4 * half : nine + 4 * half + 16].astype(jnp.float32))
-    parts = [part[0:1, :half] for part in sums] + [part[0:1, 3 * half :] for part in sums]
-    bias_out[...] = jnp.concatenate(parts, axis=1).reshape(bias_out.shape)
-    step_out[...] = sums[0][0:8]
+        sums.append(early[quarter, nine + 4 * half : nine + 4 * half + 16].astype(jnp.float32))
+    pieces = [part[0:1, :half] for part in sums] + [part[0:1, 3 * half :] for part in sums]
+    bias_out[...] = jnp.concatenate(pieces, axis=1).reshape(bias_out.shape)
     for part in range(3):
         block = jnp.concatenate(
             [
-                gathered[quarter, nine + part * half : nine + (part + 1) * half, :]
+                early[quarter, nine + part * half : nine + (part + 1) * half, :]
                 for quarter in range(HEADS)
             ],
             axis=0,
         )
         width = HEADS * half
         qkv_out[:, part * width : (part + 1) * width] = jnp.transpose(block.astype(jnp.float32))
+    leaving += started(out_sems.at[2:4], (qkv_out, qkv_far), (out_out, out_far))
+    column = lax.axis_index("img")
+    lines = (early.shape[1] + late.shape[1]) // 2
+    for step in range(4):
+        norm_one[column ^ step] = parts[2 * step][lines : lines + 16, :].astype(jnp.float32)
+    total = norm_one[0] + norm_one[1] + norm_one[2] + norm_one[3]
+    rest = late[0, nine:, :]
+    whole = jnp.concatenate([total[0:2], rest[0:16, :].astype(jnp.float32)[0:7]], axis=0)
+    for k, row in enumerate(rows):
+        row[...] = whole[k : k + 1].reshape(row.shape)
+    shifts = rest[16:32, :].astype(jnp.float32)
+    pair = jnp.concatenate([shifts[k : k + 1, :] for k in range(0, 16, 2)], axis=0)
+    other = jnp.concatenate([shifts[k : k + 1, :] for k in range(1, 16, 2)], axis=0)
+    both = jnp.concatenate([pair, other], axis=1)
+    time_bias[...] = total_of(both).reshape(time_bias.shape)
+    steps = sums[0][1:2, :] * 32.0 + sums[0][2:3, :]
+    image = lax.broadcasted_iota(jnp.int32, (8, steps.shape[1]), 0)
+    lane = lax.broadcasted_iota(jnp.int32, (8, steps.shape[1]), 1)
+    now = jnp.sum(jnp.where(image == lane, steps, 0.0), axis=1, keepdims=True)
+    angles = now * frequency[...]
+    left = jnp.concatenate([jnp.cos(angles), jnp.sin(angles)], axis=1)
+    left = left / (1.0 + jnp.exp(-left))
+    terms = []
+    for _ in range(3):
+        terms.append(left.astype(jnp.bfloat16).astype(jnp.float32))
+        left = left - terms[-1]
+    terms = jnp.concatenate(terms + [jnp.zeros_like(left)], axis=0)
+    both = jnp.concatenate([both] * 3 + [jnp.zeros_like(both)], axis=0).astype(jnp.bfloat16)
+    time_out[...] = lax.dot_general(
+        terms.astype(jnp.bfloat16), both, (((0,), (0,)), ((), ())),
+        preferred_element_type=jnp.float32,
+    )
+    leaving += started(out_sems.at[4:5], (time_out, time_far))
+    finish_all(leaving)
 
 
 def swap(value, axis, step):
@@ -1170,25 +1181,23 @@
     return lax.dynamic_index_in_dim(stacked, index, 0, keepdims=False)
 
 
-def reduce_columns(value, column):
-    lines = value.shape[0] // 4
-    parts = value.reshape(4, lines, value.shape[1])
-    got = [swap(pick(parts, column ^ step), "img", step) for step in (1, 2, 3)]
-    total = pick(parts, column).astype(jnp.float32)
-    for part in got:
+def add_up(*parts):
+    total = parts[0].astype(jnp.float32)
+    for part in parts[1:]:
         total = total + part.astype(jnp.float32)
     return total.astype(jnp.bfloat16)
 
 
-def both_images(total):
-    away = swap(total, "row", 4)
-    return (total.astype(jnp.float32) + away.astype(jnp.float32)).astype(jnp.bfloat16)
-
-
-def gather_quarters(own):
-    pair = jnp.stack([own, swap(own, "row", 2)])
-    near = [pair] + [swap(pair, "img", step) for step in (1, 2, 3)]
-    return [part for mine in near for part in (mine, swap(mine, "row", 1))]
+def from_columns(pair):
+    return [pair] + [swap(pair, "img", step) for step in (1, 2, 3)]
+
+
+def with_mates(columns):
+    return [part for mine in columns for part in (mine, swap(mine, "row", 1))]
+
+
+def gather_columns(pair):
+    return with_mates(from_columns(pair))
 
 
 def call(kernel, near_outs, far_outs, scratch, limit, work, scalars, near, far, last_outs=()):
@@ -1313,7 +1322,7 @@
             (kernel_shape, low), (tall, low), (tall, low), sems(10), sems(6),
         ],
         28,
-        cost * 16,
+        cost * 25,
         [],
         [vec],
         [*field, w_one, w_two],
@@ -1330,7 +1339,7 @@
             (head_shape, low), ((1, cells), full), sems(8), sems(5),
         ],
         36,
-        cost * 20,
+        cost * 34,
         [],
         [vec, act_three, w_heads, w_out, biases],
         grads,
@@ -1339,7 +1348,7 @@
     key_near, query_near = swap(value_key, "row", 2), swap(query_part, "row", 2)
     key_mate, query_mate = swap(value_key, "row", 1), swap(query_part, "row", 1)
     own_shape = (3, 3 * half, cells)
-    send_shape = ((2, block_cells, lanes), low)
+    send_shape = ((block_cells, lanes), low)
     own_one, own_two, weight_rows, *sends = call(
         aside_kernel,
         [],
@@ -1350,7 +1359,7 @@
             sems(6), sems(3),
         ],
         28,
-        cost * 6,
+        cost * 27,
         [],
         [vec],
         [act_one, act_two, mixed, value_key, act_three, grad_proj],
@@ -1361,45 +1370,33 @@
         value_key, query_part, key_mate, query_mate,
         key_near, query_near, swap(key_near, "row", 1), swap(query_near, "row", 1),
     ]
-    shifted_two, grad_res, quarter_two, sums_three = call(
-        residual_kernel,
+    early_lines, late_lines = 14 * half // 4, 10 * half // 4
+    lines = early_lines + late_lines
+    shifted_one, grad_res, *payload = call(
+        middle_kernel,
         [(tall, low)],
-        [(wide, full), ((14 * half, channels), low), rows_eight],
+        [(wide, full)] + [((lines, channels), low)] * 4,
         [
             ((HEADS,) + head_shape, low), ((HEADS,) + query_shape, low),
             (wide, low), (wide, full), rows_eight, (own_shape, low), (wide, full),
-            ((14 * half, channels), low), rows_eight, (wide, full), sems(13), sems(3),
+            ((14 * half, channels), low), (wide, full), (tall, low), (kernel_shape, low),
+            (wide, full), (own_shape, low), rows_eight, ((10 * half, channels), low),
+            sems(17), sems(9),
         ],
-        24,
-        cost * 6,
+        40,
+        cost * 26,
         [],
         [vec, qkv_t],
-        [*packed_all, grad_proj, residual, stats, own_two, weight_rows],
-    )
-    early_total = reduce_columns(quarter_two, column)
-    *sends, shifted_two = lax.optimization_barrier((*sends, shifted_two))
+        [
+            *packed_all, grad_proj, residual, stats, own_two, weight_rows, w_two_back, conv_one,
+            own_one, out_sums,
+        ],
+    )
+    *sends, shifted_one = lax.optimization_barrier((*sends, shifted_one))
+    total = add_up(payload[0], *[swap(payload[step], "img", step) for step in (1, 2, 3)])
     heads_got = [sends[0]] + [swap(sends[step], "row", step) for step in (1, 2, 3)]
-    shifted_one, quarter_one = call(
-        second_kernel,
-        [(tall, low)],
-        [((10 * half, channels), low)],
-        [
-            (kernel_shape, low), (wide, full), rows_eight, (own_shape, low), rows_eight, rows_eight,
-            ((10 * half, channels), low), (wide, full), sems(6), sems(1),
-        ],
-        20,
-        cost * 7,
-        [],
-        [vec, shifted_two],
-        [w_two_back, conv_one, stats, own_one, sums_three, out_sums],
-    )
-    late_total = reduce_columns(quarter_one, column)
-    shifted_one, early_total, late_total = lax.optimization_barrier(
-        (shifted_one, early_total, late_total)
-    )
-    early_lines = early_total.shape[0]
-    both = both_images(jnp.concatenate([early_total, late_total], axis=0))
-    early_chunk, late_chunk = both[:early_lines], both[early_lines:]
+    shifted_one, total, *heads_got = lax.optimization_barrier((shifted_one, total, *heads_got))
+    both = add_up(total, swap(total, "row", 4))
     grad_own, grad_away, sums_one = call(
         first_kernel,
         [],
@@ -1409,7 +1406,7 @@
             ((2, block_cells, channels), low), rows_eight, (wide, full), sems(4), sems(3),
         ],
         20,
-        cost * 5,
+        cost * 12,
         [],
         [vec, shifted_one],
         [w_one_back, pix, grad_res, stats],
@@ -1425,48 +1422,39 @@
         [vec, out_weight.reshape(HEADS, half, channels), *heads_got],
         [residual],
     )
-    early_parts = gather_quarters(early_chunk)
-    late_parts = gather_quarters(late_chunk)
     out_pair = jnp.stack([block_own, grad_own])
     away_pair = swap(jnp.stack([block_away, grad_away]), "row", 4)
     first_pair = jnp.where(image == 0, out_pair, away_pair)
     second_pair = jnp.where(image == 0, away_pair, out_pair)
     finished = jnp.stack([first_pair, second_pair], axis=1).reshape((2,) + pixels.shape)
-    norm_one = sums_one + swap(sums_one, "row", 4)
-    norm_parts = [norm_one] + [swap(norm_one, "img", step) for step in (1, 2, 3)]
-
-    nine = 9 * half
-    conv2_weight_grad, qkv_weight_grad, out_weight_grad, qv_bias_grad, steps = call(
-        early_kernel,
+    norm_one = jnp.concatenate([sums_one, jnp.zeros_like(sums_one)], axis=0).astype(low)
+    norm_one = add_up(norm_one, swap(norm_one, "row", 4))
+    other = swap(both, "row", 2)
+    pair = jnp.concatenate([both, other, norm_one], axis=0)
+    parts = gather_columns(pair)
+    line = ((channels,), full)
+    kernel_out = ((3, 3, channels, channels), full)
+    time_out = ((time_weight.shape[0], 2 * channels), full)
+    qkv_out, out_out = ((channels, 3 * channels), full), ((channels, channels), full)
+    half_time = time_weight.shape[0] // 2
+    frequency = jnp.exp(-math.log(10000.0) * jnp.arange(half_time, dtype=full) / half_time)
+    (
+        conv1_weight_grad, conv2_weight_grad, qkv_weight_grad, out_weight_grad, time_weight_grad,
+        qv_bias_grad, time_bias_grad, *lines,
+    ) = call(
+        final_kernel,
+        [],
+        [kernel_out, kernel_out, qkv_out, out_out, time_out],
         [
-            ((3, 3, channels, channels), full), ((channels, 3 * channels), full),
-            ((channels, channels), full), ((2 * channels,), full), rows_eight,
+            ((HEADS, 14 * half, channels), low), ((HEADS, 10 * half, channels), low),
+            ((4, 16, channels), full), kernel_out, kernel_out, qkv_out, out_out, time_out, sems(5),
         ],
-        [],
-        [((HEADS, nine + 5 * half, channels), low)],
-        12,
+        28,
         cost,
         [],
-        early_parts,
+        [*parts, frequency[None, :]],
         [],
-    )
-    all_images = images * lax.axis_size("img")
-    steps_all = steps[1, :all_images] * 32.0 + steps[2, :all_images]
-    time_all = jax.nn.silu(embed_steps(steps_all, time_weight.shape[0]))
-    line = ((channels,), full)
-    conv1_weight_grad, time_weight_grad, time_bias_grad, *lines = call(
-        late_kernel,
-        [
-            ((3, 3, channels, channels), full), ((time_weight.shape[0], 2 * channels), full),
-            ((2 * channels,), full), line, line, line, line, line, line, line, line, line,
-        ],
-        [],
-        [((HEADS, 10 * half, channels), low), ((4, 8, channels), full)],
-        12,
-        cost,
-        [],
-        [*late_parts, *norm_parts, time_all],
-        [],
+        [((2 * channels,), full)] * 2 + [line] * 9,
     )
     norm1_gain_grad, norm1_bias_grad, norm3_gain_grad, norm3_bias_grad, conv2_bias_grad = lines[:5]
     out_bias_grad, norm2_gain_grad, norm2_bias_grad, conv1_bias_grad = lines[5:]

time: 168 us -> 156 us (0.929)
  starting transfers between devices: 41.8 us -> 28.5 us
  Pallas kernels: 80.1 us -> 76 us
  waiting for transfers between devices: 35.3 us -> 39.3 us
    ppermute x51 -> x37, starting transfers between devices: 41.8 us -> 28.5 us  [swap(): return lax.ppermute(value, axis, [(k, k ^ step) for k in range(count)])]
    pallas_call x10 -> x8, Pallas kernels: 80.1 us -> 76 us  [call(): pl.pallas_call(kernel, out_shape=[jax.ShapeDtypeStruct(*kind) for kind in...]
    ppermute x51 -> x37, waiting for transfers between devices: 35.3 us -> 39.3 us  [swap(): return lax.ppermute(value, axis, [(k, k ^ step) for k in range(count)])]
  transfers between devices with their start and end apart: 51 -> 37, of which waited for: 19 -> 15; matrix products, arithmetic and copies ran while one was open for 3% -> 4% of each run, Pallas kernels for 25% -> 25%
where the time goes in v3:
time: 156 us
  Pallas kernels  76 us (49%)
  waiting for transfers between devices  39.3 us (25%)
  starting transfers between devices  28.5 us (18%)
  other arithmetic  6.01 us (4%)
  local copies, waits for them, and re-layouts  3.99 us (3%)
    pallas_call x8, Pallas kernels, call(): pl.pallas_call(kernel, out_shape=[jax.ShapeDtypeStruct(*kind) for kind in...  76 us
    ppermute x37, waiting for transfers between devices, swap(): return lax.ppermute(value, axis, [(k, k ^ step) for k in range(count)])  39.3 us
    ppermute x37, starting transfers between devices, swap(): return lax.ppermute(value, axis, [(k, k ^ step) for k in range(count)])  28.5 us
  transfers between devices with their start and end apart: 37, of which 15 were waited for; matrix products, arithmetic and copies ran while one was open for 4% of the time, Pallas kernels for 25%

profile of v3, /device:TPU:0, one launch (start us, length us, event | category | flops | bytes accessed | tf_op | source)
XLA Modules:
  0.0 155.6 jit_solution(15297960215435095336)
XLA Ops:
  0.7 1.1 dynamic-slice_bitcast_fusion
  1.8 0.5 collective-permute-start
  2.3 2.6 %collective-permute-start.1 = (bf16[256,256]{1,0:T(8,128)(2,1)S(1)}, bf16[256,256]{1,0:T(8,128)(2,1)S(1)}, u32[]{:S(2)}, u32[]{:S(2)}) collective-permute-start(bf16[256,256]{1,0:T(8,128)(2,1)S(1)} %get-tuple-element.177.refs_0_), channel_id=1, source_target_pairs={{0,2},{1,3},{2,0},{3,1},{4,6},{5,7},{6,4},{7,5},{8,10},{9,11},{10,... | collective-permute-start | bytes 393224 | tf_op jit(solution)/shard_map/ppermute | solution.py:1177
  5.0 2.6 %collective-permute-start.2 = (bf16[256,256]{1,0:T(8,128)(2,1)S(1)}, bf16[256,256]{1,0:T(8,128)(2,1)S(1)}, u32[]{:S(2)}, u32[]{:S(2)}) collective-permute-start(bf16[256,256]{1,0:T(8,128)(2,1)S(1)} %get-tuple-element.176), channel_id=1, source_target_pairs={{0,4},{1,5},{2,6},{3,7},{4,0},{5,1},{6,2},{7,3},{8,12},{9,13},{10,... | collective-permute-start | bytes 393224 | tf_op jit(solution)/shard_map/ppermute | solution.py:1177
  7.6 0.7 convert_element_type.41
  8.2 0.7 convert_element_type.42
  9.1 0.5 convolution_add_fusion.refs_0_
  9.6 4.8 %shard_map.331 = (f32[16,256]{1,0:T(8,128)S(1)}, bf16[256,384]{1,0:T(8,128)(2,1)S(1)}, bf16[256,128]{1,0:T(8,128)(2,1)S(1)}, f32[8,384]{1,0:T(8,128)S(1)}, bf16[...) custom-call(f32[2,512]{1,0:T(2,128)S(1)} %convolution_add_fusion.refs_0_, ...), custom_call_target="tpu_custom_call" | custom-call | flops 256 | bytes 2893328 | tf_op jit(solution)/shard_map/pallas_call | solution.py:1208
  14.4 3.4 %collective-permute-done.2.refs_4_ = bf16[256,256]{1,0:T(8,128)(2,1)S(1)} collective-permute-done((bf16[256,256]{1,0:T(8,128)(2,1)S(1)}, bf16[256,256]{1,0:T(8,128)(2,1)S(1)}, u32[]{:S(2)}, u32[]{:S(2)}) %collective-permute-start.2) | collective-permute-done | bytes 131104 | tf_op jit(solution)/shard_map/ppermute | solution.py:1177
  19.0 2.6 %collective-permute-start.8 = (bf16[256,256]{1,0:T(8,128)(2,1)S(1)}, bf16[256,256]{1,0:T(8,128)(2,1)S(1)}, u32[]{:S(2)}, u32[]{:S(2)}) collective-permute-start(bf16[256,256]{1,0:T(8,128)(2,1)S(1)} %get-tuple-element.107.refs_0_), channel_id=1, source_target_pairs={{0,2},{1,3},{2,0},{3,1},{4,6},{5,7},{6,4},{7,5},{8,10},{9,11},{10,... | collective-permute-start | bytes 393224 | tf_op jit(solution)/shard_map/ppermute | solution.py:1177
  21.6 1.3 collective-permute-start.9
  22.9 1.4 collective-permute-start.10
  24.3 0.6 copy-done.25
  24.9 11.9 %shard_map.332 = (bf16[2048,256]{1,0:T(8,128)(2,1)S(1)}, bf16[2048,256]{1,0:T(8,128)(2,1)}, f32[2048,256]{1,0:T(8,128)}, f32[2048,256]{1,0:T(8,128)}, bf16[2048,...) custom-call(f32[16,256]{1,0:T(8,128)S(1)} %get-tuple-element.95.vec, bf16[256,256]{1,0:T(8,128)(2,1)} %copy-done.6, ...), custom_call_target="tpu_custom_call" | custom-call | flops 15099494400 | bytes 3424256 | tf_op jit(solution)/shard_map/pallas_call | solution.py:1208
  37.6 0.8 collective-permute-done.11.refs_3_
  39.5 17.9 %shard_map.333 = (bf16[2048,128]{1,0:T(8,128)(2,1)}, bf16[1024,128]{1,0:T(8,128)(2,1)}, bf16[2048,256]{1,0:T(8,128)(2,1)}, bf16[2048,128]{1,0:T(8,128)(2,1)}, f32[8,256]{1,0:T(8,128)}) custom-call(f32[16,256]{1,0:T(8,128)S(1)} %get-tuple-element.95.vec, bf16[2048,256]{1,0:T(8,128)(2,1)S(1)} %get-tuple-element.103.act_three.refs_4_, ...), custom_call_target="tpu_custom_call" | custom-call | flops 20535312384 | bytes 2387968 | tf_op jit(solution)/shard_map/pallas_call | solution.py:1208
  57.7 0.8 collective-permute-start.16
  58.5 1.2 collective-permute-start.17
  59.8 13.9 %shard_map.334 = (bf16[3,192,2048]{2,1,0:T(8,128)(2,1)}, bf16[3,192,2048]{2,1,0:T(8,128)(2,1)}, bf16[320,256]{1,0:T(8,128)(2,1)}, bf16[256,128]{1,0:T(8,128)(2,1...) custom-call(f32[16,256]{1,0:T(8,128)S(1)} %get-tuple-element.95.vec, ...), custom_call_target="tpu_custom_call" | custom-call | flops 16307453952 | bytes 5259264 | tf_op jit(solution)/shard_map/pallas_call | solution.py:1208
  73.7 4.1 %collective-permute-done.17.refs_5_ = bf16[1024,128]{1,0:T(8,128)(2,1)S(1)} collective-permute-done((bf16[1024,128]{1,0:T(8,128)(2,1)}, bf16[1024,128]{1,0:T(8,128)(2,1)S(1)}, u32[]{:S(2)}, u32[]{:S(2)}) %collective-permute-start.17) | collective-permute-done | bytes 262176 | tf_op jit(solution)/shard_map/ppermute | solution.py:1177
  78.4 1.7 %collective-permute-done.15.refs_3_ = bf16[1024,128]{1,0:T(8,128)(2,1)S(1)} collective-permute-done((bf16[1024,128]{1,0:T(8,128)(2,1)S(1)}, bf16[1024,128]{1,0:T(8,128)(2,1)S(1)}, u32[]{:S(2)}, u32[]{:S(2)}) %collective-permute-start.15) | collective-permute-done | bytes 262176 | tf_op jit(solution)/shard_map/ppermute | solution.py:1177
  81.3 13.6 %shard_map.335 = (bf16[2176,768]{1,0:T(8,128)(2,1)S(1)}, f32[2048,256]{1,0:T(8,128)}, bf16[384,256]{1,0:T(8,128)(2,1)}, bf16[384,256]{1,0:T(8,128)(2,1)}, bf16[3...) custom-call(f32[16,256]{1,0:T(8,128)S(1)} %get-tuple-element.95.vec, bf16[12,64,256]{2,1,0:T(8,128)(2,1)S(1)} %get-tuple-element.119.qkv_t, ...), custom_call_target="tpu_custom_call" | custom-call | flops 15703474176 | bytes 14876672 | tf_op jit(solution)/shard_map/pallas_call | solution.py:1208
  95.0 2.5 %collective-permute-start.22 = (bf16[384,256]{1,0:T(8,128)(2,1)}, bf16[384,256]{1,0:T(8,128)(2,1)S(1)}, u32[]{:S(2)}, u32[]{:S(2)}) collective-permute-start(bf16[384,256]{1,0:T(8,128)(2,1)} %get-tuple-element.137), channel_id=1, source_target_pairs={{0,24},{8,16},{16,8},{24,0},{1,25},{9,17},{17,9},{25,1},{2,26},{10... | collective-permute-start | bytes 589832 | tf_op jit(solution)/shard_map/ppermute | solution.py:1177
  97.5 0.5 collective-permute-start.21
  98.0 0.5 collective-permute-start.20
  98.5 0.8 collective-permute-start.24
  99.4 4.6 %collective-permute-done.22 = bf16[384,256]{1,0:T(8,128)(2,1)S(1)} collective-permute-done((bf16[384,256]{1,0:T(8,128)(2,1)}, bf16[384,256]{1,0:T(8,128)(2,1)S(1)}, u32[]{:S(2)}, u32[]{:S(2)}) %collective-permute-start.22) | collective-permute-done | bytes 196640 | tf_op jit(solution)/shard_map/ppermute | solution.py:1177
  104.0 3.4 %collective-permute-done.21 = bf16[384,256]{1,0:T(8,128)(2,1)S(1)} collective-permute-done((bf16[384,256]{1,0:T(8,128)(2,1)}, bf16[384,256]{1,0:T(8,128)(2,1)S(1)}, u32[]{:S(2)}, u32[]{:S(2)}) %collective-permute-start.21) | collective-permute-done | bytes 196640 | tf_op jit(solution)/shard_map/ppermute | solution.py:1177
  107.4 1.0 add_convert_fusion.1
  108.5 1.9 %collective-permute-start.27 = (bf16[384,256]{1,0:T(8,128)(2,1)S(1)}, bf16[384,256]{1,0:T(8,128)(2,1)S(1)}, u32[]{:S(2)}, u32[]{:S(2)}) collective-permute-start(bf16[384,256]{1,0:T(8,128)(2,1)S(1)} %add_convert_fusion.1), channel_id=1, source_target_pairs={{0,4},{1,5},{2,6},{3,7},{4,0},{5,1},{6,2},{7,3},{8,12},{9,13},{10,... | collective-permute-start | bytes 589832 | tf_op jit(solution)/shard_map/ppermute | solution.py:1177
  110.4 6.5 %shard_map.337 = (bf16[256,256]{1,0:T(8,128)(2,1)}, bf16[256,256]{1,0:T(8,128)(2,1)}, f32[8,256]{1,0:T(8,128)}) custom-call(f32[16,256]{1,0:T(8,128)S(1)} %get-tuple-element.95.vec, bf16[2176,768]{1,0:T(8,128)(2,1)S(1)} %get-tuple-element.147.shifted, bf16[3,768,256]{2,1,0:T(8,128)(2,1)} %get-tuple-element.148.weight_far, ...), custom_call_target="tpu_custom_call" | custom-call | flops 7247757312 | bytes 7692288 | tf_op jit(solution)/shard_map/pallas_call | solution.py:1208
  116.9 0.7 convert.4
  117.6 1.1 collective-permute-start.29
  118.7 1.7 %collective-permute-done.27 = bf16[384,256]{1,0:T(8,128)(2,1)S(1)} collective-permute-done((bf16[384,256]{1,0:T(8,128)(2,1)S(1)}, bf16[384,256]{1,0:T(8,128)(2,1)S(1)}, u32[]{:S(2)}, u32[]{:S(2)}) %collective-permute-start.27) | collective-permute-done | bytes 196640 | tf_op jit(solution)/shard_map/ppermute | solution.py:1177
  120.5 1.7 %collective-permute-done.29 = bf16[16,256]{1,0:T(8,128)(2,1)S(1)} collective-permute-done((bf16[16,256]{1,0:T(8,128)(2,1)S(1)}, bf16[16,256]{1,0:T(8,128)(2,1)S(1)}, u32[]{:S(2)}, u32[]{:S(2)}) %collective-permute-start.29) | collective-permute-done | bytes 8224 | tf_op jit(solution)/shard_map/ppermute | solution.py:1177
  122.2 4.9 %collective-permute-done.28 = bf16[384,256]{1,0:T(8,128)(2,1)S(1)} collective-permute-done((bf16[384,256]{1,0:T(8,128)(2,1)S(1)}, bf16[384,256]{1,0:T(8,128)(2,1)S(1)}, u32[]{:S(2)}, u32[]{:S(2)}) %collective-permute-start.28) | collective-permute-done | bytes 196640 | tf_op jit(solution)/shard_map/ppermute | solution.py:1177
  127.1 1.6 %collective-permute-start.31 = (bf16[784,256]{1,0:T(8,128)(2,1)S(1)}, bf16[784,256]{1,0:T(8,128)(2,1)S(1)}, u32[]{:S(2)}, u32[]{:S(2)}) collective-permute-start(bf16[784,256]{1,0:T(8,128)(2,1)S(1)} %pad_maximum_fusion.refs_0_), channel_id=1, source_target_pairs={{0,8},{8,0},{16,24},{24,16},{1,9},{9,1},{17,25},{25,17},{2,10},{10... | collective-permute-start | bytes 1204232 | tf_op jit(solution)/shard_map/ppermute | solution.py:1177
  128.8 1.9 %collective-permute-start.35 = (bf16[784,256]{1,0:T(8,128)(2,1)S(1)}, bf16[784,256]{1,0:T(8,128)(2,1)S(1)}, u32[]{:S(2)}, u32[]{:S(2)}) collective-permute-start(bf16[784,256]{1,0:T(8,128)(2,1)S(1)} %pad_maximum_fusion.refs_0_), channel_id=1, source_target_pairs={{0,24},{8,16},{16,8},{24,0},{1,25},{9,17},{17,9},{25,1},{2,26},{10... | collective-permute-start | bytes 1204232 | tf_op jit(solution)/shard_map/ppermute | solution.py:1177
  130.7 1.5 shard_map.336
  132.2 0.6 copy-done.2
  132.8 0.7 pad_maximum_fusion.3
  133.6 1.3 collective-permute-start.26
  134.9 4.5 %collective-permute-done.31.refs_2_ = bf16[784,256]{1,0:T(8,128)(2,1)S(1)} collective-permute-done((bf16[784,256]{1,0:T(8,128)(2,1)S(1)}, bf16[784,256]{1,0:T(8,128)(2,1)S(1)}, u32[]{:S(2)}, u32[]{:S(2)}) %collective-permute-start.31) | collective-permute-done | bytes 401440 | tf_op jit(solution)/shard_map/ppermute | solution.py:1177
  139.4 7.7 %collective-permute-done.33.refs_4_ = bf16[784,256]{1,0:T(8,128)(2,1)S(1)} collective-permute-done((bf16[784,256]{1,0:T(8,128)(2,1)S(1)}, bf16[784,256]{1,0:T(8,128)(2,1)S(1)}, u32[]{:S(2)}, u32[]{:S(2)}) %collective-permute-start.33) | collective-permute-done | bytes 401440 | tf_op jit(solution)/shard_map/ppermute | solution.py:1177
  147.1 0.5 collective-permute-start.36
  147.6 1.1 select_bitcast_fusion
  148.7 0.8 pad_maximum_fusion.1
  149.6 5.9 %shard_map.338 = (f32[3,3,256,256]{3,2,1,0:T(8,128)}, f32[3,3,256,256]{3,2,1,0:T(8,128)}, f32[256,768]{1,0:T(8,128)}, f32[256,256]{1,0:T(8,128)}, f32[1024,512]{...) custom-call(bf16[784,256]{1,0:T(8,128)(2,1)S(1)} %pad_maximum_fusion, ...), custom_call_target="tpu_custom_call" | custom-call | flops 603979776 | bytes 3213312 | tf_op jit(solution)/shard_map/pallas_call | solution.py:1208
  (109 shorter events, 5.7 us)
Async XLA Ops:
  0.7 8.4 %copy-start = (bf16[1024,512]{1,0:T(8,128)(2,1)S(1)}, bf16[1024,512]{1,0:T(8,128)(2,1)}, u32[]{:S(2)}) copy-start(bf16[1024,512]{1,0:T(8,128)(2,1)} %param.27) | copy-start | bytes 3145732
  1.8 12.6 %copy-start.6 = (bf16[256,256]{1,0:T(8,128)(2,1)}, bf16[256,256]{1,0:T(8,128)(2,1)S(1)}, u32[]{:S(2)}) copy-start(bf16[256,256]{1,0:T(8,128)(2,1)S(1)} %get-tuple-element.177.refs_0_) | copy-start | bytes 393220
  1.8 12.6 %copy-start.4 = (bf16[2,4,64,256]{3,2,1,0:T(8,128)(2,1)S(1)}, bf16[2,4,64,256]{3,2,1,0:T(8,128)(2,1)}, u32[]{:S(2)}) copy-start(bf16[2,4,64,256]{3,2,1,0:T(8,128)(2,1)} %param.39) | copy-start | bytes 786436
  1.8 17.2 %collective-permute-start = (bf16[256,256]{1,0:T(8,128)(2,1)S(1)}, bf16[256,256]{1,0:T(8,128)(2,1)S(1)}, u32[]{:S(2)}, u32[]{:S(2)}) collective-permute-start(bf16[256,256]{1,0:T(8,128)(2,1)S(1)} %get-tuple-element.177.refs_0_), channel_id=1, source_target_pairs={{0,1},{1,0},{2,3},{3,2},{4,5},{5,4},{6,7},{7,6},{8,9},{9,8},{10,11... | collective-permute-start | bytes 393224 | tf_op jit(solution)/shard_map/ppermute | solution.py:1177
  2.3 15.6 %collective-permute-start.1 = (bf16[256,256]{1,0:T(8,128)(2,1)S(1)}, bf16[256,256]{1,0:T(8,128)(2,1)S(1)}, u32[]{:S(2)}, u32[]{:S(2)}) collective-permute-start(bf16[256,256]{1,0:T(8,128)(2,1)S(1)} %get-tuple-element.177.refs_0_), channel_id=1, source_target_pairs={{0,2},{1,3},{2,0},{3,1},{4,6},{5,7},{6,4},{7,5},{8,10},{9,11},{10,... | collective-permute-start | bytes 393224 | tf_op jit(solution)/shard_map/ppermute | solution.py:1177
  5.0 12.9 %collective-permute-start.2 = (bf16[256,256]{1,0:T(8,128)(2,1)S(1)}, bf16[256,256]{1,0:T(8,128)(2,1)S(1)}, u32[]{:S(2)}, u32[]{:S(2)}) collective-permute-start(bf16[256,256]{1,0:T(8,128)(2,1)S(1)} %get-tuple-element.176), channel_id=1, source_target_pairs={{0,4},{1,5},{2,6},{3,7},{4,0},{5,1},{6,2},{7,3},{8,12},{9,13},{10,... | collective-permute-start | bytes 393224 | tf_op jit(solution)/shard_map/ppermute | solution.py:1177
  7.6 10.3 %collective-permute-start.3 = (bf16[256,256]{1,0:T(8,128)(2,1)S(1)}, bf16[256,256]{1,0:T(8,128)(2,1)S(1)}, u32[]{:S(2)}, u32[]{:S(2)}) collective-permute-start(bf16[256,256]{1,0:T(8,128)(2,1)S(1)} %get-tuple-element.176), channel_id=1, source_target_pairs={{0,6},{1,7},{2,4},{3,5},{4,2},{5,3},{6,0},{7,1},{8,14},{9,15},{10,... | collective-permute-start | bytes 393224 | tf_op jit(solution)/shard_map/ppermute | solution.py:1177
  14.4 22.4 %copy-start.5 = (bf16[256,256]{1,0:T(8,128)(2,1)}, bf16[256,256]{1,0:T(8,128)(2,1)S(1)}, u32[]{:S(2)}) copy-start(bf16[256,256]{1,0:T(8,128)(2,1)S(1)} %get-tuple-element.107.refs_0_) | copy-start | bytes 393220
  17.9 6.4 %copy-start.17 = (bf16[256,256]{1,0:T(8,128)(2,1)}, bf16[256,256]{1,0:T(8,128)(2,1)S(1)}, u32[]{:S(2)}) copy-start(bf16[256,256]{1,0:T(8,128)(2,1)S(1)} %collective-permute-done.2.refs_4_) | copy-start | bytes 393220
  17.9 6.4 %copy-start.18 = (bf16[256,256]{1,0:T(8,128)(2,1)}, bf16[256,256]{1,0:T(8,128)(2,1)S(1)}, u32[]{:S(2)}) copy-start(bf16[256,256]{1,0:T(8,128)(2,1)S(1)} %collective-permute-done.3.refs_6_) | copy-start | bytes 393220
  17.9 6.4 %copy-start.16 = (bf16[256,256]{1,0:T(8,128)(2,1)}, bf16[256,256]{1,0:T(8,128)(2,1)S(1)}, u32[]{:S(2)}) copy-start(bf16[256,256]{1,0:T(8,128)(2,1)S(1)} %collective-permute-done.1.refs_2_) | copy-start | bytes 393220
  17.9 3.7 %collective-permute-start.4 = (bf16[256,256]{1,0:T(8,128)(2,1)S(1)}, bf16[256,256]{1,0:T(8,128)(2,1)S(1)}, u32[]{:S(2)}, u32[]{:S(2)}) collective-permute-start(bf16[256,256]{1,0:T(8,128)(2,1)S(1)} %collective-permute-done.1.refs_2_), channel_id=1, source_target_pairs={{0,1},{1,0},{2,3},{3,2},{4,5},{5,4},{6,7},{7,6},{8,9},{9,8},{10,11... | collective-permute-start | bytes 393224 | tf_op jit(solution)/shard_map/ppermute | solution.py:1177
  18.0 4.9 %collective-permute-start.5 = (bf16[256,256]{1,0:T(8,128)(2,1)S(1)}, bf16[256,256]{1,0:T(8,128)(2,1)S(1)}, u32[]{:S(2)}, u32[]{:S(2)}) collective-permute-start(bf16[256,256]{1,0:T(8,128)(2,1)S(1)} %collective-permute-done.2.refs_4_), channel_id=1, source_target_pairs={{0,1},{1,0},{2,3},{3,2},{4,5},{5,4},{6,7},{7,6},{8,9},{9,8},{10,11... | collective-permute-start | bytes 393224 | tf_op jit(solution)/shard_map/ppermute | solution.py:1177
  18.5 5.8 %collective-permute-start.6 = (bf16[256,256]{1,0:T(8,128)(2,1)S(1)}, bf16[256,256]{1,0:T(8,128)(2,1)S(1)}, u32[]{:S(2)}, u32[]{:S(2)}) collective-permute-start(bf16[256,256]{1,0:T(8,128)(2,1)S(1)} %collective-permute-done.3.refs_6_), channel_id=1, source_target_pairs={{0,1},{1,0},{2,3},{3,2},{4,5},{5,4},{6,7},{7,6},{8,9},{9,8},{10,11... | collective-permute-start | bytes 393224 | tf_op jit(solution)/shard_map/ppermute | solution.py:1177
  18.6 19.0 %collective-permute-start.7 = (bf16[256,256]{1,0:T(8,128)(2,1)S(1)}, bf16[256,256]{1,0:T(8,128)(2,1)S(1)}, u32[]{:S(2)}, u32[]{:S(2)}) collective-permute-start(bf16[256,256]{1,0:T(8,128)(2,1)S(1)} %get-tuple-element.107.refs_0_), channel_id=1, source_target_pairs={{0,1},{1,0},{2,3},{3,2},{4,5},{5,4},{6,7},{7,6},{8,9},{9,8},{10,11... | collective-permute-start | bytes 393224 | tf_op jit(solution)/shard_map/ppermute | solution.py:1177
  19.0 17.9 %collective-permute-start.8 = (bf16[256,256]{1,0:T(8,128)(2,1)S(1)}, bf16[256,256]{1,0:T(8,128)(2,1)S(1)}, u32[]{:S(2)}, u32[]{:S(2)}) collective-permute-start(bf16[256,256]{1,0:T(8,128)(2,1)S(1)} %get-tuple-element.107.refs_0_), channel_id=1, source_target_pairs={{0,2},{1,3},{2,0},{3,1},{4,6},{5,7},{6,4},{7,5},{8,10},{9,11},{10,... | collective-permute-start | bytes 393224 | tf_op jit(solution)/shard_map/ppermute | solution.py:1177
  21.6 15.3 %collective-permute-start.9 = (bf16[256,256]{1,0:T(8,128)(2,1)S(1)}, bf16[256,256]{1,0:T(8,128)(2,1)S(1)}, u32[]{:S(2)}, u32[]{:S(2)}) collective-permute-start(bf16[256,256]{1,0:T(8,128)(2,1)S(1)} %get-tuple-element.108), channel_id=1, source_target_pairs={{0,4},{1,5},{2,6},{3,7},{4,0},{5,1},{6,2},{7,3},{8,12},{9,13},{10,... | collective-permute-start | bytes 393224 | tf_op jit(solution)/shard_map/ppermute | solution.py:1177
  22.9 14.0 %collective-permute-start.10 = (bf16[256,256]{1,0:T(8,128)(2,1)S(1)}, bf16[256,256]{1,0:T(8,128)(2,1)S(1)}, u32[]{:S(2)}, u32[]{:S(2)}) collective-permute-start(bf16[256,256]{1,0:T(8,128)(2,1)S(1)} %get-tuple-element.108), channel_id=1, source_target_pairs={{0,6},{1,7},{2,4},{3,5},{4,2},{5,3},{6,0},{7,1},{8,14},{9,15},{10,... | collective-permute-start | bytes 393224 | tf_op jit(solution)/shard_map/ppermute | solution.py:1177
  36.9 20.6 %copy-start.3 = (bf16[2048,256]{1,0:T(8,128)(2,1)}, bf16[2048,256]{1,0:T(8,128)(2,1)S(1)}, u32[]{:S(2)}) copy-start(bf16[2048,256]{1,0:T(8,128)(2,1)S(1)} %get-tuple-element.103.act_three.refs_4_) | copy-start | bytes 3145732
  36.9 1.4 collective-permute-start.11
  37.0 1.5 collective-permute-start.12
  37.5 1.3 collective-permute-start.13
  57.5 22.6 %collective-permute-start.14 = (bf16[2048,128]{1,0:T(8,128)(2,1)}, bf16[2048,128]{1,0:T(8,128)(2,1)S(1)}, u32[]{:S(2)}, u32[]{:S(2)}) collective-permute-start(bf16[2048,128]{1,0:T(8,128)(2,1)} %get-tuple-element.113.refs_3_.refs_0_), channel_id=1, source_target_pairs={{0,1},{1,0},{2,3},{3,2},{4,5},{5,4},{6,7},{7,6},{8,9},{9,8},{10,11... | collective-permute-start | bytes 1572872 | tf_op jit(solution)/shard_map/ppermute | solution.py:1177
  57.7 20.0 %collective-permute-start.16 = (bf16[2048,128]{1,0:T(8,128)(2,1)}, bf16[2048,128]{1,0:T(8,128)(2,1)S(1)}, u32[]{:S(2)}, u32[]{:S(2)}) collective-permute-start(bf16[2048,128]{1,0:T(8,128)(2,1)} %get-tuple-element.113.refs_3_.refs_0_), channel_id=1, source_target_pairs={{0,2},{1,3},{2,0},{3,1},{4,6},{5,7},{6,4},{7,5},{8,10},{9,11},{10,... | collective-permute-start | bytes 1572872 | tf_op jit(solution)/shard_map/ppermute | solution.py:1177
  58.5 19.2 %collective-permute-start.17 = (bf16[1024,128]{1,0:T(8,128)(2,1)}, bf16[1024,128]{1,0:T(8,128)(2,1)S(1)}, u32[]{:S(2)}, u32[]{:S(2)}) collective-permute-start(bf16[1024,128]{1,0:T(8,128)(2,1)} %get-tuple-element.120.refs_1_), channel_id=1, source_target_pairs={{0,2},{1,3},{2,0},{3,1},{4,6},{5,7},{6,4},{7,5},{8,10},{9,11},{10,... | collective-permute-start | bytes 786440 | tf_op jit(solution)/shard_map/ppermute | solution.py:1177
  59.8 18.0 %copy-start.11 = (bf16[1024,128]{1,0:T(8,128)(2,1)S(1)}, bf16[1024,128]{1,0:T(8,128)(2,1)}, u32[]{:S(2)}) copy-start(bf16[1024,128]{1,0:T(8,128)(2,1)} %get-tuple-element.120.refs_1_) | copy-start | bytes 786436
  77.7 2.7 %collective-permute-start.18 = (bf16[2048,128]{1,0:T(8,128)(2,1)S(1)}, bf16[2048,128]{1,0:T(8,128)(2,1)S(1)}, u32[]{:S(2)}, u32[]{:S(2)}) collective-permute-start(bf16[2048,128]{1,0:T(8,128)(2,1)S(1)} %collective-permute-done.16.refs_4_), channel_id=1, source_target_pairs={{0,1},{1,0},{2,3},{3,2},{4,5},{5,4},{6,7},{7,6},{8,9},{9,8},{10,11... | collective-permute-start | bytes 1572872 | tf_op jit(solution)/shard_map/ppermute | solution.py:1177
  77.8 2.3 %collective-permute-start.15 = (bf16[1024,128]{1,0:T(8,128)(2,1)S(1)}, bf16[1024,128]{1,0:T(8,128)(2,1)S(1)}, u32[]{:S(2)}, u32[]{:S(2)}) collective-permute-start(bf16[1024,128]{1,0:T(8,128)(2,1)S(1)} %copy-done.11), channel_id=1, source_target_pairs={{0,1},{1,0},{2,3},{3,2},{4,5},{5,4},{6,7},{7,6},{8,9},{9,8},{10,11... | collective-permute-start | bytes 786440 | tf_op jit(solution)/shard_map/ppermute | solution.py:1177
  78.3 2.1 %collective-permute-start.19 = (bf16[1024,128]{1,0:T(8,128)(2,1)S(1)}, bf16[1024,128]{1,0:T(8,128)(2,1)S(1)}, u32[]{:S(2)}, u32[]{:S(2)}) collective-permute-start(bf16[1024,128]{1,0:T(8,128)(2,1)S(1)} %collective-permute-done.17.refs_5_), channel_id=1, source_target_pairs={{0,1},{1,0},{2,3},{3,2},{4,5},{5,4},{6,7},{7,6},{8,9},{9,8},{10,11... | collective-permute-start | bytes 786440 | tf_op jit(solution)/shard_map/ppermute | solution.py:1177
  95.0 9.0 %collective-permute-start.22 = (bf16[384,256]{1,0:T(8,128)(2,1)}, bf16[384,256]{1,0:T(8,128)(2,1)S(1)}, u32[]{:S(2)}, u32[]{:S(2)}) collective-permute-start(bf16[384,256]{1,0:T(8,128)(2,1)} %get-tuple-element.137), channel_id=1, source_target_pairs={{0,24},{8,16},{16,8},{24,0},{1,25},{9,17},{17,9},{25,1},{2,26},{10... | collective-permute-start | bytes 589832 | tf_op jit(solution)/shard_map/ppermute | solution.py:1177
  97.5 9.8 %collective-permute-start.21 = (bf16[384,256]{1,0:T(8,128)(2,1)}, bf16[384,256]{1,0:T(8,128)(2,1)S(1)}, u32[]{:S(2)}, u32[]{:S(2)}) collective-permute-start(bf16[384,256]{1,0:T(8,128)(2,1)} %get-tuple-element.136), channel_id=1, source_target_pairs={{0,16},{8,24},{16,0},{24,8},{1,17},{9,25},{17,1},{25,9},{2,18},{10... | collective-permute-start | bytes 589832 | tf_op jit(solution)/shard_map/ppermute | solution.py:1177
  98.0 9.4 %collective-permute-start.20 = (bf16[384,256]{1,0:T(8,128)(2,1)}, bf16[384,256]{1,0:T(8,128)(2,1)S(1)}, u32[]{:S(2)}, u32[]{:S(2)}) collective-permute-start(bf16[384,256]{1,0:T(8,128)(2,1)} %get-tuple-element.135), channel_id=1, source_target_pairs={{0,8},{8,0},{16,24},{24,16},{1,9},{9,1},{17,25},{25,17},{2,10},{10... | collective-permute-start | bytes 589832 | tf_op jit(solution)/shard_map/ppermute | solution.py:1177
  98.5 9.9 %collective-permute-start.23 = (bf16[256,128]{1,0:T(8,128)(2,1)S(1)}, bf16[256,128]{1,0:T(8,128)(2,1)S(1)}, u32[]{:S(2)}, u32[]{:S(2)}) collective-permute-start(bf16[256,128]{1,0:T(8,128)(2,1)S(1)} %get-tuple-element.139), channel_id=1, source_target_pairs={{0,1},{1,0},{2,3},{3,2},{4,5},{5,4},{6,7},{7,6},{8,9},{9,8},{10,11... | collective-permute-start | bytes 196616 | tf_op jit(solution)/shard_map/ppermute | solution.py:1177
  98.5 9.9 %collective-permute-start.24 = (bf16[256,128]{1,0:T(8,128)(2,1)S(1)}, bf16[256,128]{1,0:T(8,128)(2,1)S(1)}, u32[]{:S(2)}, u32[]{:S(2)}) collective-permute-start(bf16[256,128]{1,0:T(8,128)(2,1)S(1)} %get-tuple-element.140), channel_id=1, source_target_pairs={{0,2},{1,3},{2,0},{3,1},{4,6},{5,7},{6,4},{7,5},{8,10},{9,11},{10,... | collective-permute-start | bytes 196616 | tf_op jit(solution)/shard_map/ppermute | solution.py:1177
  103.9 4.5 %collective-permute-start.25 = (bf16[256,128]{1,0:T(8,128)(2,1)S(1)}, bf16[256,128]{1,0:T(8,128)(2,1)S(1)}, u32[]{:S(2)}, u32[]{:S(2)}) collective-permute-start(bf16[256,128]{1,0:T(8,128)(2,1)S(1)} %get-tuple-element.141), channel_id=1, source_target_pairs={{0,3},{1,2},{2,1},{3,0},{4,7},{5,6},{6,5},{7,4},{8,11},{9,10},{10,... | collective-permute-start | bytes 196616 | tf_op jit(solution)/shard_map/ppermute | solution.py:1177
  108.5 11.9 %collective-permute-start.27 = (bf16[384,256]{1,0:T(8,128)(2,1)S(1)}, bf16[384,256]{1,0:T(8,128)(2,1)S(1)}, u32[]{:S(2)}, u32[]{:S(2)}) collective-permute-start(bf16[384,256]{1,0:T(8,128)(2,1)S(1)} %add_convert_fusion.1), channel_id=1, source_target_pairs={{0,4},{1,5},{2,6},{3,7},{4,0},{5,1},{6,2},{7,3},{8,12},{9,13},{10,... | collective-permute-start | bytes 589832 | tf_op jit(solution)/shard_map/ppermute | solution.py:1177
  110.4 20.3 %copy-start.1 = (bf16[256,256]{1,0:T(8,128)(2,1)S(1)}, bf16[256,256]{1,0:T(8,128)(2,1)}, u32[]{:S(2)}) copy-start(bf16[256,256]{1,0:T(8,128)(2,1)} %refs_12_.1) | copy-start | bytes 393220
  116.9 16.0 %copy-start.7 = (bf16[256,256]{1,0:T(8,128)(2,1)S(1)}, bf16[256,256]{1,0:T(8,128)(2,1)}, u32[]{:S(2)}) copy-start(bf16[256,256]{1,0:T(8,128)(2,1)} %get-tuple-element.153) | copy-start | bytes 393220
  117.6 4.5 %collective-permute-start.29 = (bf16[16,256]{1,0:T(8,128)(2,1)S(1)}, bf16[16,256]{1,0:T(8,128)(2,1)S(1)}, u32[]{:S(2)}, u32[]{:S(2)}) collective-permute-start(bf16[16,256]{1,0:T(8,128)(2,1)S(1)} %concatenate.10), channel_id=1, source_target_pairs={{0,4},{1,5},{2,6},{3,7},{4,0},{5,1},{6,2},{7,3},{8,12},{9,13},{10,... | collective-permute-start | bytes 24584 | tf_op jit(solution)/shard_map/ppermute | solution.py:1177
  120.4 6.6 %collective-permute-start.28 = (bf16[384,256]{1,0:T(8,128)(2,1)S(1)}, bf16[384,256]{1,0:T(8,128)(2,1)S(1)}, u32[]{:S(2)}, u32[]{:S(2)}) collective-permute-start(bf16[384,256]{1,0:T(8,128)(2,1)S(1)} %add_convert_fusion), channel_id=1, source_target_pairs={{0,2},{1,3},{2,0},{3,1},{4,6},{5,7},{6,4},{7,5},{8,10},{9,11},{10,... | collective-permute-start | bytes 589832 | tf_op jit(solution)/shard_map/ppermute | solution.py:1177
  127.1 12.3 %collective-permute-start.31 = (bf16[784,256]{1,0:T(8,128)(2,1)S(1)}, bf16[784,256]{1,0:T(8,128)(2,1)S(1)}, u32[]{:S(2)}, u32[]{:S(2)}) collective-permute-start(bf16[784,256]{1,0:T(8,128)(2,1)S(1)} %pad_maximum_fusion.refs_0_), channel_id=1, source_target_pairs={{0,8},{8,0},{16,24},{24,16},{1,9},{9,1},{17,25},{25,17},{2,10},{10... | collective-permute-start | bytes 1204232 | tf_op jit(solution)/shard_map/ppermute | solution.py:1177
  128.7 18.4 %collective-permute-start.33 = (bf16[784,256]{1,0:T(8,128)(2,1)S(1)}, bf16[784,256]{1,0:T(8,128)(2,1)S(1)}, u32[]{:S(2)}, u32[]{:S(2)}) collective-permute-start(bf16[784,256]{1,0:T(8,128)(2,1)S(1)} %pad_maximum_fusion.refs_0_), channel_id=1, source_target_pairs={{0,16},{8,24},{16,0},{24,8},{1,17},{9,25},{17,1},{25,9},{2,18},{10... | collective-permute-start | bytes 1204232 | tf_op jit(solution)/shard_map/ppermute | solution.py:1177
  128.8 18.3 %collective-permute-start.35 = (bf16[784,256]{1,0:T(8,128)(2,1)S(1)}, bf16[784,256]{1,0:T(8,128)(2,1)S(1)}, u32[]{:S(2)}, u32[]{:S(2)}) collective-permute-start(bf16[784,256]{1,0:T(8,128)(2,1)S(1)} %pad_maximum_fusion.refs_0_), channel_id=1, source_target_pairs={{0,24},{8,16},{16,8},{24,0},{1,25},{9,17},{17,9},{25,1},{2,26},{10... | collective-permute-start | bytes 1204232 | tf_op jit(solution)/shard_map/ppermute | solution.py:1177
  133.6 14.1 %collective-permute-start.26 = (bf16[2,256,256]{2,1,0:T(8,128)(2,1)}, bf16[2,256,256]{2,1,0:T(8,128)(2,1)}, u32[]{:S(2)}, u32[]{:S(2)}) collective-permute-start(bf16[2,256,256]{2,1,0:T(8,128)(2,1)} %pad_maximum_fusion.3), channel_id=1, source_target_pairs={{0,4},{1,5},{2,6},{3,7},{4,0},{5,1},{6,2},{7,3},{8,12},{9,13},{10,... | collective-permute-start | bytes 786440 | tf_op jit(solution)/shard_map/ppermute | solution.py:1177
  134.9 14.7 %collective-permute-start.30 = (bf16[784,256]{1,0:T(8,128)(2,1)S(1)}, bf16[784,256]{1,0:T(8,128)(2,1)S(1)}, u32[]{:S(2)}, u32[]{:S(2)}) collective-permute-start(bf16[784,256]{1,0:T(8,128)(2,1)S(1)} %pad_maximum_fusion.refs_0_), channel_id=1, source_target_pairs={{0,1},{1,0},{2,3},{3,2},{4,5},{5,4},{6,7},{7,6},{8,9},{9,8},{10,11... | collective-permute-start | bytes 1204232 | tf_op jit(solution)/shard_map/ppermute | solution.py:1177
  139.4 10.2 %collective-permute-start.32 = (bf16[784,256]{1,0:T(8,128)(2,1)S(1)}, bf16[784,256]{1,0:T(8,128)(2,1)S(1)}, u32[]{:S(2)}, u32[]{:S(2)}) collective-permute-start(bf16[784,256]{1,0:T(8,128)(2,1)S(1)} %collective-permute-done.31.refs_2_), channel_id=1, source_target_pairs={{0,1},{1,0},{2,3},{3,2},{4,5},{5,4},{6,7},{7,6},{8,9},{9,8},{10,11... | collective-permute-start | bytes 1204232 | tf_op jit(solution)/shard_map/ppermute | solution.py:1177
  147.1 2.5 %collective-permute-start.34 = (bf16[784,256]{1,0:T(8,128)(2,1)S(1)}, bf16[784,256]{1,0:T(8,128)(2,1)}, u32[]{:S(2)}, u32[]{:S(2)}) collective-permute-start(bf16[784,256]{1,0:T(8,128)(2,1)S(1)} %collective-permute-done.33.refs_4_), channel_id=1, source_target_pairs={{0,1},{1,0},{2,3},{3,2},{4,5},{5,4},{6,7},{7,6},{8,9},{9,8},{10,11... | collective-permute-start | bytes 1204232 | tf_op jit(solution)/shard_map/ppermute | solution.py:1177
  147.1 2.5 %collective-permute-start.36 = (bf16[784,256]{1,0:T(8,128)(2,1)S(1)}, bf16[784,256]{1,0:T(8,128)(2,1)}, u32[]{:S(2)}, u32[]{:S(2)}) collective-permute-start(bf16[784,256]{1,0:T(8,128)(2,1)S(1)} %collective-permute-done.35.refs_6_), channel_id=1, source_target_pairs={{0,1},{1,0},{2,3},{3,2},{4,5},{5,4},{6,7},{7,6},{8,9},{9,8},{10,11... | collective-permute-start | bytes 1204232 | tf_op jit(solution)/shard_map/ppermute | solution.py:1177
  (18 other events, 28.5 us)

commit v4 on v3

--- a/solution.py
+++ b/solution.py
@@ -376,6 +376,9 @@
     )
 
 
+ARRIVAL = (3, 5, 7, 0, 1, 2, 4, 6)
+
+
 def mib(count):
     return pltpu.CompilerParams(vmem_limit_bytes=count * 2**20)
 
@@ -417,22 +420,45 @@
     return jnp.sum(tile, axis=0, keepdims=True)
 
 
-def field_stats(read, height, rows, cols, channels):
-    width = channels // GROUPS
+def cell_sums(tiles, about, height):
+    first, square = 0.0, 0.0
+    for index, tile in tiles:
+        off = (tile - about) * valid_row(index, height)
+        first, square = first + fold(off), square + fold(off * off)
+    return first, square
+
+
+def stats_of(first, square, about, height, cols):
+    width = about.shape[1] // GROUPS
     each = (height * cols).astype(jnp.float32)
-    about = jnp.sum(read(0), axis=0, keepdims=True) * (1.0 / cols)
-    zero = jnp.zeros((8, channels), jnp.float32)
-
-    def add(index, totals):
-        off = (read(index) - about) * valid_row(index, height)
-        return totals[0] + fold(off), totals[1] + fold(off * off)
-
-    first, square = lax.fori_loop(0, rows, add, (zero, zero), unroll=4)
     first, square = total_of(first), total_of(square)
     mean = group_sums(first + about * each, width) / (each * width)
     shift = about - mean
     spread = group_sums(square + 2.0 * first * shift + each * shift * shift, width)
     return mean, lax.rsqrt(spread / (each * width) + EPSILON)
+
+
+def row_mean(tile):
+    return jnp.sum(tile, axis=0, keepdims=True) * (1.0 / tile.shape[0])
+
+
+def in_turn(count, before, main, after):
+    for step in range(count + 2):
+        if step < count:
+            before(step)
+        if 0 <= step - 1 < count:
+            main(step - 1)
+        if 0 <= step - 2:
+            after(step - 2)
+
+
+def conv_block(shifted, weight, block, size, cols):
+    base = block * size
+    total = dot(shifted[base : base + size, :], weight[0])
+    for tap in (1, 2):
+        at = base + tap * cols
+        total = total + dot(shifted[at : at + size, :], weight[tap])
+    return total
 
 
 def half_line(mean, inverse, gain, bias, scale=1.0, shift=0.0):
@@ -475,13 +501,16 @@
     lax.fori_loop(0, out.shape[0] // step, block, 0, unroll=True)
 
 
-def kernel_quarter(shifted, own_t, out, cols):
-    cells = own_t.shape[2]
-    channels = shifted.shape[1] // 3
-    width = own_t.shape[1]
-    grad = shifted[cols : cols + cells, channels : 2 * channels]
-    for tap in range(3):
-        out[tap * width : (tap + 1) * width, :] = dot(own_t[tap], grad).astype(jnp.bfloat16)
+def put_quarter(parts, payload, start):
+    half = parts[0].shape[0] // 3
+    unit = half // 4
+    for line, part in enumerate(parts):
+        part = part.astype(jnp.bfloat16)
+        for shift in range(3):
+            at = start + (3 * line + shift) * unit
+            for chunk in range(4):
+                base = shift * half + chunk * unit
+                payload[chunk, at : at + unit, :] = part[base : base + unit]
 
 
 def own_place(vec):
@@ -516,7 +545,7 @@
     rows = cells // cols
     spot, _, _, height = own_place(vec)
     pairs = []
-    for step, block in enumerate(blocks):
+    for step, block in zip(ARRIVAL, blocks):
         base = pl.multiple_of((spot ^ step) * block_cells, block_cells)
         pairs.append((block, pix.at[pl.ds(base, block_cells), :]))
     arriving = started(in_sems, *pairs, (w_one_far, w_one), (w_two_far, w_two))
@@ -524,42 +553,63 @@
     scale, shift, conv_bias_two, gain_three, bias_three = (vec[k : k + 1, :] for k in range(5, 10))
     inner = (pl.ds(cols, cells), pl.ds(channels, channels))
 
-    def read_pix(index):
-        return pix[row_at(index, cols), :].astype(jnp.float32)
-
-    def read_conv(index):
-        return conv_one[row_at(index, cols), :]
-
-    def read_res(index):
-        return residual[row_at(index, cols), :]
-
-    def activate(read, line, shifted):
-        def body(index, carry):
-            part = read(index) * line[0] + line[1]
-            part = (part + part * jnp.tanh(part)) * valid_row(index, height)
-            put_shifted(shifted, index, part, cols)
-            return carry
-
-        lax.fori_loop(0, rows, body, 0, unroll=2)
+    group = 4
+    size = group * cols
+    count = rows // group
+    zero = jnp.zeros((8, channels), jnp.float32)
+
+    def tile_of(ref, index):
+        return ref[index * cols : (index + 1) * cols, :].astype(jnp.float32)
+
+    def tiles_of(ref, block):
+        return [(k, tile_of(ref, k)) for k in range(block * group, (block + 1) * group)]
+
+    def stage(source, line, shifted, weight, out, bias, added=None):
+        sums = [zero, zero, None]
+
+        def activate(block):
+            for index, tile in tiles_of(source, block):
+                part = tile * line[0] + line[1]
+                part = (part + part * jnp.tanh(part)) * valid_row(index, height)
+                put_shifted(shifted, index, part, cols)
+
+        def conv(block):
+            total = conv_block(shifted, weight, block, size, cols) + bias
+            if added is not None:
+                total = total + added[block * size : (block + 1) * size, :].astype(jnp.float32)
+            out[block * size : (block + 1) * size, :] = total
+
+        def measure(block):
+            if block == 0:
+                sums[2] = row_mean(tile_of(out, 0))
+            first, square = cell_sums(tiles_of(out, block), sums[2], height)
+            sums[0], sums[1] = sums[0] + first, sums[1] + square
+
+        in_turn(count, activate, conv, measure)
+        return stats_of(*sums, height, cols)
 
     clear_rims(shift_one, cols)
     clear_rims(shift_two, cols)
     finish_all(arriving[:8])
     leaving = started(out_sems, (pix, pix_far))
-    mean_one, inv_one = field_stats(read_pix, height, rows, cols, channels)
-    activate(read_pix, half_line(mean_one, inv_one, gain_one, bias_one), shift_one)
-    leaving += started(out_sems.at[1:2], (shift_one.at[inner], act_one_far))
+    about = row_mean(tile_of(pix, 0))
+    first, square = zero, zero
+    for block in range(count):
+        more = cell_sums(tiles_of(pix, block), about, height)
+        first, square = first + more[0], square + more[1]
+    mean_one, inv_one = stats_of(first, square, about, height, cols)
     arriving[8].wait()
-    conv_shifted(shift_one, w_one, conv_one, conv_bias_one, cols)
-    leaving += started(out_sems.at[2:3], (conv_one, conv_far))
-    mean_two, inv_two = field_stats(read_conv, height, rows, cols, channels)
+    line = half_line(mean_one, inv_one, gain_one, bias_one)
+    mean_two, inv_two = stage(pix, line, shift_one, w_one, conv_one, conv_bias_one)
+    leaving += started(
+        out_sems.at[1:3], (shift_one.at[inner], act_one_far), (conv_one, conv_far)
+    )
+    arriving[9].wait()
     line = half_line(mean_two, inv_two, gain_two, bias_two, scale, shift)
-    activate(read_conv, line, shift_two)
-    leaving += started(out_sems.at[3:4], (shift_two.at[inner], act_two_far))
-    arriving[9].wait()
-    conv_shifted(shift_two, w_two, residual, conv_bias_two, cols, pix)
-    leaving += started(out_sems.at[4:5], (residual, residual_far))
-    mean_three, inv_three = field_stats(read_res, height, rows, cols, channels)
+    mean_three, inv_three = stage(conv_one, line, shift_two, w_two, residual, conv_bias_two, pix)
+    leaving += started(
+        out_sems.at[3:5], (shift_two.at[inner], act_two_far), (residual, residual_far)
+    )
     stats[...] = jnp.concatenate(
         [mean_one, inv_one, mean_two, inv_two, mean_three, inv_three, mean_one, mean_one], axis=0
     )
@@ -568,21 +618,43 @@
     start = bias_three - mean_three * slope
 
     def third(index, carry):
-        act_three[row_at(index, cols), :] = (read_res(index) * slope + start).astype(jnp.bfloat16)
+        at = row_at(index, cols)
+        act_three[at, :] = (residual[at, :] * slope + start).astype(jnp.bfloat16)
         return carry
 
     lax.fori_loop(0, rows, third, 0, unroll=4)
     finish_all(leaving)
 
 
-def attention_kernel(columns, vec, act_three, w_heads, w_out, biases, *refs):
+def project_kernel(act_three, w_heads, biases, query_only, key_pad, value_pad, sizes):
+    cells, lanes = query_only.shape
+    scaling = (lanes // 2) ** -0.5
+
+    def project(index, carry):
+        at = pl.ds(pl.multiple_of(index * 512, 512), 512)
+        parts = dot(act_three[at, :], w_heads[...]) + biases[0:1, :]
+        query, key, value = (parts[:, k * lanes : (k + 1) * lanes] for k in range(3))
+        query_only[at, :] = query.astype(jnp.bfloat16) * jnp.bfloat16(scaling)
+        key_pad[at, :] = key.astype(jnp.bfloat16)
+        value_pad[at, :] = value.astype(jnp.bfloat16)
+        query_size = jnp.sum(query * query, axis=1, keepdims=True) * (scaling * scaling)
+        key_size = jnp.sum(key * key, axis=1, keepdims=True)
+        return jnp.maximum(carry[0], jnp.max(query_size)), jnp.maximum(carry[1], jnp.max(key_size))
+
+    start = (jnp.float32(0.0), jnp.float32(0.0))
+    query_most, key_most = lax.fori_loop(0, cells // 512, project, start)
+    line = lax.broadcasted_iota(jnp.int32, sizes.shape, 0)
+    sizes[...] = jnp.where(line == 0, query_most, key_most)
+
+
+def attention_kernel(columns, vec, query_only, key_pad, value_pad, sizes, w_out, *refs):
     blocks = refs[:8]
     value_key_far, query_far, grad_far, mixed_far, sums_far = refs[8:13]
     (
         grad_blocks, grad_proj, value_key, query_part, sums,
-        query_grad, key_pad, value_pad, heads_t, mixed, mask_row, in_sems, out_sems,
+        query_grad, heads_t, mixed, mask_row, in_sems, out_sems,
     ) = refs[13:]
-    cells, channels = act_three.shape
+    cells, channels = grad_proj.shape
     block_cells = blocks[0].shape[0]
     spot, _, _, height = own_place(vec)
     half = mixed.shape[1] // 2
@@ -591,23 +663,11 @@
     valid_cells = height * cols
     step = 256
     pairs = []
-    for index, block in enumerate(blocks):
+    for index, block in zip(ARRIVAL, blocks):
         base = pl.multiple_of((spot ^ index) * block_cells, block_cells)
         pairs.append((block, grad_blocks.at[pl.ds(base, block_cells), :]))
     arriving = started(in_sems, *pairs)
 
-    def project(index, carry):
-        at = pl.ds(pl.multiple_of(index * 512, 512), 512)
-        parts = dot(act_three[at, :], w_heads[...]) + biases[0:1, :]
-        query_grad[at, :] = parts[:, 0 : 2 * half].astype(jnp.bfloat16) * jnp.bfloat16(scaling)
-        key_pad[at, :] = parts[:, 2 * half : 4 * half].astype(jnp.bfloat16)
-        value_pad[at, :] = parts[:, 4 * half : 6 * half].astype(jnp.bfloat16)
-        query, key = parts[:, 0 : 2 * half], parts[:, 2 * half : 4 * half]
-        query_size = jnp.sum(query * query, axis=1, keepdims=True) * (scaling * scaling)
-        key_size = jnp.sum(key * key, axis=1, keepdims=True)
-        return jnp.maximum(carry[0], jnp.max(query_size)), jnp.maximum(carry[1], jnp.max(key_size))
-
-    norms = lax.fori_loop(0, cells // 512, project, (jnp.float32(0.0), jnp.float32(0.0)))
     lane = lax.broadcasted_iota(jnp.int32, (1, cells), 1)
     mask_row[...] = jnp.where(lane < valid_cells, 0.0, MASKED)
     heads_t[...] = jnp.zeros(heads_t.shape, jnp.float32)
@@ -620,12 +680,11 @@
         kept = jnp.where(cell < valid_cells, grad_blocks[at, :].astype(jnp.float32), 0.0)
         low = kept.astype(jnp.bfloat16)
         grad_proj[at, :] = low
-        query_grad[at, :] = query_grad[at, :] + dot(low, w_out[...]).astype(jnp.bfloat16)
+        query_grad[at, :] = query_only[at, :] + dot(low, w_out[...]).astype(jnp.bfloat16)
         return total + fold(kept)
 
-    total = lax.fori_loop(
-        0, cells // block_cells, clean, jnp.zeros((8, channels), jnp.float32)
-    )
+    start = jnp.zeros((8, channels), jnp.float32)
+    total = lax.fori_loop(0, cells // block_cells, clean, start, unroll=True)
     sums[...] = jnp.concatenate([total_of(total), jnp.zeros((7, channels), jnp.float32)], axis=0)
     leaving = started(out_sems, (grad_proj, grad_far), (sums, sums_far))
 
@@ -653,8 +712,7 @@
         heads_t[half : 2 * half, :] += dot(turned[half : 2 * half], low)
         return carry
 
-    query_most, key_most = norms
-    narrow = query_most * key_most <= 3600.0
+    narrow = jnp.max(sizes[0:1, :]) * jnp.max(sizes[1:2, :]) <= 3600.0
 
     @pl.when(narrow)
     def _():
@@ -727,17 +785,21 @@
     from_query, from_heads, from_out, query_sum, value_sum = lax.fori_loop(
         0, cells // step, gather, (square, square, square, line, line)
     )
-    weight_rows[0:half, :] = from_query[0:half].astype(jnp.bfloat16)
-    weight_rows[half : 3 * half, :] = from_heads.astype(jnp.bfloat16)
-    weight_rows[3 * half : 4 * half, :] = from_out[half:lanes].astype(jnp.bfloat16)
+    unit = half // 4
+    parts = (from_query[0:half], from_heads[0:half], from_heads[half:lanes], from_out[half:lanes])
+    for chunk in range(4):
+        for k, part in enumerate(parts):
+            piece = part[chunk * unit : (chunk + 1) * unit].astype(jnp.bfloat16)
+            weight_rows[chunk, k * unit : (k + 1) * unit, :] = piece
+    weight_rows[:, half:, :] = jnp.zeros((4, 16, channels), jnp.bfloat16)
     which = lax.axis_index("img") * 2 + image
     lane = lax.broadcasted_iota(jnp.int32, (1, channels), 1)
     now = jnp.max(vec[12:13, :]).astype(jnp.int32)
     high = jnp.where(lane == which, (now // 32).astype(jnp.float32), 0.0)
     rest = jnp.where(lane == which, (now % 32).astype(jnp.float32), 0.0)
     row = jnp.concatenate([total_of(query_sum), total_of(value_sum)], axis=1)
-    below = jnp.zeros((weight_rows.shape[0] - 4 * half - 3, channels), jnp.float32)
-    weight_rows[4 * half :, :] = jnp.concatenate([row, high, rest, below], axis=0).astype(
+    below = jnp.zeros((13, channels), jnp.float32)
+    weight_rows[2, half:, :] = jnp.concatenate([row, high, rest, below], axis=0).astype(
         jnp.bfloat16
     )
     source = lax.broadcasted_iota(jnp.int32, (channels, 3 * half), 0)
@@ -774,13 +836,14 @@
 
 
 def middle_kernel(vec, qkv_t, *refs):
-    heads_far, sides_far = refs[0:8:2], refs[1:8:2]
+    heads_far = (refs[4], refs[0], refs[6], refs[2])
+    sides_far = (refs[5], refs[1], refs[7], refs[3])
     grad_far, residual_far, stats_far, own_two_far, rows_far = refs[8:13]
     weight_far, conv_far, own_one_far, out_sums_far = refs[13:17]
     shifted_one, grad_res_far, payload_far = refs[17], refs[18], refs[19:23]
     (
-        heads, sides, grad_proj, residual, stats, own_two, grad_res, early, grad_act, shifted,
-        weight, conv_one, own_one, out_sums, late, in_sems, out_sems,
+        heads, sides, grad_proj, residual, stats, own_two, grad_res, payload, grad_act, shifted,
+        weight, conv_one, own_one, out_sums, in_sems, out_sems,
     ) = refs[23:]
     cells, channels = grad_proj.shape
     cols = (shifted.shape[0] - cells) // 2
@@ -790,6 +853,8 @@
     width = channels // GROUPS
     count = (height * (cols * width)).astype(jnp.float32)
     half = qkv_t.shape[1]
+    unit = half // 4
+    small_at = 18 * unit + half
     pairs = [(far, heads.at[head ^ k]) for k, far in enumerate(heads_far)]
     pairs += [(far, sides.at[head ^ k]) for k, far in enumerate(sides_far)]
     arriving = started(
@@ -799,12 +864,14 @@
         (residual_far, residual),
         (grad_far, grad_proj),
         (own_two_far, own_two),
-        (rows_far, early.at[pl.ds(9 * half, 5 * half), :]),
+        (rows_far.at[:, pl.ds(0, half), :], payload.at[:, pl.ds(9 * unit, half), :]),
+        (rows_far.at[:, pl.ds(half, 16), :], payload.at[:, pl.ds(small_at, 16), :]),
         (weight_far, weight),
         (conv_far, conv_one),
         (own_one_far, own_one),
         (out_sums_far, out_sums),
     )
+    finish_all(arriving[:10])
     zeros = jnp.zeros((half, channels), jnp.bfloat16)
     halfway = cells // 2
     step = 512
@@ -813,7 +880,14 @@
     for a, b in pairs:
         order = [HEADS + a, 2 * HEADS + a, HEADS + b, 2 * HEADS + b]
         w_main.append(jnp.concatenate([qkv_t[k] for k in order], axis=0))
-    finish_all(arriving[:8])
+    mean, inverse = stats[4:5, :], stats[5:6, :]
+    gain = vec[8:9, :]
+    zero = jnp.zeros((8, channels), jnp.float32)
+    plain, cross = zero, zero
+
+    def normed(index):
+        return (residual[index * cols : (index + 1) * cols, :] - mean) * inverse
+
     for part in range(2):
         w_side = []
         for a, b in pairs:
@@ -833,83 +907,90 @@
                 term = dot(main, w_main[k]) + dot(side, w_side[k])
                 total = term if total is None else total + term
             grad_act[start : start + step, :] = total
-    finish_all(arriving[8:10])
-    mean, inverse = stats[4:5, :], stats[5:6, :]
-    gain = vec[8:9, :]
-    zero = jnp.zeros((8, channels), jnp.float32)
-
-    def normed(index):
-        return (residual[row_at(index, cols), :] - mean) * inverse
-
-    def add(index, totals):
-        grad = grad_act[row_at(index, cols), :]
-        return totals[0] + fold(grad), totals[1] + fold(grad * normed(index))
-
-    plain, cross = lax.fori_loop(0, rows, add, (zero, zero), unroll=2)
+            for index in range(start // cols, (start + step) // cols):
+                tile = total[index * cols - start : (index + 1) * cols - start]
+                plain = plain + fold(tile)
+                cross = cross + fold(tile * normed(index))
     plain, cross = total_of(plain), total_of(cross)
     mean_plain = group_sums(plain * gain, width) / count
     mean_cross = group_sums(cross * gain, width) / count
     clear_rims(shifted, cols)
-    arriving[10].wait()
-
-    def finish(index, total):
-        at = row_at(index, cols)
-        inner = (grad_act[at, :] * gain - mean_plain - normed(index) * mean_cross) * inverse
-        grad = grad_proj[at, :].astype(jnp.float32) + inner * valid_row(index, height)
-        grad_res[at, :] = grad
-        put_shifted(shifted, index, grad, cols)
-        return total + fold(grad)
-
-    total = total_of(lax.fori_loop(0, rows, finish, zero, unroll=2))
+    clear_rims(shifted_one, cols)
+    finish_all(arriving[10:16])
+    group = 4
+    size = group * cols
+    steps = rows // group
+    totals = [zero, zero, zero, zero]
+    one, two = gain * inverse, mean_cross * inverse * inverse
+    three = (mean_plain - mean * inverse * mean_cross) * inverse
+    gain_two, bias_two, scale, shift = (vec[k : k + 1, :] for k in range(3, 7))
+    mean_two, inverse_two = stats[2:3, :], stats[3:4, :]
+    line = half_line(mean_two, inverse_two, gain_two, bias_two, scale, shift)
+    begin_two = mean_two * inverse_two
+
+    def tiles(block):
+        for index in range(block * group, (block + 1) * group):
+            yield index, slice(index * cols, (index + 1) * cols)
+
+    def through_three(block):
+        for index, at in tiles(block):
+            inner = grad_act[at, :] * one - residual[at, :] * two - three
+            grad = grad_proj[at, :].astype(jnp.float32) + inner * valid_row(index, height)
+            grad_res[at, :] = grad
+            put_shifted(shifted, index, grad, cols)
+            totals[0] = totals[0] + fold(grad)
+
+    def conv_back(block):
+        grad_act[block * size : (block + 1) * size, :] = conv_block(
+            shifted, weight, block, size, cols
+        )
+
+    def through_act(block):
+        for index, at in tiles(block):
+            value = conv_one[at, :]
+            unit_value = value * inverse_two - begin_two
+            part = value * line[0] + line[1]
+            sigmoid = 0.5 + 0.5 * jnp.tanh(part)
+            slope = sigmoid + 2.0 * part * sigmoid * (1.0 - sigmoid)
+            grad = grad_act[at, :] * valid_row(index, height) * slope
+            grad_act[at, :] = grad
+            totals[1] = totals[1] + fold(grad)
+            totals[2] = totals[2] + fold(grad * unit_value)
+
+    in_turn(steps, through_three, conv_back, through_act)
+    total = total_of(totals[0])
     three_lines = [cross, plain, total]
     leaving = started(out_sems, (grad_res, grad_res_far))
-    finish_all(arriving[11:13])
-    kernel_quarter(shifted, own_two, early, cols)
-    before = early.shape[0] // 4
-    chunks = [pl.ds(pl.multiple_of((column ^ k) * before, 16), before) for k in range(4)]
-    leaving += started(
-        out_sems.at[1:5],
-        *[(early.at[at, :], far.at[pl.ds(0, before), :]) for at, far in zip(chunks, payload_far)],
-    )
-
-    gain, bias, scale, shift = (vec[k : k + 1, :] for k in range(3, 7))
-    clear_rims(shifted_one, cols)
-    arriving[13].wait()
-    conv_shifted(shifted, weight, grad_act, 0.0, cols)
-    arriving[14].wait()
-    mean, inverse = stats[2:3, :], stats[3:4, :]
-    line = half_line(mean, inverse, gain, bias, scale, shift)
-    begin = mean * inverse
-
-    def add(index, totals):
-        at = row_at(index, cols)
-        value = conv_one[at, :]
-        unit = value * inverse - begin
-        part = value * line[0] + line[1]
-        sigmoid = 0.5 + 0.5 * jnp.tanh(part)
-        slope = sigmoid + 2.0 * part * sigmoid * (1.0 - sigmoid)
-        grad = grad_act[at, :] * valid_row(index, height) * slope
-        grad_act[at, :] = grad
-        return totals[0] + fold(grad), totals[1] + fold(grad * unit)
-
-    plain, cross = lax.fori_loop(0, rows, add, (zero, zero), unroll=2)
-    plain, cross = total_of(plain), total_of(cross)
+    plain, cross = total_of(totals[1]), total_of(totals[2])
+    gain, bias = gain_two, bias_two
     factor = gain * scale
     mean_plain = group_sums(plain * factor, width) / count
     mean_cross = group_sums(cross * factor, width) / count
-    one, two = factor * inverse, mean_cross * inverse * inverse
-    three = (mean_plain - begin * mean_cross) * inverse
-
-    def finish(index, total):
-        at = row_at(index, cols)
-        grad = grad_act[at, :] * one - conv_one[at, :] * two - three
-        grad = grad * valid_row(index, height)
-        put_shifted(shifted_one, index, grad, cols)
-        return total + fold(grad)
-
-    total = total_of(lax.fori_loop(0, rows, finish, zero, unroll=2))
-    finish_all(arriving[15:])
-    kernel_quarter(shifted_one, own_one, late, cols)
+    one, two = factor * inverse_two, mean_cross * inverse_two * inverse_two
+    three = (mean_plain - begin_two * mean_cross) * inverse_two
+    finish_all(arriving[16:])
+    parts = [[None] * 3, [None] * 3]
+
+    def through_two(block):
+        for index, at in tiles(block):
+            grad = grad_act[at, :] * one - conv_one[at, :] * two - three
+            grad = grad * valid_row(index, height)
+            put_shifted(shifted_one, index, grad, cols)
+            totals[3] = totals[3] + fold(grad)
+
+    def weigh(block):
+        at = slice(block * size, (block + 1) * size)
+        inner = slice(cols + block * size, cols + (block + 1) * size)
+        for k, (own, moved) in enumerate(((own_two, shifted), (own_one, shifted_one))):
+            grad = moved[inner, channels : 2 * channels]
+            for tap in range(3):
+                part = dot(own[tap, :, at], grad)
+                parts[k][tap] = part if block == 0 else parts[k][tap] + part
+
+    in_turn(steps, through_two, weigh, lambda block: None)
+    put_quarter(parts[0], payload, 0)
+    put_quarter(parts[1], payload, 9 * unit + half)
+    total = total_of(totals[3])
     lines = [
         *three_lines, out_sums[0:1, :], cross * scale, plain * scale, total,
         jnp.zeros((9, channels), jnp.float32),
@@ -917,18 +998,11 @@
     mine = 2 * (column * 2 + image)
     place = lax.broadcasted_iota(jnp.int32, (16, channels), 0)
     both = jnp.where(place == mine, gain * cross + bias * plain, 0.0)
-    lines.append(jnp.where(place == mine + 1, plain, both))
-    base = 3 * own_one.shape[1]
-    lines.append(jnp.zeros((late.shape[0] - base - 32, channels), jnp.float32))
-    late[base:, :] = jnp.concatenate(lines, axis=0).astype(jnp.bfloat16)
-    after = late.shape[0] // 4
-    chunks = [pl.ds(pl.multiple_of((column ^ k) * after, 16), after) for k in range(4)]
+    payload[0, small_at:, :] = jnp.concatenate(lines, axis=0).astype(jnp.bfloat16)
+    payload[1, small_at:, :] = jnp.where(place == mine + 1, plain, both).astype(jnp.bfloat16)
     leaving += started(
-        out_sems.at[5:9],
-        *[
-            (late.at[at, :], far.at[pl.ds(before, after), :])
-            for at, far in zip(chunks, payload_far)
-        ],
+        out_sems.at[1:5],
+        *[(payload.at[column ^ k], far) for k, far in enumerate(payload_far)],
     )
     finish_all(leaving)
 
@@ -1081,72 +1155,55 @@
     finish_all(leaving)
 
 
-def gathered_rows(parts, early, late):
-    spot = lax.axis_index("row")
-    head, column = spot % HEADS, lax.axis_index("img")
-    early_lines, late_lines = early.shape[1] // 4, late.shape[1] // 4
-    lines = early_lines + late_lines
-    for index, part in enumerate(parts):
-        away = column ^ (index // 2)
-        early_at = pl.ds(pl.multiple_of(away * early_lines, 16), early_lines)
-        late_at = pl.ds(pl.multiple_of(away * late_lines, 16), late_lines)
-        for pair in range(2):
-            quarter, base = head ^ (index % 2 + 2 * pair), pair * lines
-            early[quarter, early_at, :] = part[base : base + early_lines]
-            late[quarter, late_at, :] = part[base + early_lines : base + lines]
-
-
-def place_taps(gathered, out):
-    half = out.shape[2] // HEADS
-    for quarter in range(HEADS):
-        for tap in range(9):
-            base = tap * half
-            out[tap // 3, tap % 3, quarter * half : (quarter + 1) * half, :] = gathered[
-                quarter, base : base + half, :
-            ].astype(jnp.float32)
-
-
 def final_kernel(*refs):
     parts, frequency = refs[:8], refs[8]
     one_far, two_far, qkv_far, out_far, time_far = refs[9:14]
     bias_out, time_bias, rows = refs[14], refs[15], refs[16:25]
-    early, late, norm_one, one, two, qkv_out, out_out, time_out, out_sems = refs[25:]
-    gathered_rows(parts, early, late)
-    place_taps(late, one)
-    leaving = started(out_sems, (one, one_far))
-    place_taps(early, two)
-    leaving += started(out_sems.at[1:2], (two, two_far))
-    half = out_out.shape[0] // HEADS
-    nine = 9 * half
-    sums = []
-    for quarter in range(HEADS):
-        out_out[quarter * half : (quarter + 1) * half, :] = early[
-            quarter, nine + 3 * half : nine + 4 * half, :
-        ].astype(jnp.float32)
-        sums.append(early[quarter, nine + 4 * half : nine + 4 * half + 16].astype(jnp.float32))
+    one, two, qkv_rows, qkv_out, out_out, time_out, small, norm_one, sems, out_sems = refs[25:]
+    channels = one.shape[1]
+    half = channels // HEADS
+    unit = half // 4
+    lines = 18 * unit + half + 16
+    spot = lax.axis_index("row")
+    head, column = spot % HEADS, lax.axis_index("img")
+    leaving = []
+    for index, part in enumerate(parts):
+        away = column ^ (index // 2)
+        for pair in range(2):
+            quarter, base = head ^ (index % 2 + 2 * pair), pair * lines
+            first = pl.multiple_of(quarter * half + away * unit, unit)
+            at = pl.ds(first, unit)
+            shape = (9, unit, channels)
+            late = base + 9 * unit + half
+            two[:, at, :] = part[base : base + 9 * unit].astype(jnp.float32).reshape(shape)
+            one[:, at, :] = part[late : late + 9 * unit].astype(jnp.float32).reshape(shape)
+            here = len(leaving)
+            leaving += started(
+                sems.at[here : here + 2],
+                (two.at[:, at, :], two_far.at[:, at, :]),
+                (one.at[:, at, :], one_far.at[:, at, :]),
+            )
+            middle = base + 9 * unit
+            for k in range(3):
+                to = pl.ds(pl.multiple_of(first + k * channels, unit), unit)
+                piece = part[middle + k * unit : middle + (k + 1) * unit]
+                qkv_rows[to, :] = piece.astype(jnp.float32)
+            out_out[at, :] = part[middle + 3 * unit : middle + half].astype(jnp.float32)
+            small[quarter, away] = part[base + lines - 16 : base + lines].astype(jnp.float32)
+    for part in range(3):
+        across = slice(part * channels, (part + 1) * channels)
+        qkv_out[:, across] = jnp.transpose(qkv_rows[across, :])
+    leaving += started(out_sems, (qkv_out, qkv_far), (out_out, out_far))
+    sums = [small[quarter, 2] for quarter in range(HEADS)]
     pieces = [part[0:1, :half] for part in sums] + [part[0:1, 3 * half :] for part in sums]
     bias_out[...] = jnp.concatenate(pieces, axis=1).reshape(bias_out.shape)
-    for part in range(3):
-        block = jnp.concatenate(
-            [
-                early[quarter, nine + part * half : nine + (part + 1) * half, :]
-                for quarter in range(HEADS)
-            ],
-            axis=0,
-        )
-        width = HEADS * half
-        qkv_out[:, part * width : (part + 1) * width] = jnp.transpose(block.astype(jnp.float32))
-    leaving += started(out_sems.at[2:4], (qkv_out, qkv_far), (out_out, out_far))
-    column = lax.axis_index("img")
-    lines = (early.shape[1] + late.shape[1]) // 2
     for step in range(4):
-        norm_one[column ^ step] = parts[2 * step][lines : lines + 16, :].astype(jnp.float32)
+        norm_one[column ^ step] = parts[2 * step][2 * lines : 2 * lines + 16].astype(jnp.float32)
     total = norm_one[0] + norm_one[1] + norm_one[2] + norm_one[3]
-    rest = late[0, nine:, :]
-    whole = jnp.concatenate([total[0:2], rest[0:16, :].astype(jnp.float32)[0:7]], axis=0)
+    whole = jnp.concatenate([total[0:2], small[0, 0, 0:7, :]], axis=0)
     for k, row in enumerate(rows):
         row[...] = whole[k : k + 1].reshape(row.shape)
-    shifts = rest[16:32, :].astype(jnp.float32)
+    shifts = small[0, 1]
     pair = jnp.concatenate([shifts[k : k + 1, :] for k in range(0, 16, 2)], axis=0)
     other = jnp.concatenate([shifts[k : k + 1, :] for k in range(1, 16, 2)], axis=0)
     both = jnp.concatenate([pair, other], axis=1)
@@ -1168,7 +1225,7 @@
         terms.astype(jnp.bfloat16), both, (((0,), (0,)), ((), ())),
         preferred_element_type=jnp.float32,
     )
-    leaving += started(out_sems.at[4:5], (time_out, time_far))
+    leaving += started(out_sems.at[2:3], (time_out, time_far))
     finish_all(leaving)
 
 
@@ -1236,9 +1293,7 @@
     if after is not None:
         sent = lax.optimization_barrier((*sent, after))[:3]
     odd = [swap(block, "row", 1) for block in sent]
-    return [
-        blocks[0], blocks[1], blocks[2], odd[0], blocks[4], odd[1], blocks[6], odd[2],
-    ]
+    return odd, [blocks[step] for step in ARRIVAL[3:]]
 
 
 def local_image(
@@ -1306,7 +1361,7 @@
             conv2_weight,
         ],
     )
-    field = relayed(field, vec)
+    field_late, field = relayed(field, vec)
     w_one, w_two = conv1_weight.reshape(kernel_shape), conv2_weight.reshape(kernel_shape)
     rim_cells = cells + 2 * cols
     cost = 9 * cells * channels * channels // 2
@@ -1324,24 +1379,35 @@
         28,
         cost * 25,
         [],
-        [vec],
+        [vec, *field_late],
         [*field, w_one, w_two],
     )
-    grads = relayed(grads, act_three)
+    grads_late, grads = relayed(grads, act_three)
     query_shape, head_shape = (cells // 2, lanes), (cells, lanes)
+    query_only, key_pad, value_pad, sizes = call(
+        project_kernel,
+        [(head_shape, low), (head_shape, low), (head_shape, low), ((8, lanes), full)],
+        [],
+        [],
+        12,
+        cost * 2,
+        [],
+        [act_three, w_heads, biases],
+        [],
+    )
     value_key, query_part, grad_proj, mixed, out_sums = call(
         functools.partial(attention_kernel, cols),
         [],
         [(head_shape, low), (query_shape, low), (wide, low), (head_shape, low), rows_eight],
         [
             (wide, low), (wide, low), (head_shape, low), (query_shape, low), rows_eight,
-            (head_shape, low), (head_shape, low), (head_shape, low), ((lanes, cells), full),
-            (head_shape, low), ((1, cells), full), sems(8), sems(5),
+            (head_shape, low), ((lanes, cells), full), (head_shape, low), ((1, cells), full),
+            sems(8), sems(5),
         ],
         36,
         cost * 34,
         [],
-        [vec, act_three, w_heads, w_out, biases],
+        [vec, query_only, key_pad, value_pad, sizes, w_out, *grads_late],
         grads,
     )
 
@@ -1352,10 +1418,10 @@
     own_one, own_two, weight_rows, *sends = call(
         aside_kernel,
         [],
-        [(own_shape, low), (own_shape, low), ((5 * half, channels), low)],
+        [(own_shape, low), (own_shape, low), ((4, half + 16, channels), low)],
         [
             ((2,) + wide, low), (head_shape, low), (head_shape, low), (wide, low), (wide, low),
-            ((rim_cells, 3 * half), full), ((2,) + own_shape, low), ((5 * half, channels), low),
+            ((rim_cells, 3 * half), full), ((2,) + own_shape, low), ((4, half + 16, channels), low),
             sems(6), sems(3),
         ],
         28,
@@ -1366,12 +1432,9 @@
         [send_shape] * 4,
     )
     key_near, query_near, own_two = lax.optimization_barrier((key_near, query_near, own_two))
-    packed_all = [
-        value_key, query_part, key_mate, query_mate,
-        key_near, query_near, swap(key_near, "row", 1), swap(query_near, "row", 1),
-    ]
-    early_lines, late_lines = 14 * half // 4, 10 * half // 4
-    lines = early_lines + late_lines
+    relays = [key_mate, query_mate, swap(key_near, "row", 1), swap(query_near, "row", 1)]
+    packed = [value_key, query_part, key_near, query_near]
+    lines = 18 * (half // 4) + half + 16
     shifted_one, grad_res, *payload = call(
         middle_kernel,
         [(tall, low)],
@@ -1379,16 +1442,15 @@
         [
             ((HEADS,) + head_shape, low), ((HEADS,) + query_shape, low),
             (wide, low), (wide, full), rows_eight, (own_shape, low), (wide, full),
-            ((14 * half, channels), low), (wide, full), (tall, low), (kernel_shape, low),
-            (wide, full), (own_shape, low), rows_eight, ((10 * half, channels), low),
-            sems(17), sems(9),
+            ((4, lines, channels), low), (wide, full), (tall, low), (kernel_shape, low),
+            (wide, full), (own_shape, low), rows_eight, sems(18), sems(5),
         ],
         40,
         cost * 26,
         [],
-        [vec, qkv_t],
+        [vec, qkv_t, *relays],
         [
-            *packed_all, grad_proj, residual, stats, own_two, weight_rows, w_two_back, conv_one,
+            *packed, grad_proj, residual, stats, own_two, weight_rows, w_two_back, conv_one,
             own_one, out_sums,
         ],
     )
@@ -1433,7 +1495,7 @@
     pair = jnp.concatenate([both, other, norm_one], axis=0)
     parts = gather_columns(pair)
     line = ((channels,), full)
-    kernel_out = ((3, 3, channels, channels), full)
+    kernel_out = ((9, channels, channels), full)
     time_out = ((time_weight.shape[0], 2 * channels), full)
     qkv_out, out_out = ((channels, 3 * channels), full), ((channels, channels), full)
     half_time = time_weight.shape[0] // 2
@@ -1446,8 +1508,8 @@
         [],
         [kernel_out, kernel_out, qkv_out, out_out, time_out],
         [
-            ((HEADS, 14 * half, channels), low), ((HEADS, 10 * half, channels), low),
-            ((4, 16, channels), full), kernel_out, kernel_out, qkv_out, out_out, time_out, sems(5),
+            kernel_out, kernel_out, ((3 * channels, channels), full), qkv_out, out_out, time_out,
+            ((HEADS, 4, 16, channels), full), ((4, 16, channels), full), sems(32), sems(3),
         ],
         28,
         cost,
@@ -1463,13 +1525,13 @@
         finished[1],
         norm1_gain_grad,
         norm1_bias_grad,
-        conv1_weight_grad,
+        conv1_weight_grad.reshape(conv1_weight.shape),
         conv1_bias_grad,
         time_weight_grad,
         time_bias_grad,
         norm2_gain_grad,
         norm2_bias_grad,
-        conv2_weight_grad,
+        conv2_weight_grad.reshape(conv2_weight.shape),
         conv2_bias_grad,
         norm3_gain_grad,
         norm3_bias_grad,

time: 156 us -> 148 us (0.949)
  waiting for transfers between devices: 39.3 us -> 35.8 us
  Pallas kernels: 76 us -> 73.4 us
  local copies, waits for them, and re-layouts: 3.99 us -> 1.81 us
    ppermute x37, waiting for transfers between devices: 39.3 us -> 35.8 us  [swap(): return lax.ppermute(value, axis, [(k, k ^ step) for k in range(count)])]
    pallas_call x8 -> x9, Pallas kernels: 76 us -> 73.4 us  [call(): pl.pallas_call(kernel, out_shape=[jax.ShapeDtypeStruct(*kind) for kind in...]
    unnamed x58 -> x36, local copies, waits for them, and re-layouts: 2.88 us -> 0.7 us
  transfers between devices with their start and end apart: 37 -> 37, of which waited for: 15 -> 13; matrix products, arithmetic and copies ran while one was open for 4% -> 4% of each run, Pallas kernels for 25% -> 27%
where the time goes in v4:
time: 148 us
  Pallas kernels  73.4 us (50%)
  waiting for transfers between devices  35.8 us (24%)
  starting transfers between devices  29.2 us (20%)
  other arithmetic  5.95 us (4%)
  local copies, waits for them, and re-layouts  1.81 us (1%)
    pallas_call x9, Pallas kernels, call(): pl.pallas_call(kernel, out_shape=[jax.ShapeDtypeStruct(*kind) for kind in...  73.4 us
    ppermute x37, waiting for transfers between devices, swap(): return lax.ppermute(value, axis, [(k, k ^ step) for k in range(count)])  35.8 us
    ppermute x37, starting transfers between devices, swap(): return lax.ppermute(value, axis, [(k, k ^ step) for k in range(count)])  29.2 us
  transfers between devices with their start and end apart: 37, of which 13 were waited for; matrix products, arithmetic and copies ran while one was open for 4% of the time, Pallas kernels for 27%

profile of v4, /device:TPU:0, one launch (start us, length us, event | category | flops | bytes accessed | tf_op | source)
XLA Modules:
  0.0 147.9 jit_solution(1426222513661285179)
XLA Ops:
  0.7 1.1 dynamic-slice_bitcast_fusion
  1.8 4.1 %collective-permute-start.1 = (bf16[256,256]{1,0:T(8,128)(2,1)S(1)}, bf16[256,256]{1,0:T(8,128)(2,1)S(1)}, u32[]{:S(2)}, u32[]{:S(2)}) collective-permute-start(bf16[256,256]{1,0:T(8,128)(2,1)S(1)} %get-tuple-element.184), channel_id=1, source_target_pairs={{0,4},{1,5},{2,6},{3,7},{4,0},{5,1},{6,2},{7,3},{8,12},{9,13},{10,... | collective-permute-start | bytes 393224 | tf_op jit(solution)/shard_map/ppermute | solution.py:1234
  5.9 1.3 collective-permute-start.2
  7.5 0.7 convert_element_type.41
  8.2 0.7 convert_element_type.42
  9.0 0.5 convolution_add_fusion.refs_0_
  9.5 4.8 %shard_map.331 = (f32[16,256]{1,0:T(8,128)S(1)}, bf16[256,384]{1,0:T(8,128)(2,1)S(1)}, bf16[256,128]{1,0:T(8,128)(2,1)S(1)}, f32[8,384]{1,0:T(8,128)S(1)}, bf16[...) custom-call(f32[2,512]{1,0:T(2,128)S(1)} %convolution_add_fusion.refs_0_, ...), custom_call_target="tpu_custom_call" | custom-call | flops 256 | bytes 2893328 | tf_op jit(solution)/shard_map/pallas_call | solution.py:1265
  14.3 1.5 %collective-permute-done.1.refs_6_ = bf16[256,256]{1,0:T(8,128)(2,1)S(1)} collective-permute-done((bf16[256,256]{1,0:T(8,128)(2,1)S(1)}, bf16[256,256]{1,0:T(8,128)(2,1)S(1)}, u32[]{:S(2)}, u32[]{:S(2)}) %collective-permute-start.1) | collective-permute-done | bytes 131104 | tf_op jit(solution)/shard_map/ppermute | solution.py:1234
  15.9 0.5 collective-permute-done.refs_5_
  16.4 0.5 collective-permute-start.4
  16.9 4.2 %collective-permute-start.8 = (bf16[256,256]{1,0:T(8,128)(2,1)S(1)}, bf16[256,256]{1,0:T(8,128)(2,1)S(1)}, u32[]{:S(2)}, u32[]{:S(2)}) collective-permute-start(bf16[256,256]{1,0:T(8,128)(2,1)S(1)} %get-tuple-element.116), channel_id=1, source_target_pairs={{0,4},{1,5},{2,6},{3,7},{4,0},{5,1},{6,2},{7,3},{8,12},{9,13},{10,... | collective-permute-start | bytes 393224 | tf_op jit(solution)/shard_map/ppermute | solution.py:1234
  21.2 0.4 collective-permute-start.9
  21.9 10.8 %shard_map.332 = (bf16[2048,256]{1,0:T(8,128)(2,1)S(1)}, bf16[2048,256]{1,0:T(8,128)(2,1)}, f32[2048,256]{1,0:T(8,128)}, f32[2048,256]{1,0:T(8,128)}, bf16[2048,...) custom-call(f32[16,256]{1,0:T(8,128)S(1)} %get-tuple-element.99.vec, ...), custom_call_target="tpu_custom_call" | custom-call | flops 15099494400 | bytes 3424256 | tf_op jit(solution)/shard_map/pallas_call | solution.py:1265
  32.7 0.6 collective-permute-start.10
  33.4 0.4 collective-permute-start.12
  33.8 1.7 %shard_map.333 = (bf16[2048,128]{1,0:T(8,128)(2,1)S(1)}, bf16[2048,128]{1,0:T(8,128)(2,1)S(1)}, bf16[2048,128]{1,0:T(8,128)(2,1)S(1)}, f32[8,128]{1,0:T(8,128)S(1)}) custom-call(bf16[2048,256]{1,0:T(8,128)(2,1)S(1)} %get-tuple-element.107.act_three.refs_4_, bf16[256,384]{1,0:T(8,128)(2,1)S(1)} %get-tuple-element.108.w_heads, ...), custom_call_target="tpu_custom_call" | custom-call | flops 1207959552 | bytes 1257472 | tf_op jit(solution)/shard_map/pallas_call | solution.py:1265
  35.6 0.6 copy-done.17
  36.2 17.4 %shard_map.334 = (bf16[2048,128]{1,0:T(8,128)(2,1)}, bf16[1024,128]{1,0:T(8,128)(2,1)}, bf16[2048,256]{1,0:T(8,128)(2,1)}, bf16[2048,128]{1,0:T(8,128)(2,1)}, f32[8,256]{1,0:T(8,128)}) custom-call(f32[16,256]{1,0:T(8,128)S(1)} %get-tuple-element.99.vec, bf16[2048,128]{1,0:T(8,128)(2,1)S(1)} %get-tuple-element.110.query_only, ...), custom_call_target="tpu_custom_call" | custom-call | flops 20535312384 | bytes 2707456 | tf_op jit(solution)/shard_map/pallas_call | solution.py:1265
  53.7 1.8 %collective-permute-start.16 = (bf16[2048,128]{1,0:T(8,128)(2,1)}, bf16[2048,128]{1,0:T(8,128)(2,1)S(1)}, u32[]{:S(2)}, u32[]{:S(2)}) collective-permute-start(bf16[2048,128]{1,0:T(8,128)(2,1)} %get-tuple-element.121.refs_3_.refs_4_), channel_id=1, source_target_pairs={{0,2},{1,3},{2,0},{3,1},{4,6},{5,7},{6,4},{7,5},{8,10},{9,11},{10,... | collective-permute-start | bytes 1572872 | tf_op jit(solution)/shard_map/ppermute | solution.py:1234
  55.7 13.9 %shard_map.335 = (bf16[3,192,2048]{2,1,0:T(8,128)(2,1)}, bf16[3,192,2048]{2,1,0:T(8,128)(2,1)}, bf16[4,80,256]{2,1,0:T(8,128)(2,1)}, bf16[256,128]{1,0:T(8,128)(...) custom-call(f32[16,256]{1,0:T(8,128)S(1)} %get-tuple-element.99.vec, ...), custom_call_target="tpu_custom_call" | custom-call | flops 16307453952 | bytes 5259264 | tf_op jit(solution)/shard_map/pallas_call | solution.py:1265
  69.6 4.2 %collective-permute-done.17.refs_7_ = bf16[1024,128]{1,0:T(8,128)(2,1)S(1)} collective-permute-done((bf16[1024,128]{1,0:T(8,128)(2,1)}, bf16[1024,128]{1,0:T(8,128)(2,1)S(1)}, u32[]{:S(2)}, u32[]{:S(2)}) %collective-permute-start.17) | collective-permute-done | bytes 262176 | tf_op jit(solution)/shard_map/ppermute | solution.py:1234
  73.9 0.5 collective-permute-start.15
  74.5 1.7 %collective-permute-done.15.refs_1_ = bf16[1024,128]{1,0:T(8,128)(2,1)S(1)} collective-permute-done((bf16[1024,128]{1,0:T(8,128)(2,1)S(1)}, bf16[1024,128]{1,0:T(8,128)(2,1)S(1)}, u32[]{:S(2)}, u32[]{:S(2)}) %collective-permute-start.15) | collective-permute-done | bytes 262176 | tf_op jit(solution)/shard_map/ppermute | solution.py:1234
  76.6 10.9 %shard_map.336 = (bf16[2176,768]{1,0:T(8,128)(2,1)S(1)}, f32[2048,256]{1,0:T(8,128)}, bf16[368,256]{1,0:T(8,128)(2,1)}, bf16[368,256]{1,0:T(8,128)(2,1)}, bf16[3...) custom-call(f32[16,256]{1,0:T(8,128)S(1)} %get-tuple-element.99.vec, bf16[12,64,256]{2,1,0:T(8,128)(2,1)S(1)} %get-tuple-element.127.qkv_t, ...), custom_call_target="tpu_custom_call" | custom-call | flops 15703474176 | bytes 14876672 | tf_op jit(solution)/shard_map/pallas_call | solution.py:1265
  87.5 2.5 %collective-permute-start.22 = (bf16[368,256]{1,0:T(8,128)(2,1)}, bf16[368,256]{1,0:T(8,128)(2,1)S(1)}, u32[]{:S(2)}, u32[]{:S(2)}) collective-permute-start(bf16[368,256]{1,0:T(8,128)(2,1)} %get-tuple-element.145), channel_id=1, source_target_pairs={{0,24},{8,16},{16,8},{24,0},{1,25},{9,17},{17,9},{25,1},{2,26},{10... | collective-permute-start | bytes 565256 | tf_op jit(solution)/shard_map/ppermute | solution.py:1234
  90.0 0.5 collective-permute-start.21
  90.5 0.5 collective-permute-start.20
  91.0 1.8 %collective-permute-start.24 = (bf16[256,128]{1,0:T(8,128)(2,1)S(1)}, bf16[256,128]{1,0:T(8,128)(2,1)S(1)}, u32[]{:S(2)}, u32[]{:S(2)}) collective-permute-start(bf16[256,128]{1,0:T(8,128)(2,1)S(1)} %get-tuple-element.148), channel_id=1, source_target_pairs={{0,2},{1,3},{2,0},{3,1},{4,6},{5,7},{6,4},{7,5},{8,10},{9,11},{10,... | collective-permute-start | bytes 196616 | tf_op jit(solution)/shard_map/ppermute | solution.py:1234
  92.8 3.5 %collective-permute-done.22 = bf16[368,256]{1,0:T(8,128)(2,1)S(1)} collective-permute-done((bf16[368,256]{1,0:T(8,128)(2,1)}, bf16[368,256]{1,0:T(8,128)(2,1)S(1)}, u32[]{:S(2)}, u32[]{:S(2)}) %collective-permute-start.22) | collective-permute-done | bytes 188448 | tf_op jit(solution)/shard_map/ppermute | solution.py:1234
  96.3 3.2 %collective-permute-done.21 = bf16[368,256]{1,0:T(8,128)(2,1)S(1)} collective-permute-done((bf16[368,256]{1,0:T(8,128)(2,1)}, bf16[368,256]{1,0:T(8,128)(2,1)S(1)}, u32[]{:S(2)}, u32[]{:S(2)}) %collective-permute-start.21) | collective-permute-done | bytes 188448 | tf_op jit(solution)/shard_map/ppermute | solution.py:1234
  99.5 1.0 add_convert_fusion.1
  100.6 3.8 %collective-permute-start.27 = (bf16[368,256]{1,0:T(8,128)(2,1)S(1)}, bf16[368,256]{1,0:T(8,128)(2,1)S(1)}, u32[]{:S(2)}, u32[]{:S(2)}) collective-permute-start(bf16[368,256]{1,0:T(8,128)(2,1)S(1)} %add_convert_fusion.1), channel_id=1, source_target_pairs={{0,4},{1,5},{2,6},{3,7},{4,0},{5,1},{6,2},{7,3},{8,12},{9,13},{10,... | collective-permute-start | bytes 565256 | tf_op jit(solution)/shard_map/ppermute | solution.py:1234
  104.4 6.7 %shard_map.338 = (bf16[256,256]{1,0:T(8,128)(2,1)}, bf16[256,256]{1,0:T(8,128)(2,1)}, f32[8,256]{1,0:T(8,128)}) custom-call(f32[16,256]{1,0:T(8,128)S(1)} %get-tuple-element.99.vec, bf16[2176,768]{1,0:T(8,128)(2,1)S(1)} %get-tuple-element.155.shifted, bf16[3,768,256]{2,1,0:T(8,128)(2,1)} %get-tuple-element.156.weight_far, ...), custom_call_target="tpu_custom_call" | custom-call | flops 7247757312 | bytes 7692288 | tf_op jit(solution)/shard_map/pallas_call | solution.py:1265
  111.2 0.7 convert.4
  111.9 1.3 collective-permute-done.27
  113.4 3.1 %collective-permute-done.29 = bf16[16,256]{1,0:T(8,128)(2,1)S(1)} collective-permute-done((bf16[16,256]{1,0:T(8,128)(2,1)S(1)}, bf16[16,256]{1,0:T(8,128)(2,1)S(1)}, u32[]{:S(2)}, u32[]{:S(2)}) %collective-permute-start.29) | collective-permute-done | bytes 8224 | tf_op jit(solution)/shard_map/ppermute | solution.py:1234
  116.6 3.5 %collective-permute-done.28 = bf16[368,256]{1,0:T(8,128)(2,1)S(1)} collective-permute-done((bf16[368,256]{1,0:T(8,128)(2,1)S(1)}, bf16[368,256]{1,0:T(8,128)(2,1)S(1)}, u32[]{:S(2)}, u32[]{:S(2)}) %collective-permute-start.28) | collective-permute-done | bytes 188448 | tf_op jit(solution)/shard_map/ppermute | solution.py:1234
  120.0 1.6 %collective-permute-start.31 = (bf16[752,256]{1,0:T(8,128)(2,1)S(1)}, bf16[752,256]{1,0:T(8,128)(2,1)S(1)}, u32[]{:S(2)}, u32[]{:S(2)}) collective-permute-start(bf16[752,256]{1,0:T(8,128)(2,1)S(1)} %pad_maximum_fusion.refs_0_), channel_id=1, source_target_pairs={{0,8},{8,0},{16,24},{24,16},{1,9},{9,1},{17,25},{25,17},{2,10},{10... | collective-permute-start | bytes 1155080 | tf_op jit(solution)/shard_map/ppermute | solution.py:1234
  121.7 1.9 %collective-permute-start.35 = (bf16[752,256]{1,0:T(8,128)(2,1)S(1)}, bf16[752,256]{1,0:T(8,128)(2,1)S(1)}, u32[]{:S(2)}, u32[]{:S(2)}) collective-permute-start(bf16[752,256]{1,0:T(8,128)(2,1)S(1)} %pad_maximum_fusion.refs_0_), channel_id=1, source_target_pairs={{0,24},{8,16},{16,8},{24,0},{1,25},{9,17},{17,9},{25,1},{2,26},{10... | collective-permute-start | bytes 1155080 | tf_op jit(solution)/shard_map/ppermute | solution.py:1234
  123.6 1.5 %shard_map.337 = (bf16[256,256]{1,0:T(8,128)(2,1)S(1)}, bf16[256,256]{1,0:T(8,128)(2,1)S(1)}) custom-call(f32[16,256]{1,0:T(8,128)S(1)} %get-tuple-element.99.vec, bf16[4,64,256]{2,1,0:T(8,128)(2,1)S(1)} %bitcast.26, bf16[256,128]{1,0:T(8,128)(2,1)S(1)} %get-tuple-element.150.refs_0_, bf16[256,128]{1,0:T(8,128)(2,1)S(1)} %collective-permute-done.23.refs_1_, ...), custom_call_target="tpu_custom_call" | custom-call | flops 603979776 | bytes 2506752 | tf_op jit(solution)/shard_map/pallas_call | solution.py:1265
  125.1 0.7 pad_maximum_fusion.3
  125.9 0.9 collective-permute-start.26
  126.8 5.2 %collective-permute-done.31.refs_2_ = bf16[752,256]{1,0:T(8,128)(2,1)S(1)} collective-permute-done((bf16[752,256]{1,0:T(8,128)(2,1)S(1)}, bf16[752,256]{1,0:T(8,128)(2,1)S(1)}, u32[]{:S(2)}, u32[]{:S(2)}) %collective-permute-start.31) | collective-permute-done | bytes 385056 | tf_op jit(solution)/shard_map/ppermute | solution.py:1234
  132.0 7.6 %collective-permute-done.33.refs_4_ = bf16[752,256]{1,0:T(8,128)(2,1)S(1)} collective-permute-done((bf16[752,256]{1,0:T(8,128)(2,1)S(1)}, bf16[752,256]{1,0:T(8,128)(2,1)S(1)}, u32[]{:S(2)}, u32[]{:S(2)}) %collective-permute-start.33) | collective-permute-done | bytes 385056 | tf_op jit(solution)/shard_map/ppermute | solution.py:1234
  139.6 0.5 collective-permute-start.36
  140.1 1.0 select_bitcast_fusion
  141.1 0.8 pad_maximum_fusion.1
  142.0 5.8 %shard_map.339 = (f32[9,256,256]{2,1,0:T(8,128)}, f32[9,256,256]{2,1,0:T(8,128)}, f32[256,768]{1,0:T(8,128)}, f32[256,256]{1,0:T(8,128)}, f32[1024,512]{1,0:T(8,...) custom-call(bf16[752,256]{1,0:T(8,128)(2,1)S(1)} %pad_maximum_fusion, ...), custom_call_target="tpu_custom_call" | custom-call | flops 603979776 | bytes 3082240 | tf_op jit(solution)/shard_map/pallas_call | solution.py:1265
  (88 shorter events, 2.2 us)
Async XLA Ops:
  0.7 8.3 %copy-start = (bf16[1024,512]{1,0:T(8,128)(2,1)S(1)}, bf16[1024,512]{1,0:T(8,128)(2,1)}, u32[]{:S(2)}) copy-start(bf16[1024,512]{1,0:T(8,128)(2,1)} %param.27) | copy-start | bytes 3145732
  1.8 12.6 %copy-start.5 = (bf16[256,256]{1,0:T(8,128)(2,1)}, bf16[256,256]{1,0:T(8,128)(2,1)S(1)}, u32[]{:S(2)}) copy-start(bf16[256,256]{1,0:T(8,128)(2,1)S(1)} %get-tuple-element.185.refs_3_) | copy-start | bytes 393220
  1.8 12.5 %copy-start.3 = (bf16[2,4,64,256]{3,2,1,0:T(8,128)(2,1)S(1)}, bf16[2,4,64,256]{3,2,1,0:T(8,128)(2,1)}, u32[]{:S(2)}) copy-start(bf16[2,4,64,256]{3,2,1,0:T(8,128)(2,1)} %param.39) | copy-start | bytes 786436
  1.8 14.1 %collective-permute-start.1 = (bf16[256,256]{1,0:T(8,128)(2,1)S(1)}, bf16[256,256]{1,0:T(8,128)(2,1)S(1)}, u32[]{:S(2)}, u32[]{:S(2)}) collective-permute-start(bf16[256,256]{1,0:T(8,128)(2,1)S(1)} %get-tuple-element.184), channel_id=1, source_target_pairs={{0,4},{1,5},{2,6},{3,7},{4,0},{5,1},{6,2},{7,3},{8,12},{9,13},{10,... | collective-permute-start | bytes 393224 | tf_op jit(solution)/shard_map/ppermute | solution.py:1234
  5.9 10.0 %collective-permute-start.2 = (bf16[256,256]{1,0:T(8,128)(2,1)S(1)}, bf16[256,256]{1,0:T(8,128)(2,1)S(1)}, u32[]{:S(2)}, u32[]{:S(2)}) collective-permute-start(bf16[256,256]{1,0:T(8,128)(2,1)S(1)} %get-tuple-element.184), channel_id=1, source_target_pairs={{0,6},{1,7},{2,4},{3,5},{4,2},{5,3},{6,0},{7,1},{8,14},{9,15},{10,... | collective-permute-start | bytes 393224 | tf_op jit(solution)/shard_map/ppermute | solution.py:1234
  7.2 9.2 %collective-permute-start = (bf16[256,256]{1,0:T(8,128)(2,1)S(1)}, bf16[256,256]{1,0:T(8,128)(2,1)S(1)}, u32[]{:S(2)}, u32[]{:S(2)}) collective-permute-start(bf16[256,256]{1,0:T(8,128)(2,1)S(1)} %get-tuple-element.185.refs_3_), channel_id=1, source_target_pairs={{0,2},{1,3},{2,0},{3,1},{4,6},{5,7},{6,4},{7,5},{8,10},{9,11},{10,... | collective-permute-start | bytes 393224 | tf_op jit(solution)/shard_map/ppermute | solution.py:1234
  7.5 13.7 %collective-permute-start.6 = (bf16[256,256]{1,0:T(8,128)(2,1)S(1)}, bf16[256,256]{1,0:T(8,128)(2,1)S(1)}, u32[]{:S(2)}, u32[]{:S(2)}) collective-permute-start(bf16[256,256]{1,0:T(8,128)(2,1)S(1)} %get-tuple-element.185.refs_3_), channel_id=1, source_target_pairs={{0,1},{1,0},{2,3},{3,2},{4,5},{5,4},{6,7},{7,6},{8,9},{9,8},{10,11... | collective-permute-start | bytes 393224 | tf_op jit(solution)/shard_map/ppermute | solution.py:1234
  14.3 18.3 %copy-start.4 = (bf16[256,256]{1,0:T(8,128)(2,1)}, bf16[256,256]{1,0:T(8,128)(2,1)S(1)}, u32[]{:S(2)}) copy-start(bf16[256,256]{1,0:T(8,128)(2,1)S(1)} %get-tuple-element.115.refs_3_) | copy-start | bytes 393220
  15.9 5.9 %copy-start.10 = (bf16[256,256]{1,0:T(8,128)(2,1)}, bf16[256,256]{1,0:T(8,128)(2,1)S(1)}, u32[]{:S(2)}) copy-start(bf16[256,256]{1,0:T(8,128)(2,1)S(1)} %collective-permute-done.1.refs_6_) | copy-start | bytes 393220
  15.9 5.9 %copy-start.11 = (bf16[256,256]{1,0:T(8,128)(2,1)}, bf16[256,256]{1,0:T(8,128)(2,1)S(1)}, u32[]{:S(2)}) copy-start(bf16[256,256]{1,0:T(8,128)(2,1)S(1)} %collective-permute-done.2.refs_7_) | copy-start | bytes 393220
  16.4 5.4 %copy-start.12 = (bf16[256,256]{1,0:T(8,128)(2,1)}, bf16[256,256]{1,0:T(8,128)(2,1)S(1)}, u32[]{:S(2)}) copy-start(bf16[256,256]{1,0:T(8,128)(2,1)S(1)} %collective-permute-done.refs_5_) | copy-start | bytes 393220
  16.4 5.1 %collective-permute-start.3 = (bf16[256,256]{1,0:T(8,128)(2,1)S(1)}, bf16[256,256]{1,0:T(8,128)(2,1)S(1)}, u32[]{:S(2)}, u32[]{:S(2)}) collective-permute-start(bf16[256,256]{1,0:T(8,128)(2,1)S(1)} %collective-permute-done.refs_5_), channel_id=1, source_target_pairs={{0,1},{1,0},{2,3},{3,2},{4,5},{5,4},{6,7},{7,6},{8,9},{9,8},{10,11... | collective-permute-start | bytes 393224 | tf_op jit(solution)/shard_map/ppermute | solution.py:1234
  16.4 5.4 %collective-permute-start.4 = (bf16[256,256]{1,0:T(8,128)(2,1)S(1)}, bf16[256,256]{1,0:T(8,128)(2,1)S(1)}, u32[]{:S(2)}, u32[]{:S(2)}) collective-permute-start(bf16[256,256]{1,0:T(8,128)(2,1)S(1)} %collective-permute-done.1.refs_6_), channel_id=1, source_target_pairs={{0,1},{1,0},{2,3},{3,2},{4,5},{5,4},{6,7},{7,6},{8,9},{9,8},{10,11... | collective-permute-start | bytes 393224 | tf_op jit(solution)/shard_map/ppermute | solution.py:1234
  16.9 4.9 %collective-permute-start.5 = (bf16[256,256]{1,0:T(8,128)(2,1)S(1)}, bf16[256,256]{1,0:T(8,128)(2,1)S(1)}, u32[]{:S(2)}, u32[]{:S(2)}) collective-permute-start(bf16[256,256]{1,0:T(8,128)(2,1)S(1)} %collective-permute-done.2.refs_7_), channel_id=1, source_target_pairs={{0,1},{1,0},{2,3},{3,2},{4,5},{5,4},{6,7},{7,6},{8,9},{9,8},{10,11... | collective-permute-start | bytes 393224 | tf_op jit(solution)/shard_map/ppermute | solution.py:1234
  16.9 15.8 %collective-permute-start.8 = (bf16[256,256]{1,0:T(8,128)(2,1)S(1)}, bf16[256,256]{1,0:T(8,128)(2,1)S(1)}, u32[]{:S(2)}, u32[]{:S(2)}) collective-permute-start(bf16[256,256]{1,0:T(8,128)(2,1)S(1)} %get-tuple-element.116), channel_id=1, source_target_pairs={{0,4},{1,5},{2,6},{3,7},{4,0},{5,1},{6,2},{7,3},{8,12},{9,13},{10,... | collective-permute-start | bytes 393224 | tf_op jit(solution)/shard_map/ppermute | solution.py:1234
  21.2 11.5 %collective-permute-start.9 = (bf16[256,256]{1,0:T(8,128)(2,1)S(1)}, bf16[256,256]{1,0:T(8,128)(2,1)S(1)}, u32[]{:S(2)}, u32[]{:S(2)}) collective-permute-start(bf16[256,256]{1,0:T(8,128)(2,1)S(1)} %get-tuple-element.116), channel_id=1, source_target_pairs={{0,6},{1,7},{2,4},{3,5},{4,2},{5,3},{6,0},{7,1},{8,14},{9,15},{10,... | collective-permute-start | bytes 393224 | tf_op jit(solution)/shard_map/ppermute | solution.py:1234
  21.6 11.1 %collective-permute-start.7 = (bf16[256,256]{1,0:T(8,128)(2,1)S(1)}, bf16[256,256]{1,0:T(8,128)(2,1)S(1)}, u32[]{:S(2)}, u32[]{:S(2)}) collective-permute-start(bf16[256,256]{1,0:T(8,128)(2,1)S(1)} %get-tuple-element.115.refs_3_), channel_id=1, source_target_pairs={{0,2},{1,3},{2,0},{3,1},{4,6},{5,7},{6,4},{7,5},{8,10},{9,11},{10,... | collective-permute-start | bytes 393224 | tf_op jit(solution)/shard_map/ppermute | solution.py:1234
  21.8 13.7 %collective-permute-start.13 = (bf16[256,256]{1,0:T(8,128)(2,1)S(1)}, bf16[256,256]{1,0:T(8,128)(2,1)S(1)}, u32[]{:S(2)}, u32[]{:S(2)}) collective-permute-start(bf16[256,256]{1,0:T(8,128)(2,1)S(1)} %get-tuple-element.115.refs_3_), channel_id=1, source_target_pairs={{0,1},{1,0},{2,3},{3,2},{4,5},{5,4},{6,7},{7,6},{8,9},{9,8},{10,11... | collective-permute-start | bytes 393224 | tf_op jit(solution)/shard_map/ppermute | solution.py:1234
  32.6 2.8 %copy-start.2 = (bf16[2048,256]{1,0:T(8,128)(2,1)}, bf16[2048,256]{1,0:T(8,128)(2,1)S(1)}, u32[]{:S(2)}) copy-start(bf16[2048,256]{1,0:T(8,128)(2,1)S(1)} %get-tuple-element.107.act_three.refs_4_) | copy-start | bytes 3145732
  32.7 2.8 %collective-permute-start.10 = (bf16[256,256]{1,0:T(8,128)(2,1)S(1)}, bf16[256,256]{1,0:T(8,128)(2,1)S(1)}, u32[]{:S(2)}, u32[]{:S(2)}) collective-permute-start(bf16[256,256]{1,0:T(8,128)(2,1)S(1)} %collective-permute-done.7.refs_5_), channel_id=1, source_target_pairs={{0,1},{1,0},{2,3},{3,2},{4,5},{5,4},{6,7},{7,6},{8,9},{9,8},{10,11... | collective-permute-start | bytes 393224 | tf_op jit(solution)/shard_map/ppermute | solution.py:1234
  33.3 2.3 %collective-permute-start.11 = (bf16[256,256]{1,0:T(8,128)(2,1)S(1)}, bf16[256,256]{1,0:T(8,128)(2,1)S(1)}, u32[]{:S(2)}, u32[]{:S(2)}) collective-permute-start(bf16[256,256]{1,0:T(8,128)(2,1)S(1)} %collective-permute-done.8.refs_6_), channel_id=1, source_target_pairs={{0,1},{1,0},{2,3},{3,2},{4,5},{5,4},{6,7},{7,6},{8,9},{9,8},{10,11... | collective-permute-start | bytes 393224 | tf_op jit(solution)/shard_map/ppermute | solution.py:1234
  33.4 2.2 %collective-permute-start.12 = (bf16[256,256]{1,0:T(8,128)(2,1)S(1)}, bf16[256,256]{1,0:T(8,128)(2,1)S(1)}, u32[]{:S(2)}, u32[]{:S(2)}) collective-permute-start(bf16[256,256]{1,0:T(8,128)(2,1)S(1)} %collective-permute-done.9.refs_7_), channel_id=1, source_target_pairs={{0,1},{1,0},{2,3},{3,2},{4,5},{5,4},{6,7},{7,6},{8,9},{9,8},{10,11... | collective-permute-start | bytes 393224 | tf_op jit(solution)/shard_map/ppermute | solution.py:1234
  53.6 22.6 %collective-permute-start.14 = (bf16[2048,128]{1,0:T(8,128)(2,1)}, bf16[2048,128]{1,0:T(8,128)(2,1)S(1)}, u32[]{:S(2)}, u32[]{:S(2)}) collective-permute-start(bf16[2048,128]{1,0:T(8,128)(2,1)} %get-tuple-element.121.refs_3_.refs_4_), channel_id=1, source_target_pairs={{0,1},{1,0},{2,3},{3,2},{4,5},{5,4},{6,7},{7,6},{8,9},{9,8},{10,11... | collective-permute-start | bytes 1572872 | tf_op jit(solution)/shard_map/ppermute | solution.py:1234
  53.7 20.1 %collective-permute-start.16 = (bf16[2048,128]{1,0:T(8,128)(2,1)}, bf16[2048,128]{1,0:T(8,128)(2,1)S(1)}, u32[]{:S(2)}, u32[]{:S(2)}) collective-permute-start(bf16[2048,128]{1,0:T(8,128)(2,1)} %get-tuple-element.121.refs_3_.refs_4_), channel_id=1, source_target_pairs={{0,2},{1,3},{2,0},{3,1},{4,6},{5,7},{6,4},{7,5},{8,10},{9,11},{10,... | collective-permute-start | bytes 1572872 | tf_op jit(solution)/shard_map/ppermute | solution.py:1234
  55.5 18.3 %collective-permute-start.17 = (bf16[1024,128]{1,0:T(8,128)(2,1)}, bf16[1024,128]{1,0:T(8,128)(2,1)S(1)}, u32[]{:S(2)}, u32[]{:S(2)}) collective-permute-start(bf16[1024,128]{1,0:T(8,128)(2,1)} %get-tuple-element.128.refs_5_), channel_id=1, source_target_pairs={{0,2},{1,3},{2,0},{3,1},{4,6},{5,7},{6,4},{7,5},{8,10},{9,11},{10,... | collective-permute-start | bytes 786440 | tf_op jit(solution)/shard_map/ppermute | solution.py:1234
  55.7 18.2 %copy-start.8 = (bf16[1024,128]{1,0:T(8,128)(2,1)S(1)}, bf16[1024,128]{1,0:T(8,128)(2,1)}, u32[]{:S(2)}) copy-start(bf16[1024,128]{1,0:T(8,128)(2,1)} %get-tuple-element.128.refs_5_) | copy-start | bytes 786436
  73.8 2.7 %collective-permute-start.18 = (bf16[2048,128]{1,0:T(8,128)(2,1)S(1)}, bf16[2048,128]{1,0:T(8,128)(2,1)S(1)}, u32[]{:S(2)}, u32[]{:S(2)}) collective-permute-start(bf16[2048,128]{1,0:T(8,128)(2,1)S(1)} %collective-permute-done.16.refs_6_), channel_id=1, source_target_pairs={{0,1},{1,0},{2,3},{3,2},{4,5},{5,4},{6,7},{7,6},{8,9},{9,8},{10,11... | collective-permute-start | bytes 1572872 | tf_op jit(solution)/shard_map/ppermute | solution.py:1234
  73.9 2.3 %collective-permute-start.15 = (bf16[1024,128]{1,0:T(8,128)(2,1)S(1)}, bf16[1024,128]{1,0:T(8,128)(2,1)S(1)}, u32[]{:S(2)}, u32[]{:S(2)}) collective-permute-start(bf16[1024,128]{1,0:T(8,128)(2,1)S(1)} %copy-done.8), channel_id=1, source_target_pairs={{0,1},{1,0},{2,3},{3,2},{4,5},{5,4},{6,7},{7,6},{8,9},{9,8},{10,11... | collective-permute-start | bytes 786440 | tf_op jit(solution)/shard_map/ppermute | solution.py:1234
  74.4 2.1 %collective-permute-start.19 = (bf16[1024,128]{1,0:T(8,128)(2,1)S(1)}, bf16[1024,128]{1,0:T(8,128)(2,1)S(1)}, u32[]{:S(2)}, u32[]{:S(2)}) collective-permute-start(bf16[1024,128]{1,0:T(8,128)(2,1)S(1)} %collective-permute-done.17.refs_7_), channel_id=1, source_target_pairs={{0,1},{1,0},{2,3},{3,2},{4,5},{5,4},{6,7},{7,6},{8,9},{9,8},{10,11... | collective-permute-start | bytes 786440 | tf_op jit(solution)/shard_map/ppermute | solution.py:1234
  87.5 8.8 %collective-permute-start.22 = (bf16[368,256]{1,0:T(8,128)(2,1)}, bf16[368,256]{1,0:T(8,128)(2,1)S(1)}, u32[]{:S(2)}, u32[]{:S(2)}) collective-permute-start(bf16[368,256]{1,0:T(8,128)(2,1)} %get-tuple-element.145), channel_id=1, source_target_pairs={{0,24},{8,16},{16,8},{24,0},{1,25},{9,17},{17,9},{25,1},{2,26},{10... | collective-permute-start | bytes 565256 | tf_op jit(solution)/shard_map/ppermute | solution.py:1234
  90.0 9.5 %collective-permute-start.21 = (bf16[368,256]{1,0:T(8,128)(2,1)}, bf16[368,256]{1,0:T(8,128)(2,1)S(1)}, u32[]{:S(2)}, u32[]{:S(2)}) collective-permute-start(bf16[368,256]{1,0:T(8,128)(2,1)} %get-tuple-element.144), channel_id=1, source_target_pairs={{0,16},{8,24},{16,0},{24,8},{1,17},{9,25},{17,1},{25,9},{2,18},{10... | collective-permute-start | bytes 565256 | tf_op jit(solution)/shard_map/ppermute | solution.py:1234
  90.5 9.0 %collective-permute-start.20 = (bf16[368,256]{1,0:T(8,128)(2,1)}, bf16[368,256]{1,0:T(8,128)(2,1)S(1)}, u32[]{:S(2)}, u32[]{:S(2)}) collective-permute-start(bf16[368,256]{1,0:T(8,128)(2,1)} %get-tuple-element.143), channel_id=1, source_target_pairs={{0,8},{8,0},{16,24},{24,16},{1,9},{9,1},{17,25},{25,17},{2,10},{10... | collective-permute-start | bytes 565256 | tf_op jit(solution)/shard_map/ppermute | solution.py:1234
  91.0 9.5 %collective-permute-start.23 = (bf16[256,128]{1,0:T(8,128)(2,1)S(1)}, bf16[256,128]{1,0:T(8,128)(2,1)S(1)}, u32[]{:S(2)}, u32[]{:S(2)}) collective-permute-start(bf16[256,128]{1,0:T(8,128)(2,1)S(1)} %get-tuple-element.147), channel_id=1, source_target_pairs={{0,1},{1,0},{2,3},{3,2},{4,5},{5,4},{6,7},{7,6},{8,9},{9,8},{10,11... | collective-permute-start | bytes 196616 | tf_op jit(solution)/shard_map/ppermute | solution.py:1234
  91.0 9.6 %collective-permute-start.24 = (bf16[256,128]{1,0:T(8,128)(2,1)S(1)}, bf16[256,128]{1,0:T(8,128)(2,1)S(1)}, u32[]{:S(2)}, u32[]{:S(2)}) collective-permute-start(bf16[256,128]{1,0:T(8,128)(2,1)S(1)} %get-tuple-element.148), channel_id=1, source_target_pairs={{0,2},{1,3},{2,0},{3,1},{4,6},{5,7},{6,4},{7,5},{8,10},{9,11},{10,... | collective-permute-start | bytes 196616 | tf_op jit(solution)/shard_map/ppermute | solution.py:1234
  96.3 4.3 %collective-permute-start.25 = (bf16[256,128]{1,0:T(8,128)(2,1)S(1)}, bf16[256,128]{1,0:T(8,128)(2,1)S(1)}, u32[]{:S(2)}, u32[]{:S(2)}) collective-permute-start(bf16[256,128]{1,0:T(8,128)(2,1)S(1)} %get-tuple-element.149), channel_id=1, source_target_pairs={{0,3},{1,2},{2,1},{3,0},{4,7},{5,6},{6,5},{7,4},{8,11},{9,10},{10,... | collective-permute-start | bytes 196616 | tf_op jit(solution)/shard_map/ppermute | solution.py:1234
  100.6 12.7 %collective-permute-start.27 = (bf16[368,256]{1,0:T(8,128)(2,1)S(1)}, bf16[368,256]{1,0:T(8,128)(2,1)S(1)}, u32[]{:S(2)}, u32[]{:S(2)}) collective-permute-start(bf16[368,256]{1,0:T(8,128)(2,1)S(1)} %add_convert_fusion.1), channel_id=1, source_target_pairs={{0,4},{1,5},{2,6},{3,7},{4,0},{5,1},{6,2},{7,3},{8,12},{9,13},{10,... | collective-permute-start | bytes 565256 | tf_op jit(solution)/shard_map/ppermute | solution.py:1234
  104.4 19.2 %copy-start.1 = (bf16[256,256]{1,0:T(8,128)(2,1)S(1)}, bf16[256,256]{1,0:T(8,128)(2,1)}, u32[]{:S(2)}) copy-start(bf16[256,256]{1,0:T(8,128)(2,1)} %refs_12_.1) | copy-start | bytes 393220
  111.1 14.0 %copy-start.6 = (bf16[256,256]{1,0:T(8,128)(2,1)S(1)}, bf16[256,256]{1,0:T(8,128)(2,1)}, u32[]{:S(2)}) copy-start(bf16[256,256]{1,0:T(8,128)(2,1)} %get-tuple-element.161) | copy-start | bytes 393220
  111.9 4.7 %collective-permute-start.29 = (bf16[16,256]{1,0:T(8,128)(2,1)S(1)}, bf16[16,256]{1,0:T(8,128)(2,1)S(1)}, u32[]{:S(2)}, u32[]{:S(2)}) collective-permute-start(bf16[16,256]{1,0:T(8,128)(2,1)S(1)} %concatenate.10), channel_id=1, source_target_pairs={{0,4},{1,5},{2,6},{3,7},{4,0},{5,1},{6,2},{7,3},{8,12},{9,13},{10,... | collective-permute-start | bytes 24584 | tf_op jit(solution)/shard_map/ppermute | solution.py:1234
  113.3 6.7 %collective-permute-start.28 = (bf16[368,256]{1,0:T(8,128)(2,1)S(1)}, bf16[368,256]{1,0:T(8,128)(2,1)S(1)}, u32[]{:S(2)}, u32[]{:S(2)}) collective-permute-start(bf16[368,256]{1,0:T(8,128)(2,1)S(1)} %add_convert_fusion), channel_id=1, source_target_pairs={{0,2},{1,3},{2,0},{3,1},{4,6},{5,7},{6,4},{7,5},{8,10},{9,11},{10,... | collective-permute-start | bytes 565256 | tf_op jit(solution)/shard_map/ppermute | solution.py:1234
  120.0 11.9 %collective-permute-start.31 = (bf16[752,256]{1,0:T(8,128)(2,1)S(1)}, bf16[752,256]{1,0:T(8,128)(2,1)S(1)}, u32[]{:S(2)}, u32[]{:S(2)}) collective-permute-start(bf16[752,256]{1,0:T(8,128)(2,1)S(1)} %pad_maximum_fusion.refs_0_), channel_id=1, source_target_pairs={{0,8},{8,0},{16,24},{24,16},{1,9},{9,1},{17,25},{25,17},{2,10},{10... | collective-permute-start | bytes 1155080 | tf_op jit(solution)/shard_map/ppermute | solution.py:1234
  121.6 18.0 %collective-permute-start.33 = (bf16[752,256]{1,0:T(8,128)(2,1)S(1)}, bf16[752,256]{1,0:T(8,128)(2,1)S(1)}, u32[]{:S(2)}, u32[]{:S(2)}) collective-permute-start(bf16[752,256]{1,0:T(8,128)(2,1)S(1)} %pad_maximum_fusion.refs_0_), channel_id=1, source_target_pairs={{0,16},{8,24},{16,0},{24,8},{1,17},{9,25},{17,1},{25,9},{2,18},{10... | collective-permute-start | bytes 1155080 | tf_op jit(solution)/shard_map/ppermute | solution.py:1234
  121.7 17.9 %collective-permute-start.35 = (bf16[752,256]{1,0:T(8,128)(2,1)S(1)}, bf16[752,256]{1,0:T(8,128)(2,1)S(1)}, u32[]{:S(2)}, u32[]{:S(2)}) collective-permute-start(bf16[752,256]{1,0:T(8,128)(2,1)S(1)} %pad_maximum_fusion.refs_0_), channel_id=1, source_target_pairs={{0,24},{8,16},{16,8},{24,0},{1,25},{9,17},{17,9},{25,1},{2,26},{10... | collective-permute-start | bytes 1155080 | tf_op jit(solution)/shard_map/ppermute | solution.py:1234
  125.9 14.2 %collective-permute-start.26 = (bf16[2,256,256]{2,1,0:T(8,128)(2,1)}, bf16[2,256,256]{2,1,0:T(8,128)(2,1)}, u32[]{:S(2)}, u32[]{:S(2)}) collective-permute-start(bf16[2,256,256]{2,1,0:T(8,128)(2,1)} %pad_maximum_fusion.3), channel_id=1, source_target_pairs={{0,4},{1,5},{2,6},{3,7},{4,0},{5,1},{6,2},{7,3},{8,12},{9,13},{10,... | collective-permute-start | bytes 786440 | tf_op jit(solution)/shard_map/ppermute | solution.py:1234
  126.8 15.2 %collective-permute-start.30 = (bf16[752,256]{1,0:T(8,128)(2,1)S(1)}, bf16[752,256]{1,0:T(8,128)(2,1)S(1)}, u32[]{:S(2)}, u32[]{:S(2)}) collective-permute-start(bf16[752,256]{1,0:T(8,128)(2,1)S(1)} %pad_maximum_fusion.refs_0_), channel_id=1, source_target_pairs={{0,1},{1,0},{2,3},{3,2},{4,5},{5,4},{6,7},{7,6},{8,9},{9,8},{10,11... | collective-permute-start | bytes 1155080 | tf_op jit(solution)/shard_map/ppermute | solution.py:1234
  132.0 10.0 %collective-permute-start.32 = (bf16[752,256]{1,0:T(8,128)(2,1)S(1)}, bf16[752,256]{1,0:T(8,128)(2,1)S(1)}, u32[]{:S(2)}, u32[]{:S(2)}) collective-permute-start(bf16[752,256]{1,0:T(8,128)(2,1)S(1)} %collective-permute-done.31.refs_2_), channel_id=1, source_target_pairs={{0,1},{1,0},{2,3},{3,2},{4,5},{5,4},{6,7},{7,6},{8,9},{9,8},{10,11... | collective-permute-start | bytes 1155080 | tf_op jit(solution)/shard_map/ppermute | solution.py:1234
  139.6 2.4 %collective-permute-start.34 = (bf16[752,256]{1,0:T(8,128)(2,1)S(1)}, bf16[752,256]{1,0:T(8,128)(2,1)}, u32[]{:S(2)}, u32[]{:S(2)}) collective-permute-start(bf16[752,256]{1,0:T(8,128)(2,1)S(1)} %collective-permute-done.33.refs_4_), channel_id=1, source_target_pairs={{0,1},{1,0},{2,3},{3,2},{4,5},{5,4},{6,7},{7,6},{8,9},{9,8},{10,11... | collective-permute-start | bytes 1155080 | tf_op jit(solution)/shard_map/ppermute | solution.py:1234
  139.6 2.4 %collective-permute-start.36 = (bf16[752,256]{1,0:T(8,128)(2,1)S(1)}, bf16[752,256]{1,0:T(8,128)(2,1)}, u32[]{:S(2)}, u32[]{:S(2)}) collective-permute-start(bf16[752,256]{1,0:T(8,128)(2,1)S(1)} %collective-permute-done.35.refs_6_), channel_id=1, source_target_pairs={{0,1},{1,0},{2,3},{3,2},{4,5},{5,4},{6,7},{7,6},{8,9},{9,8},{10,11... | collective-permute-start | bytes 1155080 | tf_op jit(solution)/shard_map/ppermute | solution.py:1234
  (7 other events, 15.3 us)

commit v5 on v4

--- a/solution.py
+++ b/solution.py
@@ -626,33 +626,12 @@
     finish_all(leaving)
 
 
-def project_kernel(act_three, w_heads, biases, query_only, key_pad, value_pad, sizes):
-    cells, lanes = query_only.shape
-    scaling = (lanes // 2) ** -0.5
-
-    def project(index, carry):
-        at = pl.ds(pl.multiple_of(index * 512, 512), 512)
-        parts = dot(act_three[at, :], w_heads[...]) + biases[0:1, :]
-        query, key, value = (parts[:, k * lanes : (k + 1) * lanes] for k in range(3))
-        query_only[at, :] = query.astype(jnp.bfloat16) * jnp.bfloat16(scaling)
-        key_pad[at, :] = key.astype(jnp.bfloat16)
-        value_pad[at, :] = value.astype(jnp.bfloat16)
-        query_size = jnp.sum(query * query, axis=1, keepdims=True) * (scaling * scaling)
-        key_size = jnp.sum(key * key, axis=1, keepdims=True)
-        return jnp.maximum(carry[0], jnp.max(query_size)), jnp.maximum(carry[1], jnp.max(key_size))
-
-    start = (jnp.float32(0.0), jnp.float32(0.0))
-    query_most, key_most = lax.fori_loop(0, cells // 512, project, start)
-    line = lax.broadcasted_iota(jnp.int32, sizes.shape, 0)
-    sizes[...] = jnp.where(line == 0, query_most, key_most)
-
-
-def attention_kernel(columns, vec, query_only, key_pad, value_pad, sizes, w_out, *refs):
+def attention_kernel(columns, vec, act_three, w_heads, w_out, biases, *refs):
     blocks = refs[:8]
     value_key_far, query_far, grad_far, mixed_far, sums_far = refs[8:13]
     (
         grad_blocks, grad_proj, value_key, query_part, sums,
-        query_grad, heads_t, mixed, mask_row, in_sems, out_sems,
+        query_grad, key_pad, value_pad, heads_t, mixed, mask_row, in_sems, out_sems,
     ) = refs[13:]
     cells, channels = grad_proj.shape
     block_cells = blocks[0].shape[0]
@@ -668,6 +647,17 @@
         pairs.append((block, grad_blocks.at[pl.ds(base, block_cells), :]))
     arriving = started(in_sems, *pairs)
 
+    sizes = []
+    for start in range(0, cells, 512):
+        at = slice(start, start + 512)
+        parts = dot(act_three[at, :], w_heads[...]) + biases[0:1, :]
+        query, key, value = (parts[:, 2 * half * k : 2 * half * (k + 1)] for k in range(3))
+        query_grad[at, :] = query.astype(jnp.bfloat16) * jnp.bfloat16(scaling)
+        key_pad[at, :] = key.astype(jnp.bfloat16)
+        value_pad[at, :] = value.astype(jnp.bfloat16)
+        query_size = jnp.sum(query * query, axis=1, keepdims=True) * (scaling * scaling)
+        key_size = jnp.sum(key * key, axis=1, keepdims=True)
+        sizes.append((jnp.max(query_size), jnp.max(key_size)))
     lane = lax.broadcasted_iota(jnp.int32, (1, cells), 1)
     mask_row[...] = jnp.where(lane < valid_cells, 0.0, MASKED)
     heads_t[...] = jnp.zeros(heads_t.shape, jnp.float32)
@@ -680,7 +670,7 @@
         kept = jnp.where(cell < valid_cells, grad_blocks[at, :].astype(jnp.float32), 0.0)
         low = kept.astype(jnp.bfloat16)
         grad_proj[at, :] = low
-        query_grad[at, :] = query_only[at, :] + dot(low, w_out[...]).astype(jnp.bfloat16)
+        query_grad[at, :] = query_grad[at, :] + dot(low, w_out[...]).astype(jnp.bfloat16)
         return total + fold(kept)
 
     start = jnp.zeros((8, channels), jnp.float32)
@@ -712,7 +702,8 @@
         heads_t[half : 2 * half, :] += dot(turned[half : 2 * half], low)
         return carry
 
-    narrow = jnp.max(sizes[0:1, :]) * jnp.max(sizes[1:2, :]) <= 3600.0
+    query_most, key_most = (functools.reduce(jnp.maximum, size) for size in zip(*sizes))
+    narrow = query_most * key_most <= 3600.0
 
     @pl.when(narrow)
     def _():
@@ -1384,30 +1375,19 @@
     )
     grads_late, grads = relayed(grads, act_three)
     query_shape, head_shape = (cells // 2, lanes), (cells, lanes)
-    query_only, key_pad, value_pad, sizes = call(
-        project_kernel,
-        [(head_shape, low), (head_shape, low), (head_shape, low), ((8, lanes), full)],
-        [],
-        [],
-        12,
-        cost * 2,
-        [],
-        [act_three, w_heads, biases],
-        [],
-    )
     value_key, query_part, grad_proj, mixed, out_sums = call(
         functools.partial(attention_kernel, cols),
         [],
         [(head_shape, low), (query_shape, low), (wide, low), (head_shape, low), rows_eight],
         [
             (wide, low), (wide, low), (head_shape, low), (query_shape, low), rows_eight,
-            (head_shape, low), ((lanes, cells), full), (head_shape, low), ((1, cells), full),
-            sems(8), sems(5),
+            (head_shape, low), (head_shape, low), (head_shape, low), ((lanes, cells), full),
+            (head_shape, low), ((1, cells), full), sems(8), sems(5),
         ],
         36,
         cost * 34,
         [],
-        [vec, query_only, key_pad, value_pad, sizes, w_out, *grads_late],
+        [vec, act_three, w_heads, w_out, biases, *grads_late],
         grads,
     )
 
@@ -1431,7 +1411,9 @@
         [act_one, act_two, mixed, value_key, act_three, grad_proj],
         [send_shape] * 4,
     )
-    key_near, query_near, own_two = lax.optimization_barrier((key_near, query_near, own_two))
+    key_near, query_near, key_mate, query_mate, own_two = lax.optimization_barrier(
+        (key_near, query_near, key_mate, query_mate, own_two)
+    )
     relays = [key_mate, query_mate, swap(key_near, "row", 1), swap(query_near, "row", 1)]
     packed = [value_key, query_part, key_near, query_near]
     lines = 18 * (half // 4) + half + 16

time: 148 us -> 147 us (level)
  Pallas kernels: 73.4 us -> 71.9 us
    pallas_call x9 -> x8, Pallas kernels: 73.4 us -> 71.9 us  [call(): pl.pallas_call(kernel, out_shape=[jax.ShapeDtypeStruct(*kind) for kind in...]
  transfers between devices with their start and end apart: 37 -> 37, of which waited for: 13 -> 15; matrix products, arithmetic and copies ran while one was open for 4% -> 4% of each run, Pallas kernels for 27% -> 26%
where the time goes in v5:
time: 147 us; the launch traced here: 146 us
  Pallas kernels  71.9 us (49%)
  waiting for transfers between devices  36.2 us (25%)
  starting transfers between devices  29.2 us (20%)
  other arithmetic  5.95 us (4%)
    pallas_call x8, Pallas kernels, call(): pl.pallas_call(kernel, out_shape=[jax.ShapeDtypeStruct(*kind) for kind in...  71.9 us
    ppermute x37, waiting for transfers between devices, swap(): return lax.ppermute(value, axis, [(k, k ^ step) for k in range(count)])  36.2 us
    ppermute x37, starting transfers between devices, swap(): return lax.ppermute(value, axis, [(k, k ^ step) for k in range(count)])  29.2 us
  transfers between devices with their start and end apart: 37, of which 15 were waited for; matrix products, arithmetic and copies ran while one was open for 4% of the time, Pallas kernels for 26%

profile of v5, /device:TPU:0, one launch (start us, length us, event | category | flops | bytes accessed | tf_op | source)
XLA Modules:
  0.0 146.2 jit_solution(18175673484601500164)
XLA Ops:
  0.7 1.1 dynamic-slice_bitcast_fusion
  1.8 4.1 %collective-permute-start.1 = (bf16[256,256]{1,0:T(8,128)(2,1)S(1)}, bf16[256,256]{1,0:T(8,128)(2,1)S(1)}, u32[]{:S(2)}, u32[]{:S(2)}) collective-permute-start(bf16[256,256]{1,0:T(8,128)(2,1)S(1)} %get-tuple-element.180), channel_id=1, source_target_pairs={{0,4},{1,5},{2,6},{3,7},{4,0},{5,1},{6,2},{7,3},{8,12},{9,13},{10,... | collective-permute-start | bytes 393224 | tf_op jit(solution)/shard_map/ppermute | solution.py:1225
  5.9 1.3 collective-permute-start.2
  7.5 0.7 convert_element_type.41
  8.2 0.7 convert_element_type.42
  9.0 0.5 convolution_add_fusion.refs_0_
  9.5 4.8 %shard_map.331 = (f32[16,256]{1,0:T(8,128)S(1)}, bf16[256,384]{1,0:T(8,128)(2,1)S(1)}, bf16[256,128]{1,0:T(8,128)(2,1)S(1)}, f32[8,384]{1,0:T(8,128)S(1)}, bf16[...) custom-call(f32[2,512]{1,0:T(2,128)S(1)} %convolution_add_fusion.refs_0_, ...), custom_call_target="tpu_custom_call" | custom-call | flops 256 | bytes 2893328 | tf_op jit(solution)/shard_map/pallas_call | solution.py:1256
  14.4 1.5 %collective-permute-done.1.refs_6_ = bf16[256,256]{1,0:T(8,128)(2,1)S(1)} collective-permute-done((bf16[256,256]{1,0:T(8,128)(2,1)S(1)}, bf16[256,256]{1,0:T(8,128)(2,1)S(1)}, u32[]{:S(2)}, u32[]{:S(2)}) %collective-permute-start.1) | collective-permute-done | bytes 131104 | tf_op jit(solution)/shard_map/ppermute | solution.py:1225
  15.9 0.5 collective-permute-done.refs_5_
  16.4 0.5 collective-permute-start.4
  16.9 4.2 %collective-permute-start.8 = (bf16[256,256]{1,0:T(8,128)(2,1)S(1)}, bf16[256,256]{1,0:T(8,128)(2,1)S(1)}, u32[]{:S(2)}, u32[]{:S(2)}) collective-permute-start(bf16[256,256]{1,0:T(8,128)(2,1)S(1)} %get-tuple-element.110), channel_id=1, source_target_pairs={{0,4},{1,5},{2,6},{3,7},{4,0},{5,1},{6,2},{7,3},{8,12},{9,13},{10,... | collective-permute-start | bytes 393224 | tf_op jit(solution)/shard_map/ppermute | solution.py:1225
  21.2 0.4 collective-permute-start.9
  21.9 10.8 %shard_map.332 = (bf16[2048,256]{1,0:T(8,128)(2,1)S(1)}, bf16[2048,256]{1,0:T(8,128)(2,1)}, f32[2048,256]{1,0:T(8,128)}, f32[2048,256]{1,0:T(8,128)}, bf16[2048,...) custom-call(f32[16,256]{1,0:T(8,128)S(1)} %get-tuple-element.97.vec, ...), custom_call_target="tpu_custom_call" | custom-call | flops 15099494400 | bytes 3424256 | tf_op jit(solution)/shard_map/pallas_call | solution.py:1256
  32.7 0.6 collective-permute-start.10
  33.4 0.4 collective-permute-start.12
  33.8 0.5 collective-permute-done.10.refs_0_
  34.3 0.4 collective-permute-done.11.refs_1_
  34.8 17.6 %shard_map.333 = (bf16[2048,128]{1,0:T(8,128)(2,1)}, bf16[1024,128]{1,0:T(8,128)(2,1)}, bf16[2048,256]{1,0:T(8,128)(2,1)}, bf16[2048,128]{1,0:T(8,128)(2,1)}, f32[8,256]{1,0:T(8,128)}) custom-call(f32[16,256]{1,0:T(8,128)S(1)} %get-tuple-element.97.vec, bf16[2048,256]{1,0:T(8,128)(2,1)S(1)} %get-tuple-element.105.act_three.refs_4_, ...), custom_call_target="tpu_custom_call" | custom-call | flops 20535312384 | bytes 2387968 | tf_op jit(solution)/shard_map/pallas_call | solution.py:1256
  52.4 1.8 %collective-permute-start.14 = (bf16[2048,128]{1,0:T(8,128)(2,1)}, bf16[2048,128]{1,0:T(8,128)(2,1)S(1)}, u32[]{:S(2)}, u32[]{:S(2)}) collective-permute-start(bf16[2048,128]{1,0:T(8,128)(2,1)} %get-tuple-element.115.refs_3_.refs_4_), channel_id=1, source_target_pairs={{0,2},{1,3},{2,0},{3,1},{4,6},{5,7},{6,4},{7,5},{8,10},{9,11},{10,... | collective-permute-start | bytes 1572872 | tf_op jit(solution)/shard_map/ppermute | solution.py:1225
  54.8 13.9 %shard_map.334 = (bf16[3,192,2048]{2,1,0:T(8,128)(2,1)}, bf16[3,192,2048]{2,1,0:T(8,128)(2,1)}, bf16[4,80,256]{2,1,0:T(8,128)(2,1)}, bf16[256,128]{1,0:T(8,128)(...) custom-call(f32[16,256]{1,0:T(8,128)S(1)} %get-tuple-element.97.vec, ...), custom_call_target="tpu_custom_call" | custom-call | flops 16307453952 | bytes 5259264 | tf_op jit(solution)/shard_map/pallas_call | solution.py:1256
  68.6 3.9 %collective-permute-done.15.refs_7_ = bf16[1024,128]{1,0:T(8,128)(2,1)S(1)} collective-permute-done((bf16[1024,128]{1,0:T(8,128)(2,1)}, bf16[1024,128]{1,0:T(8,128)(2,1)S(1)}, u32[]{:S(2)}, u32[]{:S(2)}) %collective-permute-start.15) | collective-permute-done | bytes 262176 | tf_op jit(solution)/shard_map/ppermute | solution.py:1225
  72.6 0.5 collective-permute-start.19
  73.1 1.8 %collective-permute-done.19.refs_3_ = bf16[1024,128]{1,0:T(8,128)(2,1)S(1)} collective-permute-done((bf16[1024,128]{1,0:T(8,128)(2,1)S(1)}, bf16[1024,128]{1,0:T(8,128)(2,1)S(1)}, u32[]{:S(2)}, u32[]{:S(2)}) %collective-permute-start.19) | collective-permute-done | bytes 262176 | tf_op jit(solution)/shard_map/ppermute | solution.py:1225
  74.9 10.9 %shard_map.335 = (bf16[2176,768]{1,0:T(8,128)(2,1)S(1)}, f32[2048,256]{1,0:T(8,128)}, bf16[368,256]{1,0:T(8,128)(2,1)}, bf16[368,256]{1,0:T(8,128)(2,1)}, bf16[3...) custom-call(f32[16,256]{1,0:T(8,128)S(1)} %get-tuple-element.97.vec, bf16[12,64,256]{2,1,0:T(8,128)(2,1)S(1)} %get-tuple-element.121.qkv_t, ...), custom_call_target="tpu_custom_call" | custom-call | flops 15703474176 | bytes 14876672 | tf_op jit(solution)/shard_map/pallas_call | solution.py:1256
  85.8 2.5 %collective-permute-start.22 = (bf16[368,256]{1,0:T(8,128)(2,1)}, bf16[368,256]{1,0:T(8,128)(2,1)S(1)}, u32[]{:S(2)}, u32[]{:S(2)}) collective-permute-start(bf16[368,256]{1,0:T(8,128)(2,1)} %get-tuple-element.141), channel_id=1, source_target_pairs={{0,24},{8,16},{16,8},{24,0},{1,25},{9,17},{17,9},{25,1},{2,26},{10... | collective-permute-start | bytes 565256 | tf_op jit(solution)/shard_map/ppermute | solution.py:1225
  88.3 0.5 collective-permute-start.21
  88.8 0.5 collective-permute-start.20
  89.4 1.7 %collective-permute-start.24 = (bf16[256,128]{1,0:T(8,128)(2,1)S(1)}, bf16[256,128]{1,0:T(8,128)(2,1)S(1)}, u32[]{:S(2)}, u32[]{:S(2)}) collective-permute-start(bf16[256,128]{1,0:T(8,128)(2,1)S(1)} %get-tuple-element.144), channel_id=1, source_target_pairs={{0,2},{1,3},{2,0},{3,1},{4,6},{5,7},{6,4},{7,5},{8,10},{9,11},{10,... | collective-permute-start | bytes 196616 | tf_op jit(solution)/shard_map/ppermute | solution.py:1225
  91.1 3.5 %collective-permute-done.22 = bf16[368,256]{1,0:T(8,128)(2,1)S(1)} collective-permute-done((bf16[368,256]{1,0:T(8,128)(2,1)}, bf16[368,256]{1,0:T(8,128)(2,1)S(1)}, u32[]{:S(2)}, u32[]{:S(2)}) %collective-permute-start.22) | collective-permute-done | bytes 188448 | tf_op jit(solution)/shard_map/ppermute | solution.py:1225
  94.6 3.2 %collective-permute-done.21 = bf16[368,256]{1,0:T(8,128)(2,1)S(1)} collective-permute-done((bf16[368,256]{1,0:T(8,128)(2,1)}, bf16[368,256]{1,0:T(8,128)(2,1)S(1)}, u32[]{:S(2)}, u32[]{:S(2)}) %collective-permute-start.21) | collective-permute-done | bytes 188448 | tf_op jit(solution)/shard_map/ppermute | solution.py:1225
  97.9 1.0 add_convert_fusion.1
  99.0 3.8 %collective-permute-start.27 = (bf16[368,256]{1,0:T(8,128)(2,1)S(1)}, bf16[368,256]{1,0:T(8,128)(2,1)S(1)}, u32[]{:S(2)}, u32[]{:S(2)}) collective-permute-start(bf16[368,256]{1,0:T(8,128)(2,1)S(1)} %add_convert_fusion.1), channel_id=1, source_target_pairs={{0,4},{1,5},{2,6},{3,7},{4,0},{5,1},{6,2},{7,3},{8,12},{9,13},{10,... | collective-permute-start | bytes 565256 | tf_op jit(solution)/shard_map/ppermute | solution.py:1225
  102.7 6.7 %shard_map.337 = (bf16[256,256]{1,0:T(8,128)(2,1)}, bf16[256,256]{1,0:T(8,128)(2,1)}, f32[8,256]{1,0:T(8,128)}) custom-call(f32[16,256]{1,0:T(8,128)S(1)} %get-tuple-element.97.vec, bf16[2176,768]{1,0:T(8,128)(2,1)S(1)} %get-tuple-element.151.shifted, bf16[3,768,256]{2,1,0:T(8,128)(2,1)} %get-tuple-element.152.weight_far, ...), custom_call_target="tpu_custom_call" | custom-call | flops 7247757312 | bytes 7692288 | tf_op jit(solution)/shard_map/pallas_call | solution.py:1256
  109.5 0.7 convert.4
  110.2 1.3 collective-permute-done.27
  111.7 3.2 %collective-permute-done.29 = bf16[16,256]{1,0:T(8,128)(2,1)S(1)} collective-permute-done((bf16[16,256]{1,0:T(8,128)(2,1)S(1)}, bf16[16,256]{1,0:T(8,128)(2,1)S(1)}, u32[]{:S(2)}, u32[]{:S(2)}) %collective-permute-start.29) | collective-permute-done | bytes 8224 | tf_op jit(solution)/shard_map/ppermute | solution.py:1225
  114.9 3.5 %collective-permute-done.28 = bf16[368,256]{1,0:T(8,128)(2,1)S(1)} collective-permute-done((bf16[368,256]{1,0:T(8,128)(2,1)S(1)}, bf16[368,256]{1,0:T(8,128)(2,1)S(1)}, u32[]{:S(2)}, u32[]{:S(2)}) %collective-permute-start.28) | collective-permute-done | bytes 188448 | tf_op jit(solution)/shard_map/ppermute | solution.py:1225
  118.4 1.6 %collective-permute-start.31 = (bf16[752,256]{1,0:T(8,128)(2,1)S(1)}, bf16[752,256]{1,0:T(8,128)(2,1)S(1)}, u32[]{:S(2)}, u32[]{:S(2)}) collective-permute-start(bf16[752,256]{1,0:T(8,128)(2,1)S(1)} %pad_maximum_fusion.refs_0_), channel_id=1, source_target_pairs={{0,8},{8,0},{16,24},{24,16},{1,9},{9,1},{17,25},{25,17},{2,10},{10... | collective-permute-start | bytes 1155080 | tf_op jit(solution)/shard_map/ppermute | solution.py:1225
  120.0 1.9 %collective-permute-start.35 = (bf16[752,256]{1,0:T(8,128)(2,1)S(1)}, bf16[752,256]{1,0:T(8,128)(2,1)S(1)}, u32[]{:S(2)}, u32[]{:S(2)}) collective-permute-start(bf16[752,256]{1,0:T(8,128)(2,1)S(1)} %pad_maximum_fusion.refs_0_), channel_id=1, source_target_pairs={{0,24},{8,16},{16,8},{24,0},{1,25},{9,17},{17,9},{25,1},{2,26},{10... | collective-permute-start | bytes 1155080 | tf_op jit(solution)/shard_map/ppermute | solution.py:1225
  121.9 1.5 %shard_map.336 = (bf16[256,256]{1,0:T(8,128)(2,1)S(1)}, bf16[256,256]{1,0:T(8,128)(2,1)S(1)}) custom-call(f32[16,256]{1,0:T(8,128)S(1)} %get-tuple-element.97.vec, bf16[4,64,256]{2,1,0:T(8,128)(2,1)S(1)} %bitcast.26, bf16[256,128]{1,0:T(8,128)(2,1)S(1)} %get-tuple-element.146.refs_0_, bf16[256,128]{1,0:T(8,128)(2,1)S(1)} %collective-permute-done.23.refs_1_, ...), custom_call_target="tpu_custom_call" | custom-call | flops 603979776 | bytes 2506752 | tf_op jit(solution)/shard_map/pallas_call | solution.py:1256
  123.4 0.7 pad_maximum_fusion.3
  124.2 0.9 collective-permute-start.26
  125.1 5.2 %collective-permute-done.31.refs_2_ = bf16[752,256]{1,0:T(8,128)(2,1)S(1)} collective-permute-done((bf16[752,256]{1,0:T(8,128)(2,1)S(1)}, bf16[752,256]{1,0:T(8,128)(2,1)S(1)}, u32[]{:S(2)}, u32[]{:S(2)}) %collective-permute-start.31) | collective-permute-done | bytes 385056 | tf_op jit(solution)/shard_map/ppermute | solution.py:1225
  130.3 7.6 %collective-permute-done.33.refs_4_ = bf16[752,256]{1,0:T(8,128)(2,1)S(1)} collective-permute-done((bf16[752,256]{1,0:T(8,128)(2,1)S(1)}, bf16[752,256]{1,0:T(8,128)(2,1)S(1)}, u32[]{:S(2)}, u32[]{:S(2)}) %collective-permute-start.33) | collective-permute-done | bytes 385056 | tf_op jit(solution)/shard_map/ppermute | solution.py:1225
  137.9 0.5 collective-permute-start.36
  138.4 1.0 select_bitcast_fusion
  139.4 0.8 pad_maximum_fusion.1
  140.3 5.8 %shard_map.338 = (f32[9,256,256]{2,1,0:T(8,128)}, f32[9,256,256]{2,1,0:T(8,128)}, f32[256,768]{1,0:T(8,128)}, f32[256,256]{1,0:T(8,128)}, f32[1024,512]{1,0:T(8,...) custom-call(bf16[752,256]{1,0:T(8,128)(2,1)S(1)} %pad_maximum_fusion, ...), custom_call_target="tpu_custom_call" | custom-call | flops 603979776 | bytes 3082240 | tf_op jit(solution)/shard_map/pallas_call | solution.py:1256
  (85 shorter events, 2.1 us)
Async XLA Ops:
  0.7 8.3 %copy-start = (bf16[1024,512]{1,0:T(8,128)(2,1)S(1)}, bf16[1024,512]{1,0:T(8,128)(2,1)}, u32[]{:S(2)}) copy-start(bf16[1024,512]{1,0:T(8,128)(2,1)} %param.27) | copy-start | bytes 3145732
  1.8 12.6 %copy-start.5 = (bf16[256,256]{1,0:T(8,128)(2,1)}, bf16[256,256]{1,0:T(8,128)(2,1)S(1)}, u32[]{:S(2)}) copy-start(bf16[256,256]{1,0:T(8,128)(2,1)S(1)} %get-tuple-element.181.refs_3_) | copy-start | bytes 393220
  1.8 12.5 %copy-start.3 = (bf16[2,4,64,256]{3,2,1,0:T(8,128)(2,1)S(1)}, bf16[2,4,64,256]{3,2,1,0:T(8,128)(2,1)}, u32[]{:S(2)}) copy-start(bf16[2,4,64,256]{3,2,1,0:T(8,128)(2,1)} %param.39) | copy-start | bytes 786436
  1.8 14.1 %collective-permute-start.1 = (bf16[256,256]{1,0:T(8,128)(2,1)S(1)}, bf16[256,256]{1,0:T(8,128)(2,1)S(1)}, u32[]{:S(2)}, u32[]{:S(2)}) collective-permute-start(bf16[256,256]{1,0:T(8,128)(2,1)S(1)} %get-tuple-element.180), channel_id=1, source_target_pairs={{0,4},{1,5},{2,6},{3,7},{4,0},{5,1},{6,2},{7,3},{8,12},{9,13},{10,... | collective-permute-start | bytes 393224 | tf_op jit(solution)/shard_map/ppermute | solution.py:1225
  5.9 10.0 %collective-permute-start.2 = (bf16[256,256]{1,0:T(8,128)(2,1)S(1)}, bf16[256,256]{1,0:T(8,128)(2,1)S(1)}, u32[]{:S(2)}, u32[]{:S(2)}) collective-permute-start(bf16[256,256]{1,0:T(8,128)(2,1)S(1)} %get-tuple-element.180), channel_id=1, source_target_pairs={{0,6},{1,7},{2,4},{3,5},{4,2},{5,3},{6,0},{7,1},{8,14},{9,15},{10,... | collective-permute-start | bytes 393224 | tf_op jit(solution)/shard_map/ppermute | solution.py:1225
  7.2 9.2 %collective-permute-start = (bf16[256,256]{1,0:T(8,128)(2,1)S(1)}, bf16[256,256]{1,0:T(8,128)(2,1)S(1)}, u32[]{:S(2)}, u32[]{:S(2)}) collective-permute-start(bf16[256,256]{1,0:T(8,128)(2,1)S(1)} %get-tuple-element.181.refs_3_), channel_id=1, source_target_pairs={{0,2},{1,3},{2,0},{3,1},{4,6},{5,7},{6,4},{7,5},{8,10},{9,11},{10,... | collective-permute-start | bytes 393224 | tf_op jit(solution)/shard_map/ppermute | solution.py:1225
  7.5 13.7 %collective-permute-start.6 = (bf16[256,256]{1,0:T(8,128)(2,1)S(1)}, bf16[256,256]{1,0:T(8,128)(2,1)S(1)}, u32[]{:S(2)}, u32[]{:S(2)}) collective-permute-start(bf16[256,256]{1,0:T(8,128)(2,1)S(1)} %get-tuple-element.181.refs_3_), channel_id=1, source_target_pairs={{0,1},{1,0},{2,3},{3,2},{4,5},{5,4},{6,7},{7,6},{8,9},{9,8},{10,11... | collective-permute-start | bytes 393224 | tf_op jit(solution)/shard_map/ppermute | solution.py:1225
  14.4 18.3 %copy-start.4 = (bf16[256,256]{1,0:T(8,128)(2,1)}, bf16[256,256]{1,0:T(8,128)(2,1)S(1)}, u32[]{:S(2)}) copy-start(bf16[256,256]{1,0:T(8,128)(2,1)S(1)} %get-tuple-element.109.refs_3_) | copy-start | bytes 393220
  15.9 5.9 %copy-start.9 = (bf16[256,256]{1,0:T(8,128)(2,1)}, bf16[256,256]{1,0:T(8,128)(2,1)S(1)}, u32[]{:S(2)}) copy-start(bf16[256,256]{1,0:T(8,128)(2,1)S(1)} %collective-permute-done.1.refs_6_) | copy-start | bytes 393220
  15.9 5.9 %copy-start.10 = (bf16[256,256]{1,0:T(8,128)(2,1)}, bf16[256,256]{1,0:T(8,128)(2,1)S(1)}, u32[]{:S(2)}) copy-start(bf16[256,256]{1,0:T(8,128)(2,1)S(1)} %collective-permute-done.2.refs_7_) | copy-start | bytes 393220
  16.4 5.4 %copy-start.11 = (bf16[256,256]{1,0:T(8,128)(2,1)}, bf16[256,256]{1,0:T(8,128)(2,1)S(1)}, u32[]{:S(2)}) copy-start(bf16[256,256]{1,0:T(8,128)(2,1)S(1)} %collective-permute-done.refs_5_) | copy-start | bytes 393220
  16.4 5.1 %collective-permute-start.3 = (bf16[256,256]{1,0:T(8,128)(2,1)S(1)}, bf16[256,256]{1,0:T(8,128)(2,1)S(1)}, u32[]{:S(2)}, u32[]{:S(2)}) collective-permute-start(bf16[256,256]{1,0:T(8,128)(2,1)S(1)} %collective-permute-done.refs_5_), channel_id=1, source_target_pairs={{0,1},{1,0},{2,3},{3,2},{4,5},{5,4},{6,7},{7,6},{8,9},{9,8},{10,11... | collective-permute-start | bytes 393224 | tf_op jit(solution)/shard_map/ppermute | solution.py:1225
  16.4 5.4 %collective-permute-start.4 = (bf16[256,256]{1,0:T(8,128)(2,1)S(1)}, bf16[256,256]{1,0:T(8,128)(2,1)S(1)}, u32[]{:S(2)}, u32[]{:S(2)}) collective-permute-start(bf16[256,256]{1,0:T(8,128)(2,1)S(1)} %collective-permute-done.1.refs_6_), channel_id=1, source_target_pairs={{0,1},{1,0},{2,3},{3,2},{4,5},{5,4},{6,7},{7,6},{8,9},{9,8},{10,11... | collective-permute-start | bytes 393224 | tf_op jit(solution)/shard_map/ppermute | solution.py:1225
  16.9 4.9 %collective-permute-start.5 = (bf16[256,256]{1,0:T(8,128)(2,1)S(1)}, bf16[256,256]{1,0:T(8,128)(2,1)S(1)}, u32[]{:S(2)}, u32[]{:S(2)}) collective-permute-start(bf16[256,256]{1,0:T(8,128)(2,1)S(1)} %collective-permute-done.2.refs_7_), channel_id=1, source_target_pairs={{0,1},{1,0},{2,3},{3,2},{4,5},{5,4},{6,7},{7,6},{8,9},{9,8},{10,11... | collective-permute-start | bytes 393224 | tf_op jit(solution)/shard_map/ppermute | solution.py:1225
  16.9 15.8 %collective-permute-start.8 = (bf16[256,256]{1,0:T(8,128)(2,1)S(1)}, bf16[256,256]{1,0:T(8,128)(2,1)S(1)}, u32[]{:S(2)}, u32[]{:S(2)}) collective-permute-start(bf16[256,256]{1,0:T(8,128)(2,1)S(1)} %get-tuple-element.110), channel_id=1, source_target_pairs={{0,4},{1,5},{2,6},{3,7},{4,0},{5,1},{6,2},{7,3},{8,12},{9,13},{10,... | collective-permute-start | bytes 393224 | tf_op jit(solution)/shard_map/ppermute | solution.py:1225
  21.2 11.5 %collective-permute-start.9 = (bf16[256,256]{1,0:T(8,128)(2,1)S(1)}, bf16[256,256]{1,0:T(8,128)(2,1)S(1)}, u32[]{:S(2)}, u32[]{:S(2)}) collective-permute-start(bf16[256,256]{1,0:T(8,128)(2,1)S(1)} %get-tuple-element.110), channel_id=1, source_target_pairs={{0,6},{1,7},{2,4},{3,5},{4,2},{5,3},{6,0},{7,1},{8,14},{9,15},{10,... | collective-permute-start | bytes 393224 | tf_op jit(solution)/shard_map/ppermute | solution.py:1225
  21.6 11.1 %collective-permute-start.7 = (bf16[256,256]{1,0:T(8,128)(2,1)S(1)}, bf16[256,256]{1,0:T(8,128)(2,1)S(1)}, u32[]{:S(2)}, u32[]{:S(2)}) collective-permute-start(bf16[256,256]{1,0:T(8,128)(2,1)S(1)} %get-tuple-element.109.refs_3_), channel_id=1, source_target_pairs={{0,2},{1,3},{2,0},{3,1},{4,6},{5,7},{6,4},{7,5},{8,10},{9,11},{10,... | collective-permute-start | bytes 393224 | tf_op jit(solution)/shard_map/ppermute | solution.py:1225
  21.8 12.0 %collective-permute-start.13 = (bf16[256,256]{1,0:T(8,128)(2,1)S(1)}, bf16[256,256]{1,0:T(8,128)(2,1)S(1)}, u32[]{:S(2)}, u32[]{:S(2)}) collective-permute-start(bf16[256,256]{1,0:T(8,128)(2,1)S(1)} %get-tuple-element.109.refs_3_), channel_id=1, source_target_pairs={{0,1},{1,0},{2,3},{3,2},{4,5},{5,4},{6,7},{7,6},{8,9},{9,8},{10,11... | collective-permute-start | bytes 393224 | tf_op jit(solution)/shard_map/ppermute | solution.py:1225
  32.7 19.8 %copy-start.2 = (bf16[2048,256]{1,0:T(8,128)(2,1)}, bf16[2048,256]{1,0:T(8,128)(2,1)S(1)}, u32[]{:S(2)}) copy-start(bf16[2048,256]{1,0:T(8,128)(2,1)S(1)} %get-tuple-element.105.act_three.refs_4_) | copy-start | bytes 3145732
  32.7 1.5 %collective-permute-start.10 = (bf16[256,256]{1,0:T(8,128)(2,1)S(1)}, bf16[256,256]{1,0:T(8,128)(2,1)S(1)}, u32[]{:S(2)}, u32[]{:S(2)}) collective-permute-start(bf16[256,256]{1,0:T(8,128)(2,1)S(1)} %collective-permute-done.7.refs_5_), channel_id=1, source_target_pairs={{0,1},{1,0},{2,3},{3,2},{4,5},{5,4},{6,7},{7,6},{8,9},{9,8},{10,11... | collective-permute-start | bytes 393224 | tf_op jit(solution)/shard_map/ppermute | solution.py:1225
  33.3 1.3 collective-permute-start.11
  33.4 1.5 collective-permute-start.12
  52.4 20.1 %collective-permute-start.14 = (bf16[2048,128]{1,0:T(8,128)(2,1)}, bf16[2048,128]{1,0:T(8,128)(2,1)S(1)}, u32[]{:S(2)}, u32[]{:S(2)}) collective-permute-start(bf16[2048,128]{1,0:T(8,128)(2,1)} %get-tuple-element.115.refs_3_.refs_4_), channel_id=1, source_target_pairs={{0,2},{1,3},{2,0},{3,1},{4,6},{5,7},{6,4},{7,5},{8,10},{9,11},{10,... | collective-permute-start | bytes 1572872 | tf_op jit(solution)/shard_map/ppermute | solution.py:1225
  54.3 18.3 %collective-permute-start.16 = (bf16[2048,128]{1,0:T(8,128)(2,1)}, bf16[2048,128]{1,0:T(8,128)(2,1)S(1)}, u32[]{:S(2)}, u32[]{:S(2)}) collective-permute-start(bf16[2048,128]{1,0:T(8,128)(2,1)} %get-tuple-element.115.refs_3_.refs_4_), channel_id=1, source_target_pairs={{0,1},{1,0},{2,3},{3,2},{4,5},{5,4},{6,7},{7,6},{8,9},{9,8},{10,11... | collective-permute-start | bytes 1572872 | tf_op jit(solution)/shard_map/ppermute | solution.py:1225
  54.3 18.2 %collective-permute-start.15 = (bf16[1024,128]{1,0:T(8,128)(2,1)}, bf16[1024,128]{1,0:T(8,128)(2,1)S(1)}, u32[]{:S(2)}, u32[]{:S(2)}) collective-permute-start(bf16[1024,128]{1,0:T(8,128)(2,1)} %get-tuple-element.122.refs_5_), channel_id=1, source_target_pairs={{0,2},{1,3},{2,0},{3,1},{4,6},{5,7},{6,4},{7,5},{8,10},{9,11},{10,... | collective-permute-start | bytes 786440 | tf_op jit(solution)/shard_map/ppermute | solution.py:1225
  54.7 17.8 %collective-permute-start.17 = (bf16[1024,128]{1,0:T(8,128)(2,1)}, bf16[1024,128]{1,0:T(8,128)(2,1)S(1)}, u32[]{:S(2)}, u32[]{:S(2)}) collective-permute-start(bf16[1024,128]{1,0:T(8,128)(2,1)} %get-tuple-element.122.refs_5_), channel_id=1, source_target_pairs={{0,1},{1,0},{2,3},{3,2},{4,5},{5,4},{6,7},{7,6},{8,9},{9,8},{10,11... | collective-permute-start | bytes 786440 | tf_op jit(solution)/shard_map/ppermute | solution.py:1225
  72.5 2.4 %copy-start.8 = (bf16[1024,128]{1,0:T(8,128)(2,1)}, bf16[1024,128]{1,0:T(8,128)(2,1)S(1)}, u32[]{:S(2)}) copy-start(bf16[1024,128]{1,0:T(8,128)(2,1)S(1)} %collective-permute-done.15.refs_7_) | copy-start | bytes 786436
  72.5 2.4 %collective-permute-start.18 = (bf16[2048,128]{1,0:T(8,128)(2,1)S(1)}, bf16[2048,128]{1,0:T(8,128)(2,1)S(1)}, u32[]{:S(2)}, u32[]{:S(2)}) collective-permute-start(bf16[2048,128]{1,0:T(8,128)(2,1)S(1)} %collective-permute-done.14.refs_6_), channel_id=1, source_target_pairs={{0,1},{1,0},{2,3},{3,2},{4,5},{5,4},{6,7},{7,6},{8,9},{9,8},{10,11... | collective-permute-start | bytes 1572872 | tf_op jit(solution)/shard_map/ppermute | solution.py:1225
  72.6 2.3 %collective-permute-start.19 = (bf16[1024,128]{1,0:T(8,128)(2,1)S(1)}, bf16[1024,128]{1,0:T(8,128)(2,1)S(1)}, u32[]{:S(2)}, u32[]{:S(2)}) collective-permute-start(bf16[1024,128]{1,0:T(8,128)(2,1)S(1)} %collective-permute-done.15.refs_7_), channel_id=1, source_target_pairs={{0,1},{1,0},{2,3},{3,2},{4,5},{5,4},{6,7},{7,6},{8,9},{9,8},{10,11... | collective-permute-start | bytes 786440 | tf_op jit(solution)/shard_map/ppermute | solution.py:1225
  85.8 8.8 %collective-permute-start.22 = (bf16[368,256]{1,0:T(8,128)(2,1)}, bf16[368,256]{1,0:T(8,128)(2,1)S(1)}, u32[]{:S(2)}, u32[]{:S(2)}) collective-permute-start(bf16[368,256]{1,0:T(8,128)(2,1)} %get-tuple-element.141), channel_id=1, source_target_pairs={{0,24},{8,16},{16,8},{24,0},{1,25},{9,17},{17,9},{25,1},{2,26},{10... | collective-permute-start | bytes 565256 | tf_op jit(solution)/shard_map/ppermute | solution.py:1225
  88.3 9.4 %collective-permute-start.21 = (bf16[368,256]{1,0:T(8,128)(2,1)}, bf16[368,256]{1,0:T(8,128)(2,1)S(1)}, u32[]{:S(2)}, u32[]{:S(2)}) collective-permute-start(bf16[368,256]{1,0:T(8,128)(2,1)} %get-tuple-element.140), channel_id=1, source_target_pairs={{0,16},{8,24},{16,0},{24,8},{1,17},{9,25},{17,1},{25,9},{2,18},{10... | collective-permute-start | bytes 565256 | tf_op jit(solution)/shard_map/ppermute | solution.py:1225
  88.8 9.1 %collective-permute-start.20 = (bf16[368,256]{1,0:T(8,128)(2,1)}, bf16[368,256]{1,0:T(8,128)(2,1)S(1)}, u32[]{:S(2)}, u32[]{:S(2)}) collective-permute-start(bf16[368,256]{1,0:T(8,128)(2,1)} %get-tuple-element.139), channel_id=1, source_target_pairs={{0,8},{8,0},{16,24},{24,16},{1,9},{9,1},{17,25},{25,17},{2,10},{10... | collective-permute-start | bytes 565256 | tf_op jit(solution)/shard_map/ppermute | solution.py:1225
  89.4 9.6 %collective-permute-start.23 = (bf16[256,128]{1,0:T(8,128)(2,1)S(1)}, bf16[256,128]{1,0:T(8,128)(2,1)S(1)}, u32[]{:S(2)}, u32[]{:S(2)}) collective-permute-start(bf16[256,128]{1,0:T(8,128)(2,1)S(1)} %get-tuple-element.143), channel_id=1, source_target_pairs={{0,1},{1,0},{2,3},{3,2},{4,5},{5,4},{6,7},{7,6},{8,9},{9,8},{10,11... | collective-permute-start | bytes 196616 | tf_op jit(solution)/shard_map/ppermute | solution.py:1225
  89.4 9.6 %collective-permute-start.24 = (bf16[256,128]{1,0:T(8,128)(2,1)S(1)}, bf16[256,128]{1,0:T(8,128)(2,1)S(1)}, u32[]{:S(2)}, u32[]{:S(2)}) collective-permute-start(bf16[256,128]{1,0:T(8,128)(2,1)S(1)} %get-tuple-element.144), channel_id=1, source_target_pairs={{0,2},{1,3},{2,0},{3,1},{4,6},{5,7},{6,4},{7,5},{8,10},{9,11},{10,... | collective-permute-start | bytes 196616 | tf_op jit(solution)/shard_map/ppermute | solution.py:1225
  94.6 4.3 %collective-permute-start.25 = (bf16[256,128]{1,0:T(8,128)(2,1)S(1)}, bf16[256,128]{1,0:T(8,128)(2,1)S(1)}, u32[]{:S(2)}, u32[]{:S(2)}) collective-permute-start(bf16[256,128]{1,0:T(8,128)(2,1)S(1)} %get-tuple-element.145), channel_id=1, source_target_pairs={{0,3},{1,2},{2,1},{3,0},{4,7},{5,6},{6,5},{7,4},{8,11},{9,10},{10,... | collective-permute-start | bytes 196616 | tf_op jit(solution)/shard_map/ppermute | solution.py:1225
  99.0 12.6 %collective-permute-start.27 = (bf16[368,256]{1,0:T(8,128)(2,1)S(1)}, bf16[368,256]{1,0:T(8,128)(2,1)S(1)}, u32[]{:S(2)}, u32[]{:S(2)}) collective-permute-start(bf16[368,256]{1,0:T(8,128)(2,1)S(1)} %add_convert_fusion.1), channel_id=1, source_target_pairs={{0,4},{1,5},{2,6},{3,7},{4,0},{5,1},{6,2},{7,3},{8,12},{9,13},{10,... | collective-permute-start | bytes 565256 | tf_op jit(solution)/shard_map/ppermute | solution.py:1225
  102.7 19.2 %copy-start.1 = (bf16[256,256]{1,0:T(8,128)(2,1)S(1)}, bf16[256,256]{1,0:T(8,128)(2,1)}, u32[]{:S(2)}) copy-start(bf16[256,256]{1,0:T(8,128)(2,1)} %refs_12_.1) | copy-start | bytes 393220
  109.5 14.0 %copy-start.6 = (bf16[256,256]{1,0:T(8,128)(2,1)S(1)}, bf16[256,256]{1,0:T(8,128)(2,1)}, u32[]{:S(2)}) copy-start(bf16[256,256]{1,0:T(8,128)(2,1)} %get-tuple-element.157) | copy-start | bytes 393220
  110.2 4.7 %collective-permute-start.29 = (bf16[16,256]{1,0:T(8,128)(2,1)S(1)}, bf16[16,256]{1,0:T(8,128)(2,1)S(1)}, u32[]{:S(2)}, u32[]{:S(2)}) collective-permute-start(bf16[16,256]{1,0:T(8,128)(2,1)S(1)} %concatenate.10), channel_id=1, source_target_pairs={{0,4},{1,5},{2,6},{3,7},{4,0},{5,1},{6,2},{7,3},{8,12},{9,13},{10,... | collective-permute-start | bytes 24584 | tf_op jit(solution)/shard_map/ppermute | solution.py:1225
  111.6 6.7 %collective-permute-start.28 = (bf16[368,256]{1,0:T(8,128)(2,1)S(1)}, bf16[368,256]{1,0:T(8,128)(2,1)S(1)}, u32[]{:S(2)}, u32[]{:S(2)}) collective-permute-start(bf16[368,256]{1,0:T(8,128)(2,1)S(1)} %add_convert_fusion), channel_id=1, source_target_pairs={{0,2},{1,3},{2,0},{3,1},{4,6},{5,7},{6,4},{7,5},{8,10},{9,11},{10,... | collective-permute-start | bytes 565256 | tf_op jit(solution)/shard_map/ppermute | solution.py:1225
  118.4 11.9 %collective-permute-start.31 = (bf16[752,256]{1,0:T(8,128)(2,1)S(1)}, bf16[752,256]{1,0:T(8,128)(2,1)S(1)}, u32[]{:S(2)}, u32[]{:S(2)}) collective-permute-start(bf16[752,256]{1,0:T(8,128)(2,1)S(1)} %pad_maximum_fusion.refs_0_), channel_id=1, source_target_pairs={{0,8},{8,0},{16,24},{24,16},{1,9},{9,1},{17,25},{25,17},{2,10},{10... | collective-permute-start | bytes 1155080 | tf_op jit(solution)/shard_map/ppermute | solution.py:1225
  119.9 18.0 %collective-permute-start.33 = (bf16[752,256]{1,0:T(8,128)(2,1)S(1)}, bf16[752,256]{1,0:T(8,128)(2,1)S(1)}, u32[]{:S(2)}, u32[]{:S(2)}) collective-permute-start(bf16[752,256]{1,0:T(8,128)(2,1)S(1)} %pad_maximum_fusion.refs_0_), channel_id=1, source_target_pairs={{0,16},{8,24},{16,0},{24,8},{1,17},{9,25},{17,1},{25,9},{2,18},{10... | collective-permute-start | bytes 1155080 | tf_op jit(solution)/shard_map/ppermute | solution.py:1225
  120.0 17.8 %collective-permute-start.35 = (bf16[752,256]{1,0:T(8,128)(2,1)S(1)}, bf16[752,256]{1,0:T(8,128)(2,1)S(1)}, u32[]{:S(2)}, u32[]{:S(2)}) collective-permute-start(bf16[752,256]{1,0:T(8,128)(2,1)S(1)} %pad_maximum_fusion.refs_0_), channel_id=1, source_target_pairs={{0,24},{8,16},{16,8},{24,0},{1,25},{9,17},{17,9},{25,1},{2,26},{10... | collective-permute-start | bytes 1155080 | tf_op jit(solution)/shard_map/ppermute | solution.py:1225
  124.2 14.2 %collective-permute-start.26 = (bf16[2,256,256]{2,1,0:T(8,128)(2,1)}, bf16[2,256,256]{2,1,0:T(8,128)(2,1)}, u32[]{:S(2)}, u32[]{:S(2)}) collective-permute-start(bf16[2,256,256]{2,1,0:T(8,128)(2,1)} %pad_maximum_fusion.3), channel_id=1, source_target_pairs={{0,4},{1,5},{2,6},{3,7},{4,0},{5,1},{6,2},{7,3},{8,12},{9,13},{10,... | collective-permute-start | bytes 786440 | tf_op jit(solution)/shard_map/ppermute | solution.py:1225
  125.1 15.2 %collective-permute-start.30 = (bf16[752,256]{1,0:T(8,128)(2,1)S(1)}, bf16[752,256]{1,0:T(8,128)(2,1)S(1)}, u32[]{:S(2)}, u32[]{:S(2)}) collective-permute-start(bf16[752,256]{1,0:T(8,128)(2,1)S(1)} %pad_maximum_fusion.refs_0_), channel_id=1, source_target_pairs={{0,1},{1,0},{2,3},{3,2},{4,5},{5,4},{6,7},{7,6},{8,9},{9,8},{10,11... | collective-permute-start | bytes 1155080 | tf_op jit(solution)/shard_map/ppermute | solution.py:1225
  130.3 10.0 %collective-permute-start.32 = (bf16[752,256]{1,0:T(8,128)(2,1)S(1)}, bf16[752,256]{1,0:T(8,128)(2,1)S(1)}, u32[]{:S(2)}, u32[]{:S(2)}) collective-permute-start(bf16[752,256]{1,0:T(8,128)(2,1)S(1)} %collective-permute-done.31.refs_2_), channel_id=1, source_target_pairs={{0,1},{1,0},{2,3},{3,2},{4,5},{5,4},{6,7},{7,6},{8,9},{9,8},{10,11... | collective-permute-start | bytes 1155080 | tf_op jit(solution)/shard_map/ppermute | solution.py:1225
  137.9 2.4 %collective-permute-start.34 = (bf16[752,256]{1,0:T(8,128)(2,1)S(1)}, bf16[752,256]{1,0:T(8,128)(2,1)}, u32[]{:S(2)}, u32[]{:S(2)}) collective-permute-start(bf16[752,256]{1,0:T(8,128)(2,1)S(1)} %collective-permute-done.33.refs_4_), channel_id=1, source_target_pairs={{0,1},{1,0},{2,3},{3,2},{4,5},{5,4},{6,7},{7,6},{8,9},{9,8},{10,11... | collective-permute-start | bytes 1155080 | tf_op jit(solution)/shard_map/ppermute | solution.py:1225
  137.9 2.4 %collective-permute-start.36 = (bf16[752,256]{1,0:T(8,128)(2,1)S(1)}, bf16[752,256]{1,0:T(8,128)(2,1)}, u32[]{:S(2)}, u32[]{:S(2)}) collective-permute-start(bf16[752,256]{1,0:T(8,128)(2,1)S(1)} %collective-permute-done.35.refs_6_), channel_id=1, source_target_pairs={{0,1},{1,0},{2,3},{3,2},{4,5},{5,4},{6,7},{7,6},{8,9},{9,8},{10,11... | collective-permute-start | bytes 1155080 | tf_op jit(solution)/shard_map/ppermute | solution.py:1225
  (6 other events, 10.5 us)

commit v6 on v5

--- a/solution.py
+++ b/solution.py
@@ -553,7 +553,7 @@
     scale, shift, conv_bias_two, gain_three, bias_three = (vec[k : k + 1, :] for k in range(5, 10))
     inner = (pl.ds(cols, cells), pl.ds(channels, channels))
 
-    group = 4
+    group = 2
     size = group * cols
     count = rows // group
     zero = jnp.zeros((8, channels), jnp.float32)
@@ -622,7 +622,7 @@
         act_three[at, :] = (residual[at, :] * slope + start).astype(jnp.bfloat16)
         return carry
 
-    lax.fori_loop(0, rows, third, 0, unroll=4)
+    lax.fori_loop(0, rows, third, 0, unroll=True)
     finish_all(leaving)
 
 

time: 147 us -> 146 us (level)
  transfers between devices with their start and end apart: 37 -> 37, of which waited for: 15 -> 16; matrix products, arithmetic and copies ran while one was open for 4% -> 4% of each run, Pallas kernels for 26% -> 25%
where the time goes in v6:
time: 146 us
  Pallas kernels  71.3 us (49%)
  waiting for transfers between devices  36.3 us (25%)
  starting transfers between devices  29.2 us (20%)
  other arithmetic  5.95 us (4%)
    pallas_call x8, Pallas kernels, call(): pl.pallas_call(kernel, out_shape=[jax.ShapeDtypeStruct(*kind) for kind in...  71.3 us
    ppermute x37, waiting for transfers between devices, swap(): return lax.ppermute(value, axis, [(k, k ^ step) for k in range(count)])  36.3 us
    ppermute x37, starting transfers between devices, swap(): return lax.ppermute(value, axis, [(k, k ^ step) for k in range(count)])  29.2 us
  transfers between devices with their start and end apart: 37, of which 16 were waited for; matrix products, arithmetic and copies ran while one was open for 4% of the time, Pallas kernels for 25%

profile of v6, /device:TPU:0, one launch (start us, length us, event | category | flops | bytes accessed | tf_op | source)
XLA Modules:
  0.0 145.7 jit_solution(17759401593981283547)
XLA Ops:
  0.7 1.1 dynamic-slice_bitcast_fusion
  1.8 4.1 %collective-permute-start.1 = (bf16[256,256]{1,0:T(8,128)(2,1)S(1)}, bf16[256,256]{1,0:T(8,128)(2,1)S(1)}, u32[]{:S(2)}, u32[]{:S(2)}) collective-permute-start(bf16[256,256]{1,0:T(8,128)(2,1)S(1)} %get-tuple-element.180), channel_id=1, source_target_pairs={{0,4},{1,5},{2,6},{3,7},{4,0},{5,1},{6,2},{7,3},{8,12},{9,13},{10,... | collective-permute-start | bytes 393224 | tf_op jit(solution)/shard_map/ppermute | solution.py:1225
  5.9 1.3 collective-permute-start.2
  7.5 0.7 convert_element_type.41
  8.2 0.7 convert_element_type.42
  9.0 0.5 convolution_add_fusion.refs_0_
  9.5 4.8 %shard_map.331 = (f32[16,256]{1,0:T(8,128)S(1)}, bf16[256,384]{1,0:T(8,128)(2,1)S(1)}, bf16[256,128]{1,0:T(8,128)(2,1)S(1)}, f32[8,384]{1,0:T(8,128)S(1)}, bf16[...) custom-call(f32[2,512]{1,0:T(2,128)S(1)} %convolution_add_fusion.refs_0_, ...), custom_call_target="tpu_custom_call" | custom-call | flops 256 | bytes 2893328 | tf_op jit(solution)/shard_map/pallas_call | solution.py:1256
  14.4 1.5 %collective-permute-done.1.refs_6_ = bf16[256,256]{1,0:T(8,128)(2,1)S(1)} collective-permute-done((bf16[256,256]{1,0:T(8,128)(2,1)S(1)}, bf16[256,256]{1,0:T(8,128)(2,1)S(1)}, u32[]{:S(2)}, u32[]{:S(2)}) %collective-permute-start.1) | collective-permute-done | bytes 131104 | tf_op jit(solution)/shard_map/ppermute | solution.py:1225
  15.9 0.5 collective-permute-done.refs_5_
  16.4 0.5 collective-permute-start.4
  16.9 4.2 %collective-permute-start.8 = (bf16[256,256]{1,0:T(8,128)(2,1)S(1)}, bf16[256,256]{1,0:T(8,128)(2,1)S(1)}, u32[]{:S(2)}, u32[]{:S(2)}) collective-permute-start(bf16[256,256]{1,0:T(8,128)(2,1)S(1)} %get-tuple-element.110), channel_id=1, source_target_pairs={{0,4},{1,5},{2,6},{3,7},{4,0},{5,1},{6,2},{7,3},{8,12},{9,13},{10,... | collective-permute-start | bytes 393224 | tf_op jit(solution)/shard_map/ppermute | solution.py:1225
  21.2 0.4 collective-permute-start.9
  21.9 10.2 %shard_map.332 = (bf16[2048,256]{1,0:T(8,128)(2,1)S(1)}, bf16[2048,256]{1,0:T(8,128)(2,1)}, f32[2048,256]{1,0:T(8,128)}, f32[2048,256]{1,0:T(8,128)}, bf16[2048,...) custom-call(f32[16,256]{1,0:T(8,128)S(1)} %get-tuple-element.97.vec, ...), custom_call_target="tpu_custom_call" | custom-call | flops 15099494400 | bytes 3424256 | tf_op jit(solution)/shard_map/pallas_call | solution.py:1256
  32.3 0.4 collective-permute-start.10
  32.8 0.4 collective-permute-start.12
  33.2 0.5 collective-permute-done.10.refs_0_
  33.7 0.4 collective-permute-done.11.refs_1_
  34.3 17.6 %shard_map.333 = (bf16[2048,128]{1,0:T(8,128)(2,1)}, bf16[1024,128]{1,0:T(8,128)(2,1)}, bf16[2048,256]{1,0:T(8,128)(2,1)}, bf16[2048,128]{1,0:T(8,128)(2,1)}, f32[8,256]{1,0:T(8,128)}) custom-call(f32[16,256]{1,0:T(8,128)S(1)} %get-tuple-element.97.vec, bf16[2048,256]{1,0:T(8,128)(2,1)S(1)} %get-tuple-element.105.act_three.refs_4_, ...), custom_call_target="tpu_custom_call" | custom-call | flops 20535312384 | bytes 2387968 | tf_op jit(solution)/shard_map/pallas_call | solution.py:1256
  51.9 2.0 %collective-permute-start.14 = (bf16[2048,128]{1,0:T(8,128)(2,1)}, bf16[2048,128]{1,0:T(8,128)(2,1)S(1)}, u32[]{:S(2)}, u32[]{:S(2)}) collective-permute-start(bf16[2048,128]{1,0:T(8,128)(2,1)} %get-tuple-element.115.refs_3_.refs_4_), channel_id=1, source_target_pairs={{0,2},{1,3},{2,0},{3,1},{4,6},{5,7},{6,4},{7,5},{8,10},{9,11},{10,... | collective-permute-start | bytes 1572872 | tf_op jit(solution)/shard_map/ppermute | solution.py:1225
  54.3 13.9 %shard_map.334 = (bf16[3,192,2048]{2,1,0:T(8,128)(2,1)}, bf16[3,192,2048]{2,1,0:T(8,128)(2,1)}, bf16[4,80,256]{2,1,0:T(8,128)(2,1)}, bf16[256,128]{1,0:T(8,128)(...) custom-call(f32[16,256]{1,0:T(8,128)S(1)} %get-tuple-element.97.vec, ...), custom_call_target="tpu_custom_call" | custom-call | flops 16307453952 | bytes 5259264 | tf_op jit(solution)/shard_map/pallas_call | solution.py:1256
  68.2 3.7 %collective-permute-done.15.refs_7_ = bf16[1024,128]{1,0:T(8,128)(2,1)S(1)} collective-permute-done((bf16[1024,128]{1,0:T(8,128)(2,1)}, bf16[1024,128]{1,0:T(8,128)(2,1)S(1)}, u32[]{:S(2)}, u32[]{:S(2)}) %collective-permute-start.15) | collective-permute-done | bytes 262176 | tf_op jit(solution)/shard_map/ppermute | solution.py:1225
  72.0 0.5 collective-permute-start.19
  72.5 1.8 %collective-permute-done.19.refs_3_ = bf16[1024,128]{1,0:T(8,128)(2,1)S(1)} collective-permute-done((bf16[1024,128]{1,0:T(8,128)(2,1)S(1)}, bf16[1024,128]{1,0:T(8,128)(2,1)S(1)}, u32[]{:S(2)}, u32[]{:S(2)}) %collective-permute-start.19) | collective-permute-done | bytes 262176 | tf_op jit(solution)/shard_map/ppermute | solution.py:1225
  74.3 10.9 %shard_map.335 = (bf16[2176,768]{1,0:T(8,128)(2,1)S(1)}, f32[2048,256]{1,0:T(8,128)}, bf16[368,256]{1,0:T(8,128)(2,1)}, bf16[368,256]{1,0:T(8,128)(2,1)}, bf16[3...) custom-call(f32[16,256]{1,0:T(8,128)S(1)} %get-tuple-element.97.vec, bf16[12,64,256]{2,1,0:T(8,128)(2,1)S(1)} %get-tuple-element.121.qkv_t, ...), custom_call_target="tpu_custom_call" | custom-call | flops 15703474176 | bytes 14876672 | tf_op jit(solution)/shard_map/pallas_call | solution.py:1256
  85.2 2.5 %collective-permute-start.22 = (bf16[368,256]{1,0:T(8,128)(2,1)}, bf16[368,256]{1,0:T(8,128)(2,1)S(1)}, u32[]{:S(2)}, u32[]{:S(2)}) collective-permute-start(bf16[368,256]{1,0:T(8,128)(2,1)} %get-tuple-element.141), channel_id=1, source_target_pairs={{0,24},{8,16},{16,8},{24,0},{1,25},{9,17},{17,9},{25,1},{2,26},{10... | collective-permute-start | bytes 565256 | tf_op jit(solution)/shard_map/ppermute | solution.py:1225
  87.8 0.5 collective-permute-start.21
  88.3 0.5 collective-permute-start.20
  88.8 1.7 %collective-permute-start.24 = (bf16[256,128]{1,0:T(8,128)(2,1)S(1)}, bf16[256,128]{1,0:T(8,128)(2,1)S(1)}, u32[]{:S(2)}, u32[]{:S(2)}) collective-permute-start(bf16[256,128]{1,0:T(8,128)(2,1)S(1)} %get-tuple-element.144), channel_id=1, source_target_pairs={{0,2},{1,3},{2,0},{3,1},{4,6},{5,7},{6,4},{7,5},{8,10},{9,11},{10,... | collective-permute-start | bytes 196616 | tf_op jit(solution)/shard_map/ppermute | solution.py:1225
  90.5 3.5 %collective-permute-done.22 = bf16[368,256]{1,0:T(8,128)(2,1)S(1)} collective-permute-done((bf16[368,256]{1,0:T(8,128)(2,1)}, bf16[368,256]{1,0:T(8,128)(2,1)S(1)}, u32[]{:S(2)}, u32[]{:S(2)}) %collective-permute-start.22) | collective-permute-done | bytes 188448 | tf_op jit(solution)/shard_map/ppermute | solution.py:1225
  94.0 3.2 %collective-permute-done.21 = bf16[368,256]{1,0:T(8,128)(2,1)S(1)} collective-permute-done((bf16[368,256]{1,0:T(8,128)(2,1)}, bf16[368,256]{1,0:T(8,128)(2,1)S(1)}, u32[]{:S(2)}, u32[]{:S(2)}) %collective-permute-start.21) | collective-permute-done | bytes 188448 | tf_op jit(solution)/shard_map/ppermute | solution.py:1225
  97.3 1.0 add_convert_fusion.1
  98.4 3.8 %collective-permute-start.27 = (bf16[368,256]{1,0:T(8,128)(2,1)S(1)}, bf16[368,256]{1,0:T(8,128)(2,1)S(1)}, u32[]{:S(2)}, u32[]{:S(2)}) collective-permute-start(bf16[368,256]{1,0:T(8,128)(2,1)S(1)} %add_convert_fusion.1), channel_id=1, source_target_pairs={{0,4},{1,5},{2,6},{3,7},{4,0},{5,1},{6,2},{7,3},{8,12},{9,13},{10,... | collective-permute-start | bytes 565256 | tf_op jit(solution)/shard_map/ppermute | solution.py:1225
  102.2 6.7 %shard_map.337 = (bf16[256,256]{1,0:T(8,128)(2,1)}, bf16[256,256]{1,0:T(8,128)(2,1)}, f32[8,256]{1,0:T(8,128)}) custom-call(f32[16,256]{1,0:T(8,128)S(1)} %get-tuple-element.97.vec, bf16[2176,768]{1,0:T(8,128)(2,1)S(1)} %get-tuple-element.151.shifted, bf16[3,768,256]{2,1,0:T(8,128)(2,1)} %get-tuple-element.152.weight_far, ...), custom_call_target="tpu_custom_call" | custom-call | flops 7247757312 | bytes 7692288 | tf_op jit(solution)/shard_map/pallas_call | solution.py:1256
  108.9 0.7 convert.4
  109.7 1.3 collective-permute-done.27
  111.2 3.1 %collective-permute-done.29 = bf16[16,256]{1,0:T(8,128)(2,1)S(1)} collective-permute-done((bf16[16,256]{1,0:T(8,128)(2,1)S(1)}, bf16[16,256]{1,0:T(8,128)(2,1)S(1)}, u32[]{:S(2)}, u32[]{:S(2)}) %collective-permute-start.29) | collective-permute-done | bytes 8224 | tf_op jit(solution)/shard_map/ppermute | solution.py:1225
  114.3 3.5 %collective-permute-done.28 = bf16[368,256]{1,0:T(8,128)(2,1)S(1)} collective-permute-done((bf16[368,256]{1,0:T(8,128)(2,1)S(1)}, bf16[368,256]{1,0:T(8,128)(2,1)S(1)}, u32[]{:S(2)}, u32[]{:S(2)}) %collective-permute-start.28) | collective-permute-done | bytes 188448 | tf_op jit(solution)/shard_map/ppermute | solution.py:1225
  117.8 1.5 %collective-permute-start.31 = (bf16[752,256]{1,0:T(8,128)(2,1)S(1)}, bf16[752,256]{1,0:T(8,128)(2,1)S(1)}, u32[]{:S(2)}, u32[]{:S(2)}) collective-permute-start(bf16[752,256]{1,0:T(8,128)(2,1)S(1)} %pad_maximum_fusion.refs_0_), channel_id=1, source_target_pairs={{0,8},{8,0},{16,24},{24,16},{1,9},{9,1},{17,25},{25,17},{2,10},{10... | collective-permute-start | bytes 1155080 | tf_op jit(solution)/shard_map/ppermute | solution.py:1225
  119.5 1.9 %collective-permute-start.35 = (bf16[752,256]{1,0:T(8,128)(2,1)S(1)}, bf16[752,256]{1,0:T(8,128)(2,1)S(1)}, u32[]{:S(2)}, u32[]{:S(2)}) collective-permute-start(bf16[752,256]{1,0:T(8,128)(2,1)S(1)} %pad_maximum_fusion.refs_0_), channel_id=1, source_target_pairs={{0,24},{8,16},{16,8},{24,0},{1,25},{9,17},{17,9},{25,1},{2,26},{10... | collective-permute-start | bytes 1155080 | tf_op jit(solution)/shard_map/ppermute | solution.py:1225
  121.4 1.5 %shard_map.336 = (bf16[256,256]{1,0:T(8,128)(2,1)S(1)}, bf16[256,256]{1,0:T(8,128)(2,1)S(1)}) custom-call(f32[16,256]{1,0:T(8,128)S(1)} %get-tuple-element.97.vec, bf16[4,64,256]{2,1,0:T(8,128)(2,1)S(1)} %bitcast.26, bf16[256,128]{1,0:T(8,128)(2,1)S(1)} %get-tuple-element.146.refs_0_, bf16[256,128]{1,0:T(8,128)(2,1)S(1)} %collective-permute-done.23.refs_1_, ...), custom_call_target="tpu_custom_call" | custom-call | flops 603979776 | bytes 2506752 | tf_op jit(solution)/shard_map/pallas_call | solution.py:1256
  122.9 0.7 pad_maximum_fusion.3
  123.6 0.9 collective-permute-start.26
  124.5 5.2 %collective-permute-done.31.refs_2_ = bf16[752,256]{1,0:T(8,128)(2,1)S(1)} collective-permute-done((bf16[752,256]{1,0:T(8,128)(2,1)S(1)}, bf16[752,256]{1,0:T(8,128)(2,1)S(1)}, u32[]{:S(2)}, u32[]{:S(2)}) %collective-permute-start.31) | collective-permute-done | bytes 385056 | tf_op jit(solution)/shard_map/ppermute | solution.py:1225
  129.8 7.5 %collective-permute-done.33.refs_4_ = bf16[752,256]{1,0:T(8,128)(2,1)S(1)} collective-permute-done((bf16[752,256]{1,0:T(8,128)(2,1)S(1)}, bf16[752,256]{1,0:T(8,128)(2,1)S(1)}, u32[]{:S(2)}, u32[]{:S(2)}) %collective-permute-start.33) | collective-permute-done | bytes 385056 | tf_op jit(solution)/shard_map/ppermute | solution.py:1225
  137.3 0.5 collective-permute-start.36
  137.9 1.0 select_bitcast_fusion
  138.9 0.8 pad_maximum_fusion.1
  139.7 5.8 %shard_map.338 = (f32[9,256,256]{2,1,0:T(8,128)}, f32[9,256,256]{2,1,0:T(8,128)}, f32[256,768]{1,0:T(8,128)}, f32[256,256]{1,0:T(8,128)}, f32[1024,512]{1,0:T(8,...) custom-call(bf16[752,256]{1,0:T(8,128)(2,1)S(1)} %pad_maximum_fusion, ...), custom_call_target="tpu_custom_call" | custom-call | flops 603979776 | bytes 3082240 | tf_op jit(solution)/shard_map/pallas_call | solution.py:1256
  (85 shorter events, 2.3 us)
Async XLA Ops:
  0.7 8.3 %copy-start = (bf16[1024,512]{1,0:T(8,128)(2,1)S(1)}, bf16[1024,512]{1,0:T(8,128)(2,1)}, u32[]{:S(2)}) copy-start(bf16[1024,512]{1,0:T(8,128)(2,1)} %param.27) | copy-start | bytes 3145732
  1.8 12.6 %copy-start.5 = (bf16[256,256]{1,0:T(8,128)(2,1)}, bf16[256,256]{1,0:T(8,128)(2,1)S(1)}, u32[]{:S(2)}) copy-start(bf16[256,256]{1,0:T(8,128)(2,1)S(1)} %get-tuple-element.181.refs_3_) | copy-start | bytes 393220
  1.8 12.5 %copy-start.3 = (bf16[2,4,64,256]{3,2,1,0:T(8,128)(2,1)S(1)}, bf16[2,4,64,256]{3,2,1,0:T(8,128)(2,1)}, u32[]{:S(2)}) copy-start(bf16[2,4,64,256]{3,2,1,0:T(8,128)(2,1)} %param.39) | copy-start | bytes 786436
  1.8 14.1 %collective-permute-start.1 = (bf16[256,256]{1,0:T(8,128)(2,1)S(1)}, bf16[256,256]{1,0:T(8,128)(2,1)S(1)}, u32[]{:S(2)}, u32[]{:S(2)}) collective-permute-start(bf16[256,256]{1,0:T(8,128)(2,1)S(1)} %get-tuple-element.180), channel_id=1, source_target_pairs={{0,4},{1,5},{2,6},{3,7},{4,0},{5,1},{6,2},{7,3},{8,12},{9,13},{10,... | collective-permute-start | bytes 393224 | tf_op jit(solution)/shard_map/ppermute | solution.py:1225
  5.9 10.0 %collective-permute-start.2 = (bf16[256,256]{1,0:T(8,128)(2,1)S(1)}, bf16[256,256]{1,0:T(8,128)(2,1)S(1)}, u32[]{:S(2)}, u32[]{:S(2)}) collective-permute-start(bf16[256,256]{1,0:T(8,128)(2,1)S(1)} %get-tuple-element.180), channel_id=1, source_target_pairs={{0,6},{1,7},{2,4},{3,5},{4,2},{5,3},{6,0},{7,1},{8,14},{9,15},{10,... | collective-permute-start | bytes 393224 | tf_op jit(solution)/shard_map/ppermute | solution.py:1225
  7.2 9.2 %collective-permute-start = (bf16[256,256]{1,0:T(8,128)(2,1)S(1)}, bf16[256,256]{1,0:T(8,128)(2,1)S(1)}, u32[]{:S(2)}, u32[]{:S(2)}) collective-permute-start(bf16[256,256]{1,0:T(8,128)(2,1)S(1)} %get-tuple-element.181.refs_3_), channel_id=1, source_target_pairs={{0,2},{1,3},{2,0},{3,1},{4,6},{5,7},{6,4},{7,5},{8,10},{9,11},{10,... | collective-permute-start | bytes 393224 | tf_op jit(solution)/shard_map/ppermute | solution.py:1225
  7.5 13.7 %collective-permute-start.6 = (bf16[256,256]{1,0:T(8,128)(2,1)S(1)}, bf16[256,256]{1,0:T(8,128)(2,1)S(1)}, u32[]{:S(2)}, u32[]{:S(2)}) collective-permute-start(bf16[256,256]{1,0:T(8,128)(2,1)S(1)} %get-tuple-element.181.refs_3_), channel_id=1, source_target_pairs={{0,1},{1,0},{2,3},{3,2},{4,5},{5,4},{6,7},{7,6},{8,9},{9,8},{10,11... | collective-permute-start | bytes 393224 | tf_op jit(solution)/shard_map/ppermute | solution.py:1225
  14.4 17.7 %copy-start.4 = (bf16[256,256]{1,0:T(8,128)(2,1)}, bf16[256,256]{1,0:T(8,128)(2,1)S(1)}, u32[]{:S(2)}) copy-start(bf16[256,256]{1,0:T(8,128)(2,1)S(1)} %get-tuple-element.109.refs_3_) | copy-start | bytes 393220
  15.9 5.9 %copy-start.9 = (bf16[256,256]{1,0:T(8,128)(2,1)}, bf16[256,256]{1,0:T(8,128)(2,1)S(1)}, u32[]{:S(2)}) copy-start(bf16[256,256]{1,0:T(8,128)(2,1)S(1)} %collective-permute-done.1.refs_6_) | copy-start | bytes 393220
  15.9 5.9 %copy-start.10 = (bf16[256,256]{1,0:T(8,128)(2,1)}, bf16[256,256]{1,0:T(8,128)(2,1)S(1)}, u32[]{:S(2)}) copy-start(bf16[256,256]{1,0:T(8,128)(2,1)S(1)} %collective-permute-done.2.refs_7_) | copy-start | bytes 393220
  16.4 5.4 %copy-start.11 = (bf16[256,256]{1,0:T(8,128)(2,1)}, bf16[256,256]{1,0:T(8,128)(2,1)S(1)}, u32[]{:S(2)}) copy-start(bf16[256,256]{1,0:T(8,128)(2,1)S(1)} %collective-permute-done.refs_5_) | copy-start | bytes 393220
  16.4 5.1 %collective-permute-start.3 = (bf16[256,256]{1,0:T(8,128)(2,1)S(1)}, bf16[256,256]{1,0:T(8,128)(2,1)S(1)}, u32[]{:S(2)}, u32[]{:S(2)}) collective-permute-start(bf16[256,256]{1,0:T(8,128)(2,1)S(1)} %collective-permute-done.refs_5_), channel_id=1, source_target_pairs={{0,1},{1,0},{2,3},{3,2},{4,5},{5,4},{6,7},{7,6},{8,9},{9,8},{10,11... | collective-permute-start | bytes 393224 | tf_op jit(solution)/shard_map/ppermute | solution.py:1225
  16.4 5.4 %collective-permute-start.4 = (bf16[256,256]{1,0:T(8,128)(2,1)S(1)}, bf16[256,256]{1,0:T(8,128)(2,1)S(1)}, u32[]{:S(2)}, u32[]{:S(2)}) collective-permute-start(bf16[256,256]{1,0:T(8,128)(2,1)S(1)} %collective-permute-done.1.refs_6_), channel_id=1, source_target_pairs={{0,1},{1,0},{2,3},{3,2},{4,5},{5,4},{6,7},{7,6},{8,9},{9,8},{10,11... | collective-permute-start | bytes 393224 | tf_op jit(solution)/shard_map/ppermute | solution.py:1225
  16.9 4.9 %collective-permute-start.5 = (bf16[256,256]{1,0:T(8,128)(2,1)S(1)}, bf16[256,256]{1,0:T(8,128)(2,1)S(1)}, u32[]{:S(2)}, u32[]{:S(2)}) collective-permute-start(bf16[256,256]{1,0:T(8,128)(2,1)S(1)} %collective-permute-done.2.refs_7_), channel_id=1, source_target_pairs={{0,1},{1,0},{2,3},{3,2},{4,5},{5,4},{6,7},{7,6},{8,9},{9,8},{10,11... | collective-permute-start | bytes 393224 | tf_op jit(solution)/shard_map/ppermute | solution.py:1225
  16.9 15.3 %collective-permute-start.8 = (bf16[256,256]{1,0:T(8,128)(2,1)S(1)}, bf16[256,256]{1,0:T(8,128)(2,1)S(1)}, u32[]{:S(2)}, u32[]{:S(2)}) collective-permute-start(bf16[256,256]{1,0:T(8,128)(2,1)S(1)} %get-tuple-element.110), channel_id=1, source_target_pairs={{0,4},{1,5},{2,6},{3,7},{4,0},{5,1},{6,2},{7,3},{8,12},{9,13},{10,... | collective-permute-start | bytes 393224 | tf_op jit(solution)/shard_map/ppermute | solution.py:1225
  21.2 11.1 %collective-permute-start.9 = (bf16[256,256]{1,0:T(8,128)(2,1)S(1)}, bf16[256,256]{1,0:T(8,128)(2,1)S(1)}, u32[]{:S(2)}, u32[]{:S(2)}) collective-permute-start(bf16[256,256]{1,0:T(8,128)(2,1)S(1)} %get-tuple-element.110), channel_id=1, source_target_pairs={{0,6},{1,7},{2,4},{3,5},{4,2},{5,3},{6,0},{7,1},{8,14},{9,15},{10,... | collective-permute-start | bytes 393224 | tf_op jit(solution)/shard_map/ppermute | solution.py:1225
  21.6 10.7 %collective-permute-start.7 = (bf16[256,256]{1,0:T(8,128)(2,1)S(1)}, bf16[256,256]{1,0:T(8,128)(2,1)S(1)}, u32[]{:S(2)}, u32[]{:S(2)}) collective-permute-start(bf16[256,256]{1,0:T(8,128)(2,1)S(1)} %get-tuple-element.109.refs_3_), channel_id=1, source_target_pairs={{0,2},{1,3},{2,0},{3,1},{4,6},{5,7},{6,4},{7,5},{8,10},{9,11},{10,... | collective-permute-start | bytes 393224 | tf_op jit(solution)/shard_map/ppermute | solution.py:1225
  21.8 11.4 %collective-permute-start.13 = (bf16[256,256]{1,0:T(8,128)(2,1)S(1)}, bf16[256,256]{1,0:T(8,128)(2,1)S(1)}, u32[]{:S(2)}, u32[]{:S(2)}) collective-permute-start(bf16[256,256]{1,0:T(8,128)(2,1)S(1)} %get-tuple-element.109.refs_3_), channel_id=1, source_target_pairs={{0,1},{1,0},{2,3},{3,2},{4,5},{5,4},{6,7},{7,6},{8,9},{9,8},{10,11... | collective-permute-start | bytes 393224 | tf_op jit(solution)/shard_map/ppermute | solution.py:1225
  32.1 19.8 %copy-start.2 = (bf16[2048,256]{1,0:T(8,128)(2,1)}, bf16[2048,256]{1,0:T(8,128)(2,1)S(1)}, u32[]{:S(2)}) copy-start(bf16[2048,256]{1,0:T(8,128)(2,1)S(1)} %get-tuple-element.105.act_three.refs_4_) | copy-start | bytes 3145732
  32.3 1.4 collective-permute-start.10
  32.7 1.3 collective-permute-start.11
  32.8 1.4 collective-permute-start.12
  51.9 20.1 %collective-permute-start.14 = (bf16[2048,128]{1,0:T(8,128)(2,1)}, bf16[2048,128]{1,0:T(8,128)(2,1)S(1)}, u32[]{:S(2)}, u32[]{:S(2)}) collective-permute-start(bf16[2048,128]{1,0:T(8,128)(2,1)} %get-tuple-element.115.refs_3_.refs_4_), channel_id=1, source_target_pairs={{0,2},{1,3},{2,0},{3,1},{4,6},{5,7},{6,4},{7,5},{8,10},{9,11},{10,... | collective-permute-start | bytes 1572872 | tf_op jit(solution)/shard_map/ppermute | solution.py:1225
  53.8 18.1 %collective-permute-start.16 = (bf16[2048,128]{1,0:T(8,128)(2,1)}, bf16[2048,128]{1,0:T(8,128)(2,1)S(1)}, u32[]{:S(2)}, u32[]{:S(2)}) collective-permute-start(bf16[2048,128]{1,0:T(8,128)(2,1)} %get-tuple-element.115.refs_3_.refs_4_), channel_id=1, source_target_pairs={{0,1},{1,0},{2,3},{3,2},{4,5},{5,4},{6,7},{7,6},{8,9},{9,8},{10,11... | collective-permute-start | bytes 1572872 | tf_op jit(solution)/shard_map/ppermute | solution.py:1225
  53.8 18.1 %collective-permute-start.15 = (bf16[1024,128]{1,0:T(8,128)(2,1)}, bf16[1024,128]{1,0:T(8,128)(2,1)S(1)}, u32[]{:S(2)}, u32[]{:S(2)}) collective-permute-start(bf16[1024,128]{1,0:T(8,128)(2,1)} %get-tuple-element.122.refs_5_), channel_id=1, source_target_pairs={{0,2},{1,3},{2,0},{3,1},{4,6},{5,7},{6,4},{7,5},{8,10},{9,11},{10,... | collective-permute-start | bytes 786440 | tf_op jit(solution)/shard_map/ppermute | solution.py:1225
  54.1 17.8 %collective-permute-start.17 = (bf16[1024,128]{1,0:T(8,128)(2,1)}, bf16[1024,128]{1,0:T(8,128)(2,1)S(1)}, u32[]{:S(2)}, u32[]{:S(2)}) collective-permute-start(bf16[1024,128]{1,0:T(8,128)(2,1)} %get-tuple-element.122.refs_5_), channel_id=1, source_target_pairs={{0,1},{1,0},{2,3},{3,2},{4,5},{5,4},{6,7},{7,6},{8,9},{9,8},{10,11... | collective-permute-start | bytes 786440 | tf_op jit(solution)/shard_map/ppermute | solution.py:1225
  71.9 2.4 %copy-start.8 = (bf16[1024,128]{1,0:T(8,128)(2,1)}, bf16[1024,128]{1,0:T(8,128)(2,1)S(1)}, u32[]{:S(2)}) copy-start(bf16[1024,128]{1,0:T(8,128)(2,1)S(1)} %collective-permute-done.15.refs_7_) | copy-start | bytes 786436
  72.0 2.4 %collective-permute-start.18 = (bf16[2048,128]{1,0:T(8,128)(2,1)S(1)}, bf16[2048,128]{1,0:T(8,128)(2,1)S(1)}, u32[]{:S(2)}, u32[]{:S(2)}) collective-permute-start(bf16[2048,128]{1,0:T(8,128)(2,1)S(1)} %collective-permute-done.14.refs_6_), channel_id=1, source_target_pairs={{0,1},{1,0},{2,3},{3,2},{4,5},{5,4},{6,7},{7,6},{8,9},{9,8},{10,11... | collective-permute-start | bytes 1572872 | tf_op jit(solution)/shard_map/ppermute | solution.py:1225
  72.0 2.3 %collective-permute-start.19 = (bf16[1024,128]{1,0:T(8,128)(2,1)S(1)}, bf16[1024,128]{1,0:T(8,128)(2,1)S(1)}, u32[]{:S(2)}, u32[]{:S(2)}) collective-permute-start(bf16[1024,128]{1,0:T(8,128)(2,1)S(1)} %collective-permute-done.15.refs_7_), channel_id=1, source_target_pairs={{0,1},{1,0},{2,3},{3,2},{4,5},{5,4},{6,7},{7,6},{8,9},{9,8},{10,11... | collective-permute-start | bytes 786440 | tf_op jit(solution)/shard_map/ppermute | solution.py:1225
  85.2 8.8 %collective-permute-start.22 = (bf16[368,256]{1,0:T(8,128)(2,1)}, bf16[368,256]{1,0:T(8,128)(2,1)S(1)}, u32[]{:S(2)}, u32[]{:S(2)}) collective-permute-start(bf16[368,256]{1,0:T(8,128)(2,1)} %get-tuple-element.141), channel_id=1, source_target_pairs={{0,24},{8,16},{16,8},{24,0},{1,25},{9,17},{17,9},{25,1},{2,26},{10... | collective-permute-start | bytes 565256 | tf_op jit(solution)/shard_map/ppermute | solution.py:1225
  87.8 9.4 %collective-permute-start.21 = (bf16[368,256]{1,0:T(8,128)(2,1)}, bf16[368,256]{1,0:T(8,128)(2,1)S(1)}, u32[]{:S(2)}, u32[]{:S(2)}) collective-permute-start(bf16[368,256]{1,0:T(8,128)(2,1)} %get-tuple-element.140), channel_id=1, source_target_pairs={{0,16},{8,24},{16,0},{24,8},{1,17},{9,25},{17,1},{25,9},{2,18},{10... | collective-permute-start | bytes 565256 | tf_op jit(solution)/shard_map/ppermute | solution.py:1225
  88.3 9.1 %collective-permute-start.20 = (bf16[368,256]{1,0:T(8,128)(2,1)}, bf16[368,256]{1,0:T(8,128)(2,1)S(1)}, u32[]{:S(2)}, u32[]{:S(2)}) collective-permute-start(bf16[368,256]{1,0:T(8,128)(2,1)} %get-tuple-element.139), channel_id=1, source_target_pairs={{0,8},{8,0},{16,24},{24,16},{1,9},{9,1},{17,25},{25,17},{2,10},{10... | collective-permute-start | bytes 565256 | tf_op jit(solution)/shard_map/ppermute | solution.py:1225
  88.8 9.6 %collective-permute-start.23 = (bf16[256,128]{1,0:T(8,128)(2,1)S(1)}, bf16[256,128]{1,0:T(8,128)(2,1)S(1)}, u32[]{:S(2)}, u32[]{:S(2)}) collective-permute-start(bf16[256,128]{1,0:T(8,128)(2,1)S(1)} %get-tuple-element.143), channel_id=1, source_target_pairs={{0,1},{1,0},{2,3},{3,2},{4,5},{5,4},{6,7},{7,6},{8,9},{9,8},{10,11... | collective-permute-start | bytes 196616 | tf_op jit(solution)/shard_map/ppermute | solution.py:1225
  88.8 9.6 %collective-permute-start.24 = (bf16[256,128]{1,0:T(8,128)(2,1)S(1)}, bf16[256,128]{1,0:T(8,128)(2,1)S(1)}, u32[]{:S(2)}, u32[]{:S(2)}) collective-permute-start(bf16[256,128]{1,0:T(8,128)(2,1)S(1)} %get-tuple-element.144), channel_id=1, source_target_pairs={{0,2},{1,3},{2,0},{3,1},{4,6},{5,7},{6,4},{7,5},{8,10},{9,11},{10,... | collective-permute-start | bytes 196616 | tf_op jit(solution)/shard_map/ppermute | solution.py:1225
  94.0 4.4 %collective-permute-start.25 = (bf16[256,128]{1,0:T(8,128)(2,1)S(1)}, bf16[256,128]{1,0:T(8,128)(2,1)S(1)}, u32[]{:S(2)}, u32[]{:S(2)}) collective-permute-start(bf16[256,128]{1,0:T(8,128)(2,1)S(1)} %get-tuple-element.145), channel_id=1, source_target_pairs={{0,3},{1,2},{2,1},{3,0},{4,7},{5,6},{6,5},{7,4},{8,11},{9,10},{10,... | collective-permute-start | bytes 196616 | tf_op jit(solution)/shard_map/ppermute | solution.py:1225
  98.4 12.6 %collective-permute-start.27 = (bf16[368,256]{1,0:T(8,128)(2,1)S(1)}, bf16[368,256]{1,0:T(8,128)(2,1)S(1)}, u32[]{:S(2)}, u32[]{:S(2)}) collective-permute-start(bf16[368,256]{1,0:T(8,128)(2,1)S(1)} %add_convert_fusion.1), channel_id=1, source_target_pairs={{0,4},{1,5},{2,6},{3,7},{4,0},{5,1},{6,2},{7,3},{8,12},{9,13},{10,... | collective-permute-start | bytes 565256 | tf_op jit(solution)/shard_map/ppermute | solution.py:1225
  102.2 19.2 %copy-start.1 = (bf16[256,256]{1,0:T(8,128)(2,1)S(1)}, bf16[256,256]{1,0:T(8,128)(2,1)}, u32[]{:S(2)}) copy-start(bf16[256,256]{1,0:T(8,128)(2,1)} %refs_12_.1) | copy-start | bytes 393220
  108.9 14.0 %copy-start.6 = (bf16[256,256]{1,0:T(8,128)(2,1)S(1)}, bf16[256,256]{1,0:T(8,128)(2,1)}, u32[]{:S(2)}) copy-start(bf16[256,256]{1,0:T(8,128)(2,1)} %get-tuple-element.157) | copy-start | bytes 393220
  109.6 4.7 %collective-permute-start.29 = (bf16[16,256]{1,0:T(8,128)(2,1)S(1)}, bf16[16,256]{1,0:T(8,128)(2,1)S(1)}, u32[]{:S(2)}, u32[]{:S(2)}) collective-permute-start(bf16[16,256]{1,0:T(8,128)(2,1)S(1)} %concatenate.10), channel_id=1, source_target_pairs={{0,4},{1,5},{2,6},{3,7},{4,0},{5,1},{6,2},{7,3},{8,12},{9,13},{10,... | collective-permute-start | bytes 24584 | tf_op jit(solution)/shard_map/ppermute | solution.py:1225
  111.1 6.7 %collective-permute-start.28 = (bf16[368,256]{1,0:T(8,128)(2,1)S(1)}, bf16[368,256]{1,0:T(8,128)(2,1)S(1)}, u32[]{:S(2)}, u32[]{:S(2)}) collective-permute-start(bf16[368,256]{1,0:T(8,128)(2,1)S(1)} %add_convert_fusion), channel_id=1, source_target_pairs={{0,2},{1,3},{2,0},{3,1},{4,6},{5,7},{6,4},{7,5},{8,10},{9,11},{10,... | collective-permute-start | bytes 565256 | tf_op jit(solution)/shard_map/ppermute | solution.py:1225
  117.8 11.9 %collective-permute-start.31 = (bf16[752,256]{1,0:T(8,128)(2,1)S(1)}, bf16[752,256]{1,0:T(8,128)(2,1)S(1)}, u32[]{:S(2)}, u32[]{:S(2)}) collective-permute-start(bf16[752,256]{1,0:T(8,128)(2,1)S(1)} %pad_maximum_fusion.refs_0_), channel_id=1, source_target_pairs={{0,8},{8,0},{16,24},{24,16},{1,9},{9,1},{17,25},{25,17},{2,10},{10... | collective-permute-start | bytes 1155080 | tf_op jit(solution)/shard_map/ppermute | solution.py:1225
  119.4 18.0 %collective-permute-start.33 = (bf16[752,256]{1,0:T(8,128)(2,1)S(1)}, bf16[752,256]{1,0:T(8,128)(2,1)S(1)}, u32[]{:S(2)}, u32[]{:S(2)}) collective-permute-start(bf16[752,256]{1,0:T(8,128)(2,1)S(1)} %pad_maximum_fusion.refs_0_), channel_id=1, source_target_pairs={{0,16},{8,24},{16,0},{24,8},{1,17},{9,25},{17,1},{25,9},{2,18},{10... | collective-permute-start | bytes 1155080 | tf_op jit(solution)/shard_map/ppermute | solution.py:1225
  119.5 17.9 %collective-permute-start.35 = (bf16[752,256]{1,0:T(8,128)(2,1)S(1)}, bf16[752,256]{1,0:T(8,128)(2,1)S(1)}, u32[]{:S(2)}, u32[]{:S(2)}) collective-permute-start(bf16[752,256]{1,0:T(8,128)(2,1)S(1)} %pad_maximum_fusion.refs_0_), channel_id=1, source_target_pairs={{0,24},{8,16},{16,8},{24,0},{1,25},{9,17},{17,9},{25,1},{2,26},{10... | collective-permute-start | bytes 1155080 | tf_op jit(solution)/shard_map/ppermute | solution.py:1225
  123.6 14.2 %collective-permute-start.26 = (bf16[2,256,256]{2,1,0:T(8,128)(2,1)}, bf16[2,256,256]{2,1,0:T(8,128)(2,1)}, u32[]{:S(2)}, u32[]{:S(2)}) collective-permute-start(bf16[2,256,256]{2,1,0:T(8,128)(2,1)} %pad_maximum_fusion.3), channel_id=1, source_target_pairs={{0,4},{1,5},{2,6},{3,7},{4,0},{5,1},{6,2},{7,3},{8,12},{9,13},{10,... | collective-permute-start | bytes 786440 | tf_op jit(solution)/shard_map/ppermute | solution.py:1225
  124.5 15.2 %collective-permute-start.30 = (bf16[752,256]{1,0:T(8,128)(2,1)S(1)}, bf16[752,256]{1,0:T(8,128)(2,1)S(1)}, u32[]{:S(2)}, u32[]{:S(2)}) collective-permute-start(bf16[752,256]{1,0:T(8,128)(2,1)S(1)} %pad_maximum_fusion.refs_0_), channel_id=1, source_target_pairs={{0,1},{1,0},{2,3},{3,2},{4,5},{5,4},{6,7},{7,6},{8,9},{9,8},{10,11... | collective-permute-start | bytes 1155080 | tf_op jit(solution)/shard_map/ppermute | solution.py:1225
  129.8 10.0 %collective-permute-start.32 = (bf16[752,256]{1,0:T(8,128)(2,1)S(1)}, bf16[752,256]{1,0:T(8,128)(2,1)S(1)}, u32[]{:S(2)}, u32[]{:S(2)}) collective-permute-start(bf16[752,256]{1,0:T(8,128)(2,1)S(1)} %collective-permute-done.31.refs_2_), channel_id=1, source_target_pairs={{0,1},{1,0},{2,3},{3,2},{4,5},{5,4},{6,7},{7,6},{8,9},{9,8},{10,11... | collective-permute-start | bytes 1155080 | tf_op jit(solution)/shard_map/ppermute | solution.py:1225
  137.3 2.4 %collective-permute-start.34 = (bf16[752,256]{1,0:T(8,128)(2,1)S(1)}, bf16[752,256]{1,0:T(8,128)(2,1)}, u32[]{:S(2)}, u32[]{:S(2)}) collective-permute-start(bf16[752,256]{1,0:T(8,128)(2,1)S(1)} %collective-permute-done.33.refs_4_), channel_id=1, source_target_pairs={{0,1},{1,0},{2,3},{3,2},{4,5},{5,4},{6,7},{7,6},{8,9},{9,8},{10,11... | collective-permute-start | bytes 1155080 | tf_op jit(solution)/shard_map/ppermute | solution.py:1225
  137.3 2.4 %collective-permute-start.36 = (bf16[752,256]{1,0:T(8,128)(2,1)S(1)}, bf16[752,256]{1,0:T(8,128)(2,1)}, u32[]{:S(2)}, u32[]{:S(2)}) collective-permute-start(bf16[752,256]{1,0:T(8,128)(2,1)S(1)} %collective-permute-done.35.refs_6_), channel_id=1, source_target_pairs={{0,1},{1,0},{2,3},{3,2},{4,5},{5,4},{6,7},{7,6},{8,9},{9,8},{10,11... | collective-permute-start | bytes 1155080 | tf_op jit(solution)/shard_map/ppermute | solution.py:1225
  (6 other events, 10.1 us)

commit v7 on v6

--- a/solution.py
+++ b/solution.py
@@ -1147,14 +1147,14 @@
 
 
 def final_kernel(*refs):
-    parts, frequency = refs[:8], refs[8]
-    one_far, two_far, qkv_far, out_far, time_far = refs[9:14]
-    bias_out, time_bias, rows = refs[14], refs[15], refs[16:25]
-    one, two, qkv_rows, qkv_out, out_out, time_out, small, norm_one, sems, out_sems = refs[25:]
+    parts, begins, frequency = refs[:8], refs[8:12], refs[12]
+    one_far, two_far, qkv_far, out_far, time_far = refs[13:18]
+    bias_out, time_bias, rows = refs[18], refs[19], refs[20:29]
+    one, two, qkv_rows, qkv_out, out_out, time_out, small, norm_one, sems, out_sems = refs[29:]
     channels = one.shape[1]
     half = channels // HEADS
     unit = half // 4
-    lines = 18 * unit + half + 16
+    lines = 10 * unit + half + 16
     spot = lax.axis_index("row")
     head, column = spot % HEADS, lax.axis_index("img")
     leaving = []
@@ -1165,8 +1165,10 @@
             first = pl.multiple_of(quarter * half + away * unit, unit)
             at = pl.ds(first, unit)
             shape = (9, unit, channels)
-            late = base + 9 * unit + half
-            two[:, at, :] = part[base : base + 9 * unit].astype(jnp.float32).reshape(shape)
+            late = base + unit + half
+            begin = begins[2 * pair + index % 2][8 * unit * (index // 2) : 8 * unit * (index // 2 + 1)]
+            two[0:8, at, :] = begin.astype(jnp.float32).reshape((8, unit, channels))
+            two[8, at, :] = part[base : base + unit].astype(jnp.float32)
             one[:, at, :] = part[late : late + 9 * unit].astype(jnp.float32).reshape(shape)
             here = len(leaving)
             leaving += started(
@@ -1174,7 +1176,7 @@
                 (two.at[:, at, :], two_far.at[:, at, :]),
                 (one.at[:, at, :], one_far.at[:, at, :]),
             )
-            middle = base + 9 * unit
+            middle = base + unit
             for k in range(3):
                 to = pl.ds(pl.multiple_of(first + k * channels, unit), unit)
                 piece = part[middle + k * unit : middle + (k + 1) * unit]
@@ -1440,7 +1442,7 @@
     total = add_up(payload[0], *[swap(payload[step], "img", step) for step in (1, 2, 3)])
     heads_got = [sends[0]] + [swap(sends[step], "row", step) for step in (1, 2, 3)]
     shifted_one, total, *heads_got = lax.optimization_barrier((shifted_one, total, *heads_got))
-    both = add_up(total, swap(total, "row", 4))
+    received = swap(total, "row", 4)
     grad_own, grad_away, sums_one = call(
         first_kernel,
         [],
@@ -1466,16 +1468,28 @@
         [vec, out_weight.reshape(HEADS, half, channels), *heads_got],
         [residual],
     )
+    received, sums_one, block_away = lax.optimization_barrier((received, sums_one, block_away))
+    both = add_up(total, received)
+    norm_one = jnp.concatenate([sums_one, jnp.zeros_like(sums_one)], axis=0).astype(low)
+    norm_one = add_up(norm_one, swap(norm_one, "row", 4))
+    other = swap(both[8 * (half // 4) :], "row", 2)
+    begin = 8 * (half // 4)
+    first = from_columns(both[:begin])
+    block_away, grad_away, *first[1:] = lax.optimization_barrier(
+        (block_away, grad_away, *first[1:])
+    )
     out_pair = jnp.stack([block_own, grad_own])
     away_pair = swap(jnp.stack([block_away, grad_away]), "row", 4)
+    first = jnp.concatenate(first, axis=0)
+    beside = swap(first, "row", 2)
+    pair = jnp.concatenate([both[begin:], other, norm_one], axis=0)
+    columns = from_columns(pair)
+    away_pair, *columns[1:] = lax.optimization_barrier((away_pair, *columns[1:]))
     first_pair = jnp.where(image == 0, out_pair, away_pair)
     second_pair = jnp.where(image == 0, away_pair, out_pair)
     finished = jnp.stack([first_pair, second_pair], axis=1).reshape((2,) + pixels.shape)
-    norm_one = jnp.concatenate([sums_one, jnp.zeros_like(sums_one)], axis=0).astype(low)
-    norm_one = add_up(norm_one, swap(norm_one, "row", 4))
-    other = swap(both, "row", 2)
-    pair = jnp.concatenate([both, other, norm_one], axis=0)
-    parts = gather_columns(pair)
+    columns[1], first, beside = lax.optimization_barrier((columns[1], first, beside))
+    parts = with_mates(columns) + with_mates([first, beside])
     line = ((channels,), full)
     kernel_out = ((9, channels, channels), full)
     time_out = ((time_weight.shape[0], 2 * channels), full)

time: 146 us -> 142 us (0.973)
  waiting for transfers between devices: 36.3 us -> 26.7 us
  starting transfers between devices: 29.2 us -> 38.3 us
  other arithmetic: 5.95 us -> 3.53 us
    ppermute x37 -> x43, waiting for transfers between devices: 36.3 us -> 26.7 us  [swap(): return lax.ppermute(value, axis, [(k, k ^ step) for k in range(count)])]
    ppermute x37 -> x43, starting transfers between devices: 29.2 us -> 38.3 us  [swap(): return lax.ppermute(value, axis, [(k, k ^ step) for k in range(count)])]
  transfers between devices with their start and end apart: 37 -> 43, of which waited for: 16 -> 19; matrix products, arithmetic and copies ran while one was open for 4% -> 3% of each run, Pallas kernels for 25% -> 26%
where the time goes in v7:
time: 142 us
  Pallas kernels  70.3 us (50%)
  starting transfers between devices  38.3 us (27%)
  waiting for transfers between devices  26.7 us (19%)
  other arithmetic  3.53 us (2%)
    pallas_call x8, Pallas kernels, call(): pl.pallas_call(kernel, out_shape=[jax.ShapeDtypeStruct(*kind) for kind in...  70.3 us
    ppermute x43, starting transfers between devices, swap(): return lax.ppermute(value, axis, [(k, k ^ step) for k in range(count)])  38.3 us
    ppermute x43, waiting for transfers between devices, swap(): return lax.ppermute(value, axis, [(k, k ^ step) for k in range(count)])  26.7 us
  transfers between devices with their start and end apart: 43, of which 19 were waited for; matrix products, arithmetic and copies ran while one was open for 3% of the time, Pallas kernels for 26%

profile of v7, /device:TPU:0, one launch (start us, length us, event | category | flops | bytes accessed | tf_op | source)
XLA Modules:
  0.0 141.8 jit_solution(12302813833214994778)
XLA Ops:
  0.7 1.1 dynamic-slice_bitcast_fusion
  1.8 4.1 %collective-permute-start.1 = (bf16[256,256]{1,0:T(8,128)(2,1)S(1)}, bf16[256,256]{1,0:T(8,128)(2,1)S(1)}, u32[]{:S(2)}, u32[]{:S(2)}) collective-permute-start(bf16[256,256]{1,0:T(8,128)(2,1)S(1)} %get-tuple-element.210), channel_id=1, source_target_pairs={{0,4},{1,5},{2,6},{3,7},{4,0},{5,1},{6,2},{7,3},{8,12},{9,13},{10,... | collective-permute-start | bytes 393224 | tf_op jit(solution)/shard_map/ppermute | solution.py:1227
  5.9 1.3 collective-permute-start.2
  7.5 0.7 convert_element_type.41
  8.2 0.7 convert_element_type.42
  9.0 0.5 convolution_add_fusion.refs_0_
  9.5 4.8 %shard_map.331 = (f32[16,256]{1,0:T(8,128)S(1)}, bf16[256,384]{1,0:T(8,128)(2,1)S(1)}, bf16[256,128]{1,0:T(8,128)(2,1)S(1)}, f32[8,384]{1,0:T(8,128)S(1)}, bf16[...) custom-call(f32[2,512]{1,0:T(2,128)S(1)} %convolution_add_fusion.refs_0_, ...), custom_call_target="tpu_custom_call" | custom-call | flops 256 | bytes 2893328 | tf_op jit(solution)/shard_map/pallas_call | solution.py:1258
  14.4 1.5 %collective-permute-done.1.refs_6_ = bf16[256,256]{1,0:T(8,128)(2,1)S(1)} collective-permute-done((bf16[256,256]{1,0:T(8,128)(2,1)S(1)}, bf16[256,256]{1,0:T(8,128)(2,1)S(1)}, u32[]{:S(2)}, u32[]{:S(2)}) %collective-permute-start.1) | collective-permute-done | bytes 131104 | tf_op jit(solution)/shard_map/ppermute | solution.py:1227
  15.9 0.5 collective-permute-done.refs_5_
  16.4 0.5 collective-permute-start.4
  16.9 4.2 %collective-permute-start.8 = (bf16[256,256]{1,0:T(8,128)(2,1)S(1)}, bf16[256,256]{1,0:T(8,128)(2,1)S(1)}, u32[]{:S(2)}, u32[]{:S(2)}) collective-permute-start(bf16[256,256]{1,0:T(8,128)(2,1)S(1)} %get-tuple-element.125), channel_id=1, source_target_pairs={{0,4},{1,5},{2,6},{3,7},{4,0},{5,1},{6,2},{7,3},{8,12},{9,13},{10,... | collective-permute-start | bytes 393224 | tf_op jit(solution)/shard_map/ppermute | solution.py:1227
  21.2 0.4 collective-permute-start.9
  21.9 10.2 %shard_map.332 = (bf16[2048,256]{1,0:T(8,128)(2,1)S(1)}, bf16[2048,256]{1,0:T(8,128)(2,1)}, f32[2048,256]{1,0:T(8,128)}, f32[2048,256]{1,0:T(8,128)}, bf16[2048,...) custom-call(f32[16,256]{1,0:T(8,128)S(1)} %get-tuple-element.112.vec, ...), custom_call_target="tpu_custom_call" | custom-call | flops 15099494400 | bytes 3424256 | tf_op jit(solution)/shard_map/pallas_call | solution.py:1258
  32.3 0.4 collective-permute-start.10
  33.2 0.5 collective-permute-done.10.refs_0_
  34.3 17.6 %shard_map.333 = (bf16[2048,128]{1,0:T(8,128)(2,1)}, bf16[1024,128]{1,0:T(8,128)(2,1)}, bf16[2048,256]{1,0:T(8,128)(2,1)}, bf16[2048,128]{1,0:T(8,128)(2,1)}, f32[8,256]{1,0:T(8,128)}) custom-call(f32[16,256]{1,0:T(8,128)S(1)} %get-tuple-element.112.vec, bf16[2048,256]{1,0:T(8,128)(2,1)S(1)} %get-tuple-element.120.act_three.refs_4_, ...), custom_call_target="tpu_custom_call" | custom-call | flops 20535312384 | bytes 2387968 | tf_op jit(solution)/shard_map/pallas_call | solution.py:1258
  51.9 2.0 %collective-permute-start.14 = (bf16[2048,128]{1,0:T(8,128)(2,1)}, bf16[2048,128]{1,0:T(8,128)(2,1)S(1)}, u32[]{:S(2)}, u32[]{:S(2)}) collective-permute-start(bf16[2048,128]{1,0:T(8,128)(2,1)} %get-tuple-element.130.refs_3_.refs_4_), channel_id=1, source_target_pairs={{0,2},{1,3},{2,0},{3,1},{4,6},{5,7},{6,4},{7,5},{8,10},{9,11},{10,... | collective-permute-start | bytes 1572872 | tf_op jit(solution)/shard_map/ppermute | solution.py:1227
  54.4 13.9 %shard_map.334 = (bf16[3,192,2048]{2,1,0:T(8,128)(2,1)}, bf16[3,192,2048]{2,1,0:T(8,128)(2,1)}, bf16[4,80,256]{2,1,0:T(8,128)(2,1)}, bf16[256,128]{1,0:T(8,128)(...) custom-call(f32[16,256]{1,0:T(8,128)S(1)} %get-tuple-element.112.vec, ...), custom_call_target="tpu_custom_call" | custom-call | flops 16307453952 | bytes 5259264 | tf_op jit(solution)/shard_map/pallas_call | solution.py:1258
  68.3 3.7 %collective-permute-done.15.refs_7_ = bf16[1024,128]{1,0:T(8,128)(2,1)S(1)} collective-permute-done((bf16[1024,128]{1,0:T(8,128)(2,1)}, bf16[1024,128]{1,0:T(8,128)(2,1)S(1)}, u32[]{:S(2)}, u32[]{:S(2)}) %collective-permute-start.15) | collective-permute-done | bytes 262176 | tf_op jit(solution)/shard_map/ppermute | solution.py:1227
  72.1 0.5 collective-permute-start.19
  72.6 1.8 %collective-permute-done.19.refs_3_ = bf16[1024,128]{1,0:T(8,128)(2,1)S(1)} collective-permute-done((bf16[1024,128]{1,0:T(8,128)(2,1)S(1)}, bf16[1024,128]{1,0:T(8,128)(2,1)S(1)}, u32[]{:S(2)}, u32[]{:S(2)}) %collective-permute-start.19) | collective-permute-done | bytes 262176 | tf_op jit(solution)/shard_map/ppermute | solution.py:1227
  74.3 10.9 %shard_map.335 = (bf16[2176,768]{1,0:T(8,128)(2,1)S(1)}, f32[2048,256]{1,0:T(8,128)}, bf16[368,256]{1,0:T(8,128)(2,1)}, bf16[368,256]{1,0:T(8,128)(2,1)}, bf16[3...) custom-call(f32[16,256]{1,0:T(8,128)S(1)} %get-tuple-element.112.vec, bf16[12,64,256]{2,1,0:T(8,128)(2,1)S(1)} %get-tuple-element.136.qkv_t, ...), custom_call_target="tpu_custom_call" | custom-call | flops 15703474176 | bytes 14876672 | tf_op jit(solution)/shard_map/pallas_call | solution.py:1258
  85.3 2.5 %collective-permute-start.22 = (bf16[368,256]{1,0:T(8,128)(2,1)}, bf16[368,256]{1,0:T(8,128)(2,1)S(1)}, u32[]{:S(2)}, u32[]{:S(2)}) collective-permute-start(bf16[368,256]{1,0:T(8,128)(2,1)} %get-tuple-element.156), channel_id=1, source_target_pairs={{0,24},{8,16},{16,8},{24,0},{1,25},{9,17},{17,9},{25,1},{2,26},{10... | collective-permute-start | bytes 565256 | tf_op jit(solution)/shard_map/ppermute | solution.py:1227
  87.8 0.5 collective-permute-start.21
  88.3 0.5 collective-permute-start.20
  88.8 1.7 %collective-permute-start.24 = (bf16[256,128]{1,0:T(8,128)(2,1)S(1)}, bf16[256,128]{1,0:T(8,128)(2,1)S(1)}, u32[]{:S(2)}, u32[]{:S(2)}) collective-permute-start(bf16[256,128]{1,0:T(8,128)(2,1)S(1)} %get-tuple-element.159), channel_id=1, source_target_pairs={{0,2},{1,3},{2,0},{3,1},{4,6},{5,7},{6,4},{7,5},{8,10},{9,11},{10,... | collective-permute-start | bytes 196616 | tf_op jit(solution)/shard_map/ppermute | solution.py:1227
  90.6 3.5 %collective-permute-done.22 = bf16[368,256]{1,0:T(8,128)(2,1)S(1)} collective-permute-done((bf16[368,256]{1,0:T(8,128)(2,1)}, bf16[368,256]{1,0:T(8,128)(2,1)S(1)}, u32[]{:S(2)}, u32[]{:S(2)}) %collective-permute-start.22) | collective-permute-done | bytes 188448 | tf_op jit(solution)/shard_map/ppermute | solution.py:1227
  94.1 3.2 %collective-permute-done.21 = bf16[368,256]{1,0:T(8,128)(2,1)S(1)} collective-permute-done((bf16[368,256]{1,0:T(8,128)(2,1)}, bf16[368,256]{1,0:T(8,128)(2,1)S(1)}, u32[]{:S(2)}, u32[]{:S(2)}) %collective-permute-start.21) | collective-permute-done | bytes 188448 | tf_op jit(solution)/shard_map/ppermute | solution.py:1227
  97.4 1.0 add_convert_fusion.1
  98.4 3.8 %collective-permute-start.26 = (bf16[368,256]{1,0:T(8,128)(2,1)S(1)}, bf16[368,256]{1,0:T(8,128)(2,1)S(1)}, u32[]{:S(2)}, u32[]{:S(2)}) collective-permute-start(bf16[368,256]{1,0:T(8,128)(2,1)S(1)} %add_convert_fusion.1), channel_id=1, source_target_pairs={{0,4},{1,5},{2,6},{3,7},{4,0},{5,1},{6,2},{7,3},{8,12},{9,13},{10,... | collective-permute-start | bytes 565256 | tf_op jit(solution)/shard_map/ppermute | solution.py:1227
  102.2 6.7 %shard_map.337 = (bf16[256,256]{1,0:T(8,128)(2,1)}, bf16[256,256]{1,0:T(8,128)(2,1)}, f32[8,256]{1,0:T(8,128)}) custom-call(f32[16,256]{1,0:T(8,128)S(1)} %get-tuple-element.112.vec, bf16[2176,768]{1,0:T(8,128)(2,1)S(1)} %get-tuple-element.166.shifted, bf16[3,768,256]{2,1,0:T(8,128)(2,1)} %get-tuple-element.167.weight_far, ...), custom_call_target="tpu_custom_call" | custom-call | flops 7247757312 | bytes 7692288 | tf_op jit(solution)/shard_map/pallas_call | solution.py:1258
  109.0 1.6 %shard_map.336 = (bf16[256,256]{1,0:T(8,128)(2,1)S(1)}, bf16[256,256]{1,0:T(8,128)(2,1)S(1)}) custom-call(f32[16,256]{1,0:T(8,128)S(1)} %get-tuple-element.112.vec, bf16[4,64,256]{2,1,0:T(8,128)(2,1)S(1)} %bitcast.26, bf16[256,128]{1,0:T(8,128)(2,1)S(1)} %get-tuple-element.161.refs_0_, bf16[256,128]{1,0:T(8,128)(2,1)S(1)} %collective-permute-done.23.refs_1_, ...), custom_call_target="tpu_custom_call" | custom-call | flops 603979776 | bytes 2506752 | tf_op jit(solution)/shard_map/pallas_call | solution.py:1258
  110.5 0.5 collective-permute-done.26
  111.1 1.5 %collective-permute-start.27 = (bf16[128,256]{1,0:T(8,128)(2,1)S(1)}, bf16[128,256]{1,0:T(8,128)(2,1)S(1)}, u32[]{:S(2)}, u32[]{:S(2)}) collective-permute-start(bf16[128,256]{1,0:T(8,128)(2,1)S(1)} %slice.19), channel_id=1, source_target_pairs={{0,8},{8,0},{16,24},{24,16},{1,9},{9,1},{17,25},{25,17},{2,10},{10... | collective-permute-start | bytes 196616 | tf_op jit(solution)/shard_map/ppermute | solution.py:1227
  113.0 1.7 %collective-permute-start.29 = (bf16[128,256]{1,0:T(8,128)(2,1)S(1)}, bf16[128,256]{1,0:T(8,128)(2,1)S(1)}, u32[]{:S(2)}, u32[]{:S(2)}) collective-permute-start(bf16[128,256]{1,0:T(8,128)(2,1)S(1)} %slice.19), channel_id=1, source_target_pairs={{0,24},{8,16},{16,8},{24,0},{1,25},{9,17},{17,9},{25,1},{2,26},{10... | collective-permute-start | bytes 196616 | tf_op jit(solution)/shard_map/ppermute | solution.py:1227
  114.8 2.9 %collective-permute-start.31 = (bf16[240,256]{1,0:T(8,128)(2,1)S(1)}, bf16[240,256]{1,0:T(8,128)(2,1)S(1)}, u32[]{:S(2)}, u32[]{:S(2)}) collective-permute-start(bf16[240,256]{1,0:T(8,128)(2,1)S(1)} %slice.20), channel_id=1, source_target_pairs={{0,2},{1,3},{2,0},{3,1},{4,6},{5,7},{6,4},{7,5},{8,10},{9,11},{10,... | collective-permute-start | bytes 368648 | tf_op jit(solution)/shard_map/ppermute | solution.py:1227
  117.7 0.5 collective-permute-done.29
  118.3 1.0 collective-permute-done.32
  119.4 2.9 %collective-permute-start.37 = (bf16[512,256]{1,0:T(8,128)(2,1)S(1)}, bf16[512,256]{1,0:T(8,128)(2,1)S(1)}, u32[]{:S(2)}, u32[]{:S(2)}) collective-permute-start(bf16[512,256]{1,0:T(8,128)(2,1)S(1)} %pad_maximum_fusion.3.refs_8_), channel_id=1, source_target_pairs={{0,2},{1,3},{2,0},{3,1},{4,6},{5,7},{6,4},{7,5},{8,10},{9,11},{10,... | collective-permute-start | bytes 786440 | tf_op jit(solution)/shard_map/ppermute | solution.py:1227
  122.3 0.8 collective-permute-start.33
  123.1 2.2 %collective-permute-start.34 = (bf16[496,256]{1,0:T(8,128)(2,1)S(1)}, bf16[496,256]{1,0:T(8,128)(2,1)S(1)}, u32[]{:S(2)}, u32[]{:S(2)}) collective-permute-start(bf16[496,256]{1,0:T(8,128)(2,1)S(1)} %pad_maximum_fusion.4.refs_0_), channel_id=1, source_target_pairs={{0,16},{8,24},{16,0},{24,8},{1,17},{9,25},{17,1},{25,9},{2,18},{10... | collective-permute-start | bytes 761864 | tf_op jit(solution)/shard_map/ppermute | solution.py:1227
  125.3 0.5 collective-permute-start.35
  125.8 6.1 %collective-permute-done.30 = bf16[2,256,256]{2,1,0:T(8,128)(2,1)S(1)} collective-permute-done((bf16[2,256,256]{2,1,0:T(8,128)(2,1)S(1)}, bf16[2,256,256]{2,1,0:T(8,128)(2,1)S(1)}, u32[]{:S(2)}, u32[]{:S(2)}) %collective-permute-start.30) | collective-permute-done | bytes 262176 | tf_op jit(solution)/shard_map/ppermute | solution.py:1227
  132.0 2.0 %collective-permute-done.34.refs_4_ = bf16[496,256]{1,0:T(8,128)(2,1)S(1)} collective-permute-done((bf16[496,256]{1,0:T(8,128)(2,1)S(1)}, bf16[496,256]{1,0:T(8,128)(2,1)S(1)}, u32[]{:S(2)}, u32[]{:S(2)}) %collective-permute-start.34) | collective-permute-done | bytes 253984 | tf_op jit(solution)/shard_map/ppermute | solution.py:1227
  134.0 0.5 collective-permute-start.39
  134.6 0.4 collective-permute-start.41
  135.2 0.8 pad_maximum_fusion
  137.0 4.6 %shard_map.338 = (f32[9,256,256]{2,1,0:T(8,128)}, f32[9,256,256]{2,1,0:T(8,128)}, f32[256,768]{1,0:T(8,128)}, f32[256,256]{1,0:T(8,128)}, f32[1024,512]{1,0:T(8,...) custom-call(bf16[496,256]{1,0:T(8,128)(2,1)S(1)} %pad_maximum_fusion, ...), custom_call_target="tpu_custom_call" | custom-call | flops 603979776 | bytes 3082240 | tf_op jit(solution)/shard_map/pallas_call | solution.py:1258
  (104 shorter events, 4.6 us)
Async XLA Ops:
  1.8 12.6 %copy-start.5 = (bf16[256,256]{1,0:T(8,128)(2,1)}, bf16[256,256]{1,0:T(8,128)(2,1)S(1)}, u32[]{:S(2)}) copy-start(bf16[256,256]{1,0:T(8,128)(2,1)S(1)} %get-tuple-element.211.refs_3_) | copy-start | bytes 393220
  1.8 12.5 %copy-start.3 = (bf16[2,4,64,256]{3,2,1,0:T(8,128)(2,1)S(1)}, bf16[2,4,64,256]{3,2,1,0:T(8,128)(2,1)}, u32[]{:S(2)}) copy-start(bf16[2,4,64,256]{3,2,1,0:T(8,128)(2,1)} %param.39) | copy-start | bytes 786436
  1.8 14.1 %collective-permute-start.1 = (bf16[256,256]{1,0:T(8,128)(2,1)S(1)}, bf16[256,256]{1,0:T(8,128)(2,1)S(1)}, u32[]{:S(2)}, u32[]{:S(2)}) collective-permute-start(bf16[256,256]{1,0:T(8,128)(2,1)S(1)} %get-tuple-element.210), channel_id=1, source_target_pairs={{0,4},{1,5},{2,6},{3,7},{4,0},{5,1},{6,2},{7,3},{8,12},{9,13},{10,... | collective-permute-start | bytes 393224 | tf_op jit(solution)/shard_map/ppermute | solution.py:1227
  5.9 10.0 %collective-permute-start.2 = (bf16[256,256]{1,0:T(8,128)(2,1)S(1)}, bf16[256,256]{1,0:T(8,128)(2,1)S(1)}, u32[]{:S(2)}, u32[]{:S(2)}) collective-permute-start(bf16[256,256]{1,0:T(8,128)(2,1)S(1)} %get-tuple-element.210), channel_id=1, source_target_pairs={{0,6},{1,7},{2,4},{3,5},{4,2},{5,3},{6,0},{7,1},{8,14},{9,15},{10,... | collective-permute-start | bytes 393224 | tf_op jit(solution)/shard_map/ppermute | solution.py:1227
  7.2 9.2 %collective-permute-start = (bf16[256,256]{1,0:T(8,128)(2,1)S(1)}, bf16[256,256]{1,0:T(8,128)(2,1)S(1)}, u32[]{:S(2)}, u32[]{:S(2)}) collective-permute-start(bf16[256,256]{1,0:T(8,128)(2,1)S(1)} %get-tuple-element.211.refs_3_), channel_id=1, source_target_pairs={{0,2},{1,3},{2,0},{3,1},{4,6},{5,7},{6,4},{7,5},{8,10},{9,11},{10,... | collective-permute-start | bytes 393224 | tf_op jit(solution)/shard_map/ppermute | solution.py:1227
  7.5 13.7 %collective-permute-start.6 = (bf16[256,256]{1,0:T(8,128)(2,1)S(1)}, bf16[256,256]{1,0:T(8,128)(2,1)S(1)}, u32[]{:S(2)}, u32[]{:S(2)}) collective-permute-start(bf16[256,256]{1,0:T(8,128)(2,1)S(1)} %get-tuple-element.211.refs_3_), channel_id=1, source_target_pairs={{0,1},{1,0},{2,3},{3,2},{4,5},{5,4},{6,7},{7,6},{8,9},{9,8},{10,11... | collective-permute-start | bytes 393224 | tf_op jit(solution)/shard_map/ppermute | solution.py:1227
  14.3 17.7 %copy-start.4 = (bf16[256,256]{1,0:T(8,128)(2,1)}, bf16[256,256]{1,0:T(8,128)(2,1)S(1)}, u32[]{:S(2)}) copy-start(bf16[256,256]{1,0:T(8,128)(2,1)S(1)} %get-tuple-element.124.refs_3_) | copy-start | bytes 393220
  16.4 5.1 %collective-permute-start.3 = (bf16[256,256]{1,0:T(8,128)(2,1)S(1)}, bf16[256,256]{1,0:T(8,128)(2,1)S(1)}, u32[]{:S(2)}, u32[]{:S(2)}) collective-permute-start(bf16[256,256]{1,0:T(8,128)(2,1)S(1)} %collective-permute-done.refs_5_), channel_id=1, source_target_pairs={{0,1},{1,0},{2,3},{3,2},{4,5},{5,4},{6,7},{7,6},{8,9},{9,8},{10,11... | collective-permute-start | bytes 393224 | tf_op jit(solution)/shard_map/ppermute | solution.py:1227
  16.4 5.4 %collective-permute-start.4 = (bf16[256,256]{1,0:T(8,128)(2,1)S(1)}, bf16[256,256]{1,0:T(8,128)(2,1)S(1)}, u32[]{:S(2)}, u32[]{:S(2)}) collective-permute-start(bf16[256,256]{1,0:T(8,128)(2,1)S(1)} %collective-permute-done.1.refs_6_), channel_id=1, source_target_pairs={{0,1},{1,0},{2,3},{3,2},{4,5},{5,4},{6,7},{7,6},{8,9},{9,8},{10,11... | collective-permute-start | bytes 393224 | tf_op jit(solution)/shard_map/ppermute | solution.py:1227
  16.9 4.9 %collective-permute-start.5 = (bf16[256,256]{1,0:T(8,128)(2,1)S(1)}, bf16[256,256]{1,0:T(8,128)(2,1)S(1)}, u32[]{:S(2)}, u32[]{:S(2)}) collective-permute-start(bf16[256,256]{1,0:T(8,128)(2,1)S(1)} %collective-permute-done.2.refs_7_), channel_id=1, source_target_pairs={{0,1},{1,0},{2,3},{3,2},{4,5},{5,4},{6,7},{7,6},{8,9},{9,8},{10,11... | collective-permute-start | bytes 393224 | tf_op jit(solution)/shard_map/ppermute | solution.py:1227
  16.9 15.3 %collective-permute-start.8 = (bf16[256,256]{1,0:T(8,128)(2,1)S(1)}, bf16[256,256]{1,0:T(8,128)(2,1)S(1)}, u32[]{:S(2)}, u32[]{:S(2)}) collective-permute-start(bf16[256,256]{1,0:T(8,128)(2,1)S(1)} %get-tuple-element.125), channel_id=1, source_target_pairs={{0,4},{1,5},{2,6},{3,7},{4,0},{5,1},{6,2},{7,3},{8,12},{9,13},{10,... | collective-permute-start | bytes 393224 | tf_op jit(solution)/shard_map/ppermute | solution.py:1227
  21.2 11.1 %collective-permute-start.9 = (bf16[256,256]{1,0:T(8,128)(2,1)S(1)}, bf16[256,256]{1,0:T(8,128)(2,1)S(1)}, u32[]{:S(2)}, u32[]{:S(2)}) collective-permute-start(bf16[256,256]{1,0:T(8,128)(2,1)S(1)} %get-tuple-element.125), channel_id=1, source_target_pairs={{0,6},{1,7},{2,4},{3,5},{4,2},{5,3},{6,0},{7,1},{8,14},{9,15},{10,... | collective-permute-start | bytes 393224 | tf_op jit(solution)/shard_map/ppermute | solution.py:1227
  21.6 10.7 %collective-permute-start.7 = (bf16[256,256]{1,0:T(8,128)(2,1)S(1)}, bf16[256,256]{1,0:T(8,128)(2,1)S(1)}, u32[]{:S(2)}, u32[]{:S(2)}) collective-permute-start(bf16[256,256]{1,0:T(8,128)(2,1)S(1)} %get-tuple-element.124.refs_3_), channel_id=1, source_target_pairs={{0,2},{1,3},{2,0},{3,1},{4,6},{5,7},{6,4},{7,5},{8,10},{9,11},{10,... | collective-permute-start | bytes 393224 | tf_op jit(solution)/shard_map/ppermute | solution.py:1227
  21.8 11.4 %collective-permute-start.13 = (bf16[256,256]{1,0:T(8,128)(2,1)S(1)}, bf16[256,256]{1,0:T(8,128)(2,1)S(1)}, u32[]{:S(2)}, u32[]{:S(2)}) collective-permute-start(bf16[256,256]{1,0:T(8,128)(2,1)S(1)} %get-tuple-element.124.refs_3_), channel_id=1, source_target_pairs={{0,1},{1,0},{2,3},{3,2},{4,5},{5,4},{6,7},{7,6},{8,9},{9,8},{10,11... | collective-permute-start | bytes 393224 | tf_op jit(solution)/shard_map/ppermute | solution.py:1227
  32.1 19.8 %copy-start.2 = (bf16[2048,256]{1,0:T(8,128)(2,1)}, bf16[2048,256]{1,0:T(8,128)(2,1)S(1)}, u32[]{:S(2)}) copy-start(bf16[2048,256]{1,0:T(8,128)(2,1)S(1)} %get-tuple-element.120.act_three.refs_4_) | copy-start | bytes 3145732
  32.3 1.4 collective-permute-start.10
  32.7 1.3 collective-permute-start.11
  32.8 1.4 collective-permute-start.12
  51.9 20.1 %collective-permute-start.14 = (bf16[2048,128]{1,0:T(8,128)(2,1)}, bf16[2048,128]{1,0:T(8,128)(2,1)S(1)}, u32[]{:S(2)}, u32[]{:S(2)}) collective-permute-start(bf16[2048,128]{1,0:T(8,128)(2,1)} %get-tuple-element.130.refs_3_.refs_4_), channel_id=1, source_target_pairs={{0,2},{1,3},{2,0},{3,1},{4,6},{5,7},{6,4},{7,5},{8,10},{9,11},{10,... | collective-permute-start | bytes 1572872 | tf_op jit(solution)/shard_map/ppermute | solution.py:1227
  53.9 18.1 %collective-permute-start.16 = (bf16[2048,128]{1,0:T(8,128)(2,1)}, bf16[2048,128]{1,0:T(8,128)(2,1)S(1)}, u32[]{:S(2)}, u32[]{:S(2)}) collective-permute-start(bf16[2048,128]{1,0:T(8,128)(2,1)} %get-tuple-element.130.refs_3_.refs_4_), channel_id=1, source_target_pairs={{0,1},{1,0},{2,3},{3,2},{4,5},{5,4},{6,7},{7,6},{8,9},{9,8},{10,11... | collective-permute-start | bytes 1572872 | tf_op jit(solution)/shard_map/ppermute | solution.py:1227
  53.9 18.1 %collective-permute-start.15 = (bf16[1024,128]{1,0:T(8,128)(2,1)}, bf16[1024,128]{1,0:T(8,128)(2,1)S(1)}, u32[]{:S(2)}, u32[]{:S(2)}) collective-permute-start(bf16[1024,128]{1,0:T(8,128)(2,1)} %get-tuple-element.137.refs_5_), channel_id=1, source_target_pairs={{0,2},{1,3},{2,0},{3,1},{4,6},{5,7},{6,4},{7,5},{8,10},{9,11},{10,... | collective-permute-start | bytes 786440 | tf_op jit(solution)/shard_map/ppermute | solution.py:1227
  54.1 17.8 %collective-permute-start.17 = (bf16[1024,128]{1,0:T(8,128)(2,1)}, bf16[1024,128]{1,0:T(8,128)(2,1)S(1)}, u32[]{:S(2)}, u32[]{:S(2)}) collective-permute-start(bf16[1024,128]{1,0:T(8,128)(2,1)} %get-tuple-element.137.refs_5_), channel_id=1, source_target_pairs={{0,1},{1,0},{2,3},{3,2},{4,5},{5,4},{6,7},{7,6},{8,9},{9,8},{10,11... | collective-permute-start | bytes 786440 | tf_op jit(solution)/shard_map/ppermute | solution.py:1227
  72.0 2.4 %collective-permute-start.18 = (bf16[2048,128]{1,0:T(8,128)(2,1)S(1)}, bf16[2048,128]{1,0:T(8,128)(2,1)S(1)}, u32[]{:S(2)}, u32[]{:S(2)}) collective-permute-start(bf16[2048,128]{1,0:T(8,128)(2,1)S(1)} %collective-permute-done.14.refs_6_), channel_id=1, source_target_pairs={{0,1},{1,0},{2,3},{3,2},{4,5},{5,4},{6,7},{7,6},{8,9},{9,8},{10,11... | collective-permute-start | bytes 1572872 | tf_op jit(solution)/shard_map/ppermute | solution.py:1227
  72.1 2.3 %collective-permute-start.19 = (bf16[1024,128]{1,0:T(8,128)(2,1)S(1)}, bf16[1024,128]{1,0:T(8,128)(2,1)S(1)}, u32[]{:S(2)}, u32[]{:S(2)}) collective-permute-start(bf16[1024,128]{1,0:T(8,128)(2,1)S(1)} %collective-permute-done.15.refs_7_), channel_id=1, source_target_pairs={{0,1},{1,0},{2,3},{3,2},{4,5},{5,4},{6,7},{7,6},{8,9},{9,8},{10,11... | collective-permute-start | bytes 786440 | tf_op jit(solution)/shard_map/ppermute | solution.py:1227
  85.3 8.8 %collective-permute-start.22 = (bf16[368,256]{1,0:T(8,128)(2,1)}, bf16[368,256]{1,0:T(8,128)(2,1)S(1)}, u32[]{:S(2)}, u32[]{:S(2)}) collective-permute-start(bf16[368,256]{1,0:T(8,128)(2,1)} %get-tuple-element.156), channel_id=1, source_target_pairs={{0,24},{8,16},{16,8},{24,0},{1,25},{9,17},{17,9},{25,1},{2,26},{10... | collective-permute-start | bytes 565256 | tf_op jit(solution)/shard_map/ppermute | solution.py:1227
  87.8 9.4 %collective-permute-start.21 = (bf16[368,256]{1,0:T(8,128)(2,1)}, bf16[368,256]{1,0:T(8,128)(2,1)S(1)}, u32[]{:S(2)}, u32[]{:S(2)}) collective-permute-start(bf16[368,256]{1,0:T(8,128)(2,1)} %get-tuple-element.155), channel_id=1, source_target_pairs={{0,16},{8,24},{16,0},{24,8},{1,17},{9,25},{17,1},{25,9},{2,18},{10... | collective-permute-start | bytes 565256 | tf_op jit(solution)/shard_map/ppermute | solution.py:1227
  88.3 9.1 %collective-permute-start.20 = (bf16[368,256]{1,0:T(8,128)(2,1)}, bf16[368,256]{1,0:T(8,128)(2,1)S(1)}, u32[]{:S(2)}, u32[]{:S(2)}) collective-permute-start(bf16[368,256]{1,0:T(8,128)(2,1)} %get-tuple-element.154), channel_id=1, source_target_pairs={{0,8},{8,0},{16,24},{24,16},{1,9},{9,1},{17,25},{25,17},{2,10},{10... | collective-permute-start | bytes 565256 | tf_op jit(solution)/shard_map/ppermute | solution.py:1227
  88.8 9.6 %collective-permute-start.23 = (bf16[256,128]{1,0:T(8,128)(2,1)S(1)}, bf16[256,128]{1,0:T(8,128)(2,1)S(1)}, u32[]{:S(2)}, u32[]{:S(2)}) collective-permute-start(bf16[256,128]{1,0:T(8,128)(2,1)S(1)} %get-tuple-element.158), channel_id=1, source_target_pairs={{0,1},{1,0},{2,3},{3,2},{4,5},{5,4},{6,7},{7,6},{8,9},{9,8},{10,11... | collective-permute-start | bytes 196616 | tf_op jit(solution)/shard_map/ppermute | solution.py:1227
  88.8 9.6 %collective-permute-start.24 = (bf16[256,128]{1,0:T(8,128)(2,1)S(1)}, bf16[256,128]{1,0:T(8,128)(2,1)S(1)}, u32[]{:S(2)}, u32[]{:S(2)}) collective-permute-start(bf16[256,128]{1,0:T(8,128)(2,1)S(1)} %get-tuple-element.159), channel_id=1, source_target_pairs={{0,2},{1,3},{2,0},{3,1},{4,6},{5,7},{6,4},{7,5},{8,10},{9,11},{10,... | collective-permute-start | bytes 196616 | tf_op jit(solution)/shard_map/ppermute | solution.py:1227
  94.1 4.4 %collective-permute-start.25 = (bf16[256,128]{1,0:T(8,128)(2,1)S(1)}, bf16[256,128]{1,0:T(8,128)(2,1)S(1)}, u32[]{:S(2)}, u32[]{:S(2)}) collective-permute-start(bf16[256,128]{1,0:T(8,128)(2,1)S(1)} %get-tuple-element.160), channel_id=1, source_target_pairs={{0,3},{1,2},{2,1},{3,0},{4,7},{5,6},{6,5},{7,4},{8,11},{9,10},{10,... | collective-permute-start | bytes 196616 | tf_op jit(solution)/shard_map/ppermute | solution.py:1227
  98.4 12.6 %collective-permute-start.26 = (bf16[368,256]{1,0:T(8,128)(2,1)S(1)}, bf16[368,256]{1,0:T(8,128)(2,1)S(1)}, u32[]{:S(2)}, u32[]{:S(2)}) collective-permute-start(bf16[368,256]{1,0:T(8,128)(2,1)S(1)} %add_convert_fusion.1), channel_id=1, source_target_pairs={{0,4},{1,5},{2,6},{3,7},{4,0},{5,1},{6,2},{7,3},{8,12},{9,13},{10,... | collective-permute-start | bytes 565256 | tf_op jit(solution)/shard_map/ppermute | solution.py:1227
  108.9 26.2 %copy-start.7 = (bf16[256,256]{1,0:T(8,128)(2,1)S(1)}, bf16[256,256]{1,0:T(8,128)(2,1)}, u32[]{:S(2)}) copy-start(bf16[256,256]{1,0:T(8,128)(2,1)} %get-tuple-element.170) | copy-start | bytes 393220
  111.1 6.6 %collective-permute-start.27 = (bf16[128,256]{1,0:T(8,128)(2,1)S(1)}, bf16[128,256]{1,0:T(8,128)(2,1)S(1)}, u32[]{:S(2)}, u32[]{:S(2)}) collective-permute-start(bf16[128,256]{1,0:T(8,128)(2,1)S(1)} %slice.19), channel_id=1, source_target_pairs={{0,8},{8,0},{16,24},{24,16},{1,9},{9,1},{17,25},{25,17},{2,10},{10... | collective-permute-start | bytes 196616 | tf_op jit(solution)/shard_map/ppermute | solution.py:1227
  112.7 5.1 %collective-permute-start.28 = (bf16[128,256]{1,0:T(8,128)(2,1)S(1)}, bf16[128,256]{1,0:T(8,128)(2,1)S(1)}, u32[]{:S(2)}, u32[]{:S(2)}) collective-permute-start(bf16[128,256]{1,0:T(8,128)(2,1)S(1)} %slice.19), channel_id=1, source_target_pairs={{0,16},{8,24},{16,0},{24,8},{1,17},{9,25},{17,1},{25,9},{2,18},{10... | collective-permute-start | bytes 196616 | tf_op jit(solution)/shard_map/ppermute | solution.py:1227
  113.0 5.2 %collective-permute-start.29 = (bf16[128,256]{1,0:T(8,128)(2,1)S(1)}, bf16[128,256]{1,0:T(8,128)(2,1)S(1)}, u32[]{:S(2)}, u32[]{:S(2)}) collective-permute-start(bf16[128,256]{1,0:T(8,128)(2,1)S(1)} %slice.19), channel_id=1, source_target_pairs={{0,24},{8,16},{16,8},{24,0},{1,25},{9,17},{17,9},{25,1},{2,26},{10... | collective-permute-start | bytes 196616 | tf_op jit(solution)/shard_map/ppermute | solution.py:1227
  114.7 4.6 %collective-permute-start.32 = (bf16[16,256]{1,0:T(8,128)(2,1)S(1)}, bf16[16,256]{1,0:T(8,128)(2,1)S(1)}, u32[]{:S(2)}, u32[]{:S(2)}) collective-permute-start(bf16[16,256]{1,0:T(8,128)(2,1)S(1)} %concatenate.13), channel_id=1, source_target_pairs={{0,4},{1,5},{2,6},{3,7},{4,0},{5,1},{6,2},{7,3},{8,12},{9,13},{10,... | collective-permute-start | bytes 24584 | tf_op jit(solution)/shard_map/ppermute | solution.py:1227
  114.8 7.5 %collective-permute-start.31 = (bf16[240,256]{1,0:T(8,128)(2,1)S(1)}, bf16[240,256]{1,0:T(8,128)(2,1)S(1)}, u32[]{:S(2)}, u32[]{:S(2)}) collective-permute-start(bf16[240,256]{1,0:T(8,128)(2,1)S(1)} %slice.20), channel_id=1, source_target_pairs={{0,2},{1,3},{2,0},{3,1},{4,6},{5,7},{6,4},{7,5},{8,10},{9,11},{10,... | collective-permute-start | bytes 368648 | tf_op jit(solution)/shard_map/ppermute | solution.py:1227
  118.2 13.8 %collective-permute-start.30 = (bf16[2,256,256]{2,1,0:T(8,128)(2,1)S(1)}, bf16[2,256,256]{2,1,0:T(8,128)(2,1)S(1)}, u32[]{:S(2)}, u32[]{:S(2)}) collective-permute-start(bf16[2,256,256]{2,1,0:T(8,128)(2,1)S(1)} %pad_maximum_fusion.2), channel_id=1, source_target_pairs={{0,4},{1,5},{2,6},{3,7},{4,0},{5,1},{6,2},{7,3},{8,12},{9,13},{10,... | collective-permute-start | bytes 786440 | tf_op jit(solution)/shard_map/ppermute | solution.py:1227
  119.4 14.7 %collective-permute-start.37 = (bf16[512,256]{1,0:T(8,128)(2,1)S(1)}, bf16[512,256]{1,0:T(8,128)(2,1)S(1)}, u32[]{:S(2)}, u32[]{:S(2)}) collective-permute-start(bf16[512,256]{1,0:T(8,128)(2,1)S(1)} %pad_maximum_fusion.3.refs_8_), channel_id=1, source_target_pairs={{0,2},{1,3},{2,0},{3,1},{4,6},{5,7},{6,4},{7,5},{8,10},{9,11},{10,... | collective-permute-start | bytes 786440 | tf_op jit(solution)/shard_map/ppermute | solution.py:1227
  122.3 9.7 %collective-permute-start.33 = (bf16[496,256]{1,0:T(8,128)(2,1)S(1)}, bf16[496,256]{1,0:T(8,128)(2,1)S(1)}, u32[]{:S(2)}, u32[]{:S(2)}) collective-permute-start(bf16[496,256]{1,0:T(8,128)(2,1)S(1)} %pad_maximum_fusion.4.refs_0_), channel_id=1, source_target_pairs={{0,8},{8,0},{16,24},{24,16},{1,9},{9,1},{17,25},{25,17},{2,10},{10... | collective-permute-start | bytes 761864 | tf_op jit(solution)/shard_map/ppermute | solution.py:1227
  123.1 10.9 %collective-permute-start.34 = (bf16[496,256]{1,0:T(8,128)(2,1)S(1)}, bf16[496,256]{1,0:T(8,128)(2,1)S(1)}, u32[]{:S(2)}, u32[]{:S(2)}) collective-permute-start(bf16[496,256]{1,0:T(8,128)(2,1)S(1)} %pad_maximum_fusion.4.refs_0_), channel_id=1, source_target_pairs={{0,16},{8,24},{16,0},{24,8},{1,17},{9,25},{17,1},{25,9},{2,18},{10... | collective-permute-start | bytes 761864 | tf_op jit(solution)/shard_map/ppermute | solution.py:1227
  125.3 8.7 %collective-permute-start.35 = (bf16[496,256]{1,0:T(8,128)(2,1)S(1)}, bf16[496,256]{1,0:T(8,128)(2,1)S(1)}, u32[]{:S(2)}, u32[]{:S(2)}) collective-permute-start(bf16[496,256]{1,0:T(8,128)(2,1)S(1)} %pad_maximum_fusion.4.refs_0_), channel_id=1, source_target_pairs={{0,24},{8,16},{16,8},{24,0},{1,25},{9,17},{17,9},{25,1},{2,26},{10... | collective-permute-start | bytes 761864 | tf_op jit(solution)/shard_map/ppermute | solution.py:1227
  132.0 3.1 %collective-permute-start.36 = (bf16[496,256]{1,0:T(8,128)(2,1)S(1)}, bf16[496,256]{1,0:T(8,128)(2,1)S(1)}, u32[]{:S(2)}, u32[]{:S(2)}) collective-permute-start(bf16[496,256]{1,0:T(8,128)(2,1)S(1)} %pad_maximum_fusion.4.refs_0_), channel_id=1, source_target_pairs={{0,1},{1,0},{2,3},{3,2},{4,5},{5,4},{6,7},{7,6},{8,9},{9,8},{10,11... | collective-permute-start | bytes 761864 | tf_op jit(solution)/shard_map/ppermute | solution.py:1227
  134.0 2.0 %collective-permute-start.38 = (bf16[496,256]{1,0:T(8,128)(2,1)S(1)}, bf16[496,256]{1,0:T(8,128)(2,1)S(1)}, u32[]{:S(2)}, u32[]{:S(2)}) collective-permute-start(bf16[496,256]{1,0:T(8,128)(2,1)S(1)} %collective-permute-done.33.refs_2_), channel_id=1, source_target_pairs={{0,1},{1,0},{2,3},{3,2},{4,5},{5,4},{6,7},{7,6},{8,9},{9,8},{10,11... | collective-permute-start | bytes 761864 | tf_op jit(solution)/shard_map/ppermute | solution.py:1227
  134.0 2.0 %collective-permute-start.39 = (bf16[496,256]{1,0:T(8,128)(2,1)S(1)}, bf16[496,256]{1,0:T(8,128)(2,1)S(1)}, u32[]{:S(2)}, u32[]{:S(2)}) collective-permute-start(bf16[496,256]{1,0:T(8,128)(2,1)S(1)} %collective-permute-done.34.refs_4_), channel_id=1, source_target_pairs={{0,1},{1,0},{2,3},{3,2},{4,5},{5,4},{6,7},{7,6},{8,9},{9,8},{10,11... | collective-permute-start | bytes 761864 | tf_op jit(solution)/shard_map/ppermute | solution.py:1227
  134.5 1.7 %collective-permute-start.40 = (bf16[496,256]{1,0:T(8,128)(2,1)S(1)}, bf16[496,256]{1,0:T(8,128)(2,1)S(1)}, u32[]{:S(2)}, u32[]{:S(2)}) collective-permute-start(bf16[496,256]{1,0:T(8,128)(2,1)S(1)} %collective-permute-done.35.refs_6_), channel_id=1, source_target_pairs={{0,1},{1,0},{2,3},{3,2},{4,5},{5,4},{6,7},{7,6},{8,9},{9,8},{10,11... | collective-permute-start | bytes 761864 | tf_op jit(solution)/shard_map/ppermute | solution.py:1227
  134.6 2.0 %collective-permute-start.41 = (bf16[512,256]{1,0:T(8,128)(2,1)S(1)}, bf16[512,256]{1,0:T(8,128)(2,1)S(1)}, u32[]{:S(2)}, u32[]{:S(2)}) collective-permute-start(bf16[512,256]{1,0:T(8,128)(2,1)S(1)} %pad_maximum_fusion.3.refs_8_), channel_id=1, source_target_pairs={{0,1},{1,0},{2,3},{3,2},{4,5},{5,4},{6,7},{7,6},{8,9},{9,8},{10,11... | collective-permute-start | bytes 786440 | tf_op jit(solution)/shard_map/ppermute | solution.py:1227
  135.1 2.0 %collective-permute-start.42 = (bf16[512,256]{1,0:T(8,128)(2,1)S(1)}, bf16[512,256]{1,0:T(8,128)(2,1)S(1)}, u32[]{:S(2)}, u32[]{:S(2)}) collective-permute-start(bf16[512,256]{1,0:T(8,128)(2,1)S(1)} %collective-permute-done.37.refs_10_), channel_id=1, source_target_pairs={{0,1},{1,0},{2,3},{3,2},{4,5},{5,4},{6,7},{7,6},{8,9},{9,8},{10,11... | collective-permute-start | bytes 786440 | tf_op jit(solution)/shard_map/ppermute | solution.py:1227
  (14 other events, 59.9 us)
